TPU v7x, 32 devices: a whole 2x2x4 slice. The times are simulated.
32 devices in a mesh: pipe: 2 (over x), tensor: 4 (over z), dp: 4 (over y, core).
Axes of the slice: x: 2, y: 2, z: 4, core: 2. Of those that a mesh axis runs over, the one named last changes fastest.
Arguments:
- new_coeffs: bfloat16 [1024, 256], P('dp'), may hold values from -6 to 6
- loss_grad: bfloat16 [1024, 256], P('dp'), may hold values from -6 to 6
- sent_forward: bfloat16 [2, 1024, 256], P('pipe', 'dp'), may hold values from -6 to 6
- sent_backward: bfloat16 [2, 1024, 256], P('pipe', 'dp'), may hold values from -6 to 6
- stashed: bfloat16 [2, 1024, 256], P('pipe', 'dp'), may hold values from -6 to 6
- subspace: bfloat16 [4096, 256], replicated, may hold values from -0.09375 to 0.09375
- norm_gain: float32 [2, 4096], P('pipe'), may hold values from 0.5 to 1.5
- w_query: bfloat16 [2, 4096, 4096], P('pipe', None, 'tensor'), may hold values from -3 to 3
- w_key: bfloat16 [2, 4096, 512], P('pipe', None, 'tensor'), may hold values from -3 to 3
- w_value: bfloat16 [2, 4096, 512], P('pipe', None, 'tensor'), may hold values from -0.09375 to 0.09375
- w_output: bfloat16 [2, 4096, 4096], P('pipe', 'tensor'), may hold values from -0.09375 to 0.09375
Outputs:
- forward_out: bfloat16 [2, 1024, 256], P('pipe', 'dp')
- backward_out: bfloat16 [2, 1024, 256], P('pipe', 'dp')
- grad_query: bfloat16 [2, 4096, 4096], P('pipe', 'dp', 'tensor')
- grad_key: bfloat16 [2, 4096, 512], P('pipe', 'dp', 'tensor')
- grad_value: bfloat16 [2, 4096, 512], P('pipe', 'dp', 'tensor')
- grad_output: bfloat16 [2, 4096, 4096], P('pipe', 'tensor', 'dp')
- grad_gain: float32 [2, 4096], P('pipe')
All inputs are finite; a program needn't handle non-finite values.
Results may differ from a plain program's by a relative error of at most 0.015.
Values may be sent and summed in bfloat16 or wider, within the bound.
No kernel may reach another device: no remote copies, remote signals or barrier semaphores. Data moves between devices by JAX's collectives and lax.ppermute only.
A program may use at most 192 MiB of HBM per device.

v0:
```python
import functools
import math

import jax
import jax.numpy as jnp
import numpy as np
from jax import lax
from jax.experimental import pallas as pl
from jax.experimental.pallas import tpu as pltpu
from jax.sharding import PartitionSpec as P

HD = 128
EPSILON = 1e-05
ROPE_BASE = 500000.0
BF = jnp.bfloat16
F32 = jnp.float32
VMEM_BYTES = 28 * 1024 * 1024
LOG2E = 1.4426950408889634


def shifted(x, axis, by):
    devices = lax.axis_size(axis)
    pairs = [(i, i + by) for i in range(devices) if 0 <= i + by < devices]
    return lax.ppermute(x, axis, pairs)


def swap(x, axis, bit):
    devices = lax.axis_size(axis)
    return lax.ppermute(x, axis, [(i, i ^ bit) for i in range(devices)])


def cross_pipe(sent_forward, sent_backward):
    if lax.axis_size("pipe") != 2:
        return shifted(sent_forward, "pipe", 1), shifted(sent_backward, "pipe", -1)
    first = lax.axis_index("pipe") == 0
    got = swap(jnp.where(first, sent_forward, sent_backward), "pipe", 1)
    return got, got


def add_wide(a, b):
    return a.astype(F32) + b.astype(F32)


def nt(a, b):
    return lax.dot_general(a, b, (((1,), (1,)), ((), ())), preferred_element_type=F32)


def nn(a, b):
    return jnp.dot(a, b, preferred_element_type=F32)


def split(x, parts):
    out = []
    for _ in range(parts):
        piece = x.astype(BF)
        out.append(piece)
        x = x - piece.astype(F32)
    return out


def rope_tables(length):
    half = HD // 2
    frequency = np.float32(ROPE_BASE) ** (-2.0 * np.arange(half, dtype=np.float32) / HD)
    angles = np.arange(length, dtype=np.float32)[:, None] * frequency.astype(np.float32)
    cosine, sine = np.cos(angles), np.sin(angles)
    tables = (np.concatenate([cosine, cosine], 1), np.concatenate([-sine, sine], 1))
    return tuple(jnp.asarray(t, dtype=F32) for t in tables)


def rope(x, cosine, sine):
    return x * cosine + pltpu.roll(x, HD // 2, 1) * sine


def unrope(x, cosine, sine):
    return x * cosine - pltpu.roll(x, HD // 2, 1) * sine


def inverse_root(square_sum, width):
    return 1.0 / jnp.sqrt(square_sum / width + EPSILON)


def vmem(count):
    return [pl.BlockSpec(memory_space=pltpu.VMEM)] * count


def cost(flops, num_bytes, exps=0):
    return pl.CostEstimate(flops=flops, bytes_accessed=num_bytes, transcendentals=exps)


def project_kernel(
    wide, back_ref, u_ref, gain_ref, wq_ref, wk_ref, wv_ref, wo_ref,
    m_ref, o_ref, g_ref, inv_ref,
    m_acc, o_acc, g_acc, sq_acc,
):
    step = pl.program_id(0)
    rank = u_ref.shape[1]
    nq, nk = wq_ref.shape[1], wk_ref.shape[1]

    @pl.when(step == 0)
    def _():
        m_acc[...] = jnp.zeros_like(m_acc)
        o_acc[...] = jnp.zeros_like(o_acc)
        g_acc[...] = jnp.zeros_like(g_acc)
        sq_acc[...] = jnp.zeros_like(sq_acc)

    u = u_ref[...]
    ut = u.T
    scaled = (ut.astype(F32) * gain_ref[...]).astype(BF)
    for ref, at in ((wq_ref, 0), (wk_ref, nq), (wv_ref, nq + nk)):
        size = ref.shape[1]
        m_acc[:, at : at + size] += nn(scaled, ref[...])
    o_acc[...] += nn(wo_ref[...], u)
    g_acc[...] += nn(ut, u)
    decoded = nn(back_ref[...], ut)
    square = decoded * decoded
    sq_acc[...] += jnp.broadcast_to(jnp.sum(square, axis=1, keepdims=True), sq_acc.shape)

    @pl.when(step == pl.num_programs(0) - 1)
    def _():
        for i, piece in enumerate(split(m_acc[...], 2)):
            m_ref[i * rank : (i + 1) * rank, :] = piece
        o_ref[...] = o_acc[...].astype(BF)
        for i, piece in enumerate(split(g_acc[...], 3)):
            g_ref[i * rank : (i + 1) * rank, :] = piece
        inv_ref[...] = inverse_root(sq_acc[...], wide)


def project(back, basis, gain, wq, wk, wv, wo):
    wide, rank = basis.shape
    length = back.shape[0]
    nq, nk, nv, ne = wq.shape[1], wk.shape[1], wv.shape[1], wo.shape[0]
    block = 512
    rows = lambda i: (i, 0)
    cols = lambda i: (0, i)
    fixed = lambda i: (0, 0)
    total = nq + nk + nv
    return pl.pallas_call(
        functools.partial(project_kernel, wide),
        grid=(wide // block,),
        in_specs=[
            pl.BlockSpec((length, rank), fixed),
            pl.BlockSpec((block, rank), rows),
            pl.BlockSpec((1, block), cols),
            pl.BlockSpec((block, nq), rows),
            pl.BlockSpec((block, nk), rows),
            pl.BlockSpec((block, nv), rows),
            pl.BlockSpec((ne, block), cols),
        ],
        out_specs=[
            pl.BlockSpec((2 * rank, total), fixed),
            pl.BlockSpec((ne, rank), fixed),
            pl.BlockSpec((3 * rank, rank), fixed),
            pl.BlockSpec((length, HD), fixed),
        ],
        out_shape=[
            jax.ShapeDtypeStruct((2 * rank, total), BF),
            jax.ShapeDtypeStruct((ne, rank), BF),
            jax.ShapeDtypeStruct((3 * rank, rank), BF),
            jax.ShapeDtypeStruct((length, HD), F32),
        ],
        scratch_shapes=[
            pltpu.VMEM((rank, total), F32),
            pltpu.VMEM((ne, rank), F32),
            pltpu.VMEM((rank, rank), F32),
            pltpu.VMEM((length, HD), F32),
        ],
        compiler_params=pltpu.CompilerParams(vmem_limit_bytes=VMEM_BYTES),
        cost_estimate=cost(2 * wide * rank * (total + ne + 2 * rank), 2 * wide * (total + ne + rank)),
        name="project_weights",
    )(back, basis, gain, wq, wk, wv, wo)


def project_heads(coeffs, inv, m_ref, cosine, sine, q, k, v1):
    length = coeffs.shape[0]
    heads = q.shape[0] // length
    twice = jnp.concatenate([coeffs, coeffs], axis=1)
    for h in range(heads):
        part = nn(twice, m_ref[:, h * HD : (h + 1) * HD]) * inv
        q[h * length : (h + 1) * length, :] = rope(part, cosine, sine).astype(BF)
    part = nn(twice, m_ref[:, heads * HD :]) * inv
    k[...] = rope(part[:, :HD], cosine, sine).astype(BF)
    v1[:, :HD] = part[:, HD:].astype(BF)
    v1[:, HD:] = jnp.ones_like(v1[:, HD:])


def exps_of(scores, exps, low, length):
    row = lax.broadcasted_iota(jnp.int32, (length, length), 0)
    column = lax.broadcasted_iota(jnp.int32, (length, length), 1)
    causal = row >= column

    def one(h, _):
        at = pl.ds(pl.multiple_of(h * length, length), length)
        s = jnp.where(causal, scores[at, :], -jnp.inf)
        top = jnp.max(s, axis=1, keepdims=True)
        e = jnp.exp2((s - top) * (LOG2E / math.sqrt(HD)))
        if exps is not None:
            exps[at, :] = e
        low[at, :] = e.astype(BF)
        return 0

    lax.fori_loop(0, scores.shape[0] // length, one, 0, unroll=2)


def backward_kernel(
    back_ref, loss_ref, sent_ref, m_ref, o_ref, g_ref, inv_ref, cos_ref, sin_ref,
    inner_ref, give_ref, keep_ref, x_ref, base_ref, unit_ref,
    q, k, v1, gh, ghs, scores, low, mixed, gp, ds, dq, heads, grads,
):
    length, rank = back_ref.shape
    ne = o_ref.shape[0]
    count = ne // HD
    scale = 1.0 / math.sqrt(HD)
    last = lax.axis_size("pipe") - 1
    is_last = lax.axis_index("pipe") == last
    back = back_ref[...]
    up = jnp.where(is_last, loss_ref[...], sent_ref[...])
    cosine, sine = cos_ref[...], sin_ref[...]
    inv = inv_ref[...]
    project_heads(back, inv[:, :1], m_ref, cosine, sine, q, k, v1)
    scores[...] = nt(q[...], k[...])
    for h in range(count):
        gh[h * length : (h + 1) * length, :] = nt(up, o_ref[h * HD : (h + 1) * HD, :]).astype(BF)
    exps_of(scores, scores, low, length)
    mixed[...] = nn(low[...], v1[...])
    gp[...] = nt(gh[...], v1[:, :HD])

    for h in range(count):
        at = slice(h * length, (h + 1) * length)
        inverse = 1.0 / mixed[at, HD:]
        out = mixed[at, :HD] * inverse
        heads[:, h * HD : (h + 1) * HD] = out.astype(BF)
        grad = gh[at, :].astype(F32)
        ghs[at, :] = (grad * inverse).astype(BF)
        delta = jnp.sum(grad * out, axis=1, keepdims=True)
        factor = inverse * scale
        for side in range(0, length, HD):
            part = scores[at, side : side + HD] * factor
            ds[at, side : side + HD] = (part * (gp[at, side : side + HD] - delta)).astype(BF)

    dq[...] = nn(ds[...], k[...])
    for h in range(count):
        part = dq[h * length : (h + 1) * length, :]
        grads[:, h * HD : (h + 1) * HD] = unrope(part, cosine, sine).astype(BF)
    dk = nn(q[...].T, ds[...]).T
    grads[:, ne : ne + HD] = unrope(dk, cosine, sine).astype(BF)
    grads[:, ne + HD :] = nn(ghs[...].T, low[...]).T.astype(BF)
    total = grads.shape[1]
    unit = (back.astype(F32) * inv[:, :1]).astype(BF)
    inner_ref[:, :total] = nn(unit.T, grads[...]).astype(BF)
    inner_ref[:, total:] = nn(up.T, heads[...]).astype(BF)
    half = rank // 2
    core = lax.axis_index("dp") % 2
    give_ref[...] = inner_ref[pl.ds(pl.multiple_of((1 - core) * half, half), half), :]
    keep_ref[...] = inner_ref[pl.ds(pl.multiple_of(core * half, half), half), :]
    x_ref[...] = nt(grads[...], m_ref[:rank, :]).astype(BF)
    base_ref[...] = nn(jnp.concatenate([up] * 3, axis=1), g_ref[...])
    unit_ref[...] = nn(jnp.concatenate([back] * 3, axis=1), g_ref[...]) * inv[:, :1]


def backward(back, loss, sent, m2, o2, g3, inv, cosine, sine):
    length, rank = back.shape
    total = m2.shape[1]
    ne = o2.shape[0]
    assert total == ne + 2 * HD
    width = total + ne
    stack = ne // HD * length
    return pl.pallas_call(
        backward_kernel,
        in_specs=vmem(9),
        out_specs=vmem(6),
        out_shape=[
            jax.ShapeDtypeStruct((rank, width), BF),
            jax.ShapeDtypeStruct((rank // 2, width), BF),
            jax.ShapeDtypeStruct((rank // 2, width), BF),
            jax.ShapeDtypeStruct((length, rank), BF),
            jax.ShapeDtypeStruct((length, rank), F32),
            jax.ShapeDtypeStruct((length, rank), F32),
        ],
        scratch_shapes=[
            pltpu.VMEM((stack, HD), BF),
            pltpu.VMEM((length, HD), BF),
            pltpu.VMEM((length, 2 * HD), BF),
            pltpu.VMEM((stack, HD), BF),
            pltpu.VMEM((stack, HD), BF),
            pltpu.VMEM((stack, length), F32),
            pltpu.VMEM((stack, length), BF),
            pltpu.VMEM((stack, 2 * HD), F32),
            pltpu.VMEM((stack, length), F32),
            pltpu.VMEM((stack, length), BF),
            pltpu.VMEM((stack, HD), F32),
            pltpu.VMEM((length, ne), BF),
            pltpu.VMEM((length, total), BF),
        ],
        compiler_params=pltpu.CompilerParams(vmem_limit_bytes=VMEM_BYTES),
        cost_estimate=cost(2 * 1200 * 10**6, 8 * 10**6, 8 * 65536),
        name="attention_backward",
    )(back, loss, sent, m2, o2, g3, inv, cosine, sine)


def forward_kernel(
    new_ref, sent_ref, u_ref, m_ref, o_ref, g_ref, cos_ref, sin_ref,
    y_ref, base_ref,
    q, k, v1, scores, low, mixed, heads,
):
    length, rank = new_ref.shape
    wide = u_ref.shape[0]
    is_first = lax.axis_index("pipe") == 0
    coeffs = jnp.where(is_first, new_ref[...], sent_ref[...])
    square = jnp.zeros((length, HD), F32)
    block = 512
    for at in range(0, wide, block):
        decoded = nt(coeffs, u_ref[at : at + block, :])
        for side in range(0, block, HD):
            part = decoded[:, side : side + HD]
            square = square + part * part
    inv = inverse_root(jnp.sum(square, axis=1, keepdims=True), wide)
    project_heads(coeffs, inv, m_ref, cos_ref[...], sin_ref[...], q, k, v1)
    scores[...] = nt(q[...], k[...])
    exps_of(scores, None, low, length)
    mixed[...] = nn(low[...], v1[...])
    for h in range(heads.shape[1] // HD):
        at = slice(h * length, (h + 1) * length)
        heads[:, h * HD : (h + 1) * HD] = (mixed[at, :HD] / mixed[at, HD:]).astype(BF)
    y_ref[...] = nn(heads[...], o_ref[...]).astype(BF)
    base_ref[...] = nn(jnp.concatenate([coeffs] * 3, axis=1), g_ref[...])


def forward(new, sent, basis, m2, o2, g3, cosine, sine):
    length, rank = new.shape
    ne = o2.shape[0]
    stack = ne // HD * length
    return pl.pallas_call(
        forward_kernel,
        in_specs=vmem(8),
        out_specs=vmem(2),
        out_shape=[
            jax.ShapeDtypeStruct((length, rank), BF),
            jax.ShapeDtypeStruct((length, rank), F32),
        ],
        scratch_shapes=[
            pltpu.VMEM((stack, HD), BF),
            pltpu.VMEM((length, HD), BF),
            pltpu.VMEM((length, 2 * HD), BF),
            pltpu.VMEM((stack, length), F32),
            pltpu.VMEM((stack, length), BF),
            pltpu.VMEM((stack, 2 * HD), F32),
            pltpu.VMEM((length, ne), BF),
        ],
        compiler_params=pltpu.CompilerParams(vmem_limit_bytes=VMEM_BYTES),
        cost_estimate=cost(2 * 900 * 10**6, 6 * 10**6, 8 * 65536),
        name="attention_forward",
    )(new, sent, basis, m2, o2, g3, cosine, sine)


def gain_kernel(u_ref, wq_ref, wk_ref, wv_ref, inner_ref, out_ref, turned):
    nq, nk, nv = wq_ref.shape[1], wk_ref.shape[1], wv_ref.shape[1]

    @pl.when(pl.program_id(0) == 0)
    def _():
        turned[...] = inner_ref[:, : nq + nk + nv].T

    against = nn(wq_ref[...], turned[:nq, :])
    against += nn(wk_ref[...], turned[nq : nq + nk, :])
    against += nn(wv_ref[...], turned[nq + nk :, :])
    terms = against * u_ref[...].astype(F32)
    folded = sum(terms[:, at : at + HD] for at in range(0, terms.shape[1], HD))
    out_ref[...] = jnp.sum(folded.T, axis=0, keepdims=True)


def gain_part(basis, wq, wk, wv, inner):
    wide, rank = basis.shape
    nq, nk, nv = wq.shape[1], wk.shape[1], wv.shape[1]
    block = 512
    rows = lambda i: (i, 0)
    return pl.pallas_call(
        gain_kernel,
        grid=(wide // block,),
        in_specs=[
            pl.BlockSpec((block, rank), rows),
            pl.BlockSpec((block, nq), rows),
            pl.BlockSpec((block, nk), rows),
            pl.BlockSpec((block, nv), rows),
            pl.BlockSpec(inner.shape, lambda i: (0, 0)),
        ],
        out_specs=pl.BlockSpec((1, block), lambda i: (0, i)),
        scratch_shapes=[pltpu.VMEM((nq + nk + nv, rank), BF)],
        out_shape=jax.ShapeDtypeStruct((1, wide), F32),
        compiler_params=pltpu.CompilerParams(vmem_limit_bytes=VMEM_BYTES),
        cost_estimate=cost(2 * wide * rank * (nq + nk + nv), 2 * wide * (nq + nk + nv + rank)),
        name="gain_gradient",
    )(basis, wq, wk, wv, inner)


def gather_halves(own_ref, other_ref, whole):
    half = own_ref.shape[0]
    core = lax.axis_index("dp") % 2
    whole[pl.ds(pl.multiple_of(core * half, half), half), :] = own_ref[...]
    whole[pl.ds(pl.multiple_of((1 - core) * half, half), half), :] = other_ref[...]


def inward_kernel(me_ref, u_ref, gain_ref, own_ref, other_ref, q_ref, k_ref, v_ref, inner):
    nq, nk = q_ref.shape[1], k_ref.shape[1]
    block = q_ref.shape[0]

    @pl.when(pl.program_id(0) == 0)
    def _():
        gather_halves(own_ref, other_ref, inner)

    gain = jnp.broadcast_to(gain_ref[...], (HD, block)).T[:, :1]
    grad = nn(u_ref[...], inner[...]) * gain
    q_ref[...] = grad[:, :nq].astype(BF)
    k_ref[...] = grad[:, nq : nq + nk].astype(BF)
    v_ref[...] = grad[:, nq + nk :].astype(BF)


def outward_kernel(me_ref, u_ref, own_ref, other_ref, o_ref, inner):
    @pl.when(pl.program_id(0) == 0)
    def _():
        gather_halves(own_ref, other_ref, inner)

    block = o_ref.shape[0]
    at = pl.multiple_of(pl.program_id(0) * block, block)
    o_ref[...] = nt(inner[:, pl.ds(at, block)].T, u_ref[...]).astype(BF)


STEPS = 4


def my_part():
    return lax.axis_index("dp").astype(jnp.int32).reshape(1)


def inward_grads(basis, gain, own, other, sizes):
    wide, rank = basis.shape
    rows = wide // lax.axis_size("dp")
    block = rows // STEPS
    fixed = lambda i, me: (0, 0)
    step_rows = lambda i, me: (i, 0)
    return pl.pallas_call(
        inward_kernel,
        grid_spec=pltpu.PrefetchScalarGridSpec(
            num_scalar_prefetch=1,
            grid=(STEPS,),
            in_specs=[
                pl.BlockSpec((block, rank), lambda i, me: (me[0] * STEPS + i, 0)),
                pl.BlockSpec((1, block), lambda i, me: (0, me[0] * STEPS + i)),
                pl.BlockSpec(own.shape, fixed),
                pl.BlockSpec(other.shape, fixed),
            ],
            out_specs=[pl.BlockSpec((block, n), step_rows) for n in sizes],
            scratch_shapes=[pltpu.VMEM((rank, sum(sizes)), BF)],
        ),
        out_shape=[jax.ShapeDtypeStruct((rows, n), BF) for n in sizes],
        compiler_params=pltpu.CompilerParams(vmem_limit_bytes=VMEM_BYTES),
        cost_estimate=cost(2 * rows * rank * sum(sizes), 4 * 10**6),
        name="inward_weight_gradients",
    )(my_part(), basis, gain, own, other)


def outward_grad(basis, own, other):
    wide, rank = basis.shape
    rows = wide // lax.axis_size("dp")
    ne = own.shape[1]
    fixed = lambda i, me: (0, 0)
    return pl.pallas_call(
        outward_kernel,
        grid_spec=pltpu.PrefetchScalarGridSpec(
            num_scalar_prefetch=1,
            grid=(STEPS,),
            in_specs=[
                pl.BlockSpec((rows, rank), lambda i, me: (me[0], 0)),
                pl.BlockSpec(own.shape, fixed),
                pl.BlockSpec(other.shape, fixed),
            ],
            out_specs=pl.BlockSpec((ne // STEPS, rows), lambda i, me: (i, 0)),
            scratch_shapes=[pltpu.VMEM((rank, ne), BF)],
        ),
        out_shape=jax.ShapeDtypeStruct((ne, rows), BF),
        compiler_params=pltpu.CompilerParams(vmem_limit_bytes=VMEM_BYTES),
        cost_estimate=cost(2 * rows * rank * ne, 3 * 10**6),
        name="output_weight_gradient",
    )(my_part(), basis, own, other)


def results_kernel(
    wide, fbase_ref, y_ref, ygot_ref, base_ref, unit_ref, x_ref, xgot_ref, back_ref, inv_ref,
    f_ref, b_ref,
):
    f_ref[...] = (fbase_ref[...] + add_wide(y_ref[...], ygot_ref[...])).astype(BF)
    x = add_wide(x_ref[...], xgot_ref[...])
    inv = inv_ref[:, :1]
    along = jnp.sum(x * back_ref[...].astype(F32), axis=1, keepdims=True)
    middle = along * inv * (1.0 / wide)
    b_ref[...] = (base_ref[...] + (x - unit_ref[...] * middle) * inv).astype(BF)


def results(wide, *operands):
    shape = operands[0].shape
    return pl.pallas_call(
        functools.partial(results_kernel, wide),
        in_specs=vmem(len(operands)),
        out_specs=vmem(2),
        out_shape=[jax.ShapeDtypeStruct(shape, BF)] * 2,
        compiler_params=pltpu.CompilerParams(vmem_limit_bytes=VMEM_BYTES),
        cost_estimate=cost(10**6, 2 * 10**6),
        name="section_results",
    )(*operands)


def body(
    new_coeffs,
    loss_grad,
    sent_forward,
    sent_backward,
    stashed,
    subspace,
    norm_gain,
    w_query,
    w_key,
    w_value,
    w_output,
):
    wide = subspace.shape[0]
    wq, wk, wv, wo = w_query[0], w_key[0], w_value[0], w_output[0]
    nq, nk, nv = wq.shape[1], wk.shape[1], wv.shape[1]
    back = stashed[0]
    arrived, returned = cross_pipe(sent_forward[0], sent_backward[0])
    cosine, sine = rope_tables(back.shape[0])

    m2, o2, g3, inv = project(back, subspace, norm_gain, wq, wk, wv, wo)
    inner, give, keep, x, base, unit = backward(
        back, loss_grad, returned, m2, o2, g3, inv, cosine, sine
    )
    total = nq + nk + nv
    got = swap(give, "dp", 1)
    x_got = swap(x, "tensor", 1)
    y, fbase = forward(new_coeffs, arrived, subspace, m2, o2, g3, cosine, sine)
    pair_out = add_wide(keep[:, total:], got[:, total:]).astype(BF)
    pair_in = add_wide(keep[:, :total], got[:, :total]).astype(BF)
    got_out = swap(pair_out, "dp", 2)
    got_in = swap(pair_in, "dp", 2)
    y_got = swap(y, "tensor", 1)
    x = add_wide(x, x_got).astype(BF)
    x_got = swap(x, "tensor", 2)
    gain = gain_part(subspace, wq, wk, wv, inner)
    y = add_wide(y, y_got).astype(BF)
    y_got = swap(y, "tensor", 2)
    gain = gain + swap(gain, "tensor", 1)
    gain = gain + swap(gain, "tensor", 2)
    gain = gain + swap(gain, "dp", 1)
    gain = gain + swap(gain, "dp", 2)

    own = add_wide(pair_out, got_out).astype(BF)
    grad_o = outward_grad(subspace, own, swap(own, "dp", 1))
    forward_out, backward_out = results(
        wide, fbase, y, y_got, base, unit, x, x_got, back, inv
    )
    own = add_wide(pair_in, got_in).astype(BF)
    grad_q, grad_k, grad_v = inward_grads(
        subspace, norm_gain, own, swap(own, "dp", 1), (nq, nk, nv)
    )
    return (
        forward_out[None],
        backward_out[None],
        grad_q[None],
        grad_k[None],
        grad_v[None],
        grad_o[None],
        gain,
    )


def solution(mesh):
    return jax.shard_map(
        body,
        mesh=mesh,
        in_specs=(
            P("dp", None),
            P("dp", None),
            P("pipe", "dp", None),
            P("pipe", "dp", None),
            P("pipe", "dp", None),
            P(),
            P("pipe", None),
            P("pipe", None, "tensor"),
            P("pipe", None, "tensor"),
            P("pipe", None, "tensor"),
            P("pipe", "tensor", None),
        ),
        out_specs=(
            P("pipe", "dp", None),
            P("pipe", "dp", None),
            P("pipe", "dp", "tensor"),
            P("pipe", "dp", "tensor"),
            P("pipe", "dp", "tensor"),
            P("pipe", "tensor", "dp"),
            P("pipe", None),
        ),
        check_vma=False,
    )
```

profile of v0, /device:TPU:0, one launch (start us, length us, event | category | flops | bytes accessed | tf_op | source)
XLA Modules:
  0.0 93.1 jit_solution(8716299280513869816)
XLA Ops:
  1.6 3.0 %collective-permute-start = (bf16[256,256]{1,0:T(8,128)(2,1)S(1)}, bf16[256,256]{1,0:T(8,128)(2,1)S(1)}, u32[]{:S(2)}, u32[]{:S(2)}) collective-permute-start(bf16[256,256]{1,0:T(8,128)(2,1)S(1)} %select_bitcast_fusion), channel_id=1, source_target_pairs={{0,16},{16,0},{1,17},{17,1},{2,18},{18,2},{3,19},{19,3},{4,20},{20... | collective-permute-start | bytes 393224 | tf_op jit(solution)/shard_map/ppermute | solution.py:29
  4.6 1.6 %copy-done = bf16[4096,256]{1,0:T(8,128)(2,1)S(1)} copy-done((bf16[4096,256]{1,0:T(8,128)(2,1)S(1)}, bf16[4096,256]{1,0:T(8,128)(2,1)}, u32[]{:S(2)}) %copy-start) | copy-done | bytes 2097176
  6.2 3.4 %copy-done.2 = bf16[1,4096,1024]{2,1,0:T(8,128)(2,1)S(1)} copy-done((bf16[1,4096,1024]{2,1,0:T(8,128)(2,1)S(1)}, bf16[1,4096,1024]{2,1,0:T(8,128)(2,1)}, u32[]{:S(2)}) %copy-start.2) | copy-done | bytes 8388632
  10.8 1.2 %copy-done.5 = bf16[1,4096,128]{2,1,0:T(8,128)(2,1)S(1)} copy-done((bf16[1,4096,128]{2,1,0:T(8,128)(2,1)S(1)}, bf16[1,4096,128]{2,1,0:T(8,128)(2,1)}, u32[]{:S(2)}) %copy-start.5) | copy-done | bytes 1048600
  13.6 3.4 %copy-done.19 = bf16[1,1024,4096]{2,1,0:T(8,128)(2,1)S(1)} copy-done((bf16[1,1024,4096]{2,1,0:T(8,128)(2,1)S(1)}, bf16[1,1024,4096]{2,1,0:T(8,128)(2,1)}, u32[]{:S(2)}) %copy-start.19) | copy-done | bytes 8388632
  17.0 10.0 %project_weights.1 = (bf16[512,1280]{1,0:T(8,128)(2,1)S(1)}, bf16[1024,256]{1,0:T(8,128)(2,1)S(1)}, bf16[768,256]{1,0:T(8,128)(2,1)S(1)}, f32[256,128]{1,0:T(8,128)S(1)}) custom-call(bf16[256,256]{1,0:T(8,128)(2,1)S(1)} %bitcast.22, bf16[4096,256]{1,0:T(8,128)(2,1)S(1)} %copy-done, f32[1,4096]{1,0:T(1,128)S(1)} %copy-done.17, ...), custom_call_target="tpu_custom_call" | custom-call | flops 5905580032 | bytes 20971520 | tf_op jit(solution)/shard_map/project_weights/pallas_call | solution.py:137
  27.1 5.2 %attention_backward.1 = (bf16[256,2304]{1,0:T(8,128)(2,1)S(1)}, bf16[128,2304]{1,0:T(8,128)(2,1)S(1)}, bf16[128,2304]{1,0:T(8,128)(2,1)S(1)}, bf16[256,256]{1,0:...) custom-call(bf16[256,256]{1,0:T(8,128)(2,1)S(1)} %bitcast.23, bf16[256,256]{1,0:T(8,128)(2,1)S(1)} %copy-done.20, ...), custom_call_target="tpu_custom_call" | custom-call | flops 2400000000 | bytes 8000000 | tf_op jit(solution)/shard_map/attention_backward/pallas_call | solution.py:267
  32.5 3.8 %attention_forward.1 = (bf16[256,256]{1,0:T(8,128)(2,1)S(1)}, f32[256,256]{1,0:T(8,128)S(1)}) custom-call(bf16[256,256]{1,0:T(8,128)(2,1)S(1)} %copy-done.21, bf16[256,256]{1,0:T(8,128)(2,1)S(1)} %collective-permute-done.sent_ref, bf16[4096,256]{1,0:T(8,128)(2,1)S(1)} %copy-done.1, bf16[512,1280]{1,0:T(8,128)(2,1)S(1)} %get-tuple-element.24.m_ref, ...), custom_call_target="tpu_custom_call" | custom-call | flops 1800000000 | bytes 6000000 | tf_op jit(solution)/shard_map/attention_forward/pallas_call | solution.py:332
  36.3 1.6 %collective-permute-start.1 = (bf16[256,256]{1,0:T(8,128)(2,1)S(1)}, bf16[256,256]{1,0:T(8,128)(2,1)S(1)}, u32[]{:S(2)}, u32[]{:S(2)}) collective-permute-start(bf16[256,256]{1,0:T(8,128)(2,1)S(1)} %get-tuple-element.28), channel_id=1, source_target_pairs={{0,4},{4,0},{8,12},{12,8},{1,5},{5,1},{9,13},{13,9},{2,6},{6,2},{1... | collective-permute-start | bytes 393224 | tf_op jit(solution)/shard_map/ppermute | solution.py:29
  38.4 4.3 %collective-permute-done.1 = bf16[256,256]{1,0:T(8,128)(2,1)S(1)} collective-permute-done((bf16[256,256]{1,0:T(8,128)(2,1)S(1)}, bf16[256,256]{1,0:T(8,128)(2,1)S(1)}, u32[]{:S(2)}, u32[]{:S(2)}) %collective-permute-start.1) | collective-permute-done | bytes 131104 | tf_op jit(solution)/shard_map/ppermute | solution.py:29
  42.7 2.7 %collective-permute-start.2 = (bf16[256,256]{1,0:T(8,128)(2,1)S(1)}, bf16[256,256]{1,0:T(8,128)(2,1)}, u32[]{:S(2)}, u32[]{:S(2)}) collective-permute-start(bf16[256,256]{1,0:T(8,128)(2,1)S(1)} %add_convert_fusion.5.y_ref), channel_id=1, source_target_pairs={{0,8},{4,12},{8,0},{12,4},{1,9},{5,13},{9,1},{13,5},{2,10},{6,14},... | collective-permute-start | bytes 393224 | tf_op jit(solution)/shard_map/ppermute | solution.py:29
  45.4 1.6 %collective-permute-start.8 = (bf16[128,1024]{1,0:T(8,128)(2,1)S(1)}, bf16[128,1024]{1,0:T(8,128)(2,1)S(1)}, u32[]{:S(2)}, u32[]{:S(2)}) collective-permute-start(bf16[128,1024]{1,0:T(8,128)(2,1)S(1)} %add_convert_fusion.3), channel_id=1, source_target_pairs={{0,2},{1,3},{2,0},{3,1},{4,6},{5,7},{6,4},{7,5},{8,10},{9,11},{10,... | collective-permute-start | bytes 786440 | tf_op jit(solution)/shard_map/ppermute | solution.py:29
  48.2 6.6 %collective-permute-done.8 = bf16[128,1024]{1,0:T(8,128)(2,1)S(1)} collective-permute-done((bf16[128,1024]{1,0:T(8,128)(2,1)S(1)}, bf16[128,1024]{1,0:T(8,128)(2,1)S(1)}, u32[]{:S(2)}, u32[]{:S(2)}) %collective-permute-start.8) | collective-permute-done | bytes 262176 | tf_op jit(solution)/shard_map/ppermute | solution.py:29
  54.9 4.9 %collective-permute-done.6 = bf16[128,1280]{1,0:T(8,128)(2,1)S(1)} collective-permute-done((bf16[128,1280]{1,0:T(8,128)(2,1)S(1)}, bf16[128,1280]{1,0:T(8,128)(2,1)S(1)}, u32[]{:S(2)}, u32[]{:S(2)}) %collective-permute-start.6) | collective-permute-done | bytes 327712 | tf_op jit(solution)/shard_map/ppermute | solution.py:29
  60.0 5.9 %gain_gradient.1 = f32[1,4096]{1,0:T(1,128)S(1)} custom-call(bf16[4096,256]{1,0:T(8,128)(2,1)S(1)} %copy-done.1, bf16[4096,1024]{1,0:T(8,128)(2,1)S(1)} %bitcast.17, bf16[4096,128]{1,0:T(8,128)(2,1)S(1)} %bitcast.19, bf16[4096,128]{1,0:T(8,128)(2,1)S(1)} %bitcast.21, bf16[256,2304]{1,0:T(8,128)(2,1)S(1)} %get-tuple-element.40.inner_ref), custom_call_target="tpu_custom_call" | custom-call | flops 2684354560 | bytes 12582912 | tf_op jit(solution)/shard_map/gain_gradient/pallas_call | solution.py:375
  65.8 1.6 %collective-permute-start.10 = (f32[1,4096]{1,0:T(1,128)S(1)}, f32[1,4096]{1,0:T(1,128)S(1)}, u32[]{:S(2)}, u32[]{:S(2)}) collective-permute-start(f32[1,4096]{1,0:T(1,128)S(1)} %gain_gradient.1), channel_id=1, source_target_pairs={{0,4},{4,0},{8,12},{12,8},{1,5},{5,1},{9,13},{13,9},{2,6},{6,2},{1... | collective-permute-start | bytes 49160 | tf_op jit(solution)/shard_map/ppermute | solution.py:29
  67.5 2.2 %collective-permute-done.10 = f32[1,4096]{1,0:T(1,128)S(1)} collective-permute-done((f32[1,4096]{1,0:T(1,128)S(1)}, f32[1,4096]{1,0:T(1,128)S(1)}, u32[]{:S(2)}, u32[]{:S(2)}) %collective-permute-start.10) | collective-permute-done | bytes 16416 | tf_op jit(solution)/shard_map/ppermute | solution.py:29
  70.1 4.3 %collective-permute-done.11 = f32[1,4096]{1,0:T(1,128)S(1)} collective-permute-done((f32[1,4096]{1,0:T(1,128)S(1)}, f32[1,4096]{1,0:T(1,128)S(1)}, u32[]{:S(2)}, u32[]{:S(2)}) %collective-permute-start.11) | collective-permute-done | bytes 16416 | tf_op jit(solution)/shard_map/ppermute | solution.py:29
  75.7 1.6 %collective-permute-start.13 = (f32[1,4096]{1,0:T(1,128)S(1)}, f32[1,4096]{1,0:T(1,128)}, u32[]{:S(2)}, u32[]{:S(2)}) collective-permute-start(f32[1,4096]{1,0:T(1,128)S(1)} %add.38), channel_id=1, source_target_pairs={{0,2},{1,3},{2,0},{3,1},{4,6},{5,7},{6,4},{7,5},{8,10},{9,11},{10,... | collective-permute-start | bytes 49160 | tf_op jit(solution)/shard_map/ppermute | solution.py:29
  77.3 2.3 %collective-permute-done.13 = f32[1,4096]{1,0:T(1,128)} collective-permute-done((f32[1,4096]{1,0:T(1,128)S(1)}, f32[1,4096]{1,0:T(1,128)}, u32[]{:S(2)}, u32[]{:S(2)}) %collective-permute-start.13) | collective-permute-done | bytes 16416 | tf_op jit(solution)/shard_map/ppermute | solution.py:29
  79.6 1.3 %add.39 = f32[1,4096]{1,0:T(1,128)} add(f32[1,4096]{1,0:T(1,128)S(1)} %add.38, f32[1,4096]{1,0:T(1,128)} %collective-permute-done.13) | non-fusion elementwise | flops 4096 | bytes 49152 | tf_op jit(solution)/shard_map/add | solution.py:551
  85.6 1.9 %section_results.1 = (bf16[256,256]{1,0:T(8,128)(2,1)}, bf16[256,256]{1,0:T(8,128)(2,1)}) custom-call(f32[256,256]{1,0:T(8,128)S(1)} %copy-done.12, bf16[256,256]{1,0:T(8,128)(2,1)S(1)} %add_convert_fusion.5.y_ref, bf16[256,256]{1,0:T(8,128)(2,1)} %collective-permute-done.2.ygot_ref, f32[256,256]{1,0:T(8,128)S(1)} %copy-done.8, f32[256,256]{1,0:T(8,128)S(1)} %copy-done.10, ...), custom_call_target="tpu_custom_call" | custom-call | flops 1000000 | bytes 2000000 | tf_op jit(solution)/shard_map/section_results/pallas_call | solution.py:499
  87.5 2.7 %output_weight_gradient.1 = bf16[1024,1024]{1,0:T(8,128)(2,1)} custom-call(s32[1]{0:T(128)} %bitcast.8.me_ref, bf16[4096,256]{1,0:T(8,128)(2,1)S(1)} %copy-done.1, bf16[128,1024]{1,0:T(8,128)(2,1)S(1)} %add_convert_fusion.2.own_ref, bf16[128,1024]{1,0:T(8,128)(2,1)S(1)} %collective-permute-done.9.other_ref), custom_call_target="tpu_custom_call" | custom-call | flops 536870912 | bytes 3000000 | tf_op jit(solution)/shard_map/output_weight_gradient/pallas_call | solution.py:465
  90.3 2.8 %inward_weight_gradients.1 = (bf16[1024,1024]{1,0:T(8,128)(2,1)}, bf16[1024,128]{1,0:T(8,128)(2,1)}, bf16[1024,128]{1,0:T(8,128)(2,1)}) custom-call(s32[1]{0:T(128)} %bitcast.8.me_ref, bf16[4096,256]{1,0:T(8,128)(2,1)S(1)} %copy-done.1, f32[1,4096]{1,0:T(1,128)S(1)} %copy-done.18, bf16[128,1280]{1,0:T(8,128)(2,1)S(1)} %add_convert_fusion.own_ref, ...), custom_call_target="tpu_custom_call" | custom-call | flops 671088640 | bytes 4000000 | tf_op jit(solution)/shard_map/inward_weight_gradients/pallas_call | solution.py:439
  (75 shorter events, 12.3 us)
Async XLA Ops:
  1.6 25.5 %collective-permute-start = (bf16[256,256]{1,0:T(8,128)(2,1)S(1)}, bf16[256,256]{1,0:T(8,128)(2,1)S(1)}, u32[]{:S(2)}, u32[]{:S(2)}) collective-permute-start(bf16[256,256]{1,0:T(8,128)(2,1)S(1)} %select_bitcast_fusion), channel_id=1, source_target_pairs={{0,16},{16,0},{1,17},{17,1},{2,18},{18,2},{3,19},{19,3},{4,20},{20... | collective-permute-start | bytes 393224 | tf_op jit(solution)/shard_map/ppermute | solution.py:29
  17.0 10.0 %copy-start.20 = (bf16[256,256]{1,0:T(8,128)(2,1)S(1)}, bf16[256,256]{1,0:T(8,128)(2,1)}, u32[]{:S(2)}) copy-start(bf16[256,256]{1,0:T(8,128)(2,1)} %loss_ref.1) | copy-start | bytes 393220
  17.0 10.0 %copy-start.22 = (f32[256,128]{1,0:T(8,128)S(1)}, f32[256,128]{1,0:T(8,128)}, u32[]{:S(2)}) copy-start(f32[256,128]{1,0:T(8,128)} %constant.17.clone.sin_ref) | copy-start | bytes 393220
  17.0 10.0 %copy-start.23 = (f32[256,128]{1,0:T(8,128)S(1)}, f32[256,128]{1,0:T(8,128)}, u32[]{:S(2)}) copy-start(f32[256,128]{1,0:T(8,128)} %constant.16.clone.cos_ref) | copy-start | bytes 393220
  27.1 5.4 %copy-start.1 = (bf16[4096,256]{1,0:T(8,128)(2,1)S(1)}, bf16[4096,256]{1,0:T(8,128)(2,1)}, u32[]{:S(2)}) copy-start(bf16[4096,256]{1,0:T(8,128)(2,1)} %u_ref.9) | copy-start | bytes 6291460
  27.1 5.4 %copy-start.21 = (bf16[256,256]{1,0:T(8,128)(2,1)S(1)}, bf16[256,256]{1,0:T(8,128)(2,1)}, u32[]{:S(2)}) copy-start(bf16[256,256]{1,0:T(8,128)(2,1)} %new_ref.1) | copy-start | bytes 393220
  27.1 32.8 %slice-start = ((s8[8388608]{0:T(1024)(128)(4,1)}), s8[4194304]{0:T(1024)(128)(4,1)S(1)}, s32[]{:S(2)}) async-start(s8[8388608]{0:T(1024)(128)(4,1)} %bitcast.15), calls=%async_computation | async-start | bytes 8388608
  32.4 27.5 %slice-start.1 = ((s8[8388608]{0:T(1024)(128)(4,1)}), s8[4194304]{0:T(1024)(128)(4,1)S(1)}, s32[]{:S(2)}) async-start(s8[8388608]{0:T(1024)(128)(4,1)} %bitcast.15), calls=%async_computation.1 | async-start | bytes 8388608
  32.4 13.0 %collective-permute-start.5 = (bf16[128,2304]{1,0:T(8,128)(2,1)S(1)}, bf16[128,2304]{1,0:T(8,128)(2,1)S(1)}, u32[]{:S(2)}, u32[]{:S(2)}) collective-permute-start(bf16[128,2304]{1,0:T(8,128)(2,1)S(1)} %get-tuple-element.36), channel_id=1, source_target_pairs={{0,1},{1,0},{2,3},{3,2},{4,5},{5,4},{6,7},{7,6},{8,9},{9,8},{10,11... | collective-permute-start | bytes 1769480 | tf_op jit(solution)/shard_map/ppermute | solution.py:29
  36.3 23.5 %copy-start.11 = (f32[256,256]{1,0:T(8,128)}, f32[256,256]{1,0:T(8,128)S(1)}, u32[]{:S(2)}) copy-start(f32[256,256]{1,0:T(8,128)S(1)} %get-tuple-element.27.fbase_ref) | copy-start | bytes 786436
  36.3 6.4 %collective-permute-start.1 = (bf16[256,256]{1,0:T(8,128)(2,1)S(1)}, bf16[256,256]{1,0:T(8,128)(2,1)S(1)}, u32[]{:S(2)}, u32[]{:S(2)}) collective-permute-start(bf16[256,256]{1,0:T(8,128)(2,1)S(1)} %get-tuple-element.28), channel_id=1, source_target_pairs={{0,4},{4,0},{8,12},{12,8},{1,5},{5,1},{9,13},{13,9},{2,6},{6,2},{1... | collective-permute-start | bytes 393224 | tf_op jit(solution)/shard_map/ppermute | solution.py:29
  37.9 22.0 %copy-start.4 = (bf16[1,4096,128]{2,1,0:T(8,128)(2,1)S(1)}, bf16[1,4096,128]{2,1,0:T(8,128)(2,1)}, u32[]{:S(2)}) copy-start(bf16[1,4096,128]{2,1,0:T(8,128)(2,1)} %param.21) | copy-start | bytes 3145732
  37.9 22.0 %copy-start.6 = (bf16[1,4096,128]{2,1,0:T(8,128)(2,1)S(1)}, bf16[1,4096,128]{2,1,0:T(8,128)(2,1)}, u32[]{:S(2)}) copy-start(bf16[1,4096,128]{2,1,0:T(8,128)(2,1)} %param.22) | copy-start | bytes 3145732
  37.9 9.7 %collective-permute-start.3 = (bf16[256,256]{1,0:T(8,128)(2,1)S(1)}, bf16[256,256]{1,0:T(8,128)(2,1)S(1)}, u32[]{:S(2)}, u32[]{:S(2)}) collective-permute-start(bf16[256,256]{1,0:T(8,128)(2,1)S(1)} %get-tuple-element.32), channel_id=1, source_target_pairs={{0,4},{4,0},{8,12},{12,8},{1,5},{5,1},{9,13},{13,9},{2,6},{6,2},{1... | collective-permute-start | bytes 393224 | tf_op jit(solution)/shard_map/ppermute | solution.py:29
  42.7 38.2 %collective-permute-start.2 = (bf16[256,256]{1,0:T(8,128)(2,1)S(1)}, bf16[256,256]{1,0:T(8,128)(2,1)}, u32[]{:S(2)}, u32[]{:S(2)}) collective-permute-start(bf16[256,256]{1,0:T(8,128)(2,1)S(1)} %add_convert_fusion.5.y_ref), channel_id=1, source_target_pairs={{0,8},{4,12},{8,0},{12,4},{1,9},{5,13},{9,1},{13,5},{2,10},{6,14},... | collective-permute-start | bytes 393224 | tf_op jit(solution)/shard_map/ppermute | solution.py:29
  45.4 9.3 %collective-permute-start.8 = (bf16[128,1024]{1,0:T(8,128)(2,1)S(1)}, bf16[128,1024]{1,0:T(8,128)(2,1)S(1)}, u32[]{:S(2)}, u32[]{:S(2)}) collective-permute-start(bf16[128,1024]{1,0:T(8,128)(2,1)S(1)} %add_convert_fusion.3), channel_id=1, source_target_pairs={{0,2},{1,3},{2,0},{3,1},{4,6},{5,7},{6,4},{7,5},{8,10},{9,11},{10,... | collective-permute-start | bytes 786440 | tf_op jit(solution)/shard_map/ppermute | solution.py:29
  47.1 12.7 %collective-permute-start.6 = (bf16[128,1280]{1,0:T(8,128)(2,1)S(1)}, bf16[128,1280]{1,0:T(8,128)(2,1)S(1)}, u32[]{:S(2)}, u32[]{:S(2)}) collective-permute-start(bf16[128,1280]{1,0:T(8,128)(2,1)S(1)} %add_convert_fusion.1), channel_id=1, source_target_pairs={{0,2},{1,3},{2,0},{3,1},{4,6},{5,7},{6,4},{7,5},{8,10},{9,11},{10,... | collective-permute-start | bytes 983048 | tf_op jit(solution)/shard_map/ppermute | solution.py:29
  47.7 33.2 %collective-permute-start.4 = (bf16[256,256]{1,0:T(8,128)(2,1)S(1)}, bf16[256,256]{1,0:T(8,128)(2,1)}, u32[]{:S(2)}, u32[]{:S(2)}) collective-permute-start(bf16[256,256]{1,0:T(8,128)(2,1)S(1)} %add_convert_fusion.4.x_ref), channel_id=1, source_target_pairs={{0,8},{4,12},{8,0},{12,4},{1,9},{5,13},{9,1},{13,5},{2,10},{6,14},... | collective-permute-start | bytes 393224 | tf_op jit(solution)/shard_map/ppermute | solution.py:29
  54.8 32.7 %collective-permute-start.9 = (bf16[128,1024]{1,0:T(8,128)(2,1)S(1)}, bf16[128,1024]{1,0:T(8,128)(2,1)S(1)}, u32[]{:S(2)}, u32[]{:S(2)}) collective-permute-start(bf16[128,1024]{1,0:T(8,128)(2,1)S(1)} %add_convert_fusion.2.own_ref), channel_id=1, source_target_pairs={{0,1},{1,0},{2,3},{3,2},{4,5},{5,4},{6,7},{7,6},{8,9},{9,8},{10,11... | collective-permute-start | bytes 786440 | tf_op jit(solution)/shard_map/ppermute | solution.py:29
  59.8 30.4 %collective-permute-start.7 = (bf16[128,1280]{1,0:T(8,128)(2,1)S(1)}, bf16[128,1280]{1,0:T(8,128)(2,1)S(1)}, u32[]{:S(2)}, u32[]{:S(2)}) collective-permute-start(bf16[128,1280]{1,0:T(8,128)(2,1)S(1)} %add_convert_fusion.own_ref), channel_id=1, source_target_pairs={{0,1},{1,0},{2,3},{3,2},{4,5},{5,4},{6,7},{7,6},{8,9},{9,8},{10,11... | collective-permute-start | bytes 983048 | tf_op jit(solution)/shard_map/ppermute | solution.py:29
  65.8 3.8 %collective-permute-start.10 = (f32[1,4096]{1,0:T(1,128)S(1)}, f32[1,4096]{1,0:T(1,128)S(1)}, u32[]{:S(2)}, u32[]{:S(2)}) collective-permute-start(f32[1,4096]{1,0:T(1,128)S(1)} %gain_gradient.1), channel_id=1, source_target_pairs={{0,4},{4,0},{8,12},{12,8},{1,5},{5,1},{9,13},{13,9},{2,6},{6,2},{1... | collective-permute-start | bytes 49160 | tf_op jit(solution)/shard_map/ppermute | solution.py:29
  69.7 4.7 %collective-permute-start.11 = (f32[1,4096]{1,0:T(1,128)S(1)}, f32[1,4096]{1,0:T(1,128)S(1)}, u32[]{:S(2)}, u32[]{:S(2)}) collective-permute-start(f32[1,4096]{1,0:T(1,128)S(1)} %add.36), channel_id=1, source_target_pairs={{0,8},{4,12},{8,0},{12,4},{1,9},{5,13},{9,1},{13,5},{2,10},{6,14},... | collective-permute-start | bytes 49160 | tf_op jit(solution)/shard_map/ppermute | solution.py:29
  74.4 1.2 %collective-permute-start.12 = (f32[1,4096]{1,0:T(1,128)S(1)}, f32[1,4096]{1,0:T(1,128)S(1)}, u32[]{:S(2)}, u32[]{:S(2)}) collective-permute-start(f32[1,4096]{1,0:T(1,128)S(1)} %add.37), channel_id=1, source_target_pairs={{0,1},{1,0},{2,3},{3,2},{4,5},{5,4},{6,7},{7,6},{8,9},{9,8},{10,11... | collective-permute-start | bytes 49160 | tf_op jit(solution)/shard_map/ppermute | solution.py:29
  75.7 3.9 %collective-permute-start.13 = (f32[1,4096]{1,0:T(1,128)S(1)}, f32[1,4096]{1,0:T(1,128)}, u32[]{:S(2)}, u32[]{:S(2)}) collective-permute-start(f32[1,4096]{1,0:T(1,128)S(1)} %add.38), channel_id=1, source_target_pairs={{0,2},{1,3},{2,0},{3,1},{4,6},{5,7},{6,4},{7,5},{8,10},{9,11},{10,... | collective-permute-start | bytes 49160 | tf_op jit(solution)/shard_map/ppermute | solution.py:29
  (16 other events, 33.0 us)
where the time goes:
time: 93.7 us; the launch traced here: 93.1 us
  Pallas kernels  32.3 us (34%)
  waiting for transfers between devices  25.7 us (27%)
  local copies, waits for them, and re-layouts  17.2 us (18%)
  starting transfers between devices  14.3 us (15%)
  other arithmetic  2.67 us (3%)
  between operations  0.95 us (1%)
    ppermute x14, waiting for transfers between devices, swap(): return lax.ppermute(x, axis, [(i, i ^ bit) for i in range(devices)])  25.7 us
    unnamed x52, local copies, waits for them, and re-layouts  17.2 us
    ppermute x14, starting transfers between devices, swap(): return lax.ppermute(x, axis, [(i, i ^ bit) for i in range(devices)])  14.3 us
    pallas_call x1, Pallas kernels, project(): pl.pallas_call(functools.partial(project_kernel, wide), grid=(wide // blo...  9.99 us
    pallas_call x1, Pallas kernels, gain_part(): pl.pallas_call(gain_kernel, grid=(wide // block,), in_specs=[pl.BlockSpec...  5.89 us
    pallas_call x1, Pallas kernels, backward(): pl.pallas_call(backward_kernel, in_specs=vmem(9), out_specs=vmem(6), out_...  5.24 us
    pallas_call x1, Pallas kernels, forward(): pl.pallas_call(forward_kernel, in_specs=vmem(8), out_specs=vmem(2), out_s...  3.76 us
    pallas_call x1, Pallas kernels, inward_grads(): pl.pallas_call(inward_kernel, grid_spec=pltpu.PrefetchScalarGridSpec(num_...  2.81 us
  transfers between devices with their start and end apart: 14, of which 7 were waited for; matrix products, arithmetic and copies ran while one was open for 2% of the time, Pallas kernels for 26%

commit v1 on v0

--- a/solution.py
+++ b/solution.py
@@ -14,7 +14,8 @@
 ROPE_BASE = 500000.0
 BF = jnp.bfloat16
 F32 = jnp.float32
-VMEM_BYTES = 28 * 1024 * 1024
+VMEM_BYTES = 24 * 1024 * 1024
+PIECE = 512
 LOG2E = 1.4426950408889634
 
 
@@ -83,91 +84,79 @@
     return [pl.BlockSpec(memory_space=pltpu.VMEM)] * count
 
 
+def in_hbm(arrays):
+    return tuple(pltpu.with_memory_space_constraint(a, pltpu.HBM) for a in arrays)
+
+
 def cost(flops, num_bytes, exps=0):
     return pl.CostEstimate(flops=flops, bytes_accessed=num_bytes, transcendentals=exps)
 
 
-def project_kernel(
-    wide, back_ref, u_ref, gain_ref, wq_ref, wk_ref, wv_ref, wo_ref,
-    m_ref, o_ref, g_ref, inv_ref,
-    m_acc, o_acc, g_acc, sq_acc,
+def streamed(pairs, sems, steps, ahead, work):
+    def copies(i):
+        out = []
+        for n, (source, target, axis) in enumerate(pairs):
+            size = source.shape[axis] // steps
+            at = pl.ds(pl.multiple_of(i * size, size), size)
+            index = (at, slice(None)) if axis == 0 else (slice(None), at)
+            out.append(pltpu.make_async_copy(source.at[index], target.at[index], sems.at[n, i]))
+        return out
+
+    for i in range(ahead):
+        for copy in copies(i):
+            copy.start()
+
+    def one(i, _):
+        @pl.when(i + ahead < steps)
+        def _():
+            for copy in copies(i + ahead):
+                copy.start()
+
+        for copy in copies(i):
+            copy.wait()
+        work(i)
+        return 0
+
+    lax.fori_loop(0, steps, one, 0)
+
+
+def project(
+    wide, back, u_ref, gain_ref, wq_ref, wk_ref, wv_ref, wo_ref, sems,
+    m_ref, o_ref, g_ref, u, wq, wk, wv, wo, m_acc, o_acc, g_acc, square,
 ):
-    step = pl.program_id(0)
-    rank = u_ref.shape[1]
-    nq, nk = wq_ref.shape[1], wk_ref.shape[1]
-
-    @pl.when(step == 0)
-    def _():
-        m_acc[...] = jnp.zeros_like(m_acc)
-        o_acc[...] = jnp.zeros_like(o_acc)
-        g_acc[...] = jnp.zeros_like(g_acc)
-        sq_acc[...] = jnp.zeros_like(sq_acc)
-
-    u = u_ref[...]
-    ut = u.T
-    scaled = (ut.astype(F32) * gain_ref[...]).astype(BF)
-    for ref, at in ((wq_ref, 0), (wk_ref, nq), (wv_ref, nq + nk)):
-        size = ref.shape[1]
-        m_acc[:, at : at + size] += nn(scaled, ref[...])
-    o_acc[...] += nn(wo_ref[...], u)
-    g_acc[...] += nn(ut, u)
-    decoded = nn(back_ref[...], ut)
-    square = decoded * decoded
-    sq_acc[...] += jnp.broadcast_to(jnp.sum(square, axis=1, keepdims=True), sq_acc.shape)
-
-    @pl.when(step == pl.num_programs(0) - 1)
-    def _():
-        for i, piece in enumerate(split(m_acc[...], 2)):
-            m_ref[i * rank : (i + 1) * rank, :] = piece
-        o_ref[...] = o_acc[...].astype(BF)
-        for i, piece in enumerate(split(g_acc[...], 3)):
-            g_ref[i * rank : (i + 1) * rank, :] = piece
-        inv_ref[...] = inverse_root(sq_acc[...], wide)
-
-
-def project(back, basis, gain, wq, wk, wv, wo):
-    wide, rank = basis.shape
-    length = back.shape[0]
-    nq, nk, nv, ne = wq.shape[1], wk.shape[1], wv.shape[1], wo.shape[0]
-    block = 512
-    rows = lambda i: (i, 0)
-    cols = lambda i: (0, i)
-    fixed = lambda i: (0, 0)
-    total = nq + nk + nv
-    return pl.pallas_call(
-        functools.partial(project_kernel, wide),
-        grid=(wide // block,),
-        in_specs=[
-            pl.BlockSpec((length, rank), fixed),
-            pl.BlockSpec((block, rank), rows),
-            pl.BlockSpec((1, block), cols),
-            pl.BlockSpec((block, nq), rows),
-            pl.BlockSpec((block, nk), rows),
-            pl.BlockSpec((block, nv), rows),
-            pl.BlockSpec((ne, block), cols),
-        ],
-        out_specs=[
-            pl.BlockSpec((2 * rank, total), fixed),
-            pl.BlockSpec((ne, rank), fixed),
-            pl.BlockSpec((3 * rank, rank), fixed),
-            pl.BlockSpec((length, HD), fixed),
-        ],
-        out_shape=[
-            jax.ShapeDtypeStruct((2 * rank, total), BF),
-            jax.ShapeDtypeStruct((ne, rank), BF),
-            jax.ShapeDtypeStruct((3 * rank, rank), BF),
-            jax.ShapeDtypeStruct((length, HD), F32),
-        ],
-        scratch_shapes=[
-            pltpu.VMEM((rank, total), F32),
-            pltpu.VMEM((ne, rank), F32),
-            pltpu.VMEM((rank, rank), F32),
-            pltpu.VMEM((length, HD), F32),
-        ],
-        compiler_params=pltpu.CompilerParams(vmem_limit_bytes=VMEM_BYTES),
-        cost_estimate=cost(2 * wide * rank * (total + ne + 2 * rank), 2 * wide * (total + ne + rank)),
-        name="project_weights",
-    )(back, basis, gain, wq, wk, wv, wo)
+    rank = u.shape[1]
+    nq, nk = wq.shape[1], wk.shape[1]
+    steps = wide // 1024
+    block = wide // steps
+    m_acc[...] = jnp.zeros_like(m_acc)
+    o_acc[...] = jnp.zeros_like(o_acc)
+    g_acc[...] = jnp.zeros_like(g_acc)
+    square[...] = jnp.zeros_like(square)
+
+    def work(i):
+        rows = pl.ds(pl.multiple_of(i * block, block), block)
+        basis = u[rows, :]
+        turned = basis.T
+        scaled = (turned.astype(F32) * gain_ref[:, rows]).astype(BF)
+        for ref, at in ((wq, 0), (wk, nq), (wv, nq + nk)):
+            size = ref.shape[1]
+            m_acc[:, at : at + size] += nn(scaled, ref[rows, :])
+        o_acc[...] += nn(wo[:, rows], basis)
+        g_acc[...] += nn(turned, basis)
+        decoded = nn(back, turned)
+        total = square[...]
+        for side in range(0, block, HD):
+            part = decoded[:, side : side + HD]
+            total = total + part * part
+        square[...] = total
+
+    pairs = ((u_ref, u, 0), (wq_ref, wq, 0), (wk_ref, wk, 0), (wv_ref, wv, 0), (wo_ref, wo, 1))
+    streamed(pairs, sems, steps, 2, work)
+    for i, piece in enumerate(split(m_acc[...], 2)):
+        m_ref[i * rank : (i + 1) * rank, :] = piece
+    o_ref[...] = o_acc[...].astype(BF)
+    for i, piece in enumerate(split(g_acc[...], 3)):
+        g_ref[i * rank : (i + 1) * rank, :] = piece
 
 
 def project_heads(coeffs, inv, m_ref, cosine, sine, q, k, v1):
@@ -202,11 +191,34 @@
 
 
 def backward_kernel(
-    back_ref, loss_ref, sent_ref, m_ref, o_ref, g_ref, inv_ref, cos_ref, sin_ref,
-    inner_ref, give_ref, keep_ref, x_ref, base_ref, unit_ref,
+    sent_ref, back_hbm, loss_hbm, gain_hbm, cos_hbm, sin_hbm,
+    u_ref, wq_ref, wk_ref, wv_ref, wo_ref,
+    inner_ref, give_ref, keep_ref, x_ref, base_ref, unit_ref, inv_ref, m_ref, o_ref, g_ref,
+    back_ref, loss_ref, gain_ref, cos_ref, sin_ref, small_sems,
+    u, wq, wk, wv, wo, m_acc, o_acc, g_acc, square, sems,
     q, k, v1, gh, ghs, scores, low, mixed, gp, ds, dq, heads, grads,
 ):
     length, rank = back_ref.shape
+    wide = u_ref.shape[0]
+    sources = (back_hbm, gain_hbm, loss_hbm, cos_hbm, sin_hbm)
+    targets = (back_ref, gain_ref, loss_ref, cos_ref, sin_ref)
+    small = [
+        pltpu.make_async_copy(source, target, small_sems.at[n])
+        for n, (source, target) in enumerate(zip(sources, targets))
+    ]
+    for copy in small:
+        copy.start()
+    for copy in small[:2]:
+        copy.wait()
+    project(
+        wide, back_ref[...], u_ref, gain_ref, wq_ref, wk_ref, wv_ref, wo_ref, sems,
+        m_ref, o_ref, g_ref, u, wq, wk, wv, wo, m_acc, o_acc, g_acc, square,
+    )
+    for copy in small[2:]:
+        copy.wait()
+    inv_ref[...] = jnp.broadcast_to(
+        inverse_root(jnp.sum(square[...], axis=1, keepdims=True), wide), inv_ref.shape
+    )
     ne = o_ref.shape[0]
     count = ne // HD
     scale = 1.0 / math.sqrt(HD)
@@ -257,17 +269,20 @@
     unit_ref[...] = nn(jnp.concatenate([back] * 3, axis=1), g_ref[...]) * inv[:, :1]
 
 
-def backward(back, loss, sent, m2, o2, g3, inv, cosine, sine):
+def backward(back, loss, sent, gain, cosine, sine, basis, wq, wk, wv, wo):
     length, rank = back.shape
-    total = m2.shape[1]
-    ne = o2.shape[0]
+    wide = basis.shape[0]
+    ne = wo.shape[0]
+    total = wq.shape[1] + wk.shape[1] + wv.shape[1]
     assert total == ne + 2 * HD
     width = total + ne
     stack = ne // HD * length
+    weights = in_hbm((basis, wq, wk, wv, wo))
+    small = in_hbm((back, loss, gain, cosine, sine))
     return pl.pallas_call(
         backward_kernel,
-        in_specs=vmem(9),
-        out_specs=vmem(6),
+        in_specs=vmem(1) + [pl.BlockSpec(memory_space=pltpu.HBM)] * len(small + weights),
+        out_specs=vmem(10),
         out_shape=[
             jax.ShapeDtypeStruct((rank, width), BF),
             jax.ShapeDtypeStruct((rank // 2, width), BF),
@@ -275,8 +290,20 @@
             jax.ShapeDtypeStruct((length, rank), BF),
             jax.ShapeDtypeStruct((length, rank), F32),
             jax.ShapeDtypeStruct((length, rank), F32),
+            jax.ShapeDtypeStruct((length, HD), F32),
+            jax.ShapeDtypeStruct((2 * rank, total), BF),
+            jax.ShapeDtypeStruct((ne, rank), BF),
+            jax.ShapeDtypeStruct((3 * rank, rank), BF),
         ],
-        scratch_shapes=[
+        scratch_shapes=[pltpu.VMEM(a.shape, a.dtype) for a in small]
+        + [pltpu.SemaphoreType.DMA((len(small),))]
+        + [pltpu.VMEM(w.shape, BF) for w in weights]
+        + [
+            pltpu.VMEM((rank, total), F32),
+            pltpu.VMEM((ne, rank), F32),
+            pltpu.VMEM((rank, rank), F32),
+            pltpu.VMEM((length, HD), F32),
+            pltpu.SemaphoreType.DMA((len(weights), wide // 1024)),
             pltpu.VMEM((stack, HD), BF),
             pltpu.VMEM((length, HD), BF),
             pltpu.VMEM((length, 2 * HD), BF),
@@ -291,17 +318,16 @@
             pltpu.VMEM((length, ne), BF),
             pltpu.VMEM((length, total), BF),
         ],
-        compiler_params=pltpu.CompilerParams(vmem_limit_bytes=VMEM_BYTES),
-        cost_estimate=cost(2 * 1200 * 10**6, 8 * 10**6, 8 * 65536),
-        name="attention_backward",
-    )(back, loss, sent, m2, o2, g3, inv, cosine, sine)
+        compiler_params=pltpu.CompilerParams(vmem_limit_bytes=2 * VMEM_BYTES),
+        cost_estimate=cost(8 * 10**9, 30 * 10**6, 8 * 65536),
+        name="project_and_backward",
+    )(sent, *small, *weights)
 
 
 def forward_kernel(
-    new_ref, sent_ref, u_ref, m_ref, o_ref, g_ref, cos_ref, sin_ref,
-    y_ref, base_ref,
-    q, k, v1, scores, low, mixed, heads,
+    new_ref, sent_ref, u_ref, m_ref, o_ref, g_ref, cos_ref, sin_ref, *rest,
 ):
+    y_ref, base_ref, q, k, v1, scores, low, mixed, heads = rest[-9:]
     length, rank = new_ref.shape
     wide = u_ref.shape[0]
     is_first = lax.axis_index("pipe") == 0
@@ -325,13 +351,13 @@
     base_ref[...] = nn(jnp.concatenate([coeffs] * 3, axis=1), g_ref[...])
 
 
-def forward(new, sent, basis, m2, o2, g3, cosine, sine):
+def forward(new, sent, basis, m2, o2, g3, cosine, sine, *after):
     length, rank = new.shape
     ne = o2.shape[0]
     stack = ne // HD * length
     return pl.pallas_call(
         forward_kernel,
-        in_specs=vmem(8),
+        in_specs=vmem(8) + [pl.BlockSpec(memory_space=pl.ANY)] * len(after),
         out_specs=vmem(2),
         out_shape=[
             jax.ShapeDtypeStruct((length, rank), BF),
@@ -347,48 +373,51 @@
             pltpu.VMEM((length, ne), BF),
         ],
         compiler_params=pltpu.CompilerParams(vmem_limit_bytes=VMEM_BYTES),
-        cost_estimate=cost(2 * 900 * 10**6, 6 * 10**6, 8 * 65536),
+        cost_estimate=cost(10**8, 10**6),
         name="attention_forward",
-    )(new, sent, basis, m2, o2, g3, cosine, sine)
-
-
-def gain_kernel(u_ref, wq_ref, wk_ref, wv_ref, inner_ref, out_ref, turned):
-    nq, nk, nv = wq_ref.shape[1], wk_ref.shape[1], wv_ref.shape[1]
-
-    @pl.when(pl.program_id(0) == 0)
-    def _():
-        turned[...] = inner_ref[:, : nq + nk + nv].T
-
-    against = nn(wq_ref[...], turned[:nq, :])
-    against += nn(wk_ref[...], turned[nq : nq + nk, :])
-    against += nn(wv_ref[...], turned[nq + nk :, :])
-    terms = against * u_ref[...].astype(F32)
-    folded = sum(terms[:, at : at + HD] for at in range(0, terms.shape[1], HD))
-    out_ref[...] = jnp.sum(folded.T, axis=0, keepdims=True)
+    )(new, sent, basis, m2, o2, g3, cosine, sine, *after)
+
+
+def gain_kernel(u_ref, wq_ref, wk_ref, wv_ref, inner_ref, out_ref, u, wq, wk, wv, turned, sems):
+    nq, nk, nv = wq.shape[1], wk.shape[1], wv.shape[1]
+    wide = u.shape[0]
+    steps = wide // PIECE
+
+    def work(i):
+        @pl.when(i == 0)
+        def _():
+            turned[...] = inner_ref[:, : nq + nk + nv].T
+
+        rows = pl.ds(pl.multiple_of(i * PIECE, PIECE), PIECE)
+        against = nn(wq[rows, :], turned[:nq, :])
+        against += nn(wk[rows, :], turned[nq : nq + nk, :])
+        against += nn(wv[rows, :], turned[nq + nk :, :])
+        terms = against * u[rows, :].astype(F32)
+        folded = sum(terms[:, at : at + HD] for at in range(0, terms.shape[1], HD))
+        out_ref[:, rows] = jnp.sum(folded.T, axis=0, keepdims=True)
+
+    pairs = ((u_ref, u, 0), (wq_ref, wq, 0), (wk_ref, wk, 0), (wv_ref, wv, 0))
+    streamed(pairs, sems, steps, 3, work)
 
 
 def gain_part(basis, wq, wk, wv, inner):
     wide, rank = basis.shape
-    nq, nk, nv = wq.shape[1], wk.shape[1], wv.shape[1]
-    block = 512
-    rows = lambda i: (i, 0)
+    weights = in_hbm((basis, wq, wk, wv))
+    total = wq.shape[1] + wk.shape[1] + wv.shape[1]
     return pl.pallas_call(
         gain_kernel,
-        grid=(wide // block,),
-        in_specs=[
-            pl.BlockSpec((block, rank), rows),
-            pl.BlockSpec((block, nq), rows),
-            pl.BlockSpec((block, nk), rows),
-            pl.BlockSpec((block, nv), rows),
-            pl.BlockSpec(inner.shape, lambda i: (0, 0)),
+        in_specs=[pl.BlockSpec(memory_space=pltpu.HBM)] * len(weights) + vmem(1),
+        out_specs=pl.BlockSpec(memory_space=pltpu.VMEM),
+        out_shape=jax.ShapeDtypeStruct((1, wide), F32),
+        scratch_shapes=[pltpu.VMEM(w.shape, BF) for w in weights]
+        + [
+            pltpu.VMEM((total, rank), BF),
+            pltpu.SemaphoreType.DMA((len(weights), wide // PIECE)),
         ],
-        out_specs=pl.BlockSpec((1, block), lambda i: (0, i)),
-        scratch_shapes=[pltpu.VMEM((nq + nk + nv, rank), BF)],
-        out_shape=jax.ShapeDtypeStruct((1, wide), F32),
         compiler_params=pltpu.CompilerParams(vmem_limit_bytes=VMEM_BYTES),
-        cost_estimate=cost(2 * wide * rank * (nq + nk + nv), 2 * wide * (nq + nk + nv + rank)),
+        cost_estimate=cost(10**8, 10**6),
         name="gain_gradient",
-    )(basis, wq, wk, wv, inner)
+    )(*weights, inner)
 
 
 def gather_halves(own_ref, other_ref, whole):
@@ -398,7 +427,7 @@
     whole[pl.ds(pl.multiple_of((1 - core) * half, half), half), :] = other_ref[...]
 
 
-def inward_kernel(me_ref, u_ref, gain_ref, own_ref, other_ref, q_ref, k_ref, v_ref, inner):
+def inward_kernel(me_ref, u_ref, gain_ref, own_ref, other_ref, after, q_ref, k_ref, v_ref, inner):
     nq, nk = q_ref.shape[1], k_ref.shape[1]
     block = q_ref.shape[0]
 
@@ -413,7 +442,7 @@
     v_ref[...] = grad[:, nq + nk :].astype(BF)
 
 
-def outward_kernel(me_ref, u_ref, own_ref, other_ref, o_ref, inner):
+def outward_kernel(me_ref, u_ref, own_ref, other_ref, after, o_ref, inner):
     @pl.when(pl.program_id(0) == 0)
     def _():
         gather_halves(own_ref, other_ref, inner)
@@ -430,7 +459,7 @@
     return lax.axis_index("dp").astype(jnp.int32).reshape(1)
 
 
-def inward_grads(basis, gain, own, other, sizes):
+def inward_grads(basis, gain, own, other, sizes, after):
     wide, rank = basis.shape
     rows = wide // lax.axis_size("dp")
     block = rows // STEPS
@@ -446,18 +475,19 @@
                 pl.BlockSpec((1, block), lambda i, me: (0, me[0] * STEPS + i)),
                 pl.BlockSpec(own.shape, fixed),
                 pl.BlockSpec(other.shape, fixed),
+                pl.BlockSpec(memory_space=pl.ANY),
             ],
             out_specs=[pl.BlockSpec((block, n), step_rows) for n in sizes],
             scratch_shapes=[pltpu.VMEM((rank, sum(sizes)), BF)],
         ),
         out_shape=[jax.ShapeDtypeStruct((rows, n), BF) for n in sizes],
         compiler_params=pltpu.CompilerParams(vmem_limit_bytes=VMEM_BYTES),
-        cost_estimate=cost(2 * rows * rank * sum(sizes), 4 * 10**6),
+        cost_estimate=cost(10**8, 10**6),
         name="inward_weight_gradients",
-    )(my_part(), basis, gain, own, other)
-
-
-def outward_grad(basis, own, other):
+    )(my_part(), basis, gain, own, other, after)
+
+
+def outward_grad(basis, own, other, after):
     wide, rank = basis.shape
     rows = wide // lax.axis_size("dp")
     ne = own.shape[1]
@@ -471,15 +501,16 @@
                 pl.BlockSpec((rows, rank), lambda i, me: (me[0], 0)),
                 pl.BlockSpec(own.shape, fixed),
                 pl.BlockSpec(other.shape, fixed),
+                pl.BlockSpec(memory_space=pl.ANY),
             ],
             out_specs=pl.BlockSpec((ne // STEPS, rows), lambda i, me: (i, 0)),
             scratch_shapes=[pltpu.VMEM((rank, ne), BF)],
         ),
         out_shape=jax.ShapeDtypeStruct((ne, rows), BF),
         compiler_params=pltpu.CompilerParams(vmem_limit_bytes=VMEM_BYTES),
-        cost_estimate=cost(2 * rows * rank * ne, 3 * 10**6),
+        cost_estimate=cost(10**8, 10**6),
         name="output_weight_gradient",
-    )(my_part(), basis, own, other)
+    )(my_part(), basis, own, other, after)
 
 
 def results_kernel(
@@ -502,7 +533,7 @@
         out_specs=vmem(2),
         out_shape=[jax.ShapeDtypeStruct(shape, BF)] * 2,
         compiler_params=pltpu.CompilerParams(vmem_limit_bytes=VMEM_BYTES),
-        cost_estimate=cost(10**6, 2 * 10**6),
+        cost_estimate=cost(10**8, 10**6),
         name="section_results",
     )(*operands)
 
@@ -527,37 +558,37 @@
     arrived, returned = cross_pipe(sent_forward[0], sent_backward[0])
     cosine, sine = rope_tables(back.shape[0])
 
-    m2, o2, g3, inv = project(back, subspace, norm_gain, wq, wk, wv, wo)
-    inner, give, keep, x, base, unit = backward(
-        back, loss_grad, returned, m2, o2, g3, inv, cosine, sine
+    inner, give, keep, x, base, unit, inv, m2, o2, g3 = backward(
+        back, loss_grad, returned, norm_gain, cosine, sine, subspace, wq, wk, wv, wo
     )
     total = nq + nk + nv
     got = swap(give, "dp", 1)
     x_got = swap(x, "tensor", 1)
-    y, fbase = forward(new_coeffs, arrived, subspace, m2, o2, g3, cosine, sine)
+    gain = gain_part(subspace, wq, wk, wv, inner)
     pair_out = add_wide(keep[:, total:], got[:, total:]).astype(BF)
     pair_in = add_wide(keep[:, :total], got[:, :total]).astype(BF)
     got_out = swap(pair_out, "dp", 2)
     got_in = swap(pair_in, "dp", 2)
-    y_got = swap(y, "tensor", 1)
     x = add_wide(x, x_got).astype(BF)
     x_got = swap(x, "tensor", 2)
-    gain = gain_part(subspace, wq, wk, wv, inner)
-    y = add_wide(y, y_got).astype(BF)
+    y, fbase = forward(
+        new_coeffs, arrived, subspace, m2, o2, g3, cosine, sine, gain, pair_out, pair_in, x
+    )
+    gain = gain + swap(gain, "tensor", 1)
+    gain_two = gain + swap(gain, "tensor", 2)
+    gain_three = gain_two + swap(gain_two, "dp", 1)
+    gain_sum = gain_three + swap(gain_three, "dp", 2)
+    y = add_wide(y, swap(y, "tensor", 1)).astype(BF)
     y_got = swap(y, "tensor", 2)
-    gain = gain + swap(gain, "tensor", 1)
-    gain = gain + swap(gain, "tensor", 2)
-    gain = gain + swap(gain, "dp", 1)
-    gain = gain + swap(gain, "dp", 2)
 
     own = add_wide(pair_out, got_out).astype(BF)
-    grad_o = outward_grad(subspace, own, swap(own, "dp", 1))
+    grad_o = outward_grad(subspace, own, swap(own, "dp", 1), gain)
     forward_out, backward_out = results(
         wide, fbase, y, y_got, base, unit, x, x_got, back, inv
     )
     own = add_wide(pair_in, got_in).astype(BF)
     grad_q, grad_k, grad_v = inward_grads(
-        subspace, norm_gain, own, swap(own, "dp", 1), (nq, nk, nv)
+        subspace, norm_gain, own, swap(own, "dp", 1), (nq, nk, nv), gain_three
     )
     return (
         forward_out[None],
@@ -566,7 +597,7 @@
         grad_k[None],
         grad_v[None],
         grad_o[None],
-        gain,
+        gain_sum,
     )
 
 

time: 93.7 us -> 81.7 us (0.87)
  local copies, waits for them, and re-layouts: 17.2 us -> 5.34 us
  waiting for transfers between devices: 25.7 us -> 20.1 us
  Pallas kernels: 32.3 us -> 35.5 us
  starting transfers between devices: 14.3 us -> 16.3 us
    unnamed x52 -> x28, local copies, waits for them, and re-layouts: 17.2 us -> 5.34 us
    ppermute x14, waiting for transfers between devices: 25.7 us -> 20.1 us  [swap(): return lax.ppermute(x, axis, [(i, i ^ bit) for i in range(devices)])]
    pallas_call x4 -> x3, Pallas kernels: 24.9 us -> 28 us  [the longest x1 16.7 us: backward(): pl.pallas_call(backward_kernel, in_specs=vmem(1) + [pl.BlockSpec(memory_s...]
    ppermute x14, starting transfers between devices: 14.3 us -> 16.3 us  [swap(): return lax.ppermute(x, axis, [(i, i ^ bit) for i in range(devices)])]
  transfers between devices with their start and end apart: 14 -> 14, of which waited for: 7 -> 6; matrix products, arithmetic and copies ran while one was open for 2% -> 3% of each run, Pallas kernels for 26% -> 20%
where the time goes in v1:
time: 81.7 us; the launch traced here: 81.3 us
  Pallas kernels  35.5 us (43%)
  waiting for transfers between devices  20.1 us (25%)
  starting transfers between devices  16.3 us (20%)
  local copies, waits for them, and re-layouts  5.34 us (7%)
  other arithmetic  3.29 us (4%)
  between operations  0.82 us (1%)
    ppermute x14, waiting for transfers between devices, swap(): return lax.ppermute(x, axis, [(i, i ^ bit) for i in range(devices)])  20.1 us
    pallas_call x1, Pallas kernels, backward(): pl.pallas_call(backward_kernel, in_specs=vmem(1) + [pl.BlockSpec(memory_s...  16.7 us
    ppermute x14, starting transfers between devices, swap(): return lax.ppermute(x, axis, [(i, i ^ bit) for i in range(devices)])  16.3 us
    pallas_call x1, Pallas kernels, gain_part(): pl.pallas_call(gain_kernel, in_specs=[pl.BlockSpec(memory_space=pltpu.HBM...  7.57 us
    unnamed x28, local copies, waits for them, and re-layouts  5.34 us
    pallas_call x1, Pallas kernels, forward(): pl.pallas_call(forward_kernel, in_specs=vmem(8) + [pl.BlockSpec(memory_sp...  3.77 us
    pallas_call x1, Pallas kernels, inward_grads(): pl.pallas_call(inward_kernel, grid_spec=pltpu.PrefetchScalarGridSpec(num_...  2.81 us
    pallas_call x1, Pallas kernels, outward_grad(): pl.pallas_call(outward_kernel, grid_spec=pltpu.PrefetchScalarGridSpec(num...  2.71 us
  transfers between devices with their start and end apart: 14, of which 6 were waited for; matrix products, arithmetic and copies ran while one was open for 3% of the time, Pallas kernels for 20%

profile of v1, /device:TPU:0, one launch (start us, length us, event | category | flops | bytes accessed | tf_op | source)
XLA Modules:
  0.0 81.3 jit_solution(8388082937980332638)
XLA Ops:
  0.6 0.9 %select_bitcast_fusion = bf16[256,256]{1,0:T(8,128)(2,1)S(1)} fusion(bf16[1,256,256]{2,1,0:T(8,128)(2,1)} %param.15, bf16[1,256,256]{2,1,0:T(8,128)(2,1)} %param.16, pred[]{:T(512)S(6)} %eq.3), kind=kLoop, calls=%fused_computation.6 | loop fusion | flops 65536 | bytes 393217 | tf_op jit(solution)/shard_map/jit(_where)/select_n | solution.py:37
  1.6 3.0 %collective-permute-start = (bf16[256,256]{1,0:T(8,128)(2,1)S(1)}, bf16[256,256]{1,0:T(8,128)(2,1)S(1)}, u32[]{:S(2)}, u32[]{:S(2)}) collective-permute-start(bf16[256,256]{1,0:T(8,128)(2,1)S(1)} %select_bitcast_fusion), channel_id=1, source_target_pairs={{0,16},{16,0},{1,17},{17,1},{2,18},{18,2},{3,19},{19,3},{4,20},{20... | collective-permute-start | bytes 393224 | tf_op jit(solution)/shard_map/ppermute | solution.py:30
  4.6 3.5 %collective-permute-done.sent_ref = bf16[256,256]{1,0:T(8,128)(2,1)S(1)} collective-permute-done((bf16[256,256]{1,0:T(8,128)(2,1)S(1)}, bf16[256,256]{1,0:T(8,128)(2,1)S(1)}, u32[]{:S(2)}, u32[]{:S(2)}) %collective-permute-start) | collective-permute-done | bytes 131104 | tf_op jit(solution)/shard_map/ppermute | solution.py:30
  8.1 16.7 %project_and_backward.1 = (bf16[256,2304]{1,0:T(8,128)(2,1)S(1)}, bf16[128,2304]{1,0:T(8,128)(2,1)S(1)}, bf16[128,2304]{1,0:T(8,128)(2,1)S(1)}, bf16[256,256]{1,...) custom-call(bf16[256,256]{1,0:T(8,128)(2,1)S(1)} %collective-permute, ...), custom_call_target="tpu_custom_call" | custom-call | flops 8000000000 | bytes 30000000 | tf_op jit(solution)/shard_map/project_and_backward/pallas_call | solution.py:282
  25.5 1.8 %collective-permute-start.2 = (bf16[256,256]{1,0:T(8,128)(2,1)S(1)}, bf16[256,256]{1,0:T(8,128)(2,1)S(1)}, u32[]{:S(2)}, u32[]{:S(2)}) collective-permute-start(bf16[256,256]{1,0:T(8,128)(2,1)S(1)} %get-tuple-element.30), channel_id=1, source_target_pairs={{0,4},{4,0},{8,12},{12,8},{1,5},{5,1},{9,13},{13,9},{2,6},{6,2},{1... | collective-permute-start | bytes 393224 | tf_op jit(solution)/shard_map/ppermute | solution.py:30
  27.3 7.6 %gain_gradient.1.rest_0_ = f32[1,4096]{1,0:T(1,128)S(1)} custom-call(bf16[4096,256]{1,0:T(8,128)(2,1)} %u_ref.9, bf16[4096,1024]{1,0:T(8,128)(2,1)} %bitcast.17, bf16[4096,128]{1,0:T(8,128)(2,1)} %bitcast.20, bf16[4096,128]{1,0:T(8,128)(2,1)} %bitcast.22, bf16[256,2304]{1,0:T(8,128)(2,1)S(1)} %get-tuple-element.27.inner_ref), custom_call_target="tpu_custom_call" | custom-call | flops 100000000 | bytes 1000000 | tf_op jit(solution)/shard_map/gain_gradient/pallas_call | solution.py:407
  35.0 1.6 %collective-permute-start.11 = (bf16[128,1024]{1,0:T(8,128)(2,1)S(1)}, bf16[128,1024]{1,0:T(8,128)(2,1)S(1)}, u32[]{:S(2)}, u32[]{:S(2)}) collective-permute-start(bf16[128,1024]{1,0:T(8,128)(2,1)S(1)} %add_convert_fusion.3.rest_1_), channel_id=1, source_target_pairs={{0,2},{1,3},{2,0},{3,1},{4,6},{5,7},{6,4},{7,5},{8,10},{9,11},{10,... | collective-permute-start | bytes 786440 | tf_op jit(solution)/shard_map/ppermute | solution.py:30
  37.3 2.7 %collective-permute-start.5 = (bf16[256,256]{1,0:T(8,128)(2,1)S(1)}, bf16[256,256]{1,0:T(8,128)(2,1)}, u32[]{:S(2)}, u32[]{:S(2)}) collective-permute-start(bf16[256,256]{1,0:T(8,128)(2,1)S(1)} %add_convert_fusion.5.rest_3_.x_ref), channel_id=1, source_target_pairs={{0,8},{4,12},{8,0},{12,4},{1,9},{5,13},{9,1},{13,5},{2,10},{6,14},... | collective-permute-start | bytes 393224 | tf_op jit(solution)/shard_map/ppermute | solution.py:30
  39.9 3.8 %attention_forward.1 = (bf16[256,256]{1,0:T(8,128)(2,1)S(1)}, f32[256,256]{1,0:T(8,128)S(1)}) custom-call(bf16[256,256]{1,0:T(8,128)(2,1)S(1)} %copy-done.7, bf16[256,256]{1,0:T(8,128)(2,1)S(1)} %collective-permute-done.sent_ref, bf16[4096,256]{1,0:T(8,128)(2,1)S(1)} %copy-done, bf16[512,1280]{1,0:T(8,128)(2,1)S(1)} %get-tuple-element.24.m_ref, ...), custom_call_target="tpu_custom_call" | custom-call | flops 100000000 | bytes 1000000 | tf_op jit(solution)/shard_map/attention_forward/pallas_call | solution.py:358
  44.4 6.1 %collective-permute-done.6 = bf16[128,1280]{1,0:T(8,128)(2,1)S(1)} collective-permute-done((bf16[128,1280]{1,0:T(8,128)(2,1)S(1)}, bf16[128,1280]{1,0:T(8,128)(2,1)S(1)}, u32[]{:S(2)}, u32[]{:S(2)}) %collective-permute-start.6) | collective-permute-done | bytes 327712 | tf_op jit(solution)/shard_map/ppermute | solution.py:30
  50.7 2.7 %collective-permute-start.4 = (bf16[256,256]{1,0:T(8,128)(2,1)S(1)}, bf16[256,256]{1,0:T(8,128)(2,1)}, u32[]{:S(2)}, u32[]{:S(2)}) collective-permute-start(bf16[256,256]{1,0:T(8,128)(2,1)S(1)} %add_convert_fusion.4.y_ref), channel_id=1, source_target_pairs={{0,8},{4,12},{8,0},{12,4},{1,9},{5,13},{9,1},{13,5},{2,10},{6,14},... | collective-permute-start | bytes 393224 | tf_op jit(solution)/shard_map/ppermute | solution.py:30
  53.8 3.3 %collective-permute-done.8 = f32[1,4096]{1,0:T(1,128)S(1)} collective-permute-done((f32[1,4096]{1,0:T(1,128)S(1)}, f32[1,4096]{1,0:T(1,128)S(1)}, u32[]{:S(2)}, u32[]{:S(2)}) %collective-permute-start.8) | collective-permute-done | bytes 16416 | tf_op jit(solution)/shard_map/ppermute | solution.py:30
  57.2 1.3 %collective-permute-start.9 = (f32[1,4096]{1,0:T(1,128)S(1)}, f32[1,4096]{1,0:T(1,128)S(1)}, u32[]{:S(2)}, u32[]{:S(2)}) collective-permute-start(f32[1,4096]{1,0:T(1,128)S(1)} %add.35.after), channel_id=1, source_target_pairs={{0,8},{4,12},{8,0},{12,4},{1,9},{5,13},{9,1},{13,5},{2,10},{6,14},... | collective-permute-start | bytes 49160 | tf_op jit(solution)/shard_map/ppermute | solution.py:30
  58.5 3.4 %collective-permute-done.9 = f32[1,4096]{1,0:T(1,128)S(1)} collective-permute-done((f32[1,4096]{1,0:T(1,128)S(1)}, f32[1,4096]{1,0:T(1,128)S(1)}, u32[]{:S(2)}, u32[]{:S(2)}) %collective-permute-start.9) | collective-permute-done | bytes 16416 | tf_op jit(solution)/shard_map/ppermute | solution.py:30
  62.0 1.2 %collective-permute-done.10 = f32[1,4096]{1,0:T(1,128)S(1)} collective-permute-done((f32[1,4096]{1,0:T(1,128)S(1)}, f32[1,4096]{1,0:T(1,128)S(1)}, u32[]{:S(2)}, u32[]{:S(2)}) %collective-permute-start.10) | collective-permute-done | bytes 16416 | tf_op jit(solution)/shard_map/ppermute | solution.py:30
  63.8 1.5 %collective-permute-start.13 = (f32[1,4096]{1,0:T(1,128)}, f32[1,4096]{1,0:T(1,128)}, u32[]{:S(2)}, u32[]{:S(2)}) collective-permute-start(f32[1,4096]{1,0:T(1,128)} %add.37.after), channel_id=1, source_target_pairs={{0,2},{1,3},{2,0},{3,1},{4,6},{5,7},{6,4},{7,5},{8,10},{9,11},{10,... | collective-permute-start | bytes 49160 | tf_op jit(solution)/shard_map/ppermute | solution.py:30
  65.3 2.5 %collective-permute-done.13 = f32[1,4096]{1,0:T(1,128)} collective-permute-done((f32[1,4096]{1,0:T(1,128)}, f32[1,4096]{1,0:T(1,128)}, u32[]{:S(2)}, u32[]{:S(2)}) %collective-permute-start.13) | collective-permute-done | bytes 16416 | tf_op jit(solution)/shard_map/ppermute | solution.py:30
  67.8 1.4 %add.39 = f32[1,4096]{1,0:T(1,128)} add(f32[1,4096]{1,0:T(1,128)} %add.37.after, f32[1,4096]{1,0:T(1,128)} %collective-permute-done.13) | non-fusion elementwise | flops 4096 | bytes 49152 | tf_op jit(solution)/shard_map/add | solution.py:580
  69.2 0.9 %copy-done.2 = f32[256,256]{1,0:T(8,128)S(1)} copy-done((f32[256,256]{1,0:T(8,128)S(1)}, f32[256,256]{1,0:T(8,128)}, u32[]{:S(2)}) %copy-start.2) | copy-done | bytes 262168
  70.2 0.9 %copy-done.4 = f32[256,256]{1,0:T(8,128)S(1)} copy-done((f32[256,256]{1,0:T(8,128)S(1)}, f32[256,256]{1,0:T(8,128)}, u32[]{:S(2)}) %copy-start.4) | copy-done | bytes 262168
  71.1 0.9 %copy-done.6 = f32[256,256]{1,0:T(8,128)S(1)} copy-done((f32[256,256]{1,0:T(8,128)S(1)}, f32[256,256]{1,0:T(8,128)}, u32[]{:S(2)}) %copy-start.6) | copy-done | bytes 262168
  73.9 1.9 %section_results.1 = (bf16[256,256]{1,0:T(8,128)(2,1)}, bf16[256,256]{1,0:T(8,128)(2,1)}) custom-call(f32[256,256]{1,0:T(8,128)S(1)} %copy-done.6, bf16[256,256]{1,0:T(8,128)(2,1)S(1)} %add_convert_fusion.4.y_ref, bf16[256,256]{1,0:T(8,128)(2,1)} %collective-permute-done.4.ygot_ref, f32[256,256]{1,0:T(8,128)S(1)} %copy-done.2, f32[256,256]{1,0:T(8,128)S(1)} %copy-done.4, ...), custom_call_target="tpu_custom_call" | custom-call | flops 100000000 | bytes 1000000 | tf_op jit(solution)/shard_map/section_results/pallas_call | solution.py:530
  75.8 2.7 %output_weight_gradient.1 = bf16[1024,1024]{1,0:T(8,128)(2,1)} custom-call(s32[1]{0:T(128)} %bitcast.8.me_ref, bf16[4096,256]{1,0:T(8,128)(2,1)S(1)} %copy-done, bf16[128,1024]{1,0:T(8,128)(2,1)S(1)} %add_convert_fusion.2.own_ref, bf16[128,1024]{1,0:T(8,128)(2,1)S(1)} %collective-permute-done.12.other_ref, f32[1,4096]{1,0:T(1,128)S(1)} %add.35.after), custom_call_target="tpu_custom_call" | custom-call | flops 100000000 | bytes 1000000 | tf_op jit(solution)/shard_map/output_weight_gradient/pallas_call | solution.py:495
  78.5 2.8 %inward_weight_gradients.1 = (bf16[1024,1024]{1,0:T(8,128)(2,1)}, bf16[1024,128]{1,0:T(8,128)(2,1)}, bf16[1024,128]{1,0:T(8,128)(2,1)}) custom-call(s32[1]{0:T(128)} %bitcast.8.me_ref, bf16[4096,256]{1,0:T(8,128)(2,1)S(1)} %copy-done, f32[1,4096]{1,0:T(1,128)S(1)} %copy-done.13, bf16[128,1280]{1,0:T(8,128)(2,1)S(1)} %add_convert_fusion.own_ref, ...), custom_call_target="tpu_custom_call" | custom-call | flops 100000000 | bytes 1000000 | tf_op jit(solution)/shard_map/inward_weight_gradients/pallas_call | solution.py:468
  (49 shorter events, 5.3 us)
Async XLA Ops:
  1.6 6.5 %collective-permute-start = (bf16[256,256]{1,0:T(8,128)(2,1)S(1)}, bf16[256,256]{1,0:T(8,128)(2,1)S(1)}, u32[]{:S(2)}, u32[]{:S(2)}) collective-permute-start(bf16[256,256]{1,0:T(8,128)(2,1)S(1)} %select_bitcast_fusion), channel_id=1, source_target_pairs={{0,16},{16,0},{1,17},{17,1},{2,18},{18,2},{3,19},{19,3},{4,20},{20... | collective-permute-start | bytes 393224 | tf_op jit(solution)/shard_map/ppermute | solution.py:30
  25.4 9.4 %copy-start.1 = (f32[256,256]{1,0:T(8,128)}, f32[256,256]{1,0:T(8,128)S(1)}, u32[]{:S(2)}) copy-start(f32[256,256]{1,0:T(8,128)S(1)} %get-tuple-element.33.base_ref) | copy-start | bytes 786436
  25.5 9.4 %copy-start.3 = (f32[256,256]{1,0:T(8,128)}, f32[256,256]{1,0:T(8,128)S(1)}, u32[]{:S(2)}) copy-start(f32[256,256]{1,0:T(8,128)S(1)} %get-tuple-element.34.unit_ref) | copy-start | bytes 786436
  25.5 9.4 %collective-permute-start.1 = (bf16[128,2304]{1,0:T(8,128)(2,1)S(1)}, bf16[128,2304]{1,0:T(8,128)(2,1)S(1)}, u32[]{:S(2)}, u32[]{:S(2)}) collective-permute-start(bf16[128,2304]{1,0:T(8,128)(2,1)S(1)} %get-tuple-element.29), channel_id=1, source_target_pairs={{0,1},{1,0},{2,3},{3,2},{4,5},{5,4},{6,7},{7,6},{8,9},{9,8},{10,11... | collective-permute-start | bytes 1769480 | tf_op jit(solution)/shard_map/ppermute | solution.py:30
  25.5 11.8 %collective-permute-start.2 = (bf16[256,256]{1,0:T(8,128)(2,1)S(1)}, bf16[256,256]{1,0:T(8,128)(2,1)S(1)}, u32[]{:S(2)}, u32[]{:S(2)}) collective-permute-start(bf16[256,256]{1,0:T(8,128)(2,1)S(1)} %get-tuple-element.30), channel_id=1, source_target_pairs={{0,4},{4,0},{8,12},{12,8},{1,5},{5,1},{9,13},{13,9},{2,6},{6,2},{1... | collective-permute-start | bytes 393224 | tf_op jit(solution)/shard_map/ppermute | solution.py:30
  27.3 12.6 %copy-start.7 = (bf16[256,256]{1,0:T(8,128)(2,1)S(1)}, bf16[256,256]{1,0:T(8,128)(2,1)}, u32[]{:S(2)}) copy-start(bf16[256,256]{1,0:T(8,128)(2,1)} %new_ref.1) | copy-start | bytes 393220
  27.3 12.6 %copy-start.11 = (f32[256,128]{1,0:T(8,128)S(1)}, f32[256,128]{1,0:T(8,128)}, u32[]{:S(2)}) copy-start(f32[256,128]{1,0:T(8,128)} %constant.16.clone.cos_hbm.cos_ref) | copy-start | bytes 393220
  27.3 12.6 %copy-start.12 = (f32[256,128]{1,0:T(8,128)S(1)}, f32[256,128]{1,0:T(8,128)}, u32[]{:S(2)}) copy-start(f32[256,128]{1,0:T(8,128)} %constant.17.clone.sin_hbm.sin_ref) | copy-start | bytes 393220
  34.9 5.0 %copy-start = (bf16[4096,256]{1,0:T(8,128)(2,1)S(1)}, bf16[4096,256]{1,0:T(8,128)(2,1)}, u32[]{:S(2)}) copy-start(bf16[4096,256]{1,0:T(8,128)(2,1)} %u_ref.9) | copy-start | bytes 6291460
  35.0 9.2 %collective-permute-start.11 = (bf16[128,1024]{1,0:T(8,128)(2,1)S(1)}, bf16[128,1024]{1,0:T(8,128)(2,1)S(1)}, u32[]{:S(2)}, u32[]{:S(2)}) collective-permute-start(bf16[128,1024]{1,0:T(8,128)(2,1)S(1)} %add_convert_fusion.3.rest_1_), channel_id=1, source_target_pairs={{0,2},{1,3},{2,0},{3,1},{4,6},{5,7},{6,4},{7,5},{8,10},{9,11},{10,... | collective-permute-start | bytes 786440 | tf_op jit(solution)/shard_map/ppermute | solution.py:30
  36.6 13.9 %collective-permute-start.6 = (bf16[128,1280]{1,0:T(8,128)(2,1)S(1)}, bf16[128,1280]{1,0:T(8,128)(2,1)S(1)}, u32[]{:S(2)}, u32[]{:S(2)}) collective-permute-start(bf16[128,1280]{1,0:T(8,128)(2,1)S(1)} %add_convert_fusion.1.rest_2_), channel_id=1, source_target_pairs={{0,2},{1,3},{2,0},{3,1},{4,6},{5,7},{6,4},{7,5},{8,10},{9,11},{10,... | collective-permute-start | bytes 983048 | tf_op jit(solution)/shard_map/ppermute | solution.py:30
  37.3 32.0 %collective-permute-start.5 = (bf16[256,256]{1,0:T(8,128)(2,1)S(1)}, bf16[256,256]{1,0:T(8,128)(2,1)}, u32[]{:S(2)}, u32[]{:S(2)}) collective-permute-start(bf16[256,256]{1,0:T(8,128)(2,1)S(1)} %add_convert_fusion.5.rest_3_.x_ref), channel_id=1, source_target_pairs={{0,8},{4,12},{8,0},{12,4},{1,9},{5,13},{9,1},{13,5},{2,10},{6,14},... | collective-permute-start | bytes 393224 | tf_op jit(solution)/shard_map/ppermute | solution.py:30
  43.7 7.0 %copy-start.5 = (f32[256,256]{1,0:T(8,128)}, f32[256,256]{1,0:T(8,128)S(1)}, u32[]{:S(2)}) copy-start(f32[256,256]{1,0:T(8,128)S(1)} %get-tuple-element.31.fbase_ref) | copy-start | bytes 786436
  43.7 7.0 %collective-permute-start.3 = (bf16[256,256]{1,0:T(8,128)(2,1)S(1)}, bf16[256,256]{1,0:T(8,128)(2,1)S(1)}, u32[]{:S(2)}, u32[]{:S(2)}) collective-permute-start(bf16[256,256]{1,0:T(8,128)(2,1)S(1)} %get-tuple-element.32), channel_id=1, source_target_pairs={{0,4},{4,0},{8,12},{12,8},{1,5},{5,1},{9,13},{13,9},{2,6},{6,2},{1... | collective-permute-start | bytes 393224 | tf_op jit(solution)/shard_map/ppermute | solution.py:30
  44.3 31.5 %collective-permute-start.12 = (bf16[128,1024]{1,0:T(8,128)(2,1)S(1)}, bf16[128,1024]{1,0:T(8,128)(2,1)S(1)}, u32[]{:S(2)}, u32[]{:S(2)}) collective-permute-start(bf16[128,1024]{1,0:T(8,128)(2,1)S(1)} %add_convert_fusion.2.own_ref), channel_id=1, source_target_pairs={{0,1},{1,0},{2,3},{3,2},{4,5},{5,4},{6,7},{7,6},{8,9},{9,8},{10,11... | collective-permute-start | bytes 786440 | tf_op jit(solution)/shard_map/ppermute | solution.py:30
  50.6 27.9 %collective-permute-start.7 = (bf16[128,1280]{1,0:T(8,128)(2,1)S(1)}, bf16[128,1280]{1,0:T(8,128)(2,1)S(1)}, u32[]{:S(2)}, u32[]{:S(2)}) collective-permute-start(bf16[128,1280]{1,0:T(8,128)(2,1)S(1)} %add_convert_fusion.own_ref), channel_id=1, source_target_pairs={{0,1},{1,0},{2,3},{3,2},{4,5},{5,4},{6,7},{7,6},{8,9},{9,8},{10,11... | collective-permute-start | bytes 983048 | tf_op jit(solution)/shard_map/ppermute | solution.py:30
  50.7 18.5 %collective-permute-start.4 = (bf16[256,256]{1,0:T(8,128)(2,1)S(1)}, bf16[256,256]{1,0:T(8,128)(2,1)}, u32[]{:S(2)}, u32[]{:S(2)}) collective-permute-start(bf16[256,256]{1,0:T(8,128)(2,1)S(1)} %add_convert_fusion.4.y_ref), channel_id=1, source_target_pairs={{0,8},{4,12},{8,0},{12,4},{1,9},{5,13},{9,1},{13,5},{2,10},{6,14},... | collective-permute-start | bytes 393224 | tf_op jit(solution)/shard_map/ppermute | solution.py:30
  53.4 3.8 %collective-permute-start.8 = (f32[1,4096]{1,0:T(1,128)S(1)}, f32[1,4096]{1,0:T(1,128)S(1)}, u32[]{:S(2)}, u32[]{:S(2)}) collective-permute-start(f32[1,4096]{1,0:T(1,128)S(1)} %gain_gradient.1.rest_0_), channel_id=1, source_target_pairs={{0,4},{4,0},{8,12},{12,8},{1,5},{5,1},{9,13},{13,9},{2,6},{6,2},{1... | collective-permute-start | bytes 49160 | tf_op jit(solution)/shard_map/ppermute | solution.py:30
  57.2 4.7 %collective-permute-start.9 = (f32[1,4096]{1,0:T(1,128)S(1)}, f32[1,4096]{1,0:T(1,128)S(1)}, u32[]{:S(2)}, u32[]{:S(2)}) collective-permute-start(f32[1,4096]{1,0:T(1,128)S(1)} %add.35.after), channel_id=1, source_target_pairs={{0,8},{4,12},{8,0},{12,4},{1,9},{5,13},{9,1},{13,5},{2,10},{6,14},... | collective-permute-start | bytes 49160 | tf_op jit(solution)/shard_map/ppermute | solution.py:30
  61.9 1.2 %collective-permute-start.10 = (f32[1,4096]{1,0:T(1,128)S(1)}, f32[1,4096]{1,0:T(1,128)S(1)}, u32[]{:S(2)}, u32[]{:S(2)}) collective-permute-start(f32[1,4096]{1,0:T(1,128)S(1)} %add.36), channel_id=1, source_target_pairs={{0,1},{1,0},{2,3},{3,2},{4,5},{5,4},{6,7},{7,6},{8,9},{9,8},{10,11... | collective-permute-start | bytes 49160 | tf_op jit(solution)/shard_map/ppermute | solution.py:30
  63.8 4.1 %collective-permute-start.13 = (f32[1,4096]{1,0:T(1,128)}, f32[1,4096]{1,0:T(1,128)}, u32[]{:S(2)}, u32[]{:S(2)}) collective-permute-start(f32[1,4096]{1,0:T(1,128)} %add.37.after), channel_id=1, source_target_pairs={{0,2},{1,3},{2,0},{3,1},{4,6},{5,7},{6,4},{7,5},{8,10},{9,11},{10,... | collective-permute-start | bytes 49160 | tf_op jit(solution)/shard_map/ppermute | solution.py:30
  69.2 1.0 %copy-start.2 = (f32[256,256]{1,0:T(8,128)S(1)}, f32[256,256]{1,0:T(8,128)}, u32[]{:S(2)}) copy-start(f32[256,256]{1,0:T(8,128)} %copy-done.1) | copy-start | bytes 786436
  70.2 0.9 %copy-start.4 = (f32[256,256]{1,0:T(8,128)S(1)}, f32[256,256]{1,0:T(8,128)}, u32[]{:S(2)}) copy-start(f32[256,256]{1,0:T(8,128)} %copy-done.3) | copy-start | bytes 786436
  75.8 2.7 %copy-start.13 = (f32[1,4096]{1,0:T(1,128)S(1)}, f32[1,4096]{1,0:T(1,128)}, u32[]{:S(2)}) copy-start(f32[1,4096]{1,0:T(1,128)} %gain_ref.1) | copy-start | bytes 49156
  (4 other events, 3.4 us)

commit v2 on v1

v2 whole, which is shorter than its diff:
```python
import functools
import math

import jax
import jax.numpy as jnp
import numpy as np
from jax import lax
from jax.experimental import pallas as pl
from jax.experimental.pallas import tpu as pltpu
from jax.sharding import PartitionSpec as P

HD = 128
EPSILON = 1e-05
ROPE_BASE = 500000.0
BF = jnp.bfloat16
F32 = jnp.float32
VMEM_BYTES = 24 * 1024 * 1024
CHUNK = 512
LOG2E = 1.4426950408889634


def shifted(x, axis, by):
    devices = lax.axis_size(axis)
    pairs = [(i, i + by) for i in range(devices) if 0 <= i + by < devices]
    return lax.ppermute(x, axis, pairs)


def swap(x, axis, bit):
    devices = lax.axis_size(axis)
    return lax.ppermute(x, axis, [(i, i ^ bit) for i in range(devices)])


def cross_pipe(sent_forward, sent_backward):
    if lax.axis_size("pipe") != 2:
        return shifted(sent_forward, "pipe", 1), shifted(sent_backward, "pipe", -1)
    first = lax.axis_index("pipe") == 0
    got = swap(jnp.where(first, sent_forward, sent_backward), "pipe", 1)
    return got, got


def sum_over_tensor(x):
    if lax.axis_size("tensor") != 4:
        return lax.psum(x, "tensor")
    one, two, three = (swap(x, "tensor", bit) for bit in (1, 2, 3))
    return (x + one) + (two + three)


def add_wide(a, b):
    return a.astype(F32) + b.astype(F32)


def nt(a, b):
    return lax.dot_general(a, b, (((1,), (1,)), ((), ())), preferred_element_type=F32)


def nn(a, b):
    return jnp.dot(a, b, preferred_element_type=F32)


def split(x, parts):
    out = []
    for _ in range(parts):
        piece = x.astype(BF)
        out.append(piece)
        x = x - piece.astype(F32)
    return out


def rope_tables(length):
    half = HD // 2
    frequency = np.float32(ROPE_BASE) ** (-2.0 * np.arange(half, dtype=np.float32) / HD)
    angles = np.arange(length, dtype=np.float32)[:, None] * frequency.astype(np.float32)
    cosine, sine = np.cos(angles), np.sin(angles)
    tables = (np.concatenate([cosine, cosine], 1), np.concatenate([-sine, sine], 1))
    return tuple(jnp.asarray(t, dtype=F32) for t in tables)


def rope(x, cosine, sine):
    return x * cosine + pltpu.roll(x, HD // 2, 1) * sine


def unrope(x, cosine, sine):
    return x * cosine - pltpu.roll(x, HD // 2, 1) * sine


def inverse_root(square_sum, width):
    return 1.0 / jnp.sqrt(square_sum / width + EPSILON)


def vmem(count):
    return [pl.BlockSpec(memory_space=pltpu.VMEM)] * count


def in_hbm(arrays):
    return tuple(pltpu.with_memory_space_constraint(a, pltpu.HBM) for a in arrays)


def cost(flops, num_bytes, exps=0):
    return pl.CostEstimate(flops=flops, bytes_accessed=num_bytes, transcendentals=exps)


def streamed(pairs, sems, first, steps, ahead, work):
    def copies(i):
        out = []
        for n, (source, target, axis) in enumerate(pairs):
            size = target.shape[axis] // steps
            to = pl.ds(pl.multiple_of(i * size, size), size)
            at = pl.ds(pl.multiple_of(first + i * size, size), size)
            if axis == 0:
                piece, place = source.at[at, :], target.at[to, :]
            else:
                piece, place = source.at[:, at], target.at[:, to]
            out.append(pltpu.make_async_copy(piece, place, sems.at[n, i]))
        return out

    for i in range(ahead):
        for copy in copies(i):
            copy.start()

    def one(i, _):
        @pl.when(i + ahead < steps)
        def _():
            for copy in copies(i + ahead):
                copy.start()

        for copy in copies(i):
            copy.wait()
        work(i)
        return 0

    lax.fori_loop(0, steps, one, 0)


def project_kernel(
    back_hbm, gain_hbm, u_ref, wq_ref, wk_ref, wv_ref, wo_ref,
    m_ref, o_ref, g_ref, inv_ref,
    back, gain, small_sems, u, wq, wk, wv, wo, m_acc, o_acc, g_acc, square, sems,
):
    wide, rank = u.shape
    nq, nk = wq.shape[1], wk.shape[1]
    steps = wide // CHUNK
    block = CHUNK
    small = (
        pltpu.make_async_copy(back_hbm, back, small_sems.at[0]),
        pltpu.make_async_copy(gain_hbm, gain, small_sems.at[1]),
    )
    for copy in small:
        copy.start()
    m_acc[...] = jnp.zeros_like(m_acc)
    o_acc[...] = jnp.zeros_like(o_acc)
    g_acc[...] = jnp.zeros_like(g_acc)
    square[...] = jnp.zeros_like(square)

    def work(i):
        @pl.when(i == 0)
        def _():
            for copy in small:
                copy.wait()

        rows = pl.ds(pl.multiple_of(i * block, block), block)
        basis = u[rows, :]
        turned = basis.T
        scaled = (turned.astype(F32) * gain[:, rows]).astype(BF)
        for ref, at in ((wq, 0), (wk, nq), (wv, nq + nk)):
            size = ref.shape[1]
            m_acc[:, at : at + size] += nn(scaled, ref[rows, :])
        o_acc[...] += nn(wo[:, rows], basis)
        g_acc[...] += nn(turned, basis)
        decoded = nn(back[...], turned)
        total = square[...]
        for side in range(0, block, HD):
            part = decoded[:, side : side + HD]
            total = total + part * part
        square[...] = total

    pairs = ((u_ref, u, 0), (wq_ref, wq, 0), (wk_ref, wk, 0), (wv_ref, wv, 0), (wo_ref, wo, 1))
    streamed(pairs, sems, 0, steps, 2, work)
    for i, piece in enumerate(split(m_acc[...], 2)):
        m_ref[i * rank : (i + 1) * rank, :] = piece
    o_ref[...] = o_acc[...].astype(BF)
    for i, piece in enumerate(split(g_acc[...], 3)):
        g_ref[i * rank : (i + 1) * rank, :] = piece
    inv_ref[...] = jnp.broadcast_to(
        inverse_root(jnp.sum(square[...], axis=1, keepdims=True), wide), inv_ref.shape
    )


def project(back, gain, basis, wq, wk, wv, wo):
    wide, rank = basis.shape
    length = back.shape[0]
    ne = wo.shape[0]
    total = wq.shape[1] + wk.shape[1] + wv.shape[1]
    small = in_hbm((back, gain))
    weights = in_hbm((basis, wq, wk, wv, wo))
    return pl.pallas_call(
        project_kernel,
        in_specs=[pl.BlockSpec(memory_space=pltpu.HBM)] * len(small + weights),
        out_specs=vmem(4),
        out_shape=[
            jax.ShapeDtypeStruct((2 * rank, total), BF),
            jax.ShapeDtypeStruct((ne, rank), BF),
            jax.ShapeDtypeStruct((3 * rank, rank), BF),
            jax.ShapeDtypeStruct((length, HD), F32),
        ],
        scratch_shapes=[pltpu.VMEM(a.shape, a.dtype) for a in small]
        + [pltpu.SemaphoreType.DMA((len(small),))]
        + [pltpu.VMEM(w.shape, BF) for w in weights]
        + [
            pltpu.VMEM((rank, total), F32),
            pltpu.VMEM((ne, rank), F32),
            pltpu.VMEM((rank, rank), F32),
            pltpu.VMEM((length, HD), F32),
            pltpu.SemaphoreType.DMA((len(weights), wide // CHUNK)),
        ],
        compiler_params=pltpu.CompilerParams(vmem_limit_bytes=2 * VMEM_BYTES),
        cost_estimate=cost(6 * 10**9, 20 * 10**6),
        name="project_weights",
    )(*small, *weights)


def project_heads(coeffs, inv, m_ref, cosine, sine, q, k, v1):
    length = coeffs.shape[0]
    heads = q.shape[0] // length
    twice = jnp.concatenate([coeffs, coeffs], axis=1)
    for h in range(heads):
        part = nn(twice, m_ref[:, h * HD : (h + 1) * HD]) * inv
        q[h * length : (h + 1) * length, :] = rope(part, cosine, sine).astype(BF)
    part = nn(twice, m_ref[:, heads * HD :]) * inv
    k[...] = rope(part[:, :HD], cosine, sine).astype(BF)
    v1[:, :HD] = part[:, HD:].astype(BF)
    v1[:, HD:] = jnp.ones_like(v1[:, HD:])


def exps_of(scores, exps, low, length):
    row = lax.broadcasted_iota(jnp.int32, (length, length), 0)
    column = lax.broadcasted_iota(jnp.int32, (length, length), 1)
    causal = row >= column

    def one(h, _):
        at = pl.ds(pl.multiple_of(h * length, length), length)
        s = jnp.where(causal, scores[at, :], -jnp.inf)
        top = jnp.max(s, axis=1, keepdims=True)
        e = jnp.exp2((s - top) * (LOG2E / math.sqrt(HD)))
        if exps is not None:
            exps[at, :] = e
        low[at, :] = e.astype(BF)
        return 0

    lax.fori_loop(0, scores.shape[0] // length, one, 0, unroll=2)


def backward_kernel(
    back_ref, loss_ref, sent_ref, m_ref, o_ref, g_ref, inv_ref, cos_ref, sin_ref,
    inner_ref, out_give_ref, out_keep_ref, x_ref, base_ref, unit_ref,
    q, k, v1, gh, ghs, scores, low, mixed, gp, ds, dq, heads, grads, inner, out_inner,
):
    length, rank = back_ref.shape
    ne = o_ref.shape[0]
    count = ne // HD
    scale = 1.0 / math.sqrt(HD)
    last = lax.axis_size("pipe") - 1
    is_last = lax.axis_index("pipe") == last
    back = back_ref[...]
    up = jnp.where(is_last, loss_ref[...], sent_ref[...])
    cosine, sine = cos_ref[...], sin_ref[...]
    inv = inv_ref[...]
    project_heads(back, inv[:, :1], m_ref, cosine, sine, q, k, v1)
    scores[...] = nt(q[...], k[...])
    for h in range(count):
        gh[h * length : (h + 1) * length, :] = nt(up, o_ref[h * HD : (h + 1) * HD, :]).astype(BF)
    exps_of(scores, scores, low, length)
    mixed[...] = nn(low[...], v1[...])
    gp[...] = nt(gh[...], v1[:, :HD])

    for h in range(count):
        at = slice(h * length, (h + 1) * length)
        inverse = 1.0 / mixed[at, HD:]
        out = mixed[at, :HD] * inverse
        heads[:, h * HD : (h + 1) * HD] = out.astype(BF)
        grad = gh[at, :].astype(F32)
        ghs[at, :] = (grad * inverse).astype(BF)
        delta = jnp.sum(grad * out, axis=1, keepdims=True)
        factor = inverse * scale
        for side in range(0, length, HD):
            part = scores[at, side : side + HD] * factor
            ds[at, side : side + HD] = (part * (gp[at, side : side + HD] - delta)).astype(BF)

    dq[...] = nn(ds[...], k[...])
    for h in range(count):
        part = dq[h * length : (h + 1) * length, :]
        grads[:, h * HD : (h + 1) * HD] = unrope(part, cosine, sine).astype(BF)
    dk = nn(q[...].T, ds[...]).T
    grads[:, ne : ne + HD] = unrope(dk, cosine, sine).astype(BF)
    grads[:, ne + HD :] = nn(ghs[...].T, low[...]).T.astype(BF)
    unit = (back.astype(F32) * inv[:, :1]).astype(BF)
    half = rank // 2
    core = lax.axis_index("dp") & 1
    mine = pl.ds(pl.multiple_of(core * half, half), half)
    theirs = pl.ds(pl.multiple_of((1 - core) * half, half), half)
    inner[...] = nn(unit.T, grads[...]).astype(BF)
    inner_ref[:half, :] = inner[mine, :]
    inner_ref[half:, :] = inner[theirs, :]
    out_inner[...] = nn(up.T, heads[...]).astype(BF)
    out_keep_ref[...] = out_inner[mine, :]
    out_give_ref[...] = out_inner[theirs, :]
    x_ref[...] = nt(grads[...], m_ref[:rank, :]).astype(BF)
    base_ref[...] = nn(jnp.concatenate([up] * 3, axis=1), g_ref[...])
    unit_ref[...] = nn(jnp.concatenate([back] * 3, axis=1), g_ref[...]) * inv[:, :1]


def backward(back, loss, sent, m2, o2, g3, inv, cosine, sine):
    length, rank = back.shape
    ne = o2.shape[0]
    total = m2.shape[1]
    assert total == ne + 2 * HD
    stack = ne // HD * length
    return pl.pallas_call(
        backward_kernel,
        in_specs=vmem(9),
        out_specs=vmem(6),
        out_shape=[
            jax.ShapeDtypeStruct((rank, total), BF),
            jax.ShapeDtypeStruct((rank // 2, ne), BF),
            jax.ShapeDtypeStruct((rank // 2, ne), BF),
            jax.ShapeDtypeStruct((length, rank), BF),
            jax.ShapeDtypeStruct((length, rank), F32),
            jax.ShapeDtypeStruct((length, rank), F32),
        ],
        scratch_shapes=[
            pltpu.VMEM((stack, HD), BF),
            pltpu.VMEM((length, HD), BF),
            pltpu.VMEM((length, 2 * HD), BF),
            pltpu.VMEM((stack, HD), BF),
            pltpu.VMEM((stack, HD), BF),
            pltpu.VMEM((stack, length), F32),
            pltpu.VMEM((stack, length), BF),
            pltpu.VMEM((stack, 2 * HD), F32),
            pltpu.VMEM((stack, length), F32),
            pltpu.VMEM((stack, length), BF),
            pltpu.VMEM((stack, HD), F32),
            pltpu.VMEM((length, ne), BF),
            pltpu.VMEM((length, total), BF),
            pltpu.VMEM((rank, total), BF),
            pltpu.VMEM((rank, ne), BF),
        ],
        compiler_params=pltpu.CompilerParams(vmem_limit_bytes=VMEM_BYTES),
        cost_estimate=cost(10**8, 10**6),
        name="attention_backward",
    )(back, loss, sent, m2, o2, g3, inv, cosine, sine)


def forward_kernel(
    new_ref, sent_ref, u_ref, m_ref, o_ref, g_ref, cos_ref, sin_ref, *rest,
):
    y_ref, base_ref, q, k, v1, scores, low, mixed, heads = rest[-9:]
    length, rank = new_ref.shape
    wide = u_ref.shape[0]
    is_first = lax.axis_index("pipe") == 0
    coeffs = jnp.where(is_first, new_ref[...], sent_ref[...])
    square = jnp.zeros((length, HD), F32)
    block = 512
    for at in range(0, wide, block):
        decoded = nt(coeffs, u_ref[at : at + block, :])
        for side in range(0, block, HD):
            part = decoded[:, side : side + HD]
            square = square + part * part
    inv = inverse_root(jnp.sum(square, axis=1, keepdims=True), wide)
    project_heads(coeffs, inv, m_ref, cos_ref[...], sin_ref[...], q, k, v1)
    scores[...] = nt(q[...], k[...])
    exps_of(scores, None, low, length)
    mixed[...] = nn(low[...], v1[...])
    for h in range(heads.shape[1] // HD):
        at = slice(h * length, (h + 1) * length)
        heads[:, h * HD : (h + 1) * HD] = (mixed[at, :HD] / mixed[at, HD:]).astype(BF)
    y_ref[...] = nn(heads[...], o_ref[...]).astype(BF)
    base_ref[...] = nn(jnp.concatenate([coeffs] * 3, axis=1), g_ref[...])


def forward(new, sent, basis, m2, o2, g3, cosine, sine, *after):
    length, rank = new.shape
    ne = o2.shape[0]
    stack = ne // HD * length
    return pl.pallas_call(
        forward_kernel,
        in_specs=vmem(8) + [pl.BlockSpec(memory_space=pl.ANY)] * len(after),
        out_specs=vmem(2),
        out_shape=[
            jax.ShapeDtypeStruct((length, rank), BF),
            jax.ShapeDtypeStruct((length, rank), F32),
        ],
        scratch_shapes=[
            pltpu.VMEM((stack, HD), BF),
            pltpu.VMEM((length, HD), BF),
            pltpu.VMEM((length, 2 * HD), BF),
            pltpu.VMEM((stack, length), F32),
            pltpu.VMEM((stack, length), BF),
            pltpu.VMEM((stack, 2 * HD), F32),
            pltpu.VMEM((length, ne), BF),
        ],
        compiler_params=pltpu.CompilerParams(vmem_limit_bytes=VMEM_BYTES),
        cost_estimate=cost(10**8, 10**6),
        name="attention_forward",
    )(new, sent, basis, m2, o2, g3, cosine, sine, *after)


def gain_kernel(u_ref, wq_ref, wk_ref, wv_ref, inner_ref, got_ref, after, out_ref, turned):
    nq, nk = wq_ref.shape[1], wk_ref.shape[1]
    rows = out_ref.shape[1]
    half = inner_ref.shape[0] // 2
    core = lax.axis_index("dp") & 1
    mine = add_wide(inner_ref[:half, :], got_ref[half:, :]).astype(BF)
    theirs = add_wide(inner_ref[half:, :], got_ref[:half, :]).astype(BF)
    turned[:, pl.ds(pl.multiple_of(core * half, half), half)] = mine.T
    turned[:, pl.ds(pl.multiple_of((1 - core) * half, half), half)] = theirs.T
    for at in range(0, rows, CHUNK):
        place = pl.ds(pl.multiple_of(core * rows + at, CHUNK), CHUNK)
        against = nn(wq_ref[place, :], turned[:nq, :])
        narrow = jnp.concatenate([wk_ref[place, :], wv_ref[place, :]], axis=1)
        against += nn(narrow, turned[nq:, :])
        terms = against * u_ref[place, :].astype(F32)
        folded = sum(terms[:, side : side + HD] for side in range(0, terms.shape[1], HD))
        out_ref[:, at : at + CHUNK] = jnp.sum(folded.T, axis=0, keepdims=True)


def gain_part(basis, wq, wk, wv, inner, got, after):
    wide, rank = basis.shape
    rows = wide // 2
    return pl.pallas_call(
        gain_kernel,
        in_specs=vmem(6) + [pl.BlockSpec(memory_space=pl.ANY)],
        out_specs=pl.BlockSpec(memory_space=pltpu.VMEM),
        out_shape=jax.ShapeDtypeStruct((1, rows), F32),
        scratch_shapes=[pltpu.VMEM((inner.shape[1], rank), BF)],
        compiler_params=pltpu.CompilerParams(vmem_limit_bytes=VMEM_BYTES),
        cost_estimate=cost(10**8, 10**6),
        name="gain_gradient",
    )(basis, wq, wk, wv, inner, got, after)


def add_kernel(a_ref, b_ref, after, out_ref):
    out_ref[...] = add_wide(a_ref[...], b_ref[...]).astype(BF)


def add_after(a, b, after):
    return pl.pallas_call(
        add_kernel,
        in_specs=vmem(2) + [pl.BlockSpec(memory_space=pl.ANY)],
        out_specs=pl.BlockSpec(memory_space=pltpu.VMEM),
        out_shape=jax.ShapeDtypeStruct(a.shape, BF),
        compiler_params=pltpu.CompilerParams(vmem_limit_bytes=VMEM_BYTES // 2),
        cost_estimate=cost(10**6, 10**5),
        name="pair_sum",
    )(a, b, after)


def gather_halves(own_ref, other_ref, whole):
    half = own_ref.shape[0]
    core = lax.axis_index("dp") & 1
    whole[pl.ds(pl.multiple_of(core * half, half), half), :] = own_ref[...]
    whole[pl.ds(pl.multiple_of((1 - core) * half, half), half), :] = other_ref[...]


def inward_kernel(u_ref, gain_ref, own_ref, other_ref, after, q_ref, k_ref, v_ref, inner):
    nq, nk = q_ref.shape[1], k_ref.shape[1]
    block = q_ref.shape[0]

    @pl.when(pl.program_id(0) == 0)
    def _():
        gather_halves(own_ref, other_ref, inner)

    step = lax.axis_index("dp") * pl.num_programs(0) + pl.program_id(0)
    rows = pl.ds(pl.multiple_of(step * block, block), block)
    gain = jnp.broadcast_to(gain_ref[:, rows], (HD, block)).T[:, :1]
    grad = nn(u_ref[rows, :], inner[...]) * gain
    q_ref[...] = grad[:, :nq].astype(BF)
    k_ref[...] = grad[:, nq : nq + nk].astype(BF)
    v_ref[...] = grad[:, nq + nk :].astype(BF)


def outward_kernel(u_ref, own_ref, other_ref, after, o_ref, inner):
    @pl.when(pl.program_id(0) == 0)
    def _():
        gather_halves(own_ref, other_ref, inner)

    block, rows = o_ref.shape
    at = pl.multiple_of(pl.program_id(0) * block, block)
    basis = u_ref[pl.ds(pl.multiple_of(lax.axis_index("dp") * rows, rows), rows), :]
    o_ref[...] = nt(inner[:, pl.ds(at, block)].T, basis).astype(BF)


STEPS = 2


def inward_grads(basis, gain, own, other, sizes, after):
    wide, rank = basis.shape
    rows = wide // lax.axis_size("dp")
    block = rows // STEPS
    return pl.pallas_call(
        inward_kernel,
        grid=(STEPS,),
        in_specs=vmem(4) + [pl.BlockSpec(memory_space=pl.ANY)],
        out_specs=[pl.BlockSpec((block, n), lambda i: (i, 0)) for n in sizes],
        scratch_shapes=[pltpu.VMEM((rank, sum(sizes)), BF)],
        out_shape=[jax.ShapeDtypeStruct((rows, n), BF) for n in sizes],
        compiler_params=pltpu.CompilerParams(vmem_limit_bytes=VMEM_BYTES),
        cost_estimate=cost(10**8, 10**6),
        name="inward_weight_gradients",
    )(basis, gain, own, other, after)


def outward_grad(basis, own, other, after):
    wide, rank = basis.shape
    rows = wide // lax.axis_size("dp")
    ne = own.shape[1]
    return pl.pallas_call(
        outward_kernel,
        grid=(STEPS,),
        in_specs=vmem(3) + [pl.BlockSpec(memory_space=pl.ANY)],
        out_specs=pl.BlockSpec((ne // STEPS, rows), lambda i: (i, 0)),
        scratch_shapes=[pltpu.VMEM((rank, ne), BF)],
        out_shape=jax.ShapeDtypeStruct((ne, rows), BF),
        compiler_params=pltpu.CompilerParams(vmem_limit_bytes=VMEM_BYTES),
        cost_estimate=cost(10**8, 10**6),
        name="output_weight_gradient",
    )(basis, own, other, after)


def results_kernel(
    wide, fbase_ref, y_ref, ygot_ref, base_ref, unit_ref, x_ref, xgot_ref, back_ref, inv_ref,
    gain_ref, gain_one_ref, gain_two_ref, gain_three_ref, after,
    f_ref, b_ref, gain_out_ref,
):
    f_ref[...] = (fbase_ref[...] + add_wide(y_ref[...], ygot_ref[...])).astype(BF)
    x = add_wide(x_ref[...], xgot_ref[...])
    inv = inv_ref[:, :1]
    along = jnp.sum(x * back_ref[...].astype(F32), axis=1, keepdims=True)
    middle = along * inv * (1.0 / wide)
    b_ref[...] = (base_ref[...] + (x - unit_ref[...] * middle) * inv).astype(BF)
    core = lax.axis_index("dp") & 1
    half = gain_ref.shape[1]
    mine = pl.ds(pl.multiple_of(core * half, half), half)
    theirs = pl.ds(pl.multiple_of((1 - core) * half, half), half)
    gain_out_ref[:, mine] = gain_ref[...] + gain_two_ref[...]
    gain_out_ref[:, theirs] = gain_one_ref[...] + gain_three_ref[...]


def results(wide, after, *operands):
    shape = operands[0].shape
    held = tuple(pltpu.with_memory_space_constraint(a, pltpu.VMEM) for a in operands)
    return pl.pallas_call(
        functools.partial(results_kernel, wide),
        in_specs=vmem(len(operands)) + [pl.BlockSpec(memory_space=pl.ANY)],
        out_specs=vmem(3),
        out_shape=[jax.ShapeDtypeStruct(shape, BF)] * 2 + [jax.ShapeDtypeStruct((1, wide), F32)],
        compiler_params=pltpu.CompilerParams(vmem_limit_bytes=VMEM_BYTES // 2),
        cost_estimate=cost(10**8, 10**6),
        name="section_results",
    )(*held, *in_hbm((after,)))


def body(
    new_coeffs,
    loss_grad,
    sent_forward,
    sent_backward,
    stashed,
    subspace,
    norm_gain,
    w_query,
    w_key,
    w_value,
    w_output,
):
    wide = subspace.shape[0]
    wq, wk, wv, wo = w_query[0], w_key[0], w_value[0], w_output[0]
    nq, nk, nv = wq.shape[1], wk.shape[1], wv.shape[1]
    back = stashed[0]
    arrived, returned = cross_pipe(sent_forward[0], sent_backward[0])
    cosine, sine = rope_tables(back.shape[0])

    m2, o2, g3, inv = project(back, norm_gain, subspace, wq, wk, wv, wo)
    inner, out_give, out_keep, x, base, unit = backward(
        back, loss_grad, returned, m2, o2, g3, inv, cosine, sine
    )
    half = inner.shape[0] // 2
    out_got = swap(out_give, "dp", 1)
    inner_got = swap(inner, "dp", 1)
    x_got = swap(x, "tensor", 1)
    out_pair = add_wide(out_keep, out_got).astype(BF)
    pair = add_wide(inner[:half], inner_got[half:]).astype(BF)
    out_got = swap(out_pair, "dp", 2)
    pair_got = swap(pair, "dp", 2)
    x = add_after(x, x_got, pair)
    x_got = swap(x, "tensor", 2)
    y, fbase = forward(
        new_coeffs, arrived, subspace, m2, o2, g3, cosine, sine, out_pair, x
    )
    y_got = swap(y, "tensor", 1)
    gain = gain_part(subspace, wq, wk, wv, inner, inner_got, y)
    y = add_wide(y, y_got).astype(BF)
    y_got = swap(y, "tensor", 2)
    gain = sum_over_tensor(gain)
    gains = [gain] + [swap(gain, "dp", bit) for bit in (1, 2, 3)]

    own = add_wide(out_pair, out_got).astype(BF)
    grad_o = outward_grad(subspace, own, swap(own, "dp", 1), y)
    own = add_wide(pair, pair_got).astype(BF)
    grad_q, grad_k, grad_v = inward_grads(
        subspace, norm_gain, own, swap(own, "dp", 1), (nq, nk, nv), gain
    )
    forward_out, backward_out, grad_gain = results(
        wide, grad_v, fbase, y, y_got, base, unit, x, x_got, back, inv, *gains
    )
    return (
        forward_out[None],
        backward_out[None],
        grad_q[None],
        grad_k[None],
        grad_v[None],
        grad_o[None],
        grad_gain,
    )


def solution(mesh):
    return jax.shard_map(
        body,
        mesh=mesh,
        in_specs=(
            P("dp", None),
            P("dp", None),
            P("pipe", "dp", None),
            P("pipe", "dp", None),
            P("pipe", "dp", None),
            P(),
            P("pipe", None),
            P("pipe", None, "tensor"),
            P("pipe", None, "tensor"),
            P("pipe", None, "tensor"),
            P("pipe", "tensor", None),
        ),
        out_specs=(
            P("pipe", "dp", None),
            P("pipe", "dp", None),
            P("pipe", "dp", "tensor"),
            P("pipe", "dp", "tensor"),
            P("pipe", "dp", "tensor"),
            P("pipe", "tensor", "dp"),
            P("pipe", None),
        ),
        check_vma=False,
    )
```

time: 81.7 us -> 54.6 us (0.67)
  waiting for transfers between devices: 20.1 us -> 5.73 us
  Pallas kernels: 35.5 us -> 28.4 us
  local copies, waits for them, and re-layouts: 5.34 us -> 0.06 us
  other arithmetic: 3.29 us -> 1.42 us
  starting transfers between devices: 16.3 us -> 18 us
    ppermute x14 -> x17, waiting for transfers between devices: 20.1 us -> 5.73 us  [swap(): return lax.ppermute(x, axis, [(i, i ^ bit) for i in range(devices)])]
    pallas_call x4 -> x6, Pallas kernels: 29.8 us -> 23.7 us  [the longest x1 12.4 us: project(): pl.pallas_call(project_kernel, in_specs=[pl.BlockSpec(memory_space=pltpu....]
    unnamed x28 -> x22, local copies, waits for them, and re-layouts: 5.34 us -> 0.06 us
    add x4 -> x1, other arithmetic: 2.01 us -> 0.02 us  [sum_over_tensor(): return x + one + (two + three)]
    ppermute x14 -> x17, starting transfers between devices: 16.3 us -> 18 us  [swap(): return lax.ppermute(x, axis, [(i, i ^ bit) for i in range(devices)])]
    pallas_call x1, Pallas kernels: 1.94 us -> 0.99 us  [results(): pl.pallas_call(functools.partial(results_kernel, wide), in_specs=vmem(len...]
  transfers between devices with their start and end apart: 14 -> 17, of which waited for: 6 -> 6; matrix products, arithmetic and copies ran while one was open for 3% -> 1% of each run, Pallas kernels for 20% -> 41%
where the time goes in v2:
time: 54.6 us; the launch traced here: 54.5 us
  Pallas kernels  28.4 us (52%)
  starting transfers between devices  18 us (33%)
  waiting for transfers between devices  5.73 us (10%)
  other arithmetic  1.42 us (3%)
  between operations  0.88 us (2%)
    ppermute x17, starting transfers between devices, swap(): return lax.ppermute(x, axis, [(i, i ^ bit) for i in range(devices)])  18 us
    pallas_call x1, Pallas kernels, project(): pl.pallas_call(project_kernel, in_specs=[pl.BlockSpec(memory_space=pltpu....  12.4 us
    ppermute x17, waiting for transfers between devices, swap(): return lax.ppermute(x, axis, [(i, i ^ bit) for i in range(devices)])  5.73 us
    pallas_call x1, Pallas kernels, backward(): pl.pallas_call(backward_kernel, in_specs=vmem(9), out_specs=vmem(6), out_...  5.25 us
    pallas_call x1, Pallas kernels, forward(): pl.pallas_call(forward_kernel, in_specs=vmem(8) + [pl.BlockSpec(memory_sp...  3.79 us
    pallas_call x1, Pallas kernels, inward_grads(): pl.pallas_call(inward_kernel, grid=(STEPS,), in_specs=vmem(4) + [pl.Block...  2.19 us
    pallas_call x1, Pallas kernels, outward_grad(): pl.pallas_call(outward_kernel, grid=(STEPS,), in_specs=vmem(3) + [pl.Bloc...  2.01 us
    pallas_call x1, Pallas kernels, gain_part(): pl.pallas_call(gain_kernel, in_specs=vmem(6) + [pl.BlockSpec(memory_space...  1.8 us
  transfers between devices with their start and end apart: 17, of which 6 were waited for; matrix products, arithmetic and copies ran while one was open for 1% of the time, Pallas kernels for 41%

profile of v2, /device:TPU:0, one launch (start us, length us, event | category | flops | bytes accessed | tf_op | source)
XLA Modules:
  0.0 54.5 jit_solution(1234230061920142755)
XLA Ops:
  0.7 1.1 %select_bitcast_fusion = bf16[256,256]{1,0:T(8,128)(2,1)S(1)} fusion(bf16[1,256,256]{2,1,0:T(8,128)(2,1)} %param.15, bf16[1,256,256]{2,1,0:T(8,128)(2,1)} %param.16, pred[]{:T(512)S(6)} %eq.3), kind=kLoop, calls=%fused_computation.5 | loop fusion | flops 65536 | bytes 393217 | tf_op jit(solution)/shard_map/jit(_where)/select_n | solution.py:37
  1.7 3.0 %collective-permute-start = (bf16[256,256]{1,0:T(8,128)(2,1)S(1)}, bf16[256,256]{1,0:T(8,128)(2,1)S(1)}, u32[]{:S(2)}, u32[]{:S(2)}) collective-permute-start(bf16[256,256]{1,0:T(8,128)(2,1)S(1)} %select_bitcast_fusion), channel_id=1, source_target_pairs={{0,16},{16,0},{1,17},{17,1},{2,18},{18,2},{3,19},{19,3},{4,20},{20... | collective-permute-start | bytes 393224 | tf_op jit(solution)/shard_map/ppermute | solution.py:30
  4.8 12.4 %project_weights.1 = (bf16[512,1280]{1,0:T(8,128)(2,1)S(1)}, bf16[1024,256]{1,0:T(8,128)(2,1)S(1)}, bf16[768,256]{1,0:T(8,128)(2,1)S(1)}, f32[256,128]{1,0:T(8,128)S(1)}) custom-call(bf16[256,256]{1,0:T(8,128)(2,1)} %bitcast.21, f32[1,4096]{1,0:T(1,128)} %gain_ref.1, bf16[4096,256]{1,0:T(8,128)(2,1)} %u_ref.9, bf16[4096,1024]{1,0:T(8,128)(2,1)} %bitcast.13, ...), custom_call_target="tpu_custom_call" | custom-call | flops 6000000000 | bytes 20000000 | tf_op jit(solution)/shard_map/project_weights/pallas_call | solution.py:195
  17.2 5.3 %attention_backward.1 = (bf16[256,1280]{1,0:T(8,128)(2,1)S(1)}, bf16[128,1024]{1,0:T(8,128)(2,1)S(1)}, bf16[128,1024]{1,0:T(8,128)(2,1)S(1)}, bf16[256,256]{1,0:...) custom-call(bf16[256,256]{1,0:T(8,128)(2,1)S(1)} %bitcast.22, bf16[256,256]{1,0:T(8,128)(2,1)S(1)} %copy-done.6, ...), custom_call_target="tpu_custom_call" | custom-call | flops 100000000 | bytes 1000000 | tf_op jit(solution)/shard_map/attention_backward/pallas_call | solution.py:317
  22.6 0.5 collective-permute-start.1
  23.1 1.6 %collective-permute-start.2 = (bf16[256,256]{1,0:T(8,128)(2,1)S(1)}, bf16[256,256]{1,0:T(8,128)(2,1)S(1)}, u32[]{:S(2)}, u32[]{:S(2)}) collective-permute-start(bf16[256,256]{1,0:T(8,128)(2,1)S(1)} %get-tuple-element.31.a_ref), channel_id=1, source_target_pairs={{0,4},{4,0},{8,12},{12,8},{1,5},{5,1},{9,13},{13,9},{2,6},{6,2},{1... | collective-permute-start | bytes 393224 | tf_op jit(solution)/shard_map/ppermute | solution.py:30
  24.6 0.4 collective-permute-done.1
  25.1 1.6 %collective-permute-start.15 = (bf16[128,1024]{1,0:T(8,128)(2,1)S(1)}, bf16[128,1024]{1,0:T(8,128)(2,1)S(1)}, u32[]{:S(2)}, u32[]{:S(2)}) collective-permute-start(bf16[128,1024]{1,0:T(8,128)(2,1)S(1)} %add_convert_fusion.3.rest_0_), channel_id=1, source_target_pairs={{0,2},{1,3},{2,0},{3,1},{4,6},{5,7},{6,4},{7,5},{8,10},{9,11},{10,... | collective-permute-start | bytes 786440 | tf_op jit(solution)/shard_map/ppermute | solution.py:30
  26.8 0.6 %collective-permute-start.13 = (bf16[128,1280]{1,0:T(8,128)(2,1)S(1)}, bf16[128,1280]{1,0:T(8,128)(2,1)S(1)}, u32[]{:S(2)}, u32[]{:S(2)}) collective-permute-start(bf16[128,1280]{1,0:T(8,128)(2,1)S(1)} %add_convert_fusion.1.after), channel_id=1, source_target_pairs={{0,2},{1,3},{2,0},{3,1},{4,6},{5,7},{6,4},{7,5},{8,10},{9,11},{10,... | collective-permute-start | bytes 983048 | tf_op jit(solution)/shard_map/ppermute | solution.py:30
  27.3 1.2 %collective-permute-done.2.b_ref = bf16[256,256]{1,0:T(8,128)(2,1)S(1)} collective-permute-done((bf16[256,256]{1,0:T(8,128)(2,1)S(1)}, bf16[256,256]{1,0:T(8,128)(2,1)S(1)}, u32[]{:S(2)}, u32[]{:S(2)}) %collective-permute-start.2) | collective-permute-done | bytes 131104 | tf_op jit(solution)/shard_map/ppermute | solution.py:30
  28.6 3.8 %attention_forward.1 = (bf16[256,256]{1,0:T(8,128)(2,1)S(1)}, f32[256,256]{1,0:T(8,128)S(1)}) custom-call(bf16[256,256]{1,0:T(8,128)(2,1)S(1)} %copy-done.7, bf16[256,256]{1,0:T(8,128)(2,1)S(1)} %collective-permute-done.sent_ref, bf16[4096,256]{1,0:T(8,128)(2,1)S(1)} %copy-done, bf16[512,1280]{1,0:T(8,128)(2,1)S(1)} %get-tuple-element.25.m_ref, ...), custom_call_target="tpu_custom_call" | custom-call | flops 100000000 | bytes 1000000 | tf_op jit(solution)/shard_map/attention_forward/pallas_call | solution.py:383
  32.4 1.6 %collective-permute-start.4 = (bf16[256,256]{1,0:T(8,128)(2,1)S(1)}, bf16[256,256]{1,0:T(8,128)(2,1)S(1)}, u32[]{:S(2)}, u32[]{:S(2)}) collective-permute-start(bf16[256,256]{1,0:T(8,128)(2,1)S(1)} %get-tuple-element.34.after), channel_id=1, source_target_pairs={{0,4},{4,0},{8,12},{12,8},{1,5},{5,1},{9,13},{13,9},{2,6},{6,2},{1... | collective-permute-start | bytes 393224 | tf_op jit(solution)/shard_map/ppermute | solution.py:30
  34.5 2.7 %collective-permute-start.6 = (bf16[256,256]{1,0:T(8,128)(2,1)S(1)}, bf16[256,256]{1,0:T(8,128)(2,1)S(1)}, u32[]{:S(2)}, u32[]{:S(2)}) collective-permute-start(bf16[256,256]{1,0:T(8,128)(2,1)S(1)} %pair_sum.1.rest_1_.x_ref), channel_id=1, source_target_pairs={{0,8},{4,12},{8,0},{12,4},{1,9},{5,13},{9,1},{13,5},{2,10},{6,14},... | collective-permute-start | bytes 393224 | tf_op jit(solution)/shard_map/ppermute | solution.py:30
  37.1 1.8 %gain_gradient.1 = f32[1,2048]{1,0:T(1,128)S(1)} custom-call(bf16[4096,256]{1,0:T(8,128)(2,1)S(1)} %copy-done, bf16[4096,1024]{1,0:T(8,128)(2,1)S(1)} %bitcast.16, bf16[4096,128]{1,0:T(8,128)(2,1)S(1)} %bitcast.18, bf16[4096,128]{1,0:T(8,128)(2,1)S(1)} %bitcast.20, bf16[256,1280]{1,0:T(8,128)(2,1)S(1)} %get-tuple-element.32.inner_ref, ...), custom_call_target="tpu_custom_call" | custom-call | flops 100000000 | bytes 1000000 | tf_op jit(solution)/shard_map/gain_gradient/pallas_call | solution.py:428
  38.9 0.4 collective-permute-start.8
  39.3 3.6 %collective-permute-start.9 = (f32[1,2048]{1,0:T(1,128)S(1)}, f32[1,2048]{1,0:T(1,128)S(1)}, u32[]{:S(2)}, u32[]{:S(2)}) collective-permute-start(f32[1,2048]{1,0:T(1,128)S(1)} %gain_gradient.1), channel_id=1, source_target_pairs={{0,12},{4,8},{8,4},{12,0},{1,13},{5,9},{9,5},{13,1},{2,14},{6,10},... | collective-permute-start | bytes 24584 | tf_op jit(solution)/shard_map/ppermute | solution.py:30
  43.1 1.4 %collective-permute-done.8 = f32[1,2048]{1,0:T(1,128)S(1)} collective-permute-done((f32[1,2048]{1,0:T(1,128)S(1)}, f32[1,2048]{1,0:T(1,128)S(1)}, u32[]{:S(2)}, u32[]{:S(2)}) %collective-permute-start.8) | collective-permute-done | bytes 8224 | tf_op jit(solution)/shard_map/ppermute | solution.py:30
  44.6 0.3 collective-permute-start.5
  44.9 1.8 %collective-permute-done.7 = f32[1,2048]{1,0:T(1,128)S(1)} collective-permute-done((f32[1,2048]{1,0:T(1,128)S(1)}, f32[1,2048]{1,0:T(1,128)S(1)}, u32[]{:S(2)}, u32[]{:S(2)}) %collective-permute-start.7) | collective-permute-done | bytes 8224 | tf_op jit(solution)/shard_map/ppermute | solution.py:30
  46.8 1.6 %collective-permute-start.11 = (f32[1,2048]{1,0:T(1,128)S(1)}, f32[1,2048]{1,0:T(1,128)S(1)}, u32[]{:S(2)}, u32[]{:S(2)}) collective-permute-start(f32[1,2048]{1,0:T(1,128)S(1)} %add_add_fusion.after.gain_ref), channel_id=1, source_target_pairs={{0,2},{1,3},{2,0},{3,1},{4,6},{5,7},{6,4},{7,5},{8,10},{9,11},{10,... | collective-permute-start | bytes 24584 | tf_op jit(solution)/shard_map/ppermute | solution.py:30
  48.4 2.0 %output_weight_gradient.1 = bf16[1024,1024]{1,0:T(8,128)(2,1)} custom-call(bf16[4096,256]{1,0:T(8,128)(2,1)S(1)} %copy-done, bf16[128,1024]{1,0:T(8,128)(2,1)S(1)} %add_convert_fusion.2.own_ref, bf16[128,1024]{1,0:T(8,128)(2,1)S(1)} %collective-permute-done.16.other_ref, bf16[256,256]{1,0:T(8,128)(2,1)S(1)} %add_convert_fusion.4.y_ref.after), custom_call_target="tpu_custom_call" | custom-call | flops 100000000 | bytes 1000000 | tf_op jit(solution)/shard_map/output_weight_gradient/pallas_call | solution.py:515
  50.7 2.2 %inward_weight_gradients.1 = (bf16[1024,1024]{1,0:T(8,128)(2,1)}, bf16[1024,128]{1,0:T(8,128)(2,1)}, bf16[1024,128]{1,0:T(8,128)(2,1)}) custom-call(bf16[4096,256]{1,0:T(8,128)(2,1)S(1)} %copy-done, f32[1,4096]{1,0:T(1,128)S(1)} %copy-done.8, bf16[128,1280]{1,0:T(8,128)(2,1)S(1)} %add_convert_fusion.own_ref, ...), custom_call_target="tpu_custom_call" | custom-call | flops 100000000 | bytes 1000000 | tf_op jit(solution)/shard_map/inward_weight_gradients/pallas_call | solution.py:498
  52.9 0.6 %collective-permute-done.12.gain_three_ref = f32[1,2048]{1,0:T(1,128)S(1)} collective-permute-done((f32[1,2048]{1,0:T(1,128)S(1)}, f32[1,2048]{1,0:T(1,128)S(1)}, u32[]{:S(2)}, u32[]{:S(2)}) %collective-permute-start.12) | collective-permute-done | bytes 8224 | tf_op jit(solution)/shard_map/ppermute | solution.py:30
  53.5 1.0 %section_results.1 = (bf16[256,256]{1,0:T(8,128)(2,1)}, bf16[256,256]{1,0:T(8,128)(2,1)}, f32[1,4096]{1,0:T(1,128)}) custom-call(f32[256,256]{1,0:T(8,128)S(1)} %get-tuple-element.33.fbase_ref, bf16[256,256]{1,0:T(8,128)(2,1)S(1)} %add_convert_fusion.4.y_ref.after, bf16[256,256]{1,0:T(8,128)(2,1)S(1)} %collective-permute-done.5.ygot_ref, ...), custom_call_target="tpu_custom_call" | custom-call | flops 100000000 | bytes 1000000 | tf_op jit(solution)/shard_map/section_results/pallas_call | solution.py:550
  (48 shorter events, 1.3 us)
Async XLA Ops:
  0.6 36.5 %slice-start = ((s8[8388608]{0:T(1024)(128)(4,1)}), s8[4194304]{0:T(1024)(128)(4,1)S(1)}, s32[]{:S(2)}) async-start(s8[8388608]{0:T(1024)(128)(4,1)} %bitcast.14), calls=%async_computation | async-start | bytes 8388608
  1.7 15.4 %collective-permute-start = (bf16[256,256]{1,0:T(8,128)(2,1)S(1)}, bf16[256,256]{1,0:T(8,128)(2,1)S(1)}, u32[]{:S(2)}, u32[]{:S(2)}) collective-permute-start(bf16[256,256]{1,0:T(8,128)(2,1)S(1)} %select_bitcast_fusion), channel_id=1, source_target_pairs={{0,16},{16,0},{1,17},{17,1},{2,18},{18,2},{3,19},{19,3},{4,20},{20... | collective-permute-start | bytes 393224 | tf_op jit(solution)/shard_map/ppermute | solution.py:30
  4.7 12.4 %copy-start.3 = (bf16[1,256,256]{2,1,0:T(8,128)(2,1)S(1)}, bf16[1,256,256]{2,1,0:T(8,128)(2,1)}, u32[]{:S(2)}) copy-start(bf16[1,256,256]{2,1,0:T(8,128)(2,1)} %param.17) | copy-start | bytes 393220
  4.7 12.4 %copy-start.4 = (f32[256,128]{1,0:T(8,128)S(1)}, f32[256,128]{1,0:T(8,128)}, u32[]{:S(2)}) copy-start(f32[256,128]{1,0:T(8,128)} %constant.12.clone.cos_ref) | copy-start | bytes 393220
  4.7 12.4 %copy-start.5 = (f32[256,128]{1,0:T(8,128)S(1)}, f32[256,128]{1,0:T(8,128)}, u32[]{:S(2)}) copy-start(f32[256,128]{1,0:T(8,128)} %constant.13.clone.sin_ref) | copy-start | bytes 393220
  4.7 12.4 %copy-start.6 = (bf16[256,256]{1,0:T(8,128)(2,1)S(1)}, bf16[256,256]{1,0:T(8,128)(2,1)}, u32[]{:S(2)}) copy-start(bf16[256,256]{1,0:T(8,128)(2,1)} %loss_ref.1) | copy-start | bytes 393220
  4.8 32.4 %slice-start.1 = ((s8[8388608]{0:T(1024)(128)(4,1)}), s8[4194304]{0:T(1024)(128)(4,1)S(1)}, s32[]{:S(2)}) async-start(s8[8388608]{0:T(1024)(128)(4,1)} %bitcast.14), calls=%async_computation.1 | async-start | bytes 8388608
  17.2 11.4 %copy-start = (bf16[4096,256]{1,0:T(8,128)(2,1)S(1)}, bf16[4096,256]{1,0:T(8,128)(2,1)}, u32[]{:S(2)}) copy-start(bf16[4096,256]{1,0:T(8,128)(2,1)} %u_ref.9) | copy-start | bytes 6291460
  22.5 4.2 %collective-permute-start.3 = (bf16[256,1280]{1,0:T(8,128)(2,1)S(1)}, bf16[256,1280]{1,0:T(8,128)(2,1)S(1)}, u32[]{:S(2)}, u32[]{:S(2)}) collective-permute-start(bf16[256,1280]{1,0:T(8,128)(2,1)S(1)} %get-tuple-element.32.inner_ref), channel_id=1, source_target_pairs={{0,1},{1,0},{2,3},{3,2},{4,5},{5,4},{6,7},{7,6},{8,9},{9,8},{10,11... | collective-permute-start | bytes 1966088 | tf_op jit(solution)/shard_map/ppermute | solution.py:30
  22.6 2.5 %collective-permute-start.1 = (bf16[128,1024]{1,0:T(8,128)(2,1)S(1)}, bf16[128,1024]{1,0:T(8,128)(2,1)S(1)}, u32[]{:S(2)}, u32[]{:S(2)}) collective-permute-start(bf16[128,1024]{1,0:T(8,128)(2,1)S(1)} %get-tuple-element.30), channel_id=1, source_target_pairs={{0,1},{1,0},{2,3},{3,2},{4,5},{5,4},{6,7},{7,6},{8,9},{9,8},{10,11... | collective-permute-start | bytes 786440 | tf_op jit(solution)/shard_map/ppermute | solution.py:30
  23.1 5.5 %collective-permute-start.2 = (bf16[256,256]{1,0:T(8,128)(2,1)S(1)}, bf16[256,256]{1,0:T(8,128)(2,1)S(1)}, u32[]{:S(2)}, u32[]{:S(2)}) collective-permute-start(bf16[256,256]{1,0:T(8,128)(2,1)S(1)} %get-tuple-element.31.a_ref), channel_id=1, source_target_pairs={{0,4},{4,0},{8,12},{12,8},{1,5},{5,1},{9,13},{13,9},{2,6},{6,2},{1... | collective-permute-start | bytes 393224 | tf_op jit(solution)/shard_map/ppermute | solution.py:30
  25.1 9.2 %collective-permute-start.15 = (bf16[128,1024]{1,0:T(8,128)(2,1)S(1)}, bf16[128,1024]{1,0:T(8,128)(2,1)S(1)}, u32[]{:S(2)}, u32[]{:S(2)}) collective-permute-start(bf16[128,1024]{1,0:T(8,128)(2,1)S(1)} %add_convert_fusion.3.rest_0_), channel_id=1, source_target_pairs={{0,2},{1,3},{2,0},{3,1},{4,6},{5,7},{6,4},{7,5},{8,10},{9,11},{10,... | collective-permute-start | bytes 786440 | tf_op jit(solution)/shard_map/ppermute | solution.py:30
  26.8 16.2 %collective-permute-start.13 = (bf16[128,1280]{1,0:T(8,128)(2,1)S(1)}, bf16[128,1280]{1,0:T(8,128)(2,1)S(1)}, u32[]{:S(2)}, u32[]{:S(2)}) collective-permute-start(bf16[128,1280]{1,0:T(8,128)(2,1)S(1)} %add_convert_fusion.1.after), channel_id=1, source_target_pairs={{0,2},{1,3},{2,0},{3,1},{4,6},{5,7},{6,4},{7,5},{8,10},{9,11},{10,... | collective-permute-start | bytes 983048 | tf_op jit(solution)/shard_map/ppermute | solution.py:30
  32.4 6.9 %collective-permute-start.4 = (bf16[256,256]{1,0:T(8,128)(2,1)S(1)}, bf16[256,256]{1,0:T(8,128)(2,1)S(1)}, u32[]{:S(2)}, u32[]{:S(2)}) collective-permute-start(bf16[256,256]{1,0:T(8,128)(2,1)S(1)} %get-tuple-element.34.after), channel_id=1, source_target_pairs={{0,4},{4,0},{8,12},{12,8},{1,5},{5,1},{9,13},{13,9},{2,6},{6,2},{1... | collective-permute-start | bytes 393224 | tf_op jit(solution)/shard_map/ppermute | solution.py:30
  34.4 12.4 %collective-permute-start.16 = (bf16[128,1024]{1,0:T(8,128)(2,1)S(1)}, bf16[128,1024]{1,0:T(8,128)(2,1)S(1)}, u32[]{:S(2)}, u32[]{:S(2)}) collective-permute-start(bf16[128,1024]{1,0:T(8,128)(2,1)S(1)} %add_convert_fusion.2.own_ref), channel_id=1, source_target_pairs={{0,1},{1,0},{2,3},{3,2},{4,5},{5,4},{6,7},{7,6},{8,9},{9,8},{10,11... | collective-permute-start | bytes 786440 | tf_op jit(solution)/shard_map/ppermute | solution.py:30
  34.5 19.0 %collective-permute-start.6 = (bf16[256,256]{1,0:T(8,128)(2,1)S(1)}, bf16[256,256]{1,0:T(8,128)(2,1)S(1)}, u32[]{:S(2)}, u32[]{:S(2)}) collective-permute-start(bf16[256,256]{1,0:T(8,128)(2,1)S(1)} %pair_sum.1.rest_1_.x_ref), channel_id=1, source_target_pairs={{0,8},{4,12},{8,0},{12,4},{1,9},{5,13},{9,1},{13,5},{2,10},{6,14},... | collective-permute-start | bytes 393224 | tf_op jit(solution)/shard_map/ppermute | solution.py:30
  38.9 5.6 %collective-permute-start.8 = (f32[1,2048]{1,0:T(1,128)S(1)}, f32[1,2048]{1,0:T(1,128)S(1)}, u32[]{:S(2)}, u32[]{:S(2)}) collective-permute-start(f32[1,2048]{1,0:T(1,128)S(1)} %gain_gradient.1), channel_id=1, source_target_pairs={{0,8},{4,12},{8,0},{12,4},{1,9},{5,13},{9,1},{13,5},{2,10},{6,14},... | collective-permute-start | bytes 24584 | tf_op jit(solution)/shard_map/ppermute | solution.py:30
  39.3 5.5 %collective-permute-start.9 = (f32[1,2048]{1,0:T(1,128)S(1)}, f32[1,2048]{1,0:T(1,128)S(1)}, u32[]{:S(2)}, u32[]{:S(2)}) collective-permute-start(f32[1,2048]{1,0:T(1,128)S(1)} %gain_gradient.1), channel_id=1, source_target_pairs={{0,12},{4,8},{8,4},{12,0},{1,13},{5,9},{9,5},{13,1},{2,14},{6,10},... | collective-permute-start | bytes 24584 | tf_op jit(solution)/shard_map/ppermute | solution.py:30
  43.0 3.7 %collective-permute-start.7 = (f32[1,2048]{1,0:T(1,128)S(1)}, f32[1,2048]{1,0:T(1,128)S(1)}, u32[]{:S(2)}, u32[]{:S(2)}) collective-permute-start(f32[1,2048]{1,0:T(1,128)S(1)} %gain_gradient.1), channel_id=1, source_target_pairs={{0,4},{4,0},{8,12},{12,8},{1,5},{5,1},{9,13},{13,9},{2,6},{6,2},{1... | collective-permute-start | bytes 24584 | tf_op jit(solution)/shard_map/ppermute | solution.py:30
  44.6 8.9 %collective-permute-start.5 = (bf16[256,256]{1,0:T(8,128)(2,1)S(1)}, bf16[256,256]{1,0:T(8,128)(2,1)S(1)}, u32[]{:S(2)}, u32[]{:S(2)}) collective-permute-start(bf16[256,256]{1,0:T(8,128)(2,1)S(1)} %add_convert_fusion.4.y_ref.after), channel_id=1, source_target_pairs={{0,8},{4,12},{8,0},{12,4},{1,9},{5,13},{9,1},{13,5},{2,10},{6,14},... | collective-permute-start | bytes 393224 | tf_op jit(solution)/shard_map/ppermute | solution.py:30
  44.9 5.6 %collective-permute-start.14 = (bf16[128,1280]{1,0:T(8,128)(2,1)S(1)}, bf16[128,1280]{1,0:T(8,128)(2,1)S(1)}, u32[]{:S(2)}, u32[]{:S(2)}) collective-permute-start(bf16[128,1280]{1,0:T(8,128)(2,1)S(1)} %add_convert_fusion.own_ref), channel_id=1, source_target_pairs={{0,1},{1,0},{2,3},{3,2},{4,5},{5,4},{6,7},{7,6},{8,9},{9,8},{10,11... | collective-permute-start | bytes 983048 | tf_op jit(solution)/shard_map/ppermute | solution.py:30
  46.7 6.1 %collective-permute-start.10 = (f32[1,2048]{1,0:T(1,128)S(1)}, f32[1,2048]{1,0:T(1,128)S(1)}, u32[]{:S(2)}, u32[]{:S(2)}) collective-permute-start(f32[1,2048]{1,0:T(1,128)S(1)} %add_add_fusion.after.gain_ref), channel_id=1, source_target_pairs={{0,1},{1,0},{2,3},{3,2},{4,5},{5,4},{6,7},{7,6},{8,9},{9,8},{10,11... | collective-permute-start | bytes 24584 | tf_op jit(solution)/shard_map/ppermute | solution.py:30
  46.8 6.1 %collective-permute-start.11 = (f32[1,2048]{1,0:T(1,128)S(1)}, f32[1,2048]{1,0:T(1,128)S(1)}, u32[]{:S(2)}, u32[]{:S(2)}) collective-permute-start(f32[1,2048]{1,0:T(1,128)S(1)} %add_add_fusion.after.gain_ref), channel_id=1, source_target_pairs={{0,2},{1,3},{2,0},{3,1},{4,6},{5,7},{6,4},{7,5},{8,10},{9,11},{10,... | collective-permute-start | bytes 24584 | tf_op jit(solution)/shard_map/ppermute | solution.py:30
  50.4 3.1 %collective-permute-start.12 = (f32[1,2048]{1,0:T(1,128)S(1)}, f32[1,2048]{1,0:T(1,128)S(1)}, u32[]{:S(2)}, u32[]{:S(2)}) collective-permute-start(f32[1,2048]{1,0:T(1,128)S(1)} %add_add_fusion.after.gain_ref), channel_id=1, source_target_pairs={{0,3},{1,2},{2,1},{3,0},{4,7},{5,6},{6,5},{7,4},{8,11},{9,10},{10,... | collective-permute-start | bytes 24584 | tf_op jit(solution)/shard_map/ppermute | solution.py:30
  (4 other events, 32.4 us)

commit v3 on v2

--- a/solution.py
+++ b/solution.py
@@ -16,6 +16,8 @@
 F32 = jnp.float32
 VMEM_BYTES = 24 * 1024 * 1024
 CHUNK = 512
+PIECE = 1024
+AHEAD = 3
 LOG2E = 1.4426950408889634
 
 
@@ -36,13 +38,6 @@
     first = lax.axis_index("pipe") == 0
     got = swap(jnp.where(first, sent_forward, sent_backward), "pipe", 1)
     return got, got
-
-
-def sum_over_tensor(x):
-    if lax.axis_size("tensor") != 4:
-        return lax.psum(x, "tensor")
-    one, two, three = (swap(x, "tensor", bit) for bit in (1, 2, 3))
-    return (x + one) + (two + three)
 
 
 def add_wide(a, b):
@@ -99,123 +94,117 @@
     return pl.CostEstimate(flops=flops, bytes_accessed=num_bytes, transcendentals=exps)
 
 
-def streamed(pairs, sems, first, steps, ahead, work):
-    def copies(i):
-        out = []
-        for n, (source, target, axis) in enumerate(pairs):
-            size = target.shape[axis] // steps
-            to = pl.ds(pl.multiple_of(i * size, size), size)
-            at = pl.ds(pl.multiple_of(first + i * size, size), size)
-            if axis == 0:
-                piece, place = source.at[at, :], target.at[to, :]
-            else:
-                piece, place = source.at[:, at], target.at[:, to]
-            out.append(pltpu.make_async_copy(piece, place, sems.at[n, i]))
-        return out
-
-    for i in range(ahead):
-        for copy in copies(i):
-            copy.start()
-
-    def one(i, _):
-        @pl.when(i + ahead < steps)
-        def _():
-            for copy in copies(i + ahead):
-                copy.start()
-
-        for copy in copies(i):
-            copy.wait()
-        work(i)
-        return 0
-
-    lax.fori_loop(0, steps, one, 0)
-
-
 def project_kernel(
-    back_hbm, gain_hbm, u_ref, wq_ref, wk_ref, wv_ref, wo_ref,
+    back_hbm, gain_hbm, u_hbm, wq_hbm, wk_hbm, wv_hbm, wo_hbm,
     m_ref, o_ref, g_ref, inv_ref,
-    back, gain, small_sems, u, wq, wk, wv, wo, m_acc, o_acc, g_acc, square, sems,
+    back, gain, u, wq, narrow, wo, turned, scaled, m_acc, o_acc, sems,
 ):
     wide, rank = u.shape
-    nq, nk = wq.shape[1], wk.shape[1]
-    steps = wide // CHUNK
-    block = CHUNK
-    small = (
-        pltpu.make_async_copy(back_hbm, back, small_sems.at[0]),
-        pltpu.make_async_copy(gain_hbm, gain, small_sems.at[1]),
+    nq = wq.shape[1]
+    nk = wk_hbm.shape[1]
+    parts = wide // PIECE
+    pieces = [pl.ds(i * PIECE, PIECE) for i in range(parts)]
+    pairs = [(back_hbm, back), (gain_hbm, gain), (u_hbm, u)]
+    pairs += [(wq_hbm.at[at, :], wq.at[at, :]) for at in pieces[:2]]
+    pairs += [(wk_hbm, narrow.at[:, pl.ds(0, nk)])]
+    pairs += [(wv_hbm, narrow.at[:, pl.ds(nk, narrow.shape[1] - nk)])]
+    pairs += [(wq_hbm.at[at, :], wq.at[at, :]) for at in pieces[2:]]
+    pairs += [(wo_hbm.at[:, at], wo.at[:, at]) for at in pieces]
+    copies = [
+        pltpu.make_async_copy(source, target, sems.at[n])
+        for n, (source, target) in enumerate(pairs)
+    ]
+    started = 0
+
+    def start_to(count):
+        nonlocal started
+        for copy in copies[started:count]:
+            copy.start()
+        started = max(started, min(count, len(copies)))
+
+    def wait(n):
+        start_to(n + 1 + AHEAD)
+        copies[n].wait()
+
+    start_to(3 + AHEAD)
+    for n in range(3):
+        copies[n].wait()
+    turned[...] = u[...].T
+    scaled[...] = (turned[...].astype(F32) * gain[...]).astype(BF)
+    gram = nn(turned[...], u[...])
+    for i, piece in enumerate(split(gram, 3)):
+        g_ref[i * rank : (i + 1) * rank, :] = piece
+    square = jnp.zeros((back.shape[0], HD), F32)
+    for at in range(0, wide, PIECE):
+        decoded = nn(back[...], turned[:, at : at + PIECE])
+        for side in range(0, PIECE, HD):
+            part = decoded[:, side : side + HD]
+            square = square + part * part
+    inv_ref[...] = jnp.broadcast_to(
+        inverse_root(jnp.sum(square, axis=1, keepdims=True), wide), inv_ref.shape
     )
-    for copy in small:
-        copy.start()
-    m_acc[...] = jnp.zeros_like(m_acc)
-    o_acc[...] = jnp.zeros_like(o_acc)
-    g_acc[...] = jnp.zeros_like(g_acc)
-    square[...] = jnp.zeros_like(square)
-
-    def work(i):
-        @pl.when(i == 0)
-        def _():
-            for copy in small:
-                copy.wait()
-
-        rows = pl.ds(pl.multiple_of(i * block, block), block)
-        basis = u[rows, :]
-        turned = basis.T
-        scaled = (turned.astype(F32) * gain[:, rows]).astype(BF)
-        for ref, at in ((wq, 0), (wk, nq), (wv, nq + nk)):
-            size = ref.shape[1]
-            m_acc[:, at : at + size] += nn(scaled, ref[rows, :])
-        o_acc[...] += nn(wo[:, rows], basis)
-        g_acc[...] += nn(turned, basis)
-        decoded = nn(back[...], turned)
-        total = square[...]
-        for side in range(0, block, HD):
-            part = decoded[:, side : side + HD]
-            total = total + part * part
-        square[...] = total
-
-    pairs = ((u_ref, u, 0), (wq_ref, wq, 0), (wk_ref, wk, 0), (wv_ref, wv, 0), (wo_ref, wo, 1))
-    streamed(pairs, sems, 0, steps, 2, work)
-    for i, piece in enumerate(split(m_acc[...], 2)):
-        m_ref[i * rank : (i + 1) * rank, :] = piece
+    place = 3
+    for i, at in enumerate(pieces):
+        if i == 2:
+            wait(place)
+            wait(place + 1)
+            place += 2
+            for p, piece in enumerate(split(nn(scaled[...], narrow[...]), 2)):
+                m_ref[p * rank : (p + 1) * rank, nq:] = piece
+        wait(place)
+        place += 1
+        part = nn(scaled[:, at], wq[at, :])
+        if i == 0:
+            m_acc[...] = part
+        else:
+            m_acc[...] += part
+    for p, piece in enumerate(split(m_acc[...], 2)):
+        m_ref[p * rank : (p + 1) * rank, :nq] = piece
+    for i, at in enumerate(pieces):
+        wait(place)
+        place += 1
+        part = nn(wo[:, at], u[at, :])
+        if i == 0:
+            o_acc[...] = part
+        else:
+            o_acc[...] += part
     o_ref[...] = o_acc[...].astype(BF)
-    for i, piece in enumerate(split(g_acc[...], 3)):
-        g_ref[i * rank : (i + 1) * rank, :] = piece
-    inv_ref[...] = jnp.broadcast_to(
-        inverse_root(jnp.sum(square[...], axis=1, keepdims=True), wide), inv_ref.shape
-    )
 
 
 def project(back, gain, basis, wq, wk, wv, wo):
     wide, rank = basis.shape
     length = back.shape[0]
     ne = wo.shape[0]
-    total = wq.shape[1] + wk.shape[1] + wv.shape[1]
-    small = in_hbm((back, gain))
-    weights = in_hbm((basis, wq, wk, wv, wo))
+    nq = wq.shape[1]
+    rest = wk.shape[1] + wv.shape[1]
+    operands = in_hbm((back, gain, basis, wq, wk, wv, wo))
     return pl.pallas_call(
         project_kernel,
-        in_specs=[pl.BlockSpec(memory_space=pltpu.HBM)] * len(small + weights),
+        in_specs=[pl.BlockSpec(memory_space=pltpu.HBM)] * len(operands),
         out_specs=vmem(4),
         out_shape=[
-            jax.ShapeDtypeStruct((2 * rank, total), BF),
+            jax.ShapeDtypeStruct((2 * rank, nq + rest), BF),
             jax.ShapeDtypeStruct((ne, rank), BF),
             jax.ShapeDtypeStruct((3 * rank, rank), BF),
             jax.ShapeDtypeStruct((length, HD), F32),
         ],
-        scratch_shapes=[pltpu.VMEM(a.shape, a.dtype) for a in small]
-        + [pltpu.SemaphoreType.DMA((len(small),))]
-        + [pltpu.VMEM(w.shape, BF) for w in weights]
-        + [
-            pltpu.VMEM((rank, total), F32),
+        scratch_shapes=[
+            pltpu.VMEM(back.shape, BF),
+            pltpu.VMEM(gain.shape, F32),
+            pltpu.VMEM(basis.shape, BF),
+            pltpu.VMEM(wq.shape, BF),
+            pltpu.VMEM((wide, rest), BF),
+            pltpu.VMEM(wo.shape, BF),
+            pltpu.VMEM((rank, wide), BF),
+            pltpu.VMEM((rank, wide), BF),
+            pltpu.VMEM((rank, nq), F32),
             pltpu.VMEM((ne, rank), F32),
-            pltpu.VMEM((rank, rank), F32),
-            pltpu.VMEM((length, HD), F32),
-            pltpu.SemaphoreType.DMA((len(weights), wide // CHUNK)),
+            pltpu.SemaphoreType.DMA((5 + 2 * (wide // PIECE),)),
         ],
         compiler_params=pltpu.CompilerParams(vmem_limit_bytes=2 * VMEM_BYTES),
         cost_estimate=cost(6 * 10**9, 20 * 10**6),
         name="project_weights",
-    )(*small, *weights)
+    )(*operands)
 
 
 def project_heads(coeffs, inv, m_ref, cosine, sine, q, k, v1):
@@ -344,7 +333,7 @@
             pltpu.VMEM((rank, ne), BF),
         ],
         compiler_params=pltpu.CompilerParams(vmem_limit_bytes=VMEM_BYTES),
-        cost_estimate=cost(10**8, 10**6),
+        cost_estimate=cost(10**4, 10**3),
         name="attention_backward",
     )(back, loss, sent, m2, o2, g3, inv, cosine, sine)
 
@@ -398,20 +387,36 @@
             pltpu.VMEM((length, ne), BF),
         ],
         compiler_params=pltpu.CompilerParams(vmem_limit_bytes=VMEM_BYTES),
-        cost_estimate=cost(10**8, 10**6),
+        cost_estimate=cost(10**4, 10**3),
         name="attention_forward",
     )(new, sent, basis, m2, o2, g3, cosine, sine, *after)
 
 
-def gain_kernel(u_ref, wq_ref, wk_ref, wv_ref, inner_ref, got_ref, after, out_ref, turned):
-    nq, nk = wq_ref.shape[1], wk_ref.shape[1]
-    rows = out_ref.shape[1]
+def write_split(ref, first, value):
+    high, low = split(value, 2)
+    both = jnp.concatenate([high.astype(F32), low.astype(F32)], axis=0)
+    ref[first:, : value.shape[1]] = both.astype(BF)
+
+
+def read_split(ref, first):
+    both = ref[first:, :CHUNK].astype(F32)
+    return both[:8] + both[8:]
+
+
+def gain_kernel(
+    u_ref, wq_ref, wk_ref, wv_ref, inner_ref, got_ref, after, out_ref, turned, rows_f32
+):
+    nq = wq_ref.shape[1]
+    rows = u_ref.shape[0] // 2
     half = inner_ref.shape[0] // 2
     core = lax.axis_index("dp") & 1
     mine = add_wide(inner_ref[:half, :], got_ref[half:, :]).astype(BF)
     theirs = add_wide(inner_ref[half:, :], got_ref[:half, :]).astype(BF)
+    out_ref[:half, :] = mine
+    out_ref[half:, :] = jnp.zeros_like(out_ref[half:, :])
     turned[:, pl.ds(pl.multiple_of(core * half, half), half)] = mine.T
     turned[:, pl.ds(pl.multiple_of((1 - core) * half, half), half)] = theirs.T
+    rows_f32[...] = jnp.zeros_like(rows_f32)
     for at in range(0, rows, CHUNK):
         place = pl.ds(pl.multiple_of(core * rows + at, CHUNK), CHUNK)
         against = nn(wq_ref[place, :], turned[:nq, :])
@@ -419,45 +424,86 @@
         against += nn(narrow, turned[nq:, :])
         terms = against * u_ref[place, :].astype(F32)
         folded = sum(terms[:, side : side + HD] for side in range(0, terms.shape[1], HD))
-        out_ref[:, at : at + CHUNK] = jnp.sum(folded.T, axis=0, keepdims=True)
+        rows_f32[at // CHUNK : at // CHUNK + 1, :] = jnp.sum(folded.T, axis=0, keepdims=True)
+    write_split(out_ref, half, rows_f32[...])
 
 
 def gain_part(basis, wq, wk, wv, inner, got, after):
     wide, rank = basis.shape
-    rows = wide // 2
+    assert wide // 2 // CHUNK <= 8
     return pl.pallas_call(
         gain_kernel,
         in_specs=vmem(6) + [pl.BlockSpec(memory_space=pl.ANY)],
         out_specs=pl.BlockSpec(memory_space=pltpu.VMEM),
-        out_shape=jax.ShapeDtypeStruct((1, rows), F32),
-        scratch_shapes=[pltpu.VMEM((inner.shape[1], rank), BF)],
+        out_shape=jax.ShapeDtypeStruct((rank // 2 + 16, inner.shape[1]), BF),
+        scratch_shapes=[
+            pltpu.VMEM((inner.shape[1], rank), BF),
+            pltpu.VMEM((8, CHUNK), F32),
+        ],
         compiler_params=pltpu.CompilerParams(vmem_limit_bytes=VMEM_BYTES),
-        cost_estimate=cost(10**8, 10**6),
-        name="gain_gradient",
+        cost_estimate=cost(10**4, 10**3),
+        name="pair_sum_and_gain_gradient",
     )(basis, wq, wk, wv, inner, got, after)
 
 
-def add_kernel(a_ref, b_ref, after, out_ref):
-    out_ref[...] = add_wide(a_ref[...], b_ref[...]).astype(BF)
-
-
-def add_after(a, b, after):
-    return pl.pallas_call(
-        add_kernel,
+def merge_kernel(a_ref, b_ref, after, out_ref):
+    half = out_ref.shape[0] - 16
+    out_ref[:half, :] = add_wide(a_ref[:half, :], b_ref[:half, :]).astype(BF)
+    out_ref[half:, :] = jnp.zeros_like(out_ref[half:, :])
+    write_split(out_ref, half, read_split(a_ref, half) + read_split(b_ref, half))
+
+
+def merge(a, b, after):
+    return pl.pallas_call(
+        merge_kernel,
         in_specs=vmem(2) + [pl.BlockSpec(memory_space=pl.ANY)],
         out_specs=pl.BlockSpec(memory_space=pltpu.VMEM),
         out_shape=jax.ShapeDtypeStruct(a.shape, BF),
         compiler_params=pltpu.CompilerParams(vmem_limit_bytes=VMEM_BYTES // 2),
-        cost_estimate=cost(10**6, 10**5),
+        cost_estimate=cost(10**4, 10**3),
+        name="sum_over_y",
+    )(a, b, after)
+
+
+def gather_kernel(own_ref, other_ref, out_ref):
+    half = own_ref.shape[0] - 16
+    out_ref[:8, :] = read_split(own_ref, half)
+    out_ref[8:, :] = read_split(other_ref, half)
+
+
+def gather_gain(own, other):
+    return pl.pallas_call(
+        gather_kernel,
+        in_specs=vmem(2),
+        out_specs=pl.BlockSpec(memory_space=pltpu.VMEM),
+        out_shape=jax.ShapeDtypeStruct((16, CHUNK), F32),
+        compiler_params=pltpu.CompilerParams(vmem_limit_bytes=VMEM_BYTES // 2),
+        cost_estimate=cost(10**4, 10**3),
+        name="gather_gain",
+    )(own, other)
+
+
+def add_kernel(a_ref, b_ref, after, out_ref):
+    out_ref[...] = add_wide(a_ref[...], b_ref[...]).astype(out_ref.dtype)
+
+
+def add_after(a, b, after):
+    return pl.pallas_call(
+        add_kernel,
+        in_specs=vmem(2) + [pl.BlockSpec(memory_space=pl.ANY)],
+        out_specs=pl.BlockSpec(memory_space=pltpu.VMEM),
+        out_shape=jax.ShapeDtypeStruct(a.shape, a.dtype),
+        compiler_params=pltpu.CompilerParams(vmem_limit_bytes=VMEM_BYTES // 2),
+        cost_estimate=cost(10**4, 10**3),
         name="pair_sum",
     )(a, b, after)
 
 
 def gather_halves(own_ref, other_ref, whole):
-    half = own_ref.shape[0]
+    half = whole.shape[0] // 2
     core = lax.axis_index("dp") & 1
-    whole[pl.ds(pl.multiple_of(core * half, half), half), :] = own_ref[...]
-    whole[pl.ds(pl.multiple_of((1 - core) * half, half), half), :] = other_ref[...]
+    whole[pl.ds(pl.multiple_of(core * half, half), half), :] = own_ref[:half, :]
+    whole[pl.ds(pl.multiple_of((1 - core) * half, half), half), :] = other_ref[:half, :]
 
 
 def inward_kernel(u_ref, gain_ref, own_ref, other_ref, after, q_ref, k_ref, v_ref, inner):
@@ -503,7 +549,7 @@
         scratch_shapes=[pltpu.VMEM((rank, sum(sizes)), BF)],
         out_shape=[jax.ShapeDtypeStruct((rows, n), BF) for n in sizes],
         compiler_params=pltpu.CompilerParams(vmem_limit_bytes=VMEM_BYTES),
-        cost_estimate=cost(10**8, 10**6),
+        cost_estimate=cost(10**4, 10**3),
         name="inward_weight_gradients",
     )(basis, gain, own, other, after)
 
@@ -520,14 +566,14 @@
         scratch_shapes=[pltpu.VMEM((rank, ne), BF)],
         out_shape=jax.ShapeDtypeStruct((ne, rows), BF),
         compiler_params=pltpu.CompilerParams(vmem_limit_bytes=VMEM_BYTES),
-        cost_estimate=cost(10**8, 10**6),
+        cost_estimate=cost(10**4, 10**3),
         name="output_weight_gradient",
     )(basis, own, other, after)
 
 
 def results_kernel(
     wide, fbase_ref, y_ref, ygot_ref, base_ref, unit_ref, x_ref, xgot_ref, back_ref, inv_ref,
-    gain_ref, gain_one_ref, gain_two_ref, gain_three_ref, after,
+    gain_ref, gain_got_ref, after,
     f_ref, b_ref, gain_out_ref,
 ):
     f_ref[...] = (fbase_ref[...] + add_wide(y_ref[...], ygot_ref[...])).astype(BF)
@@ -537,11 +583,14 @@
     middle = along * inv * (1.0 / wide)
     b_ref[...] = (base_ref[...] + (x - unit_ref[...] * middle) * inv).astype(BF)
     core = lax.axis_index("dp") & 1
-    half = gain_ref.shape[1]
-    mine = pl.ds(pl.multiple_of(core * half, half), half)
-    theirs = pl.ds(pl.multiple_of((1 - core) * half, half), half)
-    gain_out_ref[:, mine] = gain_ref[...] + gain_two_ref[...]
-    gain_out_ref[:, theirs] = gain_one_ref[...] + gain_three_ref[...]
+    gain = gain_ref[...] + gain_got_ref[...]
+    half = wide // 2
+    for at in range(0, half, CHUNK):
+        row = at // CHUNK
+        mine = pl.ds(pl.multiple_of(core * half + at, CHUNK), CHUNK)
+        theirs = pl.ds(pl.multiple_of((1 - core) * half + at, CHUNK), CHUNK)
+        gain_out_ref[:, mine] = gain[row : row + 1, :]
+        gain_out_ref[:, theirs] = gain[8 + row : 9 + row, :]
 
 
 def results(wide, after, *operands):
@@ -553,7 +602,7 @@
         out_specs=vmem(3),
         out_shape=[jax.ShapeDtypeStruct(shape, BF)] * 2 + [jax.ShapeDtypeStruct((1, wide), F32)],
         compiler_params=pltpu.CompilerParams(vmem_limit_bytes=VMEM_BYTES // 2),
-        cost_estimate=cost(10**8, 10**6),
+        cost_estimate=cost(10**4, 10**3),
         name="section_results",
     )(*held, *in_hbm((after,)))
 
@@ -582,34 +631,32 @@
     inner, out_give, out_keep, x, base, unit = backward(
         back, loss_grad, returned, m2, o2, g3, inv, cosine, sine
     )
-    half = inner.shape[0] // 2
     out_got = swap(out_give, "dp", 1)
     inner_got = swap(inner, "dp", 1)
+    x_got = swap(x, "tensor", 2)
+    out_pair = add_wide(out_keep, out_got).astype(BF)
+    out_got = swap(out_pair, "dp", 2)
+    pair = gain_part(subspace, wq, wk, wv, inner, inner_got, out_pair)
+    pair_got = swap(pair, "dp", 2)
+    y, fbase = forward(new_coeffs, arrived, subspace, m2, o2, g3, cosine, sine, pair)
+    y_got = swap(y, "tensor", 1)
+    x = add_after(x, x_got, y)
     x_got = swap(x, "tensor", 1)
-    out_pair = add_wide(out_keep, out_got).astype(BF)
-    pair = add_wide(inner[:half], inner_got[half:]).astype(BF)
-    out_got = swap(out_pair, "dp", 2)
-    pair_got = swap(pair, "dp", 2)
-    x = add_after(x, x_got, pair)
-    x_got = swap(x, "tensor", 2)
-    y, fbase = forward(
-        new_coeffs, arrived, subspace, m2, o2, g3, cosine, sine, out_pair, x
+    out_own = add_after(out_pair, out_got, x)
+    grad_o = outward_grad(subspace, out_own, swap(out_own, "dp", 1), x)
+    y = add_after(y, y_got, *in_hbm((grad_o,)))
+    y_got = swap(y, "tensor", 2)
+    own = merge(pair, pair_got, y)
+    other = swap(own, "dp", 1)
+    gain = gather_gain(own, other)
+    gain_got = swap(gain, "tensor", 1)
+    grad_q, grad_k, grad_v = inward_grads(
+        subspace, norm_gain, own, other, (nq, nk, nv), gain
     )
-    y_got = swap(y, "tensor", 1)
-    gain = gain_part(subspace, wq, wk, wv, inner, inner_got, y)
-    y = add_wide(y, y_got).astype(BF)
-    y_got = swap(y, "tensor", 2)
-    gain = sum_over_tensor(gain)
-    gains = [gain] + [swap(gain, "dp", bit) for bit in (1, 2, 3)]
-
-    own = add_wide(out_pair, out_got).astype(BF)
-    grad_o = outward_grad(subspace, own, swap(own, "dp", 1), y)
-    own = add_wide(pair, pair_got).astype(BF)
-    grad_q, grad_k, grad_v = inward_grads(
-        subspace, norm_gain, own, swap(own, "dp", 1), (nq, nk, nv), gain
-    )
+    gain = add_after(gain, gain_got, *in_hbm((grad_v,)))
+    gain_got = swap(gain, "tensor", 2)
     forward_out, backward_out, grad_gain = results(
-        wide, grad_v, fbase, y, y_got, base, unit, x, x_got, back, inv, *gains
+        wide, grad_v, fbase, y, y_got, base, unit, x, x_got, back, inv, gain, gain_got
     )
     return (
         forward_out[None],

time: 54.6 us -> 56.1 us (1.027)
  waiting for transfers between devices: 5.73 us -> 8.51 us
  starting transfers between devices: 18 us -> 17 us
    ppermute x17 -> x13, waiting for transfers between devices: 5.73 us -> 8.51 us  [swap(): return lax.ppermute(x, axis, [(i, i ^ bit) for i in range(devices)])]
    ppermute x17 -> x13, starting transfers between devices: 18 us -> 17 us  [swap(): return lax.ppermute(x, axis, [(i, i ^ bit) for i in range(devices)])]
  transfers between devices with their start and end apart: 17 -> 13, of which waited for: 6 -> 5; matrix products, arithmetic and copies ran while one was open for 1% -> 0% of each run, Pallas kernels for 41% -> 39%
where the time goes in v3:
time: 56.1 us; the launch traced here: 55.9 us
  Pallas kernels  28.5 us (51%)
  starting transfers between devices  17 us (30%)
  waiting for transfers between devices  8.51 us (15%)
  other arithmetic  0.99 us (2%)
  between operations  0.86 us (2%)
    ppermute x13, starting transfers between devices, swap(): return lax.ppermute(x, axis, [(i, i ^ bit) for i in range(devices)])  17 us
    pallas_call x1, Pallas kernels, project(): pl.pallas_call(project_kernel, in_specs=[pl.BlockSpec(memory_space=pltpu....  12 us
    ppermute x13, waiting for transfers between devices, swap(): return lax.ppermute(x, axis, [(i, i ^ bit) for i in range(devices)])  8.51 us
    pallas_call x1, Pallas kernels, backward(): pl.pallas_call(backward_kernel, in_specs=vmem(9), out_specs=vmem(6), out_...  5.42 us
    pallas_call x1, Pallas kernels, forward(): pl.pallas_call(forward_kernel, in_specs=vmem(8) + [pl.BlockSpec(memory_sp...  3.78 us
    pallas_call x1, Pallas kernels, inward_grads(): pl.pallas_call(inward_kernel, grid=(STEPS,), in_specs=vmem(4) + [pl.Block...  2.19 us
    pallas_call x1, Pallas kernels, outward_grad(): pl.pallas_call(outward_kernel, grid=(STEPS,), in_specs=vmem(3) + [pl.Bloc...  2.01 us
    pallas_call x1, Pallas kernels, gain_part(): pl.pallas_call(gain_kernel, in_specs=vmem(6) + [pl.BlockSpec(memory_space...  1.82 us
  transfers between devices with their start and end apart: 13, of which 5 were waited for; matrix products, arithmetic and copies ran while one was open for 0% of the time, Pallas kernels for 39%

profile of v3, /device:TPU:0, one launch (start us, length us, event | category | flops | bytes accessed | tf_op | source)
XLA Modules:
  0.0 55.9 jit_solution(14251050236188537396)
XLA Ops:
  0.6 0.9 %select_bitcast_fusion = bf16[256,256]{1,0:T(8,128)(2,1)S(1)} fusion(bf16[1,256,256]{2,1,0:T(8,128)(2,1)} %param.15, bf16[1,256,256]{2,1,0:T(8,128)(2,1)} %param.16, pred[]{:T(512)S(6)} %eq.3), kind=kLoop, calls=%fused_computation.1 | loop fusion | flops 65536 | bytes 393217 | tf_op jit(solution)/shard_map/jit(_where)/select_n | solution.py:39
  1.6 3.0 %collective-permute-start = (bf16[256,256]{1,0:T(8,128)(2,1)S(1)}, bf16[256,256]{1,0:T(8,128)(2,1)S(1)}, u32[]{:S(2)}, u32[]{:S(2)}) collective-permute-start(bf16[256,256]{1,0:T(8,128)(2,1)S(1)} %select_bitcast_fusion), channel_id=1, source_target_pairs={{0,16},{16,0},{1,17},{17,1},{2,18},{18,2},{3,19},{19,3},{4,20},{20... | collective-permute-start | bytes 393224 | tf_op jit(solution)/shard_map/ppermute | solution.py:32
  4.6 12.0 %project_weights.1 = (bf16[512,1280]{1,0:T(8,128)(2,1)S(1)}, bf16[1024,256]{1,0:T(8,128)(2,1)S(1)}, bf16[768,256]{1,0:T(8,128)(2,1)S(1)}, f32[256,128]{1,0:T(8,128)S(1)}) custom-call(bf16[256,256]{1,0:T(8,128)(2,1)} %bitcast.21, f32[1,4096]{1,0:T(1,128)} %gain_ref.1, bf16[4096,256]{1,0:T(8,128)(2,1)} %u_ref.7, bf16[4096,1024]{1,0:T(8,128)(2,1)} %bitcast.13, ...), custom_call_target="tpu_custom_call" | custom-call | flops 6000000000 | bytes 20000000 | tf_op jit(solution)/shard_map/project_weights/pallas_call | solution.py:181
  16.7 5.4 %attention_backward.1 = (bf16[256,1280]{1,0:T(8,128)(2,1)S(1)}, bf16[128,1024]{1,0:T(8,128)(2,1)S(1)}, bf16[128,1024]{1,0:T(8,128)(2,1)S(1)}, bf16[256,256]{1,0:...) custom-call(bf16[256,256]{1,0:T(8,128)(2,1)S(1)} %bitcast.22, bf16[256,256]{1,0:T(8,128)(2,1)S(1)} %copy-done.6, ...), custom_call_target="tpu_custom_call" | custom-call | flops 10000 | bytes 1000 | tf_op jit(solution)/shard_map/attention_backward/pallas_call | solution.py:306
  22.2 0.5 collective-permute-start.1
  22.7 1.0 %collective-permute-done.2 = bf16[128,1024]{1,0:T(8,128)(2,1)S(1)} collective-permute-done((bf16[128,1024]{1,0:T(8,128)(2,1)S(1)}, bf16[128,1024]{1,0:T(8,128)(2,1)S(1)}, u32[]{:S(2)}, u32[]{:S(2)}) %collective-permute-start.2) | collective-permute-done | bytes 262176 | tf_op jit(solution)/shard_map/ppermute | solution.py:32
  23.8 1.6 %collective-permute-start.4 = (bf16[128,1024]{1,0:T(8,128)(2,1)S(1)}, bf16[128,1024]{1,0:T(8,128)(2,1)S(1)}, u32[]{:S(2)}, u32[]{:S(2)}) collective-permute-start(bf16[128,1024]{1,0:T(8,128)(2,1)S(1)} %add_convert_fusion.after.a_ref), channel_id=1, source_target_pairs={{0,2},{1,3},{2,0},{3,1},{4,6},{5,7},{6,4},{7,5},{8,10},{9,11},{10,... | collective-permute-start | bytes 786440 | tf_op jit(solution)/shard_map/ppermute | solution.py:32
  25.4 2.6 %collective-permute-start.5 = (bf16[256,256]{1,0:T(8,128)(2,1)S(1)}, bf16[256,256]{1,0:T(8,128)(2,1)S(1)}, u32[]{:S(2)}, u32[]{:S(2)}) collective-permute-start(bf16[256,256]{1,0:T(8,128)(2,1)S(1)} %get-tuple-element.34.a_ref), channel_id=1, source_target_pairs={{0,8},{4,12},{8,0},{12,4},{1,9},{5,13},{9,1},{13,5},{2,10},{6,14},... | collective-permute-start | bytes 393224 | tf_op jit(solution)/shard_map/ppermute | solution.py:32
  28.0 1.8 %pair_sum_and_gain_gradient.1.rest_0_.a_ref = bf16[144,1280]{1,0:T(8,128)(2,1)S(1)} custom-call(bf16[4096,256]{1,0:T(8,128)(2,1)S(1)} %copy-done, bf16[4096,1024]{1,0:T(8,128)(2,1)S(1)} %bitcast.16, bf16[4096,128]{1,0:T(8,128)(2,1)S(1)} %bitcast.18, bf16[4096,128]{1,0:T(8,128)(2,1)S(1)} %bitcast.20, bf16[256,1280]{1,0:T(8,128)(2,1)S(1)} %get-tuple-element.29.inner_ref, ...), custom_call_target="tpu_custom_call" | custom-call | flops 10000 | bytes 1000 | tf_op jit(solution)/shard_map/pair_sum_and_gain_gradient/pallas_call | solution.py:434
  29.9 0.6 %collective-permute-start.9 = (bf16[144,1280]{1,0:T(8,128)(2,1)S(1)}, bf16[144,1280]{1,0:T(8,128)(2,1)S(1)}, u32[]{:S(2)}, u32[]{:S(2)}) collective-permute-start(bf16[144,1280]{1,0:T(8,128)(2,1)S(1)} %pair_sum_and_gain_gradient.1.rest_0_.a_ref), channel_id=1, source_target_pairs={{0,2},{1,3},{2,0},{3,1},{4,6},{5,7},{6,4},{7,5},{8,10},{9,11},{10,... | collective-permute-start | bytes 1105928 | tf_op jit(solution)/shard_map/ppermute | solution.py:32
  30.4 3.8 %attention_forward.1 = (bf16[256,256]{1,0:T(8,128)(2,1)S(1)}, f32[256,256]{1,0:T(8,128)S(1)}) custom-call(bf16[256,256]{1,0:T(8,128)(2,1)S(1)} %copy-done.7, bf16[256,256]{1,0:T(8,128)(2,1)S(1)} %collective-permute-done.sent_ref, bf16[4096,256]{1,0:T(8,128)(2,1)S(1)} %copy-done, bf16[512,1280]{1,0:T(8,128)(2,1)S(1)} %get-tuple-element.25.m_ref, ...), custom_call_target="tpu_custom_call" | custom-call | flops 10000 | bytes 1000 | tf_op jit(solution)/shard_map/attention_forward/pallas_call | solution.py:372
  34.2 0.1 collective-permute-done.5.b_ref
  34.6 1.5 %collective-permute-start.3 = (bf16[256,256]{1,0:T(8,128)(2,1)S(1)}, bf16[256,256]{1,0:T(8,128)(2,1)S(1)}, u32[]{:S(2)}, u32[]{:S(2)}) collective-permute-start(bf16[256,256]{1,0:T(8,128)(2,1)S(1)} %get-tuple-element.33.after.a_ref), channel_id=1, source_target_pairs={{0,4},{4,0},{8,12},{12,8},{1,5},{5,1},{9,13},{13,9},{2,6},{6,2},{1... | collective-permute-start | bytes 393224 | tf_op jit(solution)/shard_map/ppermute | solution.py:32
  36.1 2.0 %output_weight_gradient.1.after = bf16[1024,1024]{1,0:T(8,128)(2,1)} custom-call(bf16[4096,256]{1,0:T(8,128)(2,1)S(1)} %copy-done, bf16[128,1024]{1,0:T(8,128)(2,1)S(1)} %pair_sum.5.own_ref, bf16[128,1024]{1,0:T(8,128)(2,1)S(1)} %collective-permute-done.6.other_ref, bf16[256,256]{1,0:T(8,128)(2,1)S(1)} %pair_sum.4.after.x_ref), custom_call_target="tpu_custom_call" | custom-call | flops 10000 | bytes 1000 | tf_op jit(solution)/shard_map/output_weight_gradient/pallas_call | solution.py:561
  38.1 2.4 %collective-permute-done.3.b_ref = bf16[256,256]{1,0:T(8,128)(2,1)S(1)} collective-permute-done((bf16[256,256]{1,0:T(8,128)(2,1)S(1)}, bf16[256,256]{1,0:T(8,128)(2,1)S(1)}, u32[]{:S(2)}, u32[]{:S(2)}) %collective-permute-start.3) | collective-permute-done | bytes 131104 | tf_op jit(solution)/shard_map/ppermute | solution.py:32
  40.5 0.1 sum_over_y.1.own_ref
  40.7 1.5 %collective-permute-start.8 = (bf16[256,256]{1,0:T(8,128)(2,1)S(1)}, bf16[256,256]{1,0:T(8,128)(2,1)S(1)}, u32[]{:S(2)}, u32[]{:S(2)}) collective-permute-start(bf16[256,256]{1,0:T(8,128)(2,1)S(1)} %pair_sum.4.after.x_ref), channel_id=1, source_target_pairs={{0,4},{4,0},{8,12},{12,8},{1,5},{5,1},{9,13},{13,9},{2,6},{6,2},{1... | collective-permute-start | bytes 393224 | tf_op jit(solution)/shard_map/ppermute | solution.py:32
  42.2 2.6 %collective-permute-start.7 = (bf16[256,256]{1,0:T(8,128)(2,1)S(1)}, bf16[256,256]{1,0:T(8,128)(2,1)S(1)}, u32[]{:S(2)}, u32[]{:S(2)}) collective-permute-start(bf16[256,256]{1,0:T(8,128)(2,1)S(1)} %pair_sum.6.after.y_ref), channel_id=1, source_target_pairs={{0,8},{4,12},{8,0},{12,4},{1,9},{5,13},{9,1},{13,5},{2,10},{6,14},... | collective-permute-start | bytes 393224 | tf_op jit(solution)/shard_map/ppermute | solution.py:32
  44.8 0.3 collective-permute-start.11
  45.2 2.2 %inward_weight_gradients.1 = (bf16[1024,1024]{1,0:T(8,128)(2,1)}, bf16[1024,128]{1,0:T(8,128)(2,1)}, bf16[1024,128]{1,0:T(8,128)(2,1)}) custom-call(bf16[4096,256]{1,0:T(8,128)(2,1)S(1)} %copy-done, f32[1,4096]{1,0:T(1,128)S(1)} %copy-done.8, bf16[144,1280]{1,0:T(8,128)(2,1)S(1)} %sum_over_y.1.own_ref, ...), custom_call_target="tpu_custom_call" | custom-call | flops 10000 | bytes 1000 | tf_op jit(solution)/shard_map/inward_weight_gradients/pallas_call | solution.py:544
  47.4 2.5 %collective-permute-done.11.b_ref = f32[16,512]{1,0:T(8,128)S(1)} collective-permute-done((f32[16,512]{1,0:T(8,128)S(1)}, f32[16,512]{1,0:T(8,128)S(1)}, u32[]{:S(2)}, u32[]{:S(2)}) %collective-permute-start.11) | collective-permute-done | bytes 32800 | tf_op jit(solution)/shard_map/ppermute | solution.py:32
  49.9 2.6 %collective-permute-start.12 = (f32[16,512]{1,0:T(8,128)S(1)}, f32[16,512]{1,0:T(8,128)S(1)}, u32[]{:S(2)}, u32[]{:S(2)}) collective-permute-start(f32[16,512]{1,0:T(8,128)S(1)} %pair_sum.7.gain_ref), channel_id=1, source_target_pairs={{0,8},{4,12},{8,0},{12,4},{1,9},{5,13},{9,1},{13,5},{2,10},{6,14},... | collective-permute-start | bytes 98312 | tf_op jit(solution)/shard_map/ppermute | solution.py:32
  52.5 2.4 %collective-permute-done.12.gain_got_ref = f32[16,512]{1,0:T(8,128)S(1)} collective-permute-done((f32[16,512]{1,0:T(8,128)S(1)}, f32[16,512]{1,0:T(8,128)S(1)}, u32[]{:S(2)}, u32[]{:S(2)}) %collective-permute-start.12) | collective-permute-done | bytes 32800 | tf_op jit(solution)/shard_map/ppermute | solution.py:32
  54.9 1.0 %section_results.1 = (bf16[256,256]{1,0:T(8,128)(2,1)}, bf16[256,256]{1,0:T(8,128)(2,1)}, f32[1,4096]{1,0:T(1,128)}) custom-call(f32[256,256]{1,0:T(8,128)S(1)} %get-tuple-element.32.fbase_ref, bf16[256,256]{1,0:T(8,128)(2,1)S(1)} %pair_sum.6.after.y_ref, bf16[256,256]{1,0:T(8,128)(2,1)S(1)} %collective-permute-done.7.ygot_ref, ...), custom_call_target="tpu_custom_call" | custom-call | flops 10000 | bytes 1000 | tf_op jit(solution)/shard_map/section_results/pallas_call | solution.py:599
  (40 shorter events, 0.5 us)
Async XLA Ops:
  1.6 15.1 %collective-permute-start = (bf16[256,256]{1,0:T(8,128)(2,1)S(1)}, bf16[256,256]{1,0:T(8,128)(2,1)S(1)}, u32[]{:S(2)}, u32[]{:S(2)}) collective-permute-start(bf16[256,256]{1,0:T(8,128)(2,1)S(1)} %select_bitcast_fusion), channel_id=1, source_target_pairs={{0,16},{16,0},{1,17},{17,1},{2,18},{18,2},{3,19},{19,3},{4,20},{20... | collective-permute-start | bytes 393224 | tf_op jit(solution)/shard_map/ppermute | solution.py:32
  4.6 23.4 %slice-start = ((s8[8388608]{0:T(1024)(128)(4,1)}), s8[4194304]{0:T(1024)(128)(4,1)S(1)}, s32[]{:S(2)}) async-start(s8[8388608]{0:T(1024)(128)(4,1)} %bitcast.14), calls=%async_computation | async-start | bytes 8388608
  4.6 12.1 %copy-start.3 = (f32[256,128]{1,0:T(8,128)S(1)}, f32[256,128]{1,0:T(8,128)}, u32[]{:S(2)}) copy-start(f32[256,128]{1,0:T(8,128)} %constant.12.clone.cos_ref) | copy-start | bytes 393220
  4.6 12.1 %copy-start.4 = (f32[256,128]{1,0:T(8,128)S(1)}, f32[256,128]{1,0:T(8,128)}, u32[]{:S(2)}) copy-start(f32[256,128]{1,0:T(8,128)} %constant.13.clone.sin_ref) | copy-start | bytes 393220
  4.6 12.1 %copy-start.5 = (bf16[1,256,256]{2,1,0:T(8,128)(2,1)S(1)}, bf16[1,256,256]{2,1,0:T(8,128)(2,1)}, u32[]{:S(2)}) copy-start(bf16[1,256,256]{2,1,0:T(8,128)(2,1)} %param.17) | copy-start | bytes 393220
  4.6 12.1 %copy-start.6 = (bf16[256,256]{1,0:T(8,128)(2,1)S(1)}, bf16[256,256]{1,0:T(8,128)(2,1)}, u32[]{:S(2)}) copy-start(bf16[256,256]{1,0:T(8,128)(2,1)} %loss_ref.1) | copy-start | bytes 393220
  4.6 23.4 %slice-start.1 = ((s8[8388608]{0:T(1024)(128)(4,1)}), s8[4194304]{0:T(1024)(128)(4,1)S(1)}, s32[]{:S(2)}) async-start(s8[8388608]{0:T(1024)(128)(4,1)} %bitcast.14), calls=%async_computation.1 | async-start | bytes 8388608
  4.6 23.4 %copy-start.2 = (bf16[1,4096,128]{2,1,0:T(8,128)(2,1)S(1)}, bf16[1,4096,128]{2,1,0:T(8,128)(2,1)}, u32[]{:S(2)}) copy-start(bf16[1,4096,128]{2,1,0:T(8,128)(2,1)} %param.22) | copy-start | bytes 3145732
  16.6 11.4 %copy-start = (bf16[4096,256]{1,0:T(8,128)(2,1)S(1)}, bf16[4096,256]{1,0:T(8,128)(2,1)}, u32[]{:S(2)}) copy-start(bf16[4096,256]{1,0:T(8,128)(2,1)} %u_ref.7) | copy-start | bytes 6291460
  16.7 11.4 %copy-start.1 = (bf16[1,4096,128]{2,1,0:T(8,128)(2,1)S(1)}, bf16[1,4096,128]{2,1,0:T(8,128)(2,1)}, u32[]{:S(2)}) copy-start(bf16[1,4096,128]{2,1,0:T(8,128)(2,1)} %param.21) | copy-start | bytes 3145732
  22.1 1.6 %collective-permute-start.2 = (bf16[128,1024]{1,0:T(8,128)(2,1)S(1)}, bf16[128,1024]{1,0:T(8,128)(2,1)S(1)}, u32[]{:S(2)}, u32[]{:S(2)}) collective-permute-start(bf16[128,1024]{1,0:T(8,128)(2,1)S(1)} %get-tuple-element.31), channel_id=1, source_target_pairs={{0,1},{1,0},{2,3},{3,2},{4,5},{5,4},{6,7},{7,6},{8,9},{9,8},{10,11... | collective-permute-start | bytes 786440 | tf_op jit(solution)/shard_map/ppermute | solution.py:32
  22.2 5.8 %collective-permute-start.1 = (bf16[256,1280]{1,0:T(8,128)(2,1)S(1)}, bf16[256,1280]{1,0:T(8,128)(2,1)S(1)}, u32[]{:S(2)}, u32[]{:S(2)}) collective-permute-start(bf16[256,1280]{1,0:T(8,128)(2,1)S(1)} %get-tuple-element.29.inner_ref), channel_id=1, source_target_pairs={{0,1},{1,0},{2,3},{3,2},{4,5},{5,4},{6,7},{7,6},{8,9},{9,8},{10,11... | collective-permute-start | bytes 1966088 | tf_op jit(solution)/shard_map/ppermute | solution.py:32
  23.8 10.6 %collective-permute-start.4 = (bf16[128,1024]{1,0:T(8,128)(2,1)S(1)}, bf16[128,1024]{1,0:T(8,128)(2,1)S(1)}, u32[]{:S(2)}, u32[]{:S(2)}) collective-permute-start(bf16[128,1024]{1,0:T(8,128)(2,1)S(1)} %add_convert_fusion.after.a_ref), channel_id=1, source_target_pairs={{0,2},{1,3},{2,0},{3,1},{4,6},{5,7},{6,4},{7,5},{8,10},{9,11},{10,... | collective-permute-start | bytes 786440 | tf_op jit(solution)/shard_map/ppermute | solution.py:32
  25.4 5.0 %copy-start.7 = (bf16[256,256]{1,0:T(8,128)(2,1)S(1)}, bf16[256,256]{1,0:T(8,128)(2,1)}, u32[]{:S(2)}) copy-start(bf16[256,256]{1,0:T(8,128)(2,1)} %new_ref.1) | copy-start | bytes 393220
  25.4 9.0 %collective-permute-start.5 = (bf16[256,256]{1,0:T(8,128)(2,1)S(1)}, bf16[256,256]{1,0:T(8,128)(2,1)S(1)}, u32[]{:S(2)}, u32[]{:S(2)}) collective-permute-start(bf16[256,256]{1,0:T(8,128)(2,1)S(1)} %get-tuple-element.34.a_ref), channel_id=1, source_target_pairs={{0,8},{4,12},{8,0},{12,4},{1,9},{5,13},{9,1},{13,5},{2,10},{6,14},... | collective-permute-start | bytes 393224 | tf_op jit(solution)/shard_map/ppermute | solution.py:32
  29.9 10.7 %collective-permute-start.9 = (bf16[144,1280]{1,0:T(8,128)(2,1)S(1)}, bf16[144,1280]{1,0:T(8,128)(2,1)S(1)}, u32[]{:S(2)}, u32[]{:S(2)}) collective-permute-start(bf16[144,1280]{1,0:T(8,128)(2,1)S(1)} %pair_sum_and_gain_gradient.1.rest_0_.a_ref), channel_id=1, source_target_pairs={{0,2},{1,3},{2,0},{3,1},{4,6},{5,7},{6,4},{7,5},{8,10},{9,11},{10,... | collective-permute-start | bytes 1105928 | tf_op jit(solution)/shard_map/ppermute | solution.py:32
  34.5 1.6 %collective-permute-start.6 = (bf16[128,1024]{1,0:T(8,128)(2,1)S(1)}, bf16[128,1024]{1,0:T(8,128)(2,1)S(1)}, u32[]{:S(2)}, u32[]{:S(2)}) collective-permute-start(bf16[128,1024]{1,0:T(8,128)(2,1)S(1)} %pair_sum.5.own_ref), channel_id=1, source_target_pairs={{0,1},{1,0},{2,3},{3,2},{4,5},{5,4},{6,7},{7,6},{8,9},{9,8},{10,11... | collective-permute-start | bytes 786440 | tf_op jit(solution)/shard_map/ppermute | solution.py:32
  34.6 5.9 %collective-permute-start.3 = (bf16[256,256]{1,0:T(8,128)(2,1)S(1)}, bf16[256,256]{1,0:T(8,128)(2,1)S(1)}, u32[]{:S(2)}, u32[]{:S(2)}) collective-permute-start(bf16[256,256]{1,0:T(8,128)(2,1)S(1)} %get-tuple-element.33.after.a_ref), channel_id=1, source_target_pairs={{0,4},{4,0},{8,12},{12,8},{1,5},{5,1},{9,13},{13,9},{2,6},{6,2},{1... | collective-permute-start | bytes 393224 | tf_op jit(solution)/shard_map/ppermute | solution.py:32
  38.1 7.1 %copy-start.8 = (f32[1,4096]{1,0:T(1,128)S(1)}, f32[1,4096]{1,0:T(1,128)}, u32[]{:S(2)}) copy-start(f32[1,4096]{1,0:T(1,128)} %gain_ref.1) | copy-start | bytes 49156
  40.6 4.2 %collective-permute-start.10 = (bf16[144,1280]{1,0:T(8,128)(2,1)S(1)}, bf16[144,1280]{1,0:T(8,128)(2,1)S(1)}, u32[]{:S(2)}, u32[]{:S(2)}) collective-permute-start(bf16[144,1280]{1,0:T(8,128)(2,1)S(1)} %sum_over_y.1.own_ref), channel_id=1, source_target_pairs={{0,1},{1,0},{2,3},{3,2},{4,5},{5,4},{6,7},{7,6},{8,9},{9,8},{10,11... | collective-permute-start | bytes 1105928 | tf_op jit(solution)/shard_map/ppermute | solution.py:32
  40.7 11.8 %collective-permute-start.8 = (bf16[256,256]{1,0:T(8,128)(2,1)S(1)}, bf16[256,256]{1,0:T(8,128)(2,1)S(1)}, u32[]{:S(2)}, u32[]{:S(2)}) collective-permute-start(bf16[256,256]{1,0:T(8,128)(2,1)S(1)} %pair_sum.4.after.x_ref), channel_id=1, source_target_pairs={{0,4},{4,0},{8,12},{12,8},{1,5},{5,1},{9,13},{13,9},{2,6},{6,2},{1... | collective-permute-start | bytes 393224 | tf_op jit(solution)/shard_map/ppermute | solution.py:32
  42.2 10.3 %collective-permute-start.7 = (bf16[256,256]{1,0:T(8,128)(2,1)S(1)}, bf16[256,256]{1,0:T(8,128)(2,1)S(1)}, u32[]{:S(2)}, u32[]{:S(2)}) collective-permute-start(bf16[256,256]{1,0:T(8,128)(2,1)S(1)} %pair_sum.6.after.y_ref), channel_id=1, source_target_pairs={{0,8},{4,12},{8,0},{12,4},{1,9},{5,13},{9,1},{13,5},{2,10},{6,14},... | collective-permute-start | bytes 393224 | tf_op jit(solution)/shard_map/ppermute | solution.py:32
  44.8 5.0 %collective-permute-start.11 = (f32[16,512]{1,0:T(8,128)S(1)}, f32[16,512]{1,0:T(8,128)S(1)}, u32[]{:S(2)}, u32[]{:S(2)}) collective-permute-start(f32[16,512]{1,0:T(8,128)S(1)} %gather_gain.1.after.a_ref), channel_id=1, source_target_pairs={{0,4},{4,0},{8,12},{12,8},{1,5},{5,1},{9,13},{13,9},{2,6},{6,2},{1... | collective-permute-start | bytes 98312 | tf_op jit(solution)/shard_map/ppermute | solution.py:32
  49.9 5.1 %collective-permute-start.12 = (f32[16,512]{1,0:T(8,128)S(1)}, f32[16,512]{1,0:T(8,128)S(1)}, u32[]{:S(2)}, u32[]{:S(2)}) collective-permute-start(f32[16,512]{1,0:T(8,128)S(1)} %pair_sum.7.gain_ref), channel_id=1, source_target_pairs={{0,8},{4,12},{8,0},{12,4},{1,9},{5,13},{9,1},{13,5},{2,10},{6,14},... | collective-permute-start | bytes 98312 | tf_op jit(solution)/shard_map/ppermute | solution.py:32

commit v4 on v3

--- a/solution.py
+++ b/solution.py
@@ -96,8 +96,8 @@
 
 def project_kernel(
     back_hbm, gain_hbm, u_hbm, wq_hbm, wk_hbm, wv_hbm, wo_hbm,
-    m_ref, o_ref, g_ref, inv_ref,
-    back, gain, u, wq, narrow, wo, turned, scaled, m_acc, o_acc, sems,
+    m_ref, o_ref, g_ref, inv_ref, u, wq, narrow,
+    back, gain, wo, turned, scaled, m_acc, o_acc, sems,
 ):
     wide, rank = u.shape
     nq = wq.shape[1]
@@ -181,19 +181,19 @@
     return pl.pallas_call(
         project_kernel,
         in_specs=[pl.BlockSpec(memory_space=pltpu.HBM)] * len(operands),
-        out_specs=vmem(4),
+        out_specs=vmem(7),
         out_shape=[
             jax.ShapeDtypeStruct((2 * rank, nq + rest), BF),
             jax.ShapeDtypeStruct((ne, rank), BF),
             jax.ShapeDtypeStruct((3 * rank, rank), BF),
             jax.ShapeDtypeStruct((length, HD), F32),
+            jax.ShapeDtypeStruct(basis.shape, BF),
+            jax.ShapeDtypeStruct(wq.shape, BF),
+            jax.ShapeDtypeStruct((wide, rest), BF),
         ],
         scratch_shapes=[
             pltpu.VMEM(back.shape, BF),
             pltpu.VMEM(gain.shape, F32),
-            pltpu.VMEM(basis.shape, BF),
-            pltpu.VMEM(wq.shape, BF),
-            pltpu.VMEM((wide, rest), BF),
             pltpu.VMEM(wo.shape, BF),
             pltpu.VMEM((rank, wide), BF),
             pltpu.VMEM((rank, wide), BF),
@@ -201,7 +201,7 @@
             pltpu.VMEM((ne, rank), F32),
             pltpu.SemaphoreType.DMA((5 + 2 * (wide // PIECE),)),
         ],
-        compiler_params=pltpu.CompilerParams(vmem_limit_bytes=2 * VMEM_BYTES),
+        compiler_params=pltpu.CompilerParams(vmem_limit_bytes=VMEM_BYTES * 3 // 2),
         cost_estimate=cost(6 * 10**9, 20 * 10**6),
         name="project_weights",
     )(*operands)
@@ -392,95 +392,109 @@
     )(new, sent, basis, m2, o2, g3, cosine, sine, *after)
 
 
-def write_split(ref, first, value):
+def write_split(ref, value):
     high, low = split(value, 2)
     both = jnp.concatenate([high.astype(F32), low.astype(F32)], axis=0)
-    ref[first:, : value.shape[1]] = both.astype(BF)
-
-
-def read_split(ref, first):
-    both = ref[first:, :CHUNK].astype(F32)
+    ref[ref.shape[0] - 16 :, :] = both.astype(BF)
+
+
+def read_split(ref):
+    both = ref[ref.shape[0] - 16 :, :].astype(F32)
     return both[:8] + both[8:]
 
 
 def gain_kernel(
-    u_ref, wq_ref, wk_ref, wv_ref, inner_ref, got_ref, after, out_ref, turned, rows_f32
+    u_ref, wq_ref, narrow_ref, inner_ref, got_ref, x_ref, after,
+    pair_ref, out_ref, turned, rows_f32,
 ):
     nq = wq_ref.shape[1]
     rows = u_ref.shape[0] // 2
+    rank = u_ref.shape[1]
     half = inner_ref.shape[0] // 2
     core = lax.axis_index("dp") & 1
     mine = add_wide(inner_ref[:half, :], got_ref[half:, :]).astype(BF)
     theirs = add_wide(inner_ref[half:, :], got_ref[:half, :]).astype(BF)
-    out_ref[:half, :] = mine
-    out_ref[half:, :] = jnp.zeros_like(out_ref[half:, :])
+    pair_ref[...] = mine
+    out_ref[: x_ref.shape[0], :] = x_ref[...]
     turned[:, pl.ds(pl.multiple_of(core * half, half), half)] = mine.T
     turned[:, pl.ds(pl.multiple_of((1 - core) * half, half), half)] = theirs.T
-    rows_f32[...] = jnp.zeros_like(rows_f32)
     for at in range(0, rows, CHUNK):
         place = pl.ds(pl.multiple_of(core * rows + at, CHUNK), CHUNK)
         against = nn(wq_ref[place, :], turned[:nq, :])
-        narrow = jnp.concatenate([wk_ref[place, :], wv_ref[place, :]], axis=1)
-        against += nn(narrow, turned[nq:, :])
+        against += nn(narrow_ref[place, :], turned[nq:, :])
         terms = against * u_ref[place, :].astype(F32)
         folded = sum(terms[:, side : side + HD] for side in range(0, terms.shape[1], HD))
-        rows_f32[at // CHUNK : at // CHUNK + 1, :] = jnp.sum(folded.T, axis=0, keepdims=True)
-    write_split(out_ref, half, rows_f32[...])
-
-
-def gain_part(basis, wq, wk, wv, inner, got, after):
+        line = jnp.sum(folded.T, axis=0, keepdims=True)
+        for side in range(0, CHUNK, rank):
+            row = (at + side) // rank
+            rows_f32[row : row + 1, :] = line[:, side : side + rank]
+    write_split(out_ref, rows_f32[...])
+
+
+def gain_part(basis, wq, narrow, inner, got, x, after):
     wide, rank = basis.shape
-    assert wide // 2 // CHUNK <= 8
+    assert wide // 2 == 8 * rank
+    held = tuple(pltpu.with_memory_space_constraint(a, pltpu.VMEM) for a in (basis, wq, narrow))
     return pl.pallas_call(
         gain_kernel,
         in_specs=vmem(6) + [pl.BlockSpec(memory_space=pl.ANY)],
-        out_specs=pl.BlockSpec(memory_space=pltpu.VMEM),
-        out_shape=jax.ShapeDtypeStruct((rank // 2 + 16, inner.shape[1]), BF),
+        out_specs=vmem(2),
+        out_shape=[
+            jax.ShapeDtypeStruct((rank // 2, inner.shape[1]), BF),
+            jax.ShapeDtypeStruct((x.shape[0] + 16, rank), BF),
+        ],
         scratch_shapes=[
             pltpu.VMEM((inner.shape[1], rank), BF),
-            pltpu.VMEM((8, CHUNK), F32),
+            pltpu.VMEM((8, rank), F32),
         ],
         compiler_params=pltpu.CompilerParams(vmem_limit_bytes=VMEM_BYTES),
         cost_estimate=cost(10**4, 10**3),
         name="pair_sum_and_gain_gradient",
-    )(basis, wq, wk, wv, inner, got, after)
+    )(*held, inner, got, x, after)
 
 
 def merge_kernel(a_ref, b_ref, after, out_ref):
-    half = out_ref.shape[0] - 16
-    out_ref[:half, :] = add_wide(a_ref[:half, :], b_ref[:half, :]).astype(BF)
-    out_ref[half:, :] = jnp.zeros_like(out_ref[half:, :])
-    write_split(out_ref, half, read_split(a_ref, half) + read_split(b_ref, half))
-
-
-def merge(a, b, after):
+    rest = out_ref.shape[0] - 16
+    out_ref[:rest, :] = add_wide(a_ref[:rest, :], b_ref[:rest, :]).astype(BF)
+    write_split(out_ref, read_split(a_ref) + read_split(b_ref))
+
+
+def total_kernel(a_ref, b_ref, after, out_ref):
+    out_ref[...] = read_split(a_ref) + read_split(b_ref)
+
+
+def own_kernel(a_ref, b_ref, after, *out_refs):
+    at = 0
+    for ref in out_refs:
+        size = ref.shape[1]
+        ref[...] = add_wide(a_ref[:, at : at + size], b_ref[:, at : at + size]).astype(BF)
+        at += size
+
+
+def small_kernel(kernel, name, out_shape, a, b, after):
     return pl.pallas_call(
-        merge_kernel,
+        kernel,
         in_specs=vmem(2) + [pl.BlockSpec(memory_space=pl.ANY)],
-        out_specs=pl.BlockSpec(memory_space=pltpu.VMEM),
-        out_shape=jax.ShapeDtypeStruct(a.shape, BF),
+        out_specs=jax.tree.map(lambda _: pl.BlockSpec(memory_space=pltpu.VMEM), out_shape),
+        out_shape=out_shape,
         compiler_params=pltpu.CompilerParams(vmem_limit_bytes=VMEM_BYTES // 2),
         cost_estimate=cost(10**4, 10**3),
-        name="sum_over_y",
+        name=name,
     )(a, b, after)
 
 
-def gather_kernel(own_ref, other_ref, out_ref):
-    half = own_ref.shape[0] - 16
-    out_ref[:8, :] = read_split(own_ref, half)
-    out_ref[8:, :] = read_split(other_ref, half)
-
-
-def gather_gain(own, other):
-    return pl.pallas_call(
-        gather_kernel,
-        in_specs=vmem(2),
-        out_specs=pl.BlockSpec(memory_space=pltpu.VMEM),
-        out_shape=jax.ShapeDtypeStruct((16, CHUNK), F32),
-        compiler_params=pltpu.CompilerParams(vmem_limit_bytes=VMEM_BYTES // 2),
-        cost_estimate=cost(10**4, 10**3),
-        name="gather_gain",
-    )(own, other)
+def merge(a, b, after):
+    return small_kernel(merge_kernel, "sum_with_gain", jax.ShapeDtypeStruct(a.shape, BF), a, b, after)
+
+
+def gain_total(a, b, after):
+    shape = jax.ShapeDtypeStruct((8, a.shape[1]), F32)
+    return small_kernel(total_kernel, "gain_total", shape, a, b, after)
+
+
+def own_pieces(a, b, sizes, after):
+    shapes = [jax.ShapeDtypeStruct((a.shape[0], n), BF) for n in sizes]
+    return small_kernel(own_kernel, "sum_over_y", shapes, a, b, after)
 
 
 def add_kernel(a_ref, b_ref, after, out_ref):
@@ -488,31 +502,29 @@
 
 
 def add_after(a, b, after):
-    return pl.pallas_call(
-        add_kernel,
-        in_specs=vmem(2) + [pl.BlockSpec(memory_space=pl.ANY)],
-        out_specs=pl.BlockSpec(memory_space=pltpu.VMEM),
-        out_shape=jax.ShapeDtypeStruct(a.shape, a.dtype),
-        compiler_params=pltpu.CompilerParams(vmem_limit_bytes=VMEM_BYTES // 2),
-        cost_estimate=cost(10**4, 10**3),
-        name="pair_sum",
-    )(a, b, after)
-
-
-def gather_halves(own_ref, other_ref, whole):
+    return small_kernel(add_kernel, "pair_sum", jax.ShapeDtypeStruct(a.shape, a.dtype), a, b, after)
+
+
+def gather_halves(own_refs, other_refs, whole):
     half = whole.shape[0] // 2
     core = lax.axis_index("dp") & 1
-    whole[pl.ds(pl.multiple_of(core * half, half), half), :] = own_ref[:half, :]
-    whole[pl.ds(pl.multiple_of((1 - core) * half, half), half), :] = other_ref[:half, :]
-
-
-def inward_kernel(u_ref, gain_ref, own_ref, other_ref, after, q_ref, k_ref, v_ref, inner):
+    at = 0
+    for own_ref, other_ref in zip(own_refs, other_refs):
+        columns = pl.ds(at, own_ref.shape[1])
+        whole[pl.ds(pl.multiple_of(core * half, half), half), columns] = own_ref[...]
+        whole[pl.ds(pl.multiple_of((1 - core) * half, half), half), columns] = other_ref[...]
+        at += own_ref.shape[1]
+
+
+def inward_kernel(pieces, u_ref, gain_ref, *refs):
+    own_refs, other_refs = refs[:pieces], refs[pieces : 2 * pieces]
+    q_ref, k_ref, v_ref, inner = refs[-4:]
     nq, nk = q_ref.shape[1], k_ref.shape[1]
     block = q_ref.shape[0]
 
     @pl.when(pl.program_id(0) == 0)
     def _():
-        gather_halves(own_ref, other_ref, inner)
+        gather_halves(own_refs, other_refs, inner)
 
     step = lax.axis_index("dp") * pl.num_programs(0) + pl.program_id(0)
     rows = pl.ds(pl.multiple_of(step * block, block), block)
@@ -526,7 +538,7 @@
 def outward_kernel(u_ref, own_ref, other_ref, after, o_ref, inner):
     @pl.when(pl.program_id(0) == 0)
     def _():
-        gather_halves(own_ref, other_ref, inner)
+        gather_halves([own_ref], [other_ref], inner)
 
     block, rows = o_ref.shape
     at = pl.multiple_of(pl.program_id(0) * block, block)
@@ -542,16 +554,16 @@
     rows = wide // lax.axis_size("dp")
     block = rows // STEPS
     return pl.pallas_call(
-        inward_kernel,
+        functools.partial(inward_kernel, len(own)),
         grid=(STEPS,),
-        in_specs=vmem(4) + [pl.BlockSpec(memory_space=pl.ANY)],
+        in_specs=vmem(2 + 2 * len(own)) + [pl.BlockSpec(memory_space=pl.ANY)],
         out_specs=[pl.BlockSpec((block, n), lambda i: (i, 0)) for n in sizes],
         scratch_shapes=[pltpu.VMEM((rank, sum(sizes)), BF)],
         out_shape=[jax.ShapeDtypeStruct((rows, n), BF) for n in sizes],
         compiler_params=pltpu.CompilerParams(vmem_limit_bytes=VMEM_BYTES),
         cost_estimate=cost(10**4, 10**3),
         name="inward_weight_gradients",
-    )(basis, gain, own, other, after)
+    )(basis, gain, *own, *other, after)
 
 
 def outward_grad(basis, own, other, after):
@@ -573,24 +585,24 @@
 
 def results_kernel(
     wide, fbase_ref, y_ref, ygot_ref, base_ref, unit_ref, x_ref, xgot_ref, back_ref, inv_ref,
-    gain_ref, gain_got_ref, after,
+    gain_ref, gain_other_ref, after,
     f_ref, b_ref, gain_out_ref,
 ):
     f_ref[...] = (fbase_ref[...] + add_wide(y_ref[...], ygot_ref[...])).astype(BF)
-    x = add_wide(x_ref[...], xgot_ref[...])
+    length = back_ref.shape[0]
+    x = add_wide(x_ref[:length, :], xgot_ref[:length, :])
     inv = inv_ref[:, :1]
     along = jnp.sum(x * back_ref[...].astype(F32), axis=1, keepdims=True)
     middle = along * inv * (1.0 / wide)
     b_ref[...] = (base_ref[...] + (x - unit_ref[...] * middle) * inv).astype(BF)
     core = lax.axis_index("dp") & 1
-    gain = gain_ref[...] + gain_got_ref[...]
     half = wide // 2
-    for at in range(0, half, CHUNK):
-        row = at // CHUNK
-        mine = pl.ds(pl.multiple_of(core * half + at, CHUNK), CHUNK)
-        theirs = pl.ds(pl.multiple_of((1 - core) * half + at, CHUNK), CHUNK)
-        gain_out_ref[:, mine] = gain[row : row + 1, :]
-        gain_out_ref[:, theirs] = gain[8 + row : 9 + row, :]
+    rank = gain_ref.shape[1]
+    for row in range(half // rank):
+        mine = pl.ds(pl.multiple_of(core * half + row * rank, rank), rank)
+        theirs = pl.ds(pl.multiple_of((1 - core) * half + row * rank, rank), rank)
+        gain_out_ref[:, mine] = gain_ref[row : row + 1, :]
+        gain_out_ref[:, theirs] = gain_other_ref[row : row + 1, :]
 
 
 def results(wide, after, *operands):
@@ -627,36 +639,34 @@
     arrived, returned = cross_pipe(sent_forward[0], sent_backward[0])
     cosine, sine = rope_tables(back.shape[0])
 
-    m2, o2, g3, inv = project(back, norm_gain, subspace, wq, wk, wv, wo)
+    m2, o2, g3, inv, basis, wq, narrow = project(back, norm_gain, subspace, wq, wk, wv, wo)
     inner, out_give, out_keep, x, base, unit = backward(
         back, loss_grad, returned, m2, o2, g3, inv, cosine, sine
     )
     out_got = swap(out_give, "dp", 1)
     inner_got = swap(inner, "dp", 1)
-    x_got = swap(x, "tensor", 2)
     out_pair = add_wide(out_keep, out_got).astype(BF)
     out_got = swap(out_pair, "dp", 2)
-    pair = gain_part(subspace, wq, wk, wv, inner, inner_got, out_pair)
+    pair, x = gain_part(basis, wq, narrow, inner, inner_got, x, out_pair)
     pair_got = swap(pair, "dp", 2)
-    y, fbase = forward(new_coeffs, arrived, subspace, m2, o2, g3, cosine, sine, pair)
+    x_got = swap(x, "tensor", 1)
+    y, fbase = forward(new_coeffs, arrived, basis, m2, o2, g3, cosine, sine, pair)
     y_got = swap(y, "tensor", 1)
-    x = add_after(x, x_got, y)
-    x_got = swap(x, "tensor", 1)
+    x = merge(x, x_got, y)
+    x_got = swap(x, "tensor", 2)
     out_own = add_after(out_pair, out_got, x)
-    grad_o = outward_grad(subspace, out_own, swap(out_own, "dp", 1), x)
+    grad_o = outward_grad(basis, out_own, swap(out_own, "dp", 1), x)
     y = add_after(y, y_got, *in_hbm((grad_o,)))
     y_got = swap(y, "tensor", 2)
-    own = merge(pair, pair_got, y)
-    other = swap(own, "dp", 1)
-    gain = gather_gain(own, other)
-    gain_got = swap(gain, "tensor", 1)
-    grad_q, grad_k, grad_v = inward_grads(
-        subspace, norm_gain, own, other, (nq, nk, nv), gain
-    )
+    own = own_pieces(pair, pair_got, (nq // 2, nq - nq // 2, nk + nv), y)
+    other = [swap(piece, "dp", 1) for piece in own]
+    gain = gain_total(x, x_got, own[0])
+    gain_got = swap(gain, "dp", 2)
+    grad_q, grad_k, grad_v = inward_grads(basis, norm_gain, own, other, (nq, nk, nv), gain)
     gain = add_after(gain, gain_got, *in_hbm((grad_v,)))
-    gain_got = swap(gain, "tensor", 2)
+    gain_other = swap(gain, "dp", 1)
     forward_out, backward_out, grad_gain = results(
-        wide, grad_v, fbase, y, y_got, base, unit, x, x_got, back, inv, gain, gain_got
+        wide, grad_v, fbase, y, y_got, base, unit, x, x_got, back, inv, gain, gain_other
     )
     return (
         forward_out[None],

time: 56.1 us -> 52.6 us (0.938)
  starting transfers between devices: 17 us -> 13.7 us
  Pallas kernels: 28.5 us -> 27.7 us
  waiting for transfers between devices: 8.51 us -> 9.25 us
    ppermute x13 -> x15, starting transfers between devices: 17 us -> 13.7 us  [swap(): return lax.ppermute(x, axis, [(i, i ^ bit) for i in range(devices)])]
    pallas_call x1, Pallas kernels: 12 us -> 11.2 us  [project(): pl.pallas_call(project_kernel, in_specs=[pl.BlockSpec(memory_space=pltpu....]
    ppermute x13 -> x15, waiting for transfers between devices: 8.51 us -> 9.25 us  [swap(): return lax.ppermute(x, axis, [(i, i ^ bit) for i in range(devices)])]
  transfers between devices with their start and end apart: 13 -> 15, of which waited for: 5 -> 4; matrix products, arithmetic and copies ran while one was open for 0% -> 0% of each run, Pallas kernels for 39% -> 40%
where the time goes in v4:
time: 52.6 us; the launch traced here: 52.4 us
  Pallas kernels  27.7 us (53%)
  starting transfers between devices  13.7 us (26%)
  waiting for transfers between devices  9.25 us (18%)
  other arithmetic  0.99 us (2%)
  between operations  0.82 us (2%)
    ppermute x15, starting transfers between devices, swap(): return lax.ppermute(x, axis, [(i, i ^ bit) for i in range(devices)])  13.7 us
    pallas_call x1, Pallas kernels, project(): pl.pallas_call(project_kernel, in_specs=[pl.BlockSpec(memory_space=pltpu....  11.2 us
    ppermute x15, waiting for transfers between devices, swap(): return lax.ppermute(x, axis, [(i, i ^ bit) for i in range(devices)])  9.25 us
    pallas_call x1, Pallas kernels, backward(): pl.pallas_call(backward_kernel, in_specs=vmem(9), out_specs=vmem(6), out_...  5.45 us
    pallas_call x1, Pallas kernels, forward(): pl.pallas_call(forward_kernel, in_specs=vmem(8) + [pl.BlockSpec(memory_sp...  3.77 us
    pallas_call x1, Pallas kernels, inward_grads(): pl.pallas_call(functools.partial(inward_kernel, len(own)), grid=(STEPS,),...  2.21 us
    pallas_call x1, Pallas kernels, outward_grad(): pl.pallas_call(outward_kernel, grid=(STEPS,), in_specs=vmem(3) + [pl.Bloc...  2.01 us
    pallas_call x1, Pallas kernels, gain_part(): pl.pallas_call(gain_kernel, in_specs=vmem(6) + [pl.BlockSpec(memory_space...  1.82 us
  transfers between devices with their start and end apart: 15, of which 4 were waited for; matrix products, arithmetic and copies ran while one was open for 0% of the time, Pallas kernels for 40%

profile of v4, /device:TPU:0, one launch (start us, length us, event | category | flops | bytes accessed | tf_op | source)
XLA Modules:
  0.0 52.4 jit_solution(12077021377368380158)
XLA Ops:
  0.6 0.9 %select_bitcast_fusion = bf16[256,256]{1,0:T(8,128)(2,1)S(1)} fusion(bf16[1,256,256]{2,1,0:T(8,128)(2,1)} %param.15, bf16[1,256,256]{2,1,0:T(8,128)(2,1)} %param.16, pred[]{:T(512)S(6)} %eq.3), kind=kLoop, calls=%fused_computation.1 | loop fusion | flops 65536 | bytes 393217 | tf_op jit(solution)/shard_map/jit(_where)/select_n | solution.py:39
  1.6 3.0 %collective-permute-start = (bf16[256,256]{1,0:T(8,128)(2,1)S(1)}, bf16[256,256]{1,0:T(8,128)(2,1)S(1)}, u32[]{:S(2)}, u32[]{:S(2)}) collective-permute-start(bf16[256,256]{1,0:T(8,128)(2,1)S(1)} %select_bitcast_fusion), channel_id=1, source_target_pairs={{0,16},{16,0},{1,17},{17,1},{2,18},{18,2},{3,19},{19,3},{4,20},{20... | collective-permute-start | bytes 393224 | tf_op jit(solution)/shard_map/ppermute | solution.py:32
  4.6 11.2 %project_weights.1 = (bf16[512,1280]{1,0:T(8,128)(2,1)S(1)}, bf16[1024,256]{1,0:T(8,128)(2,1)S(1)}, bf16[768,256]{1,0:T(8,128)(2,1)S(1)}, f32[256,128]{1,0:T(8,1...) custom-call(bf16[256,256]{1,0:T(8,128)(2,1)} %bitcast.13, ...), custom_call_target="tpu_custom_call" | custom-call | flops 6000000000 | bytes 20000000 | tf_op jit(solution)/shard_map/project_weights/pallas_call | solution.py:181
  15.8 5.4 %attention_backward.1 = (bf16[256,1280]{1,0:T(8,128)(2,1)S(1)}, bf16[128,1024]{1,0:T(8,128)(2,1)S(1)}, bf16[128,1024]{1,0:T(8,128)(2,1)S(1)}, bf16[256,256]{1,0:...) custom-call(bf16[256,256]{1,0:T(8,128)(2,1)S(1)} %bitcast.14, bf16[256,256]{1,0:T(8,128)(2,1)S(1)} %copy-done.3, ...), custom_call_target="tpu_custom_call" | custom-call | flops 10000 | bytes 1000 | tf_op jit(solution)/shard_map/attention_backward/pallas_call | solution.py:306
  21.3 0.5 collective-permute-start.2
  21.8 2.0 %collective-permute-done.2 = bf16[128,1024]{1,0:T(8,128)(2,1)S(1)} collective-permute-done((bf16[128,1024]{1,0:T(8,128)(2,1)S(1)}, bf16[128,1024]{1,0:T(8,128)(2,1)S(1)}, u32[]{:S(2)}, u32[]{:S(2)}) %collective-permute-start.2) | collective-permute-done | bytes 262176 | tf_op jit(solution)/shard_map/ppermute | solution.py:32
  23.9 1.6 %collective-permute-start.4 = (bf16[128,1024]{1,0:T(8,128)(2,1)S(1)}, bf16[128,1024]{1,0:T(8,128)(2,1)S(1)}, u32[]{:S(2)}, u32[]{:S(2)}) collective-permute-start(bf16[128,1024]{1,0:T(8,128)(2,1)S(1)} %add_convert_fusion.after.a_ref), channel_id=1, source_target_pairs={{0,2},{1,3},{2,0},{3,1},{4,6},{5,7},{6,4},{7,5},{8,10},{9,11},{10,... | collective-permute-start | bytes 786440 | tf_op jit(solution)/shard_map/ppermute | solution.py:32
  25.4 1.8 %pair_sum_and_gain_gradient.1 = (bf16[128,1280]{1,0:T(8,128)(2,1)S(1)}, bf16[272,256]{1,0:T(8,128)(2,1)S(1)}) custom-call(bf16[4096,256]{1,0:T(8,128)(2,1)S(1)} %get-tuple-element.33.u_ref, bf16[4096,1024]{1,0:T(8,128)(2,1)S(1)} %get-tuple-element.37.wq_ref, bf16[4096,256]{1,0:T(8,128)(2,1)S(1)} %get-tuple-element.38.narrow_ref, ...), custom_call_target="tpu_custom_call" | custom-call | flops 10000 | bytes 1000 | tf_op jit(solution)/shard_map/pair_sum_and_gain_gradient/pallas_call | solution.py:438
  27.3 1.7 %collective-permute-start.5 = (bf16[272,256]{1,0:T(8,128)(2,1)S(1)}, bf16[272,256]{1,0:T(8,128)(2,1)S(1)}, u32[]{:S(2)}, u32[]{:S(2)}) collective-permute-start(bf16[272,256]{1,0:T(8,128)(2,1)S(1)} %get-tuple-element.47.a_ref), channel_id=1, source_target_pairs={{0,4},{4,0},{8,12},{12,8},{1,5},{5,1},{9,13},{13,9},{2,6},{6,2},{1... | collective-permute-start | bytes 417800 | tf_op jit(solution)/shard_map/ppermute | solution.py:32
  28.9 0.5 collective-permute-start.9
  29.4 3.8 %attention_forward.1 = (bf16[256,256]{1,0:T(8,128)(2,1)S(1)}, f32[256,256]{1,0:T(8,128)S(1)}) custom-call(bf16[256,256]{1,0:T(8,128)(2,1)S(1)} %copy-done.4, bf16[256,256]{1,0:T(8,128)(2,1)S(1)} %collective-permute-done.sent_ref, bf16[4096,256]{1,0:T(8,128)(2,1)S(1)} %get-tuple-element.33.u_ref, bf16[512,1280]{1,0:T(8,128)(2,1)S(1)} %get-tuple-element.34.m_ref, ...), custom_call_target="tpu_custom_call" | custom-call | flops 10000 | bytes 1000 | tf_op jit(solution)/shard_map/attention_forward/pallas_call | solution.py:372
  33.3 0.1 collective-permute-start.6
  33.4 1.5 %collective-permute-start.3 = (bf16[256,256]{1,0:T(8,128)(2,1)S(1)}, bf16[256,256]{1,0:T(8,128)(2,1)S(1)}, u32[]{:S(2)}, u32[]{:S(2)}) collective-permute-start(bf16[256,256]{1,0:T(8,128)(2,1)S(1)} %get-tuple-element.46.after.a_ref), channel_id=1, source_target_pairs={{0,4},{4,0},{8,12},{12,8},{1,5},{5,1},{9,13},{13,9},{2,6},{6,2},{1... | collective-permute-start | bytes 393224 | tf_op jit(solution)/shard_map/ppermute | solution.py:32
  34.9 2.6 %collective-permute-start.8 = (bf16[272,256]{1,0:T(8,128)(2,1)S(1)}, bf16[272,256]{1,0:T(8,128)(2,1)S(1)}, u32[]{:S(2)}, u32[]{:S(2)}) collective-permute-start(bf16[272,256]{1,0:T(8,128)(2,1)S(1)} %sum_with_gain.1.after.a_ref.x_ref), channel_id=1, source_target_pairs={{0,8},{4,12},{8,0},{12,4},{1,9},{5,13},{9,1},{13,5},{2,10},{6,14},... | collective-permute-start | bytes 417800 | tf_op jit(solution)/shard_map/ppermute | solution.py:32
  37.4 2.0 %output_weight_gradient.1.after = bf16[1024,1024]{1,0:T(8,128)(2,1)} custom-call(bf16[4096,256]{1,0:T(8,128)(2,1)S(1)} %get-tuple-element.33.u_ref, bf16[128,1024]{1,0:T(8,128)(2,1)S(1)} %pair_sum.3.own_ref, bf16[128,1024]{1,0:T(8,128)(2,1)S(1)} %collective-permute-done.6.other_ref, bf16[272,256]{1,0:T(8,128)(2,1)S(1)} %sum_with_gain.1.after.a_ref.x_ref), custom_call_target="tpu_custom_call" | custom-call | flops 10000 | bytes 1000 | tf_op jit(solution)/shard_map/output_weight_gradient/pallas_call | solution.py:573
  39.5 2.7 %collective-permute-done.3.b_ref = bf16[256,256]{1,0:T(8,128)(2,1)S(1)} collective-permute-done((bf16[256,256]{1,0:T(8,128)(2,1)S(1)}, bf16[256,256]{1,0:T(8,128)(2,1)S(1)}, u32[]{:S(2)}, u32[]{:S(2)}) %collective-permute-start.3) | collective-permute-done | bytes 131104 | tf_op jit(solution)/shard_map/ppermute | solution.py:32
  42.2 0.1 sum_over_y.1
  42.4 0.5 collective-permute-start.12
  42.9 0.2 collective-permute-start.7
  43.1 1.5 %collective-permute-done.8.b_ref.xgot_ref = bf16[272,256]{1,0:T(8,128)(2,1)S(1)} collective-permute-done((bf16[272,256]{1,0:T(8,128)(2,1)S(1)}, bf16[272,256]{1,0:T(8,128)(2,1)S(1)}, u32[]{:S(2)}, u32[]{:S(2)}) %collective-permute-start.8) | collective-permute-done | bytes 139296 | tf_op jit(solution)/shard_map/ppermute | solution.py:32
  44.6 1.5 %collective-permute-start.10 = (f32[8,256]{1,0:T(8,128)S(1)}, f32[8,256]{1,0:T(8,128)S(1)}, u32[]{:S(2)}, u32[]{:S(2)}) collective-permute-start(f32[8,256]{1,0:T(8,128)S(1)} %gain_total.1.refs_6_.a_ref), channel_id=1, source_target_pairs={{0,2},{1,3},{2,0},{3,1},{4,6},{5,7},{6,4},{7,5},{8,10},{9,11},{10,... | collective-permute-start | bytes 24584 | tf_op jit(solution)/shard_map/ppermute | solution.py:32
  46.1 2.2 %inward_weight_gradients.1 = (bf16[1024,1024]{1,0:T(8,128)(2,1)}, bf16[1024,128]{1,0:T(8,128)(2,1)}, bf16[1024,128]{1,0:T(8,128)(2,1)}) custom-call(bf16[4096,256]{1,0:T(8,128)(2,1)S(1)} %get-tuple-element.33.u_ref, f32[1,4096]{1,0:T(1,128)S(1)} %copy-done.5, bf16[128,512]{1,0:T(8,128)(2,1)S(1)} %get-tuple-element.50.after.refs_0_, ...), custom_call_target="tpu_custom_call" | custom-call | flops 10000 | bytes 1000 | tf_op jit(solution)/shard_map/inward_weight_gradients/pallas_call | solution.py:556
  48.4 3.0 %collective-permute-done.7.ygot_ref = bf16[256,256]{1,0:T(8,128)(2,1)S(1)} collective-permute-done((bf16[256,256]{1,0:T(8,128)(2,1)S(1)}, bf16[256,256]{1,0:T(8,128)(2,1)S(1)}, u32[]{:S(2)}, u32[]{:S(2)}) %collective-permute-start.7) | collective-permute-done | bytes 131104 | tf_op jit(solution)/shard_map/ppermute | solution.py:32
  51.4 1.0 %section_results.1 = (bf16[256,256]{1,0:T(8,128)(2,1)}, bf16[256,256]{1,0:T(8,128)(2,1)}, f32[1,4096]{1,0:T(1,128)}) custom-call(f32[256,256]{1,0:T(8,128)S(1)} %get-tuple-element.45.fbase_ref, bf16[256,256]{1,0:T(8,128)(2,1)S(1)} %pair_sum.4.after.y_ref, bf16[256,256]{1,0:T(8,128)(2,1)S(1)} %collective-permute-done.7.ygot_ref, ...), custom_call_target="tpu_custom_call" | custom-call | flops 10000 | bytes 1000 | tf_op jit(solution)/shard_map/section_results/pallas_call | solution.py:611
  (33 shorter events, 0.5 us)
Async XLA Ops:
  1.6 14.2 %collective-permute-start = (bf16[256,256]{1,0:T(8,128)(2,1)S(1)}, bf16[256,256]{1,0:T(8,128)(2,1)S(1)}, u32[]{:S(2)}, u32[]{:S(2)}) collective-permute-start(bf16[256,256]{1,0:T(8,128)(2,1)S(1)} %select_bitcast_fusion), channel_id=1, source_target_pairs={{0,16},{16,0},{1,17},{17,1},{2,18},{18,2},{3,19},{19,3},{4,20},{20... | collective-permute-start | bytes 393224 | tf_op jit(solution)/shard_map/ppermute | solution.py:32
  4.6 11.2 %copy-start = (bf16[1,256,256]{2,1,0:T(8,128)(2,1)S(1)}, bf16[1,256,256]{2,1,0:T(8,128)(2,1)}, u32[]{:S(2)}) copy-start(bf16[1,256,256]{2,1,0:T(8,128)(2,1)} %param.17) | copy-start | bytes 393220
  4.6 11.2 %copy-start.1 = (f32[256,128]{1,0:T(8,128)S(1)}, f32[256,128]{1,0:T(8,128)}, u32[]{:S(2)}) copy-start(f32[256,128]{1,0:T(8,128)} %constant.12.clone.cos_ref) | copy-start | bytes 393220
  4.6 11.2 %copy-start.2 = (f32[256,128]{1,0:T(8,128)S(1)}, f32[256,128]{1,0:T(8,128)}, u32[]{:S(2)}) copy-start(f32[256,128]{1,0:T(8,128)} %constant.13.clone.sin_ref) | copy-start | bytes 393220
  4.6 11.2 %copy-start.3 = (bf16[256,256]{1,0:T(8,128)(2,1)S(1)}, bf16[256,256]{1,0:T(8,128)(2,1)}, u32[]{:S(2)}) copy-start(bf16[256,256]{1,0:T(8,128)(2,1)} %loss_ref.1) | copy-start | bytes 393220
  21.3 4.2 %collective-permute-start.1 = (bf16[256,1280]{1,0:T(8,128)(2,1)S(1)}, bf16[256,1280]{1,0:T(8,128)(2,1)S(1)}, u32[]{:S(2)}, u32[]{:S(2)}) collective-permute-start(bf16[256,1280]{1,0:T(8,128)(2,1)S(1)} %get-tuple-element.40.inner_ref), channel_id=1, source_target_pairs={{0,1},{1,0},{2,3},{3,2},{4,5},{5,4},{6,7},{7,6},{8,9},{9,8},{10,11... | collective-permute-start | bytes 1966088 | tf_op jit(solution)/shard_map/ppermute | solution.py:32
  21.3 2.5 %collective-permute-start.2 = (bf16[128,1024]{1,0:T(8,128)(2,1)S(1)}, bf16[128,1024]{1,0:T(8,128)(2,1)S(1)}, u32[]{:S(2)}, u32[]{:S(2)}) collective-permute-start(bf16[128,1024]{1,0:T(8,128)(2,1)S(1)} %get-tuple-element.43), channel_id=1, source_target_pairs={{0,1},{1,0},{2,3},{3,2},{4,5},{5,4},{6,7},{7,6},{8,9},{9,8},{10,11... | collective-permute-start | bytes 786440 | tf_op jit(solution)/shard_map/ppermute | solution.py:32
  23.9 9.4 %collective-permute-start.4 = (bf16[128,1024]{1,0:T(8,128)(2,1)S(1)}, bf16[128,1024]{1,0:T(8,128)(2,1)S(1)}, u32[]{:S(2)}, u32[]{:S(2)}) collective-permute-start(bf16[128,1024]{1,0:T(8,128)(2,1)S(1)} %add_convert_fusion.after.a_ref), channel_id=1, source_target_pairs={{0,2},{1,3},{2,0},{3,1},{4,6},{5,7},{6,4},{7,5},{8,10},{9,11},{10,... | collective-permute-start | bytes 786440 | tf_op jit(solution)/shard_map/ppermute | solution.py:32
  25.4 4.0 %copy-start.4 = (bf16[256,256]{1,0:T(8,128)(2,1)S(1)}, bf16[256,256]{1,0:T(8,128)(2,1)}, u32[]{:S(2)}) copy-start(bf16[256,256]{1,0:T(8,128)(2,1)} %new_ref.1) | copy-start | bytes 393220
  27.3 5.9 %collective-permute-start.5 = (bf16[272,256]{1,0:T(8,128)(2,1)S(1)}, bf16[272,256]{1,0:T(8,128)(2,1)S(1)}, u32[]{:S(2)}, u32[]{:S(2)}) collective-permute-start(bf16[272,256]{1,0:T(8,128)(2,1)S(1)} %get-tuple-element.47.a_ref), channel_id=1, source_target_pairs={{0,4},{4,0},{8,12},{12,8},{1,5},{5,1},{9,13},{13,9},{2,6},{6,2},{1... | collective-permute-start | bytes 417800 | tf_op jit(solution)/shard_map/ppermute | solution.py:32
  28.9 13.3 %collective-permute-start.9 = (bf16[128,1280]{1,0:T(8,128)(2,1)S(1)}, bf16[128,1280]{1,0:T(8,128)(2,1)S(1)}, u32[]{:S(2)}, u32[]{:S(2)}) collective-permute-start(bf16[128,1280]{1,0:T(8,128)(2,1)S(1)} %get-tuple-element.44.rest_0_.a_ref), channel_id=1, source_target_pairs={{0,2},{1,3},{2,0},{3,1},{4,6},{5,7},{6,4},{7,5},{8,10},{9,11},{10,... | collective-permute-start | bytes 983048 | tf_op jit(solution)/shard_map/ppermute | solution.py:32
  33.3 4.1 %collective-permute-start.6 = (bf16[128,1024]{1,0:T(8,128)(2,1)S(1)}, bf16[128,1024]{1,0:T(8,128)(2,1)S(1)}, u32[]{:S(2)}, u32[]{:S(2)}) collective-permute-start(bf16[128,1024]{1,0:T(8,128)(2,1)S(1)} %pair_sum.3.own_ref), channel_id=1, source_target_pairs={{0,1},{1,0},{2,3},{3,2},{4,5},{5,4},{6,7},{7,6},{8,9},{9,8},{10,11... | collective-permute-start | bytes 786440 | tf_op jit(solution)/shard_map/ppermute | solution.py:32
  33.4 8.8 %collective-permute-start.3 = (bf16[256,256]{1,0:T(8,128)(2,1)S(1)}, bf16[256,256]{1,0:T(8,128)(2,1)S(1)}, u32[]{:S(2)}, u32[]{:S(2)}) collective-permute-start(bf16[256,256]{1,0:T(8,128)(2,1)S(1)} %get-tuple-element.46.after.a_ref), channel_id=1, source_target_pairs={{0,4},{4,0},{8,12},{12,8},{1,5},{5,1},{9,13},{13,9},{2,6},{6,2},{1... | collective-permute-start | bytes 393224 | tf_op jit(solution)/shard_map/ppermute | solution.py:32
  34.9 9.7 %collective-permute-start.8 = (bf16[272,256]{1,0:T(8,128)(2,1)S(1)}, bf16[272,256]{1,0:T(8,128)(2,1)S(1)}, u32[]{:S(2)}, u32[]{:S(2)}) collective-permute-start(bf16[272,256]{1,0:T(8,128)(2,1)S(1)} %sum_with_gain.1.after.a_ref.x_ref), channel_id=1, source_target_pairs={{0,8},{4,12},{8,0},{12,4},{1,9},{5,13},{9,1},{13,5},{2,10},{6,14},... | collective-permute-start | bytes 417800 | tf_op jit(solution)/shard_map/ppermute | solution.py:32
  39.5 6.6 %copy-start.5 = (f32[1,4096]{1,0:T(1,128)S(1)}, f32[1,4096]{1,0:T(1,128)}, u32[]{:S(2)}) copy-start(f32[1,4096]{1,0:T(1,128)} %gain_ref.1) | copy-start | bytes 49156
  42.3 3.8 %collective-permute-start.11 = (bf16[128,512]{1,0:T(8,128)(2,1)S(1)}, bf16[128,512]{1,0:T(8,128)(2,1)S(1)}, u32[]{:S(2)}, u32[]{:S(2)}) collective-permute-start(bf16[128,512]{1,0:T(8,128)(2,1)S(1)} %get-tuple-element.50.after.refs_0_), channel_id=1, source_target_pairs={{0,1},{1,0},{2,3},{3,2},{4,5},{5,4},{6,7},{7,6},{8,9},{9,8},{10,11... | collective-permute-start | bytes 393224 | tf_op jit(solution)/shard_map/ppermute | solution.py:32
  42.4 3.7 %collective-permute-start.12 = (bf16[128,512]{1,0:T(8,128)(2,1)S(1)}, bf16[128,512]{1,0:T(8,128)(2,1)S(1)}, u32[]{:S(2)}, u32[]{:S(2)}) collective-permute-start(bf16[128,512]{1,0:T(8,128)(2,1)S(1)} %get-tuple-element.51.refs_1_), channel_id=1, source_target_pairs={{0,1},{1,0},{2,3},{3,2},{4,5},{5,4},{6,7},{7,6},{8,9},{9,8},{10,11... | collective-permute-start | bytes 393224 | tf_op jit(solution)/shard_map/ppermute | solution.py:32
  42.9 8.5 %collective-permute-start.7 = (bf16[256,256]{1,0:T(8,128)(2,1)S(1)}, bf16[256,256]{1,0:T(8,128)(2,1)S(1)}, u32[]{:S(2)}, u32[]{:S(2)}) collective-permute-start(bf16[256,256]{1,0:T(8,128)(2,1)S(1)} %pair_sum.4.after.y_ref), channel_id=1, source_target_pairs={{0,8},{4,12},{8,0},{12,4},{1,9},{5,13},{9,1},{13,5},{2,10},{6,14},... | collective-permute-start | bytes 393224 | tf_op jit(solution)/shard_map/ppermute | solution.py:32
  43.1 3.0 %collective-permute-start.13 = (bf16[128,256]{1,0:T(8,128)(2,1)S(1)}, bf16[128,256]{1,0:T(8,128)(2,1)S(1)}, u32[]{:S(2)}, u32[]{:S(2)}) collective-permute-start(bf16[128,256]{1,0:T(8,128)(2,1)S(1)} %get-tuple-element.52.refs_2_), channel_id=1, source_target_pairs={{0,1},{1,0},{2,3},{3,2},{4,5},{5,4},{6,7},{7,6},{8,9},{9,8},{10,11... | collective-permute-start | bytes 196616 | tf_op jit(solution)/shard_map/ppermute | solution.py:32
  44.6 3.8 %collective-permute-start.10 = (f32[8,256]{1,0:T(8,128)S(1)}, f32[8,256]{1,0:T(8,128)S(1)}, u32[]{:S(2)}, u32[]{:S(2)}) collective-permute-start(f32[8,256]{1,0:T(8,128)S(1)} %gain_total.1.refs_6_.a_ref), channel_id=1, source_target_pairs={{0,2},{1,3},{2,0},{3,1},{4,6},{5,7},{6,4},{7,5},{8,10},{9,11},{10,... | collective-permute-start | bytes 24584 | tf_op jit(solution)/shard_map/ppermute | solution.py:32
  48.3 3.1 %collective-permute-start.14 = (f32[8,256]{1,0:T(8,128)S(1)}, f32[8,256]{1,0:T(8,128)S(1)}, u32[]{:S(2)}, u32[]{:S(2)}) collective-permute-start(f32[8,256]{1,0:T(8,128)S(1)} %pair_sum.5.gain_ref), channel_id=1, source_target_pairs={{0,1},{1,0},{2,3},{3,2},{4,5},{5,4},{6,7},{7,6},{8,9},{9,8},{10,11... | collective-permute-start | bytes 24584 | tf_op jit(solution)/shard_map/ppermute | solution.py:32

commit v5 on v4

--- a/solution.py
+++ b/solution.py
@@ -96,15 +96,16 @@
 
 def project_kernel(
     back_hbm, gain_hbm, u_hbm, wq_hbm, wk_hbm, wv_hbm, wo_hbm,
-    m_ref, o_ref, g_ref, inv_ref, u, wq, narrow,
-    back, gain, wo, turned, scaled, m_acc, o_acc, sems,
+    m_ref, o_ref, inv_ref, u, wq, narrow, turned,
+    back, gain, wo, scaled, m_acc, o_acc, sems,
 ):
     wide, rank = u.shape
     nq = wq.shape[1]
     nk = wk_hbm.shape[1]
     parts = wide // PIECE
     pieces = [pl.ds(i * PIECE, PIECE) for i in range(parts)]
-    pairs = [(back_hbm, back), (gain_hbm, gain), (u_hbm, u)]
+    pairs = [(back_hbm, back), (gain_hbm, gain)]
+    pairs += [(u_hbm.at[at, :], u.at[at, :]) for at in pieces]
     pairs += [(wq_hbm.at[at, :], wq.at[at, :]) for at in pieces[:2]]
     pairs += [(wk_hbm, narrow.at[:, pl.ds(0, nk)])]
     pairs += [(wv_hbm, narrow.at[:, pl.ds(nk, narrow.shape[1] - nk)])]
@@ -126,24 +127,22 @@
         start_to(n + 1 + AHEAD)
         copies[n].wait()
 
-    start_to(3 + AHEAD)
-    for n in range(3):
-        copies[n].wait()
-    turned[...] = u[...].T
-    scaled[...] = (turned[...].astype(F32) * gain[...]).astype(BF)
-    gram = nn(turned[...], u[...])
-    for i, piece in enumerate(split(gram, 3)):
-        g_ref[i * rank : (i + 1) * rank, :] = piece
+    start_to(2 + parts + AHEAD)
+    copies[0].wait()
+    copies[1].wait()
     square = jnp.zeros((back.shape[0], HD), F32)
-    for at in range(0, wide, PIECE):
-        decoded = nn(back[...], turned[:, at : at + PIECE])
+    for i, at in enumerate(pieces):
+        copies[2 + i].wait()
+        turned[:, at] = u[at, :].T
+        scaled[:, at] = (turned[:, at].astype(F32) * gain[:, at]).astype(BF)
+        decoded = nn(back[...], turned[:, at])
         for side in range(0, PIECE, HD):
             part = decoded[:, side : side + HD]
             square = square + part * part
     inv_ref[...] = jnp.broadcast_to(
         inverse_root(jnp.sum(square, axis=1, keepdims=True), wide), inv_ref.shape
     )
-    place = 3
+    place = 2 + parts
     for i, at in enumerate(pieces):
         if i == 2:
             wait(place)
@@ -185,21 +184,20 @@
         out_shape=[
             jax.ShapeDtypeStruct((2 * rank, nq + rest), BF),
             jax.ShapeDtypeStruct((ne, rank), BF),
-            jax.ShapeDtypeStruct((3 * rank, rank), BF),
             jax.ShapeDtypeStruct((length, HD), F32),
             jax.ShapeDtypeStruct(basis.shape, BF),
             jax.ShapeDtypeStruct(wq.shape, BF),
             jax.ShapeDtypeStruct((wide, rest), BF),
+            jax.ShapeDtypeStruct((rank, wide), BF),
         ],
         scratch_shapes=[
             pltpu.VMEM(back.shape, BF),
             pltpu.VMEM(gain.shape, F32),
             pltpu.VMEM(wo.shape, BF),
             pltpu.VMEM((rank, wide), BF),
-            pltpu.VMEM((rank, wide), BF),
             pltpu.VMEM((rank, nq), F32),
             pltpu.VMEM((ne, rank), F32),
-            pltpu.SemaphoreType.DMA((5 + 2 * (wide // PIECE),)),
+            pltpu.SemaphoreType.DMA((4 + 3 * (wide // PIECE),)),
         ],
         compiler_params=pltpu.CompilerParams(vmem_limit_bytes=VMEM_BYTES * 3 // 2),
         cost_estimate=cost(6 * 10**9, 20 * 10**6),
@@ -239,8 +237,8 @@
 
 
 def backward_kernel(
-    back_ref, loss_ref, sent_ref, m_ref, o_ref, g_ref, inv_ref, cos_ref, sin_ref,
-    inner_ref, out_give_ref, out_keep_ref, x_ref, base_ref, unit_ref,
+    back_ref, loss_ref, sent_ref, m_ref, o_ref, inv_ref, cos_ref, sin_ref,
+    inner_ref, out_give_ref, out_keep_ref, x_ref,
     q, k, v1, gh, ghs, scores, low, mixed, gp, ds, dq, heads, grads, inner, out_inner,
 ):
     length, rank = back_ref.shape
@@ -293,11 +291,9 @@
     out_keep_ref[...] = out_inner[mine, :]
     out_give_ref[...] = out_inner[theirs, :]
     x_ref[...] = nt(grads[...], m_ref[:rank, :]).astype(BF)
-    base_ref[...] = nn(jnp.concatenate([up] * 3, axis=1), g_ref[...])
-    unit_ref[...] = nn(jnp.concatenate([back] * 3, axis=1), g_ref[...]) * inv[:, :1]
-
-
-def backward(back, loss, sent, m2, o2, g3, inv, cosine, sine):
+
+
+def backward(back, loss, sent, m2, o2, inv, cosine, sine):
     length, rank = back.shape
     ne = o2.shape[0]
     total = m2.shape[1]
@@ -305,15 +301,13 @@
     stack = ne // HD * length
     return pl.pallas_call(
         backward_kernel,
-        in_specs=vmem(9),
-        out_specs=vmem(6),
+        in_specs=vmem(8),
+        out_specs=vmem(4),
         out_shape=[
             jax.ShapeDtypeStruct((rank, total), BF),
             jax.ShapeDtypeStruct((rank // 2, ne), BF),
             jax.ShapeDtypeStruct((rank // 2, ne), BF),
             jax.ShapeDtypeStruct((length, rank), BF),
-            jax.ShapeDtypeStruct((length, rank), F32),
-            jax.ShapeDtypeStruct((length, rank), F32),
         ],
         scratch_shapes=[
             pltpu.VMEM((stack, HD), BF),
@@ -335,22 +329,51 @@
         compiler_params=pltpu.CompilerParams(vmem_limit_bytes=VMEM_BYTES),
         cost_estimate=cost(10**4, 10**3),
         name="attention_backward",
-    )(back, loss, sent, m2, o2, g3, inv, cosine, sine)
+    )(back, loss, sent, m2, o2, inv, cosine, sine)
+
+
+def bases_kernel(
+    back_ref, loss_ref, returned_ref, new_ref, arrived_ref, u_ref, turned_ref, inv_ref, after,
+    base_ref, unit_ref, fbase_ref, g_ref,
+):
+    rank = u_ref.shape[1]
+    for i, piece in enumerate(split(nn(turned_ref[...], u_ref[...]), 3)):
+        g_ref[i * rank : (i + 1) * rank, :] = piece
+    is_last = lax.axis_index("pipe") == lax.axis_size("pipe") - 1
+    is_first = lax.axis_index("pipe") == 0
+    up = jnp.where(is_last, loss_ref[...], returned_ref[...])
+    coeffs = jnp.where(is_first, new_ref[...], arrived_ref[...])
+    base_ref[...] = nn(jnp.concatenate([up] * 3, axis=1), g_ref[...])
+    fbase_ref[...] = nn(jnp.concatenate([coeffs] * 3, axis=1), g_ref[...])
+    unit_ref[...] = nn(jnp.concatenate([back_ref[...]] * 3, axis=1), g_ref[...]) * inv_ref[:, :1]
+
+
+def bases(back, loss, returned, new, arrived, basis, turned, inv, after):
+    length, rank = back.shape
+    return pl.pallas_call(
+        bases_kernel,
+        in_specs=vmem(8) + [pl.BlockSpec(memory_space=pl.ANY)],
+        out_specs=vmem(3),
+        out_shape=[jax.ShapeDtypeStruct((length, rank), F32)] * 3,
+        scratch_shapes=[pltpu.VMEM((3 * rank, rank), BF)],
+        compiler_params=pltpu.CompilerParams(vmem_limit_bytes=VMEM_BYTES // 2),
+        cost_estimate=cost(10**4, 10**3),
+        name="encoded_again",
+    )(back, loss, returned, new, arrived, basis, turned, inv, after)
 
 
 def forward_kernel(
-    new_ref, sent_ref, u_ref, m_ref, o_ref, g_ref, cos_ref, sin_ref, *rest,
+    new_ref, sent_ref, turned_ref, m_ref, o_ref, cos_ref, sin_ref, after,
+    y_ref, q, k, v1, scores, low, mixed, heads,
 ):
-    y_ref, base_ref, q, k, v1, scores, low, mixed, heads = rest[-9:]
     length, rank = new_ref.shape
-    wide = u_ref.shape[0]
+    wide = turned_ref.shape[1]
     is_first = lax.axis_index("pipe") == 0
     coeffs = jnp.where(is_first, new_ref[...], sent_ref[...])
     square = jnp.zeros((length, HD), F32)
-    block = 512
-    for at in range(0, wide, block):
-        decoded = nt(coeffs, u_ref[at : at + block, :])
-        for side in range(0, block, HD):
+    for at in range(0, wide, PIECE):
+        decoded = nn(coeffs, turned_ref[:, at : at + PIECE])
+        for side in range(0, PIECE, HD):
             part = decoded[:, side : side + HD]
             square = square + part * part
     inv = inverse_root(jnp.sum(square, axis=1, keepdims=True), wide)
@@ -362,21 +385,17 @@
         at = slice(h * length, (h + 1) * length)
         heads[:, h * HD : (h + 1) * HD] = (mixed[at, :HD] / mixed[at, HD:]).astype(BF)
     y_ref[...] = nn(heads[...], o_ref[...]).astype(BF)
-    base_ref[...] = nn(jnp.concatenate([coeffs] * 3, axis=1), g_ref[...])
-
-
-def forward(new, sent, basis, m2, o2, g3, cosine, sine, *after):
+
+
+def forward(new, sent, turned, m2, o2, cosine, sine, after):
     length, rank = new.shape
     ne = o2.shape[0]
     stack = ne // HD * length
     return pl.pallas_call(
         forward_kernel,
-        in_specs=vmem(8) + [pl.BlockSpec(memory_space=pl.ANY)] * len(after),
-        out_specs=vmem(2),
-        out_shape=[
-            jax.ShapeDtypeStruct((length, rank), BF),
-            jax.ShapeDtypeStruct((length, rank), F32),
-        ],
+        in_specs=vmem(7) + [pl.BlockSpec(memory_space=pl.ANY)],
+        out_specs=pl.BlockSpec(memory_space=pltpu.VMEM),
+        out_shape=jax.ShapeDtypeStruct((length, rank), BF),
         scratch_shapes=[
             pltpu.VMEM((stack, HD), BF),
             pltpu.VMEM((length, HD), BF),
@@ -389,7 +408,7 @@
         compiler_params=pltpu.CompilerParams(vmem_limit_bytes=VMEM_BYTES),
         cost_estimate=cost(10**4, 10**3),
         name="attention_forward",
-    )(new, sent, basis, m2, o2, g3, cosine, sine, *after)
+    )(new, sent, turned, m2, o2, cosine, sine, after)
 
 
 def write_split(ref, value):
@@ -535,10 +554,13 @@
     v_ref[...] = grad[:, nq + nk :].astype(BF)
 
 
-def outward_kernel(u_ref, own_ref, other_ref, after, o_ref, inner):
+def outward_kernel(pieces, u_ref, *refs):
+    own_refs, other_refs = refs[:pieces], refs[pieces : 2 * pieces]
+    o_ref, inner = refs[-2:]
+
     @pl.when(pl.program_id(0) == 0)
     def _():
-        gather_halves([own_ref], [other_ref], inner)
+        gather_halves(own_refs, other_refs, inner)
 
     block, rows = o_ref.shape
     at = pl.multiple_of(pl.program_id(0) * block, block)
@@ -569,18 +591,18 @@
 def outward_grad(basis, own, other, after):
     wide, rank = basis.shape
     rows = wide // lax.axis_size("dp")
-    ne = own.shape[1]
-    return pl.pallas_call(
-        outward_kernel,
+    ne = sum(piece.shape[1] for piece in own)
+    return pl.pallas_call(
+        functools.partial(outward_kernel, len(own)),
         grid=(STEPS,),
-        in_specs=vmem(3) + [pl.BlockSpec(memory_space=pl.ANY)],
+        in_specs=vmem(1 + 2 * len(own)) + [pl.BlockSpec(memory_space=pl.ANY)],
         out_specs=pl.BlockSpec((ne // STEPS, rows), lambda i: (i, 0)),
         scratch_shapes=[pltpu.VMEM((rank, ne), BF)],
         out_shape=jax.ShapeDtypeStruct((ne, rows), BF),
         compiler_params=pltpu.CompilerParams(vmem_limit_bytes=VMEM_BYTES),
         cost_estimate=cost(10**4, 10**3),
         name="output_weight_gradient",
-    )(basis, own, other, after)
+    )(basis, *own, *other, after)
 
 
 def results_kernel(
@@ -639,23 +661,30 @@
     arrived, returned = cross_pipe(sent_forward[0], sent_backward[0])
     cosine, sine = rope_tables(back.shape[0])
 
-    m2, o2, g3, inv, basis, wq, narrow = project(back, norm_gain, subspace, wq, wk, wv, wo)
-    inner, out_give, out_keep, x, base, unit = backward(
-        back, loss_grad, returned, m2, o2, g3, inv, cosine, sine
+    m2, o2, inv, basis, wq, narrow, turned = project(
+        back, norm_gain, subspace, wq, wk, wv, wo
+    )
+    inner, out_give, out_keep, x = backward(
+        back, loss_grad, returned, m2, o2, inv, cosine, sine
     )
     out_got = swap(out_give, "dp", 1)
     inner_got = swap(inner, "dp", 1)
-    out_pair = add_wide(out_keep, out_got).astype(BF)
+    base, unit, fbase = bases(
+        back, loss_grad, returned, new_coeffs, arrived, basis, turned, inv, out_keep
+    )
+    out_pair = add_after(out_keep, out_got, fbase)
     out_got = swap(out_pair, "dp", 2)
     pair, x = gain_part(basis, wq, narrow, inner, inner_got, x, out_pair)
     pair_got = swap(pair, "dp", 2)
+    x_got = swap(x, "tensor", 2)
+    y = forward(new_coeffs, arrived, turned, m2, o2, cosine, sine, pair)
+    y_got = swap(y, "tensor", 1)
+    ne = wo.shape[0]
+    out_own = own_pieces(out_pair, out_got, (ne // 2, ne - ne // 2), y)
+    x = merge(x, x_got, out_own[0])
     x_got = swap(x, "tensor", 1)
-    y, fbase = forward(new_coeffs, arrived, basis, m2, o2, g3, cosine, sine, pair)
-    y_got = swap(y, "tensor", 1)
-    x = merge(x, x_got, y)
-    x_got = swap(x, "tensor", 2)
-    out_own = add_after(out_pair, out_got, x)
-    grad_o = outward_grad(basis, out_own, swap(out_own, "dp", 1), x)
+    out_other = [swap(piece, "dp", 1) for piece in out_own]
+    grad_o = outward_grad(basis, out_own, out_other, x)
     y = add_after(y, y_got, *in_hbm((grad_o,)))
     y_got = swap(y, "tensor", 2)
     own = own_pieces(pair, pair_got, (nq // 2, nq - nq // 2, nk + nv), y)

time: 52.6 us -> 51.8 us (0.985)
  waiting for transfers between devices: 9.25 us -> 5.42 us
  starting transfers between devices: 13.7 us -> 15.5 us
  Pallas kernels: 27.7 us -> 29 us
    ppermute x15 -> x16, waiting for transfers between devices: 9.25 us -> 5.42 us  [swap(): return lax.ppermute(x, axis, [(i, i ^ bit) for i in range(devices)])]
    ppermute x15 -> x16, starting transfers between devices: 13.7 us -> 15.5 us  [swap(): return lax.ppermute(x, axis, [(i, i ^ bit) for i in range(devices)])]
    pallas_call x3 -> x4, Pallas kernels: 11.2 us -> 12.7 us  [the longest x1 5.19 us: backward(): pl.pallas_call(backward_kernel, in_specs=vmem(8), out_specs=vmem(4), out_...]
  transfers between devices with their start and end apart: 15 -> 16, of which waited for: 4 -> 4; matrix products, arithmetic and copies ran while one was open for 0% -> 0% of each run, Pallas kernels for 40% -> 44%
where the time goes in v5:
time: 51.8 us; the launch traced here: 51.7 us
  Pallas kernels  29 us (56%)
  starting transfers between devices  15.5 us (30%)
  waiting for transfers between devices  5.42 us (10%)
  other arithmetic  0.93 us (2%)
  between operations  0.81 us (2%)
    ppermute x16, starting transfers between devices, swap(): return lax.ppermute(x, axis, [(i, i ^ bit) for i in range(devices)])  15.5 us
    pallas_call x1, Pallas kernels, project(): pl.pallas_call(project_kernel, in_specs=[pl.BlockSpec(memory_space=pltpu....  10.9 us
    ppermute x16, waiting for transfers between devices, swap(): return lax.ppermute(x, axis, [(i, i ^ bit) for i in range(devices)])  5.42 us
    pallas_call x1, Pallas kernels, backward(): pl.pallas_call(backward_kernel, in_specs=vmem(8), out_specs=vmem(4), out_...  5.19 us
    pallas_call x1, Pallas kernels, forward(): pl.pallas_call(forward_kernel, in_specs=vmem(7) + [pl.BlockSpec(memory_sp...  3.75 us
    pallas_call x1, Pallas kernels, inward_grads(): pl.pallas_call(functools.partial(inward_kernel, len(own)), grid=(STEPS,),...  2.21 us
    pallas_call x1, Pallas kernels, outward_grad(): pl.pallas_call(functools.partial(outward_kernel, len(own)), grid=(STEPS,)...  2.01 us
    pallas_call x1, Pallas kernels, gain_part(): pl.pallas_call(gain_kernel, in_specs=vmem(6) + [pl.BlockSpec(memory_space...  1.85 us
  transfers between devices with their start and end apart: 16, of which 4 were waited for; matrix products, arithmetic and copies ran while one was open for 0% of the time, Pallas kernels for 44%

profile of v5, /device:TPU:0, one launch (start us, length us, event | category | flops | bytes accessed | tf_op | source)
XLA Modules:
  0.0 51.7 jit_solution(11234236333014385695)
XLA Ops:
  0.6 0.9 %select_bitcast_fusion = bf16[256,256]{1,0:T(8,128)(2,1)S(1)} fusion(bf16[1,256,256]{2,1,0:T(8,128)(2,1)} %param.15, bf16[1,256,256]{2,1,0:T(8,128)(2,1)} %param.16, pred[]{:T(512)S(6)} %eq.3), kind=kLoop, calls=%fused_computation | loop fusion | flops 65536 | bytes 393217 | tf_op jit(solution)/shard_map/jit(_where)/select_n | solution.py:39
  1.6 3.0 %collective-permute-start = (bf16[256,256]{1,0:T(8,128)(2,1)S(1)}, bf16[256,256]{1,0:T(8,128)(2,1)S(1)}, u32[]{:S(2)}, u32[]{:S(2)}) collective-permute-start(bf16[256,256]{1,0:T(8,128)(2,1)S(1)} %select_bitcast_fusion), channel_id=1, source_target_pairs={{0,16},{16,0},{1,17},{17,1},{2,18},{18,2},{3,19},{19,3},{4,20},{20... | collective-permute-start | bytes 393224 | tf_op jit(solution)/shard_map/ppermute | solution.py:32
  4.6 10.9 %project_weights.1 = (bf16[512,1280]{1,0:T(8,128)(2,1)S(1)}, bf16[1024,256]{1,0:T(8,128)(2,1)S(1)}, f32[256,128]{1,0:T(8,128)S(1)}, bf16[4096,256]{1,0:T(8,128)(...) custom-call(bf16[256,256]{1,0:T(8,128)(2,1)} %bitcast.13, ...), custom_call_target="tpu_custom_call" | custom-call | flops 6000000000 | bytes 20000000 | tf_op jit(solution)/shard_map/project_weights/pallas_call | solution.py:180
  15.6 5.2 %attention_backward.1 = (bf16[256,1280]{1,0:T(8,128)(2,1)S(1)}, bf16[128,1024]{1,0:T(8,128)(2,1)S(1)}, bf16[128,1024]{1,0:T(8,128)(2,1)S(1)}, bf16[256,256]{1,0:T(8,128)(2,1)S(1)}) custom-call(bf16[256,256]{1,0:T(8,128)(2,1)S(1)} %bitcast.14, bf16[256,256]{1,0:T(8,128)(2,1)S(1)} %copy-done.1, ...), custom_call_target="tpu_custom_call" | custom-call | flops 10000 | bytes 1000 | tf_op jit(solution)/shard_map/attention_backward/pallas_call | solution.py:302
  20.9 0.5 collective-permute-start.2
  21.4 1.7 %encoded_again.1 = (f32[256,256]{1,0:T(8,128)S(1)}, f32[256,256]{1,0:T(8,128)S(1)}, f32[256,256]{1,0:T(8,128)S(1)}) custom-call(bf16[256,256]{1,0:T(8,128)(2,1)S(1)} %bitcast.15, bf16[256,256]{1,0:T(8,128)(2,1)S(1)} %copy-done.1, bf16[256,256]{1,0:T(8,128)(2,1)S(1)} %collective-permute-done.sent_ref.returned_ref.arrived_ref, bf16[256,256]{1,0:T(8,128)(2,1)S(1)} %copy-done.2, ...), custom_call_target="tpu_custom_call" | custom-call | flops 10000 | bytes 1000 | tf_op jit(solution)/shard_map/encoded_again/pallas_call | solution.py:353
  23.4 1.6 %collective-permute-start.4 = (bf16[128,1024]{1,0:T(8,128)(2,1)S(1)}, bf16[128,1024]{1,0:T(8,128)(2,1)S(1)}, u32[]{:S(2)}, u32[]{:S(2)}) collective-permute-start(bf16[128,1024]{1,0:T(8,128)(2,1)S(1)} %pair_sum.3.after.a_ref), channel_id=1, source_target_pairs={{0,2},{1,3},{2,0},{3,1},{4,6},{5,7},{6,4},{7,5},{8,10},{9,11},{10,... | collective-permute-start | bytes 786440 | tf_op jit(solution)/shard_map/ppermute | solution.py:32
  25.0 1.8 %pair_sum_and_gain_gradient.1 = (bf16[128,1280]{1,0:T(8,128)(2,1)S(1)}, bf16[272,256]{1,0:T(8,128)(2,1)S(1)}) custom-call(bf16[4096,256]{1,0:T(8,128)(2,1)S(1)} %get-tuple-element.34.u_ref, bf16[4096,1024]{1,0:T(8,128)(2,1)S(1)} %get-tuple-element.41.wq_ref, bf16[4096,256]{1,0:T(8,128)(2,1)S(1)} %get-tuple-element.42.narrow_ref, ...), custom_call_target="tpu_custom_call" | custom-call | flops 10000 | bytes 1000 | tf_op jit(solution)/shard_map/pair_sum_and_gain_gradient/pallas_call | solution.py:457
  26.8 0.6 %collective-permute-start.10 = (bf16[128,1280]{1,0:T(8,128)(2,1)S(1)}, bf16[128,1280]{1,0:T(8,128)(2,1)S(1)}, u32[]{:S(2)}, u32[]{:S(2)}) collective-permute-start(bf16[128,1280]{1,0:T(8,128)(2,1)S(1)} %get-tuple-element.46.after.a_ref), channel_id=1, source_target_pairs={{0,2},{1,3},{2,0},{3,1},{4,6},{5,7},{6,4},{7,5},{8,10},{9,11},{10,... | collective-permute-start | bytes 983048 | tf_op jit(solution)/shard_map/ppermute | solution.py:32
  27.4 2.6 %collective-permute-start.7 = (bf16[272,256]{1,0:T(8,128)(2,1)S(1)}, bf16[272,256]{1,0:T(8,128)(2,1)S(1)}, u32[]{:S(2)}, u32[]{:S(2)}) collective-permute-start(bf16[272,256]{1,0:T(8,128)(2,1)S(1)} %get-tuple-element.49.a_ref), channel_id=1, source_target_pairs={{0,8},{4,12},{8,0},{12,4},{1,9},{5,13},{9,1},{13,5},{2,10},{6,14},... | collective-permute-start | bytes 417800 | tf_op jit(solution)/shard_map/ppermute | solution.py:32
  30.0 3.8 %attention_forward.1.after.a_ref = bf16[256,256]{1,0:T(8,128)(2,1)S(1)} custom-call(bf16[256,256]{1,0:T(8,128)(2,1)S(1)} %copy-done.2, bf16[256,256]{1,0:T(8,128)(2,1)S(1)} %collective-permute-done.sent_ref.returned_ref.arrived_ref, bf16[256,4096]{1,0:T(8,128)(2,1)S(1)} %get-tuple-element.35.turned_ref, bf16[512,1280]{1,0:T(8,128)(2,1)S(1)} %get-tuple-element.37.m_ref, ...), custom_call_target="tpu_custom_call" | custom-call | flops 10000 | bytes 1000 | tf_op jit(solution)/shard_map/attention_forward/pallas_call | solution.py:394
  33.9 0.5 collective-permute-start.6
  34.4 1.6 %collective-permute-start.3 = (bf16[256,256]{1,0:T(8,128)(2,1)S(1)}, bf16[256,256]{1,0:T(8,128)(2,1)S(1)}, u32[]{:S(2)}, u32[]{:S(2)}) collective-permute-start(bf16[256,256]{1,0:T(8,128)(2,1)S(1)} %attention_forward.1.after.a_ref), channel_id=1, source_target_pairs={{0,4},{4,0},{8,12},{12,8},{1,5},{5,1},{9,13},{13,9},{2,6},{6,2},{1... | collective-permute-start | bytes 393224 | tf_op jit(solution)/shard_map/ppermute | solution.py:32
  36.0 0.5 collective-permute-done.7.b_ref
  36.5 0.7 %collective-permute-start.9 = (bf16[272,256]{1,0:T(8,128)(2,1)S(1)}, bf16[272,256]{1,0:T(8,128)(2,1)S(1)}, u32[]{:S(2)}, u32[]{:S(2)}) collective-permute-start(bf16[272,256]{1,0:T(8,128)(2,1)S(1)} %sum_with_gain.1.refs_4_.a_ref.x_ref), channel_id=1, source_target_pairs={{0,4},{4,0},{8,12},{12,8},{1,5},{5,1},{9,13},{13,9},{2,6},{6,2},{1... | collective-permute-start | bytes 417800 | tf_op jit(solution)/shard_map/ppermute | solution.py:32
  37.2 2.0 %output_weight_gradient.1.after = bf16[1024,1024]{1,0:T(8,128)(2,1)} custom-call(bf16[4096,256]{1,0:T(8,128)(2,1)S(1)} %get-tuple-element.34.u_ref, bf16[128,512]{1,0:T(8,128)(2,1)S(1)} %get-tuple-element.47.after.refs_0_, bf16[128,512]{1,0:T(8,128)(2,1)S(1)} %get-tuple-element.48.refs_1_, bf16[128,512]{1,0:T(8,128)(2,1)S(1)} %collective-permute-done.5.refs_2_, ...), custom_call_target="tpu_custom_call" | custom-call | flops 10000 | bytes 1000 | tf_op jit(solution)/shard_map/output_weight_gradient/pallas_call | solution.py:595
  39.2 1.5 %collective-permute-done.3.b_ref = bf16[256,256]{1,0:T(8,128)(2,1)S(1)} collective-permute-done((bf16[256,256]{1,0:T(8,128)(2,1)S(1)}, bf16[256,256]{1,0:T(8,128)(2,1)S(1)}, u32[]{:S(2)}, u32[]{:S(2)}) %collective-permute-start.3) | collective-permute-done | bytes 131104 | tf_op jit(solution)/shard_map/ppermute | solution.py:32
  41.0 0.5 collective-permute-start.13
  41.5 1.9 %collective-permute-start.8 = (bf16[256,256]{1,0:T(8,128)(2,1)S(1)}, bf16[256,256]{1,0:T(8,128)(2,1)S(1)}, u32[]{:S(2)}, u32[]{:S(2)}) collective-permute-start(bf16[256,256]{1,0:T(8,128)(2,1)S(1)} %pair_sum.4.after.y_ref), channel_id=1, source_target_pairs={{0,8},{4,12},{8,0},{12,4},{1,9},{5,13},{9,1},{13,5},{2,10},{6,14},... | collective-permute-start | bytes 393224 | tf_op jit(solution)/shard_map/ppermute | solution.py:32
  43.4 1.6 %collective-permute-start.11 = (f32[8,256]{1,0:T(8,128)S(1)}, f32[8,256]{1,0:T(8,128)S(1)}, u32[]{:S(2)}, u32[]{:S(2)}) collective-permute-start(f32[8,256]{1,0:T(8,128)S(1)} %gain_total.1.refs_6_.a_ref), channel_id=1, source_target_pairs={{0,2},{1,3},{2,0},{3,1},{4,6},{5,7},{6,4},{7,5},{8,10},{9,11},{10,... | collective-permute-start | bytes 24584 | tf_op jit(solution)/shard_map/ppermute | solution.py:32
  45.0 2.2 %inward_weight_gradients.1 = (bf16[1024,1024]{1,0:T(8,128)(2,1)}, bf16[1024,128]{1,0:T(8,128)(2,1)}, bf16[1024,128]{1,0:T(8,128)(2,1)}) custom-call(bf16[4096,256]{1,0:T(8,128)(2,1)S(1)} %get-tuple-element.34.u_ref, f32[1,4096]{1,0:T(1,128)S(1)} %copy-done.5, bf16[128,512]{1,0:T(8,128)(2,1)S(1)} %get-tuple-element.52.after.refs_0_, ...), custom_call_target="tpu_custom_call" | custom-call | flops 10000 | bytes 1000 | tf_op jit(solution)/shard_map/inward_weight_gradients/pallas_call | solution.py:578
  47.2 0.3 collective-permute-start.15
  47.5 3.2 %collective-permute-done.8.ygot_ref = bf16[256,256]{1,0:T(8,128)(2,1)S(1)} collective-permute-done((bf16[256,256]{1,0:T(8,128)(2,1)S(1)}, bf16[256,256]{1,0:T(8,128)(2,1)S(1)}, u32[]{:S(2)}, u32[]{:S(2)}) %collective-permute-start.8) | collective-permute-done | bytes 131104 | tf_op jit(solution)/shard_map/ppermute | solution.py:32
  50.6 1.0 %section_results.1 = (bf16[256,256]{1,0:T(8,128)(2,1)}, bf16[256,256]{1,0:T(8,128)(2,1)}, f32[1,4096]{1,0:T(1,128)}) custom-call(f32[256,256]{1,0:T(8,128)S(1)} %get-tuple-element.40.after.fbase_ref, bf16[256,256]{1,0:T(8,128)(2,1)S(1)} %pair_sum.4.after.y_ref, bf16[256,256]{1,0:T(8,128)(2,1)S(1)} %collective-permute-done.8.ygot_ref, ...), custom_call_target="tpu_custom_call" | custom-call | flops 10000 | bytes 1000 | tf_op jit(solution)/shard_map/section_results/pallas_call | solution.py:633
  (36 shorter events, 0.8 us)
Async XLA Ops:
  1.6 14.0 %collective-permute-start = (bf16[256,256]{1,0:T(8,128)(2,1)S(1)}, bf16[256,256]{1,0:T(8,128)(2,1)S(1)}, u32[]{:S(2)}, u32[]{:S(2)}) collective-permute-start(bf16[256,256]{1,0:T(8,128)(2,1)S(1)} %select_bitcast_fusion), channel_id=1, source_target_pairs={{0,16},{16,0},{1,17},{17,1},{2,18},{18,2},{3,19},{19,3},{4,20},{20... | collective-permute-start | bytes 393224 | tf_op jit(solution)/shard_map/ppermute | solution.py:32
  4.6 11.0 %copy-start = (bf16[1,256,256]{2,1,0:T(8,128)(2,1)S(1)}, bf16[1,256,256]{2,1,0:T(8,128)(2,1)}, u32[]{:S(2)}) copy-start(bf16[1,256,256]{2,1,0:T(8,128)(2,1)} %param.17) | copy-start | bytes 393220
  4.6 11.0 %copy-start.1 = (bf16[256,256]{1,0:T(8,128)(2,1)S(1)}, bf16[256,256]{1,0:T(8,128)(2,1)}, u32[]{:S(2)}) copy-start(bf16[256,256]{1,0:T(8,128)(2,1)} %loss_ref.3) | copy-start | bytes 393220
  4.6 11.0 %copy-start.3 = (f32[256,128]{1,0:T(8,128)S(1)}, f32[256,128]{1,0:T(8,128)}, u32[]{:S(2)}) copy-start(f32[256,128]{1,0:T(8,128)} %constant.12.clone.cos_ref) | copy-start | bytes 393220
  4.6 11.0 %copy-start.4 = (f32[256,128]{1,0:T(8,128)S(1)}, f32[256,128]{1,0:T(8,128)}, u32[]{:S(2)}) copy-start(f32[256,128]{1,0:T(8,128)} %constant.13.clone.sin_ref) | copy-start | bytes 393220
  15.5 5.8 %copy-start.2 = (bf16[256,256]{1,0:T(8,128)(2,1)S(1)}, bf16[256,256]{1,0:T(8,128)(2,1)}, u32[]{:S(2)}) copy-start(bf16[256,256]{1,0:T(8,128)(2,1)} %new_ref.3) | copy-start | bytes 393220
  20.8 4.2 %collective-permute-start.1 = (bf16[256,1280]{1,0:T(8,128)(2,1)S(1)}, bf16[256,1280]{1,0:T(8,128)(2,1)S(1)}, u32[]{:S(2)}, u32[]{:S(2)}) collective-permute-start(bf16[256,1280]{1,0:T(8,128)(2,1)S(1)} %get-tuple-element.43.inner_ref), channel_id=1, source_target_pairs={{0,1},{1,0},{2,3},{3,2},{4,5},{5,4},{6,7},{7,6},{8,9},{9,8},{10,11... | collective-permute-start | bytes 1966088 | tf_op jit(solution)/shard_map/ppermute | solution.py:32
  20.9 2.5 %collective-permute-start.2 = (bf16[128,1024]{1,0:T(8,128)(2,1)S(1)}, bf16[128,1024]{1,0:T(8,128)(2,1)S(1)}, u32[]{:S(2)}, u32[]{:S(2)}) collective-permute-start(bf16[128,1024]{1,0:T(8,128)(2,1)S(1)} %get-tuple-element.45), channel_id=1, source_target_pairs={{0,1},{1,0},{2,3},{3,2},{4,5},{5,4},{6,7},{7,6},{8,9},{9,8},{10,11... | collective-permute-start | bytes 786440 | tf_op jit(solution)/shard_map/ppermute | solution.py:32
  23.4 10.4 %collective-permute-start.4 = (bf16[128,1024]{1,0:T(8,128)(2,1)S(1)}, bf16[128,1024]{1,0:T(8,128)(2,1)S(1)}, u32[]{:S(2)}, u32[]{:S(2)}) collective-permute-start(bf16[128,1024]{1,0:T(8,128)(2,1)S(1)} %pair_sum.3.after.a_ref), channel_id=1, source_target_pairs={{0,2},{1,3},{2,0},{3,1},{4,6},{5,7},{6,4},{7,5},{8,10},{9,11},{10,... | collective-permute-start | bytes 786440 | tf_op jit(solution)/shard_map/ppermute | solution.py:32
  26.8 14.0 %collective-permute-start.10 = (bf16[128,1280]{1,0:T(8,128)(2,1)S(1)}, bf16[128,1280]{1,0:T(8,128)(2,1)S(1)}, u32[]{:S(2)}, u32[]{:S(2)}) collective-permute-start(bf16[128,1280]{1,0:T(8,128)(2,1)S(1)} %get-tuple-element.46.after.a_ref), channel_id=1, source_target_pairs={{0,2},{1,3},{2,0},{3,1},{4,6},{5,7},{6,4},{7,5},{8,10},{9,11},{10,... | collective-permute-start | bytes 983048 | tf_op jit(solution)/shard_map/ppermute | solution.py:32
  27.4 9.0 %collective-permute-start.7 = (bf16[272,256]{1,0:T(8,128)(2,1)S(1)}, bf16[272,256]{1,0:T(8,128)(2,1)S(1)}, u32[]{:S(2)}, u32[]{:S(2)}) collective-permute-start(bf16[272,256]{1,0:T(8,128)(2,1)S(1)} %get-tuple-element.49.a_ref), channel_id=1, source_target_pairs={{0,8},{4,12},{8,0},{12,4},{1,9},{5,13},{9,1},{13,5},{2,10},{6,14},... | collective-permute-start | bytes 417800 | tf_op jit(solution)/shard_map/ppermute | solution.py:32
  33.8 3.4 %collective-permute-start.5 = (bf16[128,512]{1,0:T(8,128)(2,1)S(1)}, bf16[128,512]{1,0:T(8,128)(2,1)S(1)}, u32[]{:S(2)}, u32[]{:S(2)}) collective-permute-start(bf16[128,512]{1,0:T(8,128)(2,1)S(1)} %get-tuple-element.47.after.refs_0_), channel_id=1, source_target_pairs={{0,1},{1,0},{2,3},{3,2},{4,5},{5,4},{6,7},{7,6},{8,9},{9,8},{10,11... | collective-permute-start | bytes 393224 | tf_op jit(solution)/shard_map/ppermute | solution.py:32
  33.9 3.3 %collective-permute-start.6 = (bf16[128,512]{1,0:T(8,128)(2,1)S(1)}, bf16[128,512]{1,0:T(8,128)(2,1)S(1)}, u32[]{:S(2)}, u32[]{:S(2)}) collective-permute-start(bf16[128,512]{1,0:T(8,128)(2,1)S(1)} %get-tuple-element.48.refs_1_), channel_id=1, source_target_pairs={{0,1},{1,0},{2,3},{3,2},{4,5},{5,4},{6,7},{7,6},{8,9},{9,8},{10,11... | collective-permute-start | bytes 393224 | tf_op jit(solution)/shard_map/ppermute | solution.py:32
  34.4 6.4 %collective-permute-start.3 = (bf16[256,256]{1,0:T(8,128)(2,1)S(1)}, bf16[256,256]{1,0:T(8,128)(2,1)S(1)}, u32[]{:S(2)}, u32[]{:S(2)}) collective-permute-start(bf16[256,256]{1,0:T(8,128)(2,1)S(1)} %attention_forward.1.after.a_ref), channel_id=1, source_target_pairs={{0,4},{4,0},{8,12},{12,8},{1,5},{5,1},{9,13},{13,9},{2,6},{6,2},{1... | collective-permute-start | bytes 393224 | tf_op jit(solution)/shard_map/ppermute | solution.py:32
  36.5 6.9 %collective-permute-start.9 = (bf16[272,256]{1,0:T(8,128)(2,1)S(1)}, bf16[272,256]{1,0:T(8,128)(2,1)S(1)}, u32[]{:S(2)}, u32[]{:S(2)}) collective-permute-start(bf16[272,256]{1,0:T(8,128)(2,1)S(1)} %sum_with_gain.1.refs_4_.a_ref.x_ref), channel_id=1, source_target_pairs={{0,4},{4,0},{8,12},{12,8},{1,5},{5,1},{9,13},{13,9},{2,6},{6,2},{1... | collective-permute-start | bytes 417800 | tf_op jit(solution)/shard_map/ppermute | solution.py:32
  39.2 5.8 %copy-start.5 = (f32[1,4096]{1,0:T(1,128)S(1)}, f32[1,4096]{1,0:T(1,128)}, u32[]{:S(2)}) copy-start(f32[1,4096]{1,0:T(1,128)} %gain_ref.1) | copy-start | bytes 49156
  40.9 4.1 %collective-permute-start.12 = (bf16[128,512]{1,0:T(8,128)(2,1)S(1)}, bf16[128,512]{1,0:T(8,128)(2,1)S(1)}, u32[]{:S(2)}, u32[]{:S(2)}) collective-permute-start(bf16[128,512]{1,0:T(8,128)(2,1)S(1)} %get-tuple-element.52.after.refs_0_), channel_id=1, source_target_pairs={{0,1},{1,0},{2,3},{3,2},{4,5},{5,4},{6,7},{7,6},{8,9},{9,8},{10,11... | collective-permute-start | bytes 393224 | tf_op jit(solution)/shard_map/ppermute | solution.py:32
  41.0 4.0 %collective-permute-start.13 = (bf16[128,512]{1,0:T(8,128)(2,1)S(1)}, bf16[128,512]{1,0:T(8,128)(2,1)S(1)}, u32[]{:S(2)}, u32[]{:S(2)}) collective-permute-start(bf16[128,512]{1,0:T(8,128)(2,1)S(1)} %get-tuple-element.53.refs_1_), channel_id=1, source_target_pairs={{0,1},{1,0},{2,3},{3,2},{4,5},{5,4},{6,7},{7,6},{8,9},{9,8},{10,11... | collective-permute-start | bytes 393224 | tf_op jit(solution)/shard_map/ppermute | solution.py:32
  41.5 9.2 %collective-permute-start.8 = (bf16[256,256]{1,0:T(8,128)(2,1)S(1)}, bf16[256,256]{1,0:T(8,128)(2,1)S(1)}, u32[]{:S(2)}, u32[]{:S(2)}) collective-permute-start(bf16[256,256]{1,0:T(8,128)(2,1)S(1)} %pair_sum.4.after.y_ref), channel_id=1, source_target_pairs={{0,8},{4,12},{8,0},{12,4},{1,9},{5,13},{9,1},{13,5},{2,10},{6,14},... | collective-permute-start | bytes 393224 | tf_op jit(solution)/shard_map/ppermute | solution.py:32
  43.3 1.6 %collective-permute-start.14 = (bf16[128,256]{1,0:T(8,128)(2,1)S(1)}, bf16[128,256]{1,0:T(8,128)(2,1)S(1)}, u32[]{:S(2)}, u32[]{:S(2)}) collective-permute-start(bf16[128,256]{1,0:T(8,128)(2,1)S(1)} %get-tuple-element.54.refs_2_), channel_id=1, source_target_pairs={{0,1},{1,0},{2,3},{3,2},{4,5},{5,4},{6,7},{7,6},{8,9},{9,8},{10,11... | collective-permute-start | bytes 196616 | tf_op jit(solution)/shard_map/ppermute | solution.py:32
  43.4 3.8 %collective-permute-start.11 = (f32[8,256]{1,0:T(8,128)S(1)}, f32[8,256]{1,0:T(8,128)S(1)}, u32[]{:S(2)}, u32[]{:S(2)}) collective-permute-start(f32[8,256]{1,0:T(8,128)S(1)} %gain_total.1.refs_6_.a_ref), channel_id=1, source_target_pairs={{0,2},{1,3},{2,0},{3,1},{4,6},{5,7},{6,4},{7,5},{8,10},{9,11},{10,... | collective-permute-start | bytes 24584 | tf_op jit(solution)/shard_map/ppermute | solution.py:32
  47.2 3.5 %collective-permute-start.15 = (f32[8,256]{1,0:T(8,128)S(1)}, f32[8,256]{1,0:T(8,128)S(1)}, u32[]{:S(2)}, u32[]{:S(2)}) collective-permute-start(f32[8,256]{1,0:T(8,128)S(1)} %pair_sum.5.gain_ref), channel_id=1, source_target_pairs={{0,1},{1,0},{2,3},{3,2},{4,5},{5,4},{6,7},{7,6},{8,9},{9,8},{10,11... | collective-permute-start | bytes 24584 | tf_op jit(solution)/shard_map/ppermute | solution.py:32

commit v6 on v5

--- a/solution.py
+++ b/solution.py
@@ -238,7 +238,7 @@
 
 def backward_kernel(
     back_ref, loss_ref, sent_ref, m_ref, o_ref, inv_ref, cos_ref, sin_ref,
-    inner_ref, out_give_ref, out_keep_ref, x_ref,
+    inner_ref, give_a_ref, give_b_ref, keep_a_ref, keep_b_ref, x_ref,
     q, k, v1, gh, ghs, scores, low, mixed, gp, ds, dq, heads, grads, inner, out_inner,
 ):
     length, rank = back_ref.shape
@@ -288,9 +288,13 @@
     inner_ref[:half, :] = inner[mine, :]
     inner_ref[half:, :] = inner[theirs, :]
     out_inner[...] = nn(up.T, heads[...]).astype(BF)
-    out_keep_ref[...] = out_inner[mine, :]
-    out_give_ref[...] = out_inner[theirs, :]
-    x_ref[...] = nt(grads[...], m_ref[:rank, :]).astype(BF)
+    middle = ne // 2
+    give_a_ref[...] = out_inner[theirs, :middle]
+    give_b_ref[...] = out_inner[theirs, middle:]
+    keep_a_ref[...] = out_inner[mine, :middle]
+    keep_b_ref[...] = out_inner[mine, middle:]
+    x_ref[:length, :] = nt(grads[...], m_ref[:rank, :]).astype(BF)
+    x_ref[length:, :] = jnp.zeros_like(x_ref[length:, :])
 
 
 def backward(back, loss, sent, m2, o2, inv, cosine, sine):
@@ -302,12 +306,14 @@
     return pl.pallas_call(
         backward_kernel,
         in_specs=vmem(8),
-        out_specs=vmem(4),
+        out_specs=vmem(6),
         out_shape=[
             jax.ShapeDtypeStruct((rank, total), BF),
-            jax.ShapeDtypeStruct((rank // 2, ne), BF),
-            jax.ShapeDtypeStruct((rank // 2, ne), BF),
-            jax.ShapeDtypeStruct((length, rank), BF),
+            jax.ShapeDtypeStruct((rank // 2, ne // 2), BF),
+            jax.ShapeDtypeStruct((rank // 2, ne // 2), BF),
+            jax.ShapeDtypeStruct((rank // 2, ne // 2), BF),
+            jax.ShapeDtypeStruct((rank // 2, ne // 2), BF),
+            jax.ShapeDtypeStruct((length + 16, rank), BF),
         ],
         scratch_shapes=[
             pltpu.VMEM((stack, HD), BF),
@@ -363,7 +369,7 @@
 
 
 def forward_kernel(
-    new_ref, sent_ref, turned_ref, m_ref, o_ref, cos_ref, sin_ref, after,
+    new_ref, sent_ref, turned_ref, m_ref, o_ref, cos_ref, sin_ref, gain_ref,
     y_ref, q, k, v1, scores, low, mixed, heads,
 ):
     length, rank = new_ref.shape
@@ -384,18 +390,19 @@
     for h in range(heads.shape[1] // HD):
         at = slice(h * length, (h + 1) * length)
         heads[:, h * HD : (h + 1) * HD] = (mixed[at, :HD] / mixed[at, HD:]).astype(BF)
-    y_ref[...] = nn(heads[...], o_ref[...]).astype(BF)
-
-
-def forward(new, sent, turned, m2, o2, cosine, sine, after):
+    y_ref[:length, :] = nn(heads[...], o_ref[...]).astype(BF)
+    y_ref[length:, :] = gain_ref[...]
+
+
+def forward(new, sent, turned, m2, o2, cosine, sine, gain):
     length, rank = new.shape
     ne = o2.shape[0]
     stack = ne // HD * length
     return pl.pallas_call(
         forward_kernel,
-        in_specs=vmem(7) + [pl.BlockSpec(memory_space=pl.ANY)],
+        in_specs=vmem(8),
         out_specs=pl.BlockSpec(memory_space=pltpu.VMEM),
-        out_shape=jax.ShapeDtypeStruct((length, rank), BF),
+        out_shape=jax.ShapeDtypeStruct((length + 16, rank), BF),
         scratch_shapes=[
             pltpu.VMEM((stack, HD), BF),
             pltpu.VMEM((length, HD), BF),
@@ -408,7 +415,7 @@
         compiler_params=pltpu.CompilerParams(vmem_limit_bytes=VMEM_BYTES),
         cost_estimate=cost(10**4, 10**3),
         name="attention_forward",
-    )(new, sent, turned, m2, o2, cosine, sine, after)
+    )(new, sent, turned, m2, o2, cosine, sine, gain)
 
 
 def write_split(ref, value):
@@ -423,8 +430,8 @@
 
 
 def gain_kernel(
-    u_ref, wq_ref, narrow_ref, inner_ref, got_ref, x_ref, after,
-    pair_ref, out_ref, turned, rows_f32,
+    u_ref, wq_ref, narrow_ref, inner_ref, got_ref, after,
+    pair_a_ref, pair_b_ref, out_ref, turned, rows_f32,
 ):
     nq = wq_ref.shape[1]
     rows = u_ref.shape[0] // 2
@@ -433,8 +440,9 @@
     core = lax.axis_index("dp") & 1
     mine = add_wide(inner_ref[:half, :], got_ref[half:, :]).astype(BF)
     theirs = add_wide(inner_ref[half:, :], got_ref[:half, :]).astype(BF)
-    pair_ref[...] = mine
-    out_ref[: x_ref.shape[0], :] = x_ref[...]
+    middle = pair_a_ref.shape[1]
+    pair_a_ref[...] = mine[:, :middle]
+    pair_b_ref[...] = mine[:, middle:]
     turned[:, pl.ds(pl.multiple_of(core * half, half), half)] = mine.T
     turned[:, pl.ds(pl.multiple_of((1 - core) * half, half), half)] = theirs.T
     for at in range(0, rows, CHUNK):
@@ -450,17 +458,18 @@
     write_split(out_ref, rows_f32[...])
 
 
-def gain_part(basis, wq, narrow, inner, got, x, after):
+def gain_part(basis, wq, narrow, inner, got, after):
     wide, rank = basis.shape
     assert wide // 2 == 8 * rank
     held = tuple(pltpu.with_memory_space_constraint(a, pltpu.VMEM) for a in (basis, wq, narrow))
     return pl.pallas_call(
         gain_kernel,
-        in_specs=vmem(6) + [pl.BlockSpec(memory_space=pl.ANY)],
-        out_specs=vmem(2),
+        in_specs=vmem(5) + [pl.BlockSpec(memory_space=pl.ANY)],
+        out_specs=vmem(3),
         out_shape=[
-            jax.ShapeDtypeStruct((rank // 2, inner.shape[1]), BF),
-            jax.ShapeDtypeStruct((x.shape[0] + 16, rank), BF),
+            jax.ShapeDtypeStruct((rank // 2, inner.shape[1] // 2), BF),
+            jax.ShapeDtypeStruct((rank // 2, inner.shape[1] // 2), BF),
+            jax.ShapeDtypeStruct((16, rank), BF),
         ],
         scratch_shapes=[
             pltpu.VMEM((inner.shape[1], rank), BF),
@@ -469,17 +478,13 @@
         compiler_params=pltpu.CompilerParams(vmem_limit_bytes=VMEM_BYTES),
         cost_estimate=cost(10**4, 10**3),
         name="pair_sum_and_gain_gradient",
-    )(*held, inner, got, x, after)
-
-
-def merge_kernel(a_ref, b_ref, after, out_ref):
-    rest = out_ref.shape[0] - 16
-    out_ref[:rest, :] = add_wide(a_ref[:rest, :], b_ref[:rest, :]).astype(BF)
-    write_split(out_ref, read_split(a_ref) + read_split(b_ref))
-
-
-def total_kernel(a_ref, b_ref, after, out_ref):
-    out_ref[...] = read_split(a_ref) + read_split(b_ref)
+    )(*held, inner, got, after)
+
+
+def merge_kernel(a_ref, b_ref, after, out_ref, gain_ref):
+    rest = out_ref.shape[0]
+    out_ref[...] = add_wide(a_ref[:rest, :], b_ref[:rest, :]).astype(BF)
+    gain_ref[...] = read_split(a_ref) + read_split(b_ref)
 
 
 def own_kernel(a_ref, b_ref, after, *out_refs):
@@ -503,12 +508,9 @@
 
 
 def merge(a, b, after):
-    return small_kernel(merge_kernel, "sum_with_gain", jax.ShapeDtypeStruct(a.shape, BF), a, b, after)
-
-
-def gain_total(a, b, after):
-    shape = jax.ShapeDtypeStruct((8, a.shape[1]), F32)
-    return small_kernel(total_kernel, "gain_total", shape, a, b, after)
+    rows, width = a.shape
+    shapes = [jax.ShapeDtypeStruct((rows - 16, width), BF), jax.ShapeDtypeStruct((8, width), F32)]
+    return small_kernel(merge_kernel, "sum_with_gain", shapes, a, b, after)
 
 
 def own_pieces(a, b, sizes, after):
@@ -664,32 +666,32 @@
     m2, o2, inv, basis, wq, narrow, turned = project(
         back, norm_gain, subspace, wq, wk, wv, wo
     )
-    inner, out_give, out_keep, x = backward(
+    inner, give_a, give_b, keep_a, keep_b, x = backward(
         back, loss_grad, returned, m2, o2, inv, cosine, sine
     )
-    out_got = swap(out_give, "dp", 1)
+    out_got = [swap(piece, "dp", 1) for piece in (give_a, give_b)]
     inner_got = swap(inner, "dp", 1)
-    base, unit, fbase = bases(
-        back, loss_grad, returned, new_coeffs, arrived, basis, turned, inv, out_keep
-    )
-    out_pair = add_after(out_keep, out_got, fbase)
-    out_got = swap(out_pair, "dp", 2)
-    pair, x = gain_part(basis, wq, narrow, inner, inner_got, x, out_pair)
-    pair_got = swap(pair, "dp", 2)
     x_got = swap(x, "tensor", 2)
-    y = forward(new_coeffs, arrived, turned, m2, o2, cosine, sine, pair)
+    out_pair = [add_wide(keep, got).astype(BF) for keep, got in zip((keep_a, keep_b), out_got)]
+    out_got = [swap(piece, "dp", 2) for piece in out_pair]
+    *pair, gain = gain_part(basis, wq, narrow, inner, inner_got, x)
+    pair_got = [swap(piece, "dp", 2) for piece in pair]
+    y = forward(new_coeffs, arrived, turned, m2, o2, cosine, sine, gain)
     y_got = swap(y, "tensor", 1)
-    ne = wo.shape[0]
-    out_own = own_pieces(out_pair, out_got, (ne // 2, ne - ne // 2), y)
-    x = merge(x, x_got, out_own[0])
+    x = add_after(x, x_got, y)
     x_got = swap(x, "tensor", 1)
+    out_own = [add_after(piece, got, x) for piece, got in zip(out_pair, out_got)]
     out_other = [swap(piece, "dp", 1) for piece in out_own]
     grad_o = outward_grad(basis, out_own, out_other, x)
-    y = add_after(y, y_got, *in_hbm((grad_o,)))
+    y, gain = merge(y, y_got, *in_hbm((grad_o,)))
+    gain_got = swap(gain, "tensor", 2)
     y_got = swap(y, "tensor", 2)
-    own = own_pieces(pair, pair_got, (nq // 2, nq - nq // 2, nk + nv), y)
+    own = [add_after(piece, got, y) for piece, got in zip(pair, pair_got)]
     other = [swap(piece, "dp", 1) for piece in own]
-    gain = gain_total(x, x_got, own[0])
+    base, unit, fbase = bases(
+        back, loss_grad, returned, new_coeffs, arrived, basis, turned, inv, own[0]
+    )
+    gain = add_after(gain, gain_got, base)
     gain_got = swap(gain, "dp", 2)
     grad_q, grad_k, grad_v = inward_grads(basis, norm_gain, own, other, (nq, nk, nv), gain)
     gain = add_after(gain, gain_got, *in_hbm((grad_v,)))

time: 51.8 us -> 57.2 us (1.10)
  starting transfers between devices: 15.5 us -> 19.7 us
  waiting for transfers between devices: 5.42 us -> 6.8 us
    ppermute x16 -> x19, starting transfers between devices: 15.5 us -> 19.7 us  [swap(): return lax.ppermute(x, axis, [(i, i ^ bit) for i in range(devices)])]
    ppermute x16 -> x19, waiting for transfers between devices: 5.42 us -> 6.8 us  [swap(): return lax.ppermute(x, axis, [(i, i ^ bit) for i in range(devices)])]
  transfers between devices with their start and end apart: 16 -> 19, of which waited for: 4 -> 4; matrix products, arithmetic and copies ran while one was open for 0% -> 0% of each run, Pallas kernels for 44% -> 40%
where the time goes in v6:
time: 57.2 us; the launch traced here: 57.1 us
  Pallas kernels  28.7 us (50%)
  starting transfers between devices  19.7 us (34%)
  waiting for transfers between devices  6.8 us (12%)
  other arithmetic  1 us (2%)
  between operations  0.85 us (1%)
    ppermute x19, starting transfers between devices, swap(): return lax.ppermute(x, axis, [(i, i ^ bit) for i in range(devices)])  19.7 us
    pallas_call x1, Pallas kernels, project(): pl.pallas_call(project_kernel, in_specs=[pl.BlockSpec(memory_space=pltpu....  10.9 us
    ppermute x19, waiting for transfers between devices, swap(): return lax.ppermute(x, axis, [(i, i ^ bit) for i in range(devices)])  6.8 us
    pallas_call x1, Pallas kernels, backward(): pl.pallas_call(backward_kernel, in_specs=vmem(8), out_specs=vmem(6), out_...  5.17 us
    pallas_call x1, Pallas kernels, forward(): pl.pallas_call(forward_kernel, in_specs=vmem(8), out_specs=pl.BlockSpec(m...  3.73 us
    pallas_call x1, Pallas kernels, inward_grads(): pl.pallas_call(functools.partial(inward_kernel, len(own)), grid=(STEPS,),...  2.22 us
    pallas_call x1, Pallas kernels, outward_grad(): pl.pallas_call(functools.partial(outward_kernel, len(own)), grid=(STEPS,)...  2.01 us
    pallas_call x1, Pallas kernels, gain_part(): pl.pallas_call(gain_kernel, in_specs=vmem(5) + [pl.BlockSpec(memory_space...  1.8 us
  transfers between devices with their start and end apart: 19, of which 4 were waited for; matrix products, arithmetic and copies ran while one was open for 0% of the time, Pallas kernels for 40%

profile of v6, /device:TPU:0, one launch (start us, length us, event | category | flops | bytes accessed | tf_op | source)
XLA Modules:
  0.0 57.1 jit_solution(1969334007436887799)
XLA Ops:
  0.6 0.9 %select_bitcast_fusion = bf16[256,256]{1,0:T(8,128)(2,1)S(1)} fusion(bf16[1,256,256]{2,1,0:T(8,128)(2,1)} %param.15, bf16[1,256,256]{2,1,0:T(8,128)(2,1)} %param.16, pred[]{:T(512)S(6)} %eq.3), kind=kLoop, calls=%fused_computation.2 | loop fusion | flops 65536 | bytes 393217 | tf_op jit(solution)/shard_map/jit(_where)/select_n | solution.py:39
  1.6 3.0 %collective-permute-start = (bf16[256,256]{1,0:T(8,128)(2,1)S(1)}, bf16[256,256]{1,0:T(8,128)(2,1)S(1)}, u32[]{:S(2)}, u32[]{:S(2)}) collective-permute-start(bf16[256,256]{1,0:T(8,128)(2,1)S(1)} %select_bitcast_fusion), channel_id=1, source_target_pairs={{0,16},{16,0},{1,17},{17,1},{2,18},{18,2},{3,19},{19,3},{4,20},{20... | collective-permute-start | bytes 393224 | tf_op jit(solution)/shard_map/ppermute | solution.py:32
  4.6 10.9 %project_weights.1 = (bf16[512,1280]{1,0:T(8,128)(2,1)S(1)}, bf16[1024,256]{1,0:T(8,128)(2,1)S(1)}, f32[256,128]{1,0:T(8,128)S(1)}, bf16[4096,256]{1,0:T(8,128)(...) custom-call(bf16[256,256]{1,0:T(8,128)(2,1)} %bitcast.13, ...), custom_call_target="tpu_custom_call" | custom-call | flops 6000000000 | bytes 20000000 | tf_op jit(solution)/shard_map/project_weights/pallas_call | solution.py:180
  15.5 5.2 %attention_backward.1 = (bf16[256,1280]{1,0:T(8,128)(2,1)S(1)}, bf16[128,512]{1,0:T(8,128)(2,1)S(1)}, bf16[128,512]{1,0:T(8,128)(2,1)S(1)}, bf16[128,512]{1,0:T(...) custom-call(bf16[256,256]{1,0:T(8,128)(2,1)S(1)} %bitcast.14, ...), custom_call_target="tpu_custom_call" | custom-call | flops 10000 | bytes 1000 | tf_op jit(solution)/shard_map/attention_backward/pallas_call | solution.py:306
  21.2 2.6 %collective-permute-start.6 = (bf16[272,256]{1,0:T(8,128)(2,1)S(1)}, bf16[272,256]{1,0:T(8,128)(2,1)S(1)}, u32[]{:S(2)}, u32[]{:S(2)}) collective-permute-start(bf16[272,256]{1,0:T(8,128)(2,1)S(1)} %get-tuple-element.42.after.a_ref), channel_id=1, source_target_pairs={{0,8},{4,12},{8,0},{12,4},{1,9},{5,13},{9,1},{13,5},{2,10},{6,14},... | collective-permute-start | bytes 417800 | tf_op jit(solution)/shard_map/ppermute | solution.py:32
  23.9 1.6 %collective-permute-start.5 = (bf16[128,512]{1,0:T(8,128)(2,1)S(1)}, bf16[128,512]{1,0:T(8,128)(2,1)S(1)}, u32[]{:S(2)}, u32[]{:S(2)}) collective-permute-start(bf16[128,512]{1,0:T(8,128)(2,1)S(1)} %add_convert_fusion.1.a_ref), channel_id=1, source_target_pairs={{0,2},{1,3},{2,0},{3,1},{4,6},{5,7},{6,4},{7,5},{8,10},{9,11},{10,... | collective-permute-start | bytes 393224 | tf_op jit(solution)/shard_map/ppermute | solution.py:32
  25.5 1.3 %collective-permute-start.8 = (bf16[128,512]{1,0:T(8,128)(2,1)S(1)}, bf16[128,512]{1,0:T(8,128)(2,1)S(1)}, u32[]{:S(2)}, u32[]{:S(2)}) collective-permute-start(bf16[128,512]{1,0:T(8,128)(2,1)S(1)} %add_convert_fusion.a_ref), channel_id=1, source_target_pairs={{0,2},{1,3},{2,0},{3,1},{4,6},{5,7},{6,4},{7,5},{8,10},{9,11},{10,... | collective-permute-start | bytes 393224 | tf_op jit(solution)/shard_map/ppermute | solution.py:32
  26.8 1.8 %pair_sum_and_gain_gradient.1 = (bf16[128,640]{1,0:T(8,128)(2,1)S(1)}, bf16[128,640]{1,0:T(8,128)(2,1)S(1)}, bf16[16,256]{1,0:T(8,128)(2,1)S(1)}) custom-call(bf16[4096,256]{1,0:T(8,128)(2,1)S(1)} %get-tuple-element.34.u_ref, bf16[4096,1024]{1,0:T(8,128)(2,1)S(1)} %get-tuple-element.37.wq_ref, bf16[4096,256]{1,0:T(8,128)(2,1)S(1)} %get-tuple-element.38.narrow_ref, ...), custom_call_target="tpu_custom_call" | custom-call | flops 10000 | bytes 1000 | tf_op jit(solution)/shard_map/pair_sum_and_gain_gradient/pallas_call | solution.py:465
  28.6 0.9 %collective-permute-start.2 = (bf16[128,640]{1,0:T(8,128)(2,1)S(1)}, bf16[128,640]{1,0:T(8,128)(2,1)S(1)}, u32[]{:S(2)}, u32[]{:S(2)}) collective-permute-start(bf16[128,640]{1,0:T(8,128)(2,1)S(1)} %get-tuple-element.43.a_ref), channel_id=1, source_target_pairs={{0,2},{1,3},{2,0},{3,1},{4,6},{5,7},{6,4},{7,5},{8,10},{9,11},{10,... | collective-permute-start | bytes 491528 | tf_op jit(solution)/shard_map/ppermute | solution.py:32
  29.5 1.2 %collective-permute-start.15 = (bf16[128,640]{1,0:T(8,128)(2,1)S(1)}, bf16[128,640]{1,0:T(8,128)(2,1)S(1)}, u32[]{:S(2)}, u32[]{:S(2)}) collective-permute-start(bf16[128,640]{1,0:T(8,128)(2,1)S(1)} %get-tuple-element.54.a_ref), channel_id=1, source_target_pairs={{0,2},{1,3},{2,0},{3,1},{4,6},{5,7},{6,4},{7,5},{8,10},{9,11},{10,... | collective-permute-start | bytes 491528 | tf_op jit(solution)/shard_map/ppermute | solution.py:32
  30.7 3.7 %attention_forward.1.after.a_ref = bf16[272,256]{1,0:T(8,128)(2,1)S(1)} custom-call(bf16[256,256]{1,0:T(8,128)(2,1)S(1)} %copy-done.2, bf16[256,256]{1,0:T(8,128)(2,1)S(1)} %collective-permute-done.sent_ref.returned_ref.arrived_ref, bf16[256,4096]{1,0:T(8,128)(2,1)S(1)} %get-tuple-element.35.turned_ref, bf16[512,1280]{1,0:T(8,128)(2,1)S(1)} %get-tuple-element.39.m_ref, ...), custom_call_target="tpu_custom_call" | custom-call | flops 10000 | bytes 1000 | tf_op jit(solution)/shard_map/attention_forward/pallas_call | solution.py:401
  34.5 1.6 %collective-permute-start.3 = (bf16[272,256]{1,0:T(8,128)(2,1)S(1)}, bf16[272,256]{1,0:T(8,128)(2,1)S(1)}, u32[]{:S(2)}, u32[]{:S(2)}) collective-permute-start(bf16[272,256]{1,0:T(8,128)(2,1)S(1)} %attention_forward.1.after.a_ref), channel_id=1, source_target_pairs={{0,4},{4,0},{8,12},{12,8},{1,5},{5,1},{9,13},{13,9},{2,6},{6,2},{1... | collective-permute-start | bytes 417800 | tf_op jit(solution)/shard_map/ppermute | solution.py:32
  36.3 0.5 collective-permute-start.10
  36.9 0.7 %collective-permute-done.9.refs_2_ = bf16[128,512]{1,0:T(8,128)(2,1)S(1)} collective-permute-done((bf16[128,512]{1,0:T(8,128)(2,1)S(1)}, bf16[128,512]{1,0:T(8,128)(2,1)S(1)}, u32[]{:S(2)}, u32[]{:S(2)}) %collective-permute-start.9) | collective-permute-done | bytes 131104 | tf_op jit(solution)/shard_map/ppermute | solution.py:32
  37.9 2.0 %output_weight_gradient.1.after = bf16[1024,1024]{1,0:T(8,128)(2,1)} custom-call(bf16[4096,256]{1,0:T(8,128)(2,1)S(1)} %get-tuple-element.34.u_ref, bf16[128,512]{1,0:T(8,128)(2,1)S(1)} %pair_sum.8.refs_0_, bf16[128,512]{1,0:T(8,128)(2,1)S(1)} %pair_sum.9.refs_1_, bf16[128,512]{1,0:T(8,128)(2,1)S(1)} %collective-permute-done.9.refs_2_, ...), custom_call_target="tpu_custom_call" | custom-call | flops 10000 | bytes 1000 | tf_op jit(solution)/shard_map/output_weight_gradient/pallas_call | solution.py:597
  40.7 1.3 %collective-permute-start.12 = (bf16[272,256]{1,0:T(8,128)(2,1)S(1)}, bf16[272,256]{1,0:T(8,128)(2,1)S(1)}, u32[]{:S(2)}, u32[]{:S(2)}) collective-permute-start(bf16[272,256]{1,0:T(8,128)(2,1)S(1)} %pair_sum.7.after.refs_4_.x_ref), channel_id=1, source_target_pairs={{0,4},{4,0},{8,12},{12,8},{1,5},{5,1},{9,13},{13,9},{2,6},{6,2},{1... | collective-permute-start | bytes 417800 | tf_op jit(solution)/shard_map/ppermute | solution.py:32
  42.0 0.6 %collective-permute-start.11 = (bf16[256,256]{1,0:T(8,128)(2,1)S(1)}, bf16[256,256]{1,0:T(8,128)(2,1)S(1)}, u32[]{:S(2)}, u32[]{:S(2)}) collective-permute-start(bf16[256,256]{1,0:T(8,128)(2,1)S(1)} %get-tuple-element.49.after.y_ref), channel_id=1, source_target_pairs={{0,8},{4,12},{8,0},{12,4},{1,9},{5,13},{9,1},{13,5},{2,10},{6,14},... | collective-permute-start | bytes 393224 | tf_op jit(solution)/shard_map/ppermute | solution.py:32
  42.6 2.3 %collective-permute-start.13 = (f32[8,256]{1,0:T(8,128)S(1)}, f32[8,256]{1,0:T(8,128)S(1)}, u32[]{:S(2)}, u32[]{:S(2)}) collective-permute-start(f32[8,256]{1,0:T(8,128)S(1)} %get-tuple-element.53.a_ref), channel_id=1, source_target_pairs={{0,8},{4,12},{8,0},{12,4},{1,9},{5,13},{9,1},{13,5},{2,10},{6,14},... | collective-permute-start | bytes 24584 | tf_op jit(solution)/shard_map/ppermute | solution.py:32
  44.9 1.7 %encoded_again.1 = (f32[256,256]{1,0:T(8,128)S(1)}, f32[256,256]{1,0:T(8,128)S(1)}, f32[256,256]{1,0:T(8,128)S(1)}) custom-call(bf16[256,256]{1,0:T(8,128)(2,1)S(1)} %bitcast.15, bf16[256,256]{1,0:T(8,128)(2,1)S(1)} %copy-done.1, bf16[256,256]{1,0:T(8,128)(2,1)S(1)} %collective-permute-done.sent_ref.returned_ref.arrived_ref, bf16[256,256]{1,0:T(8,128)(2,1)S(1)} %copy-done.2, ...), custom_call_target="tpu_custom_call" | custom-call | flops 10000 | bytes 1000 | tf_op jit(solution)/shard_map/encoded_again/pallas_call | solution.py:359
  46.6 4.6 %collective-permute-done.13.b_ref = f32[8,256]{1,0:T(8,128)S(1)} collective-permute-done((f32[8,256]{1,0:T(8,128)S(1)}, f32[8,256]{1,0:T(8,128)S(1)}, u32[]{:S(2)}, u32[]{:S(2)}) %collective-permute-start.13) | collective-permute-done | bytes 8224 | tf_op jit(solution)/shard_map/ppermute | solution.py:32
  51.2 1.4 %collective-permute-start.14 = (f32[8,256]{1,0:T(8,128)S(1)}, f32[8,256]{1,0:T(8,128)S(1)}, u32[]{:S(2)}, u32[]{:S(2)}) collective-permute-start(f32[8,256]{1,0:T(8,128)S(1)} %pair_sum.11.refs_4_.a_ref), channel_id=1, source_target_pairs={{0,2},{1,3},{2,0},{3,1},{4,6},{5,7},{6,4},{7,5},{8,10},{9,11},{10,... | collective-permute-start | bytes 24584 | tf_op jit(solution)/shard_map/ppermute | solution.py:32
  52.6 2.2 %inward_weight_gradients.1 = (bf16[1024,1024]{1,0:T(8,128)(2,1)}, bf16[1024,128]{1,0:T(8,128)(2,1)}, bf16[1024,128]{1,0:T(8,128)(2,1)}) custom-call(bf16[4096,256]{1,0:T(8,128)(2,1)S(1)} %get-tuple-element.34.u_ref, f32[1,4096]{1,0:T(1,128)S(1)} %copy-done.5, bf16[128,640]{1,0:T(8,128)(2,1)S(1)} %pair_sum.10.after.refs_0_, ...), custom_call_target="tpu_custom_call" | custom-call | flops 10000 | bytes 1000 | tf_op jit(solution)/shard_map/inward_weight_gradients/pallas_call | solution.py:580
  54.9 1.1 %collective-permute-done.18.gain_other_ref = f32[8,256]{1,0:T(8,128)S(1)} collective-permute-done((f32[8,256]{1,0:T(8,128)S(1)}, f32[8,256]{1,0:T(8,128)S(1)}, u32[]{:S(2)}, u32[]{:S(2)}) %collective-permute-start.18) | collective-permute-done | bytes 8224 | tf_op jit(solution)/shard_map/ppermute | solution.py:32
  56.1 1.0 %section_results.1 = (bf16[256,256]{1,0:T(8,128)(2,1)}, bf16[256,256]{1,0:T(8,128)(2,1)}, f32[1,4096]{1,0:T(1,128)}) custom-call(f32[256,256]{1,0:T(8,128)S(1)} %get-tuple-element.50.fbase_ref, bf16[256,256]{1,0:T(8,128)(2,1)S(1)} %get-tuple-element.49.after.y_ref, bf16[256,256]{1,0:T(8,128)(2,1)S(1)} %collective-permute-done.11.ygot_ref, ...), custom_call_target="tpu_custom_call" | custom-call | flops 10000 | bytes 1000 | tf_op jit(solution)/shard_map/section_results/pallas_call | solution.py:635
  (45 shorter events, 2.0 us)
Async XLA Ops:
  1.6 13.9 %collective-permute-start = (bf16[256,256]{1,0:T(8,128)(2,1)S(1)}, bf16[256,256]{1,0:T(8,128)(2,1)S(1)}, u32[]{:S(2)}, u32[]{:S(2)}) collective-permute-start(bf16[256,256]{1,0:T(8,128)(2,1)S(1)} %select_bitcast_fusion), channel_id=1, source_target_pairs={{0,16},{16,0},{1,17},{17,1},{2,18},{18,2},{3,19},{19,3},{4,20},{20... | collective-permute-start | bytes 393224 | tf_op jit(solution)/shard_map/ppermute | solution.py:32
  4.6 10.9 %copy-start = (bf16[1,256,256]{2,1,0:T(8,128)(2,1)S(1)}, bf16[1,256,256]{2,1,0:T(8,128)(2,1)}, u32[]{:S(2)}) copy-start(bf16[1,256,256]{2,1,0:T(8,128)(2,1)} %param.17) | copy-start | bytes 393220
  4.6 10.9 %copy-start.1 = (bf16[256,256]{1,0:T(8,128)(2,1)S(1)}, bf16[256,256]{1,0:T(8,128)(2,1)}, u32[]{:S(2)}) copy-start(bf16[256,256]{1,0:T(8,128)(2,1)} %loss_ref.3) | copy-start | bytes 393220
  4.6 10.9 %copy-start.3 = (f32[256,128]{1,0:T(8,128)S(1)}, f32[256,128]{1,0:T(8,128)}, u32[]{:S(2)}) copy-start(f32[256,128]{1,0:T(8,128)} %constant.12.clone.cos_ref) | copy-start | bytes 393220
  4.6 10.9 %copy-start.4 = (f32[256,128]{1,0:T(8,128)S(1)}, f32[256,128]{1,0:T(8,128)}, u32[]{:S(2)}) copy-start(f32[256,128]{1,0:T(8,128)} %constant.13.clone.sin_ref) | copy-start | bytes 393220
  20.7 3.2 %collective-permute-start.4 = (bf16[128,512]{1,0:T(8,128)(2,1)S(1)}, bf16[128,512]{1,0:T(8,128)(2,1)S(1)}, u32[]{:S(2)}, u32[]{:S(2)}) collective-permute-start(bf16[128,512]{1,0:T(8,128)(2,1)S(1)} %get-tuple-element.46), channel_id=1, source_target_pairs={{0,1},{1,0},{2,3},{3,2},{4,5},{5,4},{6,7},{7,6},{8,9},{9,8},{10,11... | collective-permute-start | bytes 393224 | tf_op jit(solution)/shard_map/ppermute | solution.py:32
  20.7 6.1 %collective-permute-start.1 = (bf16[256,1280]{1,0:T(8,128)(2,1)S(1)}, bf16[256,1280]{1,0:T(8,128)(2,1)S(1)}, u32[]{:S(2)}, u32[]{:S(2)}) collective-permute-start(bf16[256,1280]{1,0:T(8,128)(2,1)S(1)} %get-tuple-element.41.inner_ref), channel_id=1, source_target_pairs={{0,1},{1,0},{2,3},{3,2},{4,5},{5,4},{6,7},{7,6},{8,9},{9,8},{10,11... | collective-permute-start | bytes 1966088 | tf_op jit(solution)/shard_map/ppermute | solution.py:32
  21.2 13.2 %collective-permute-start.6 = (bf16[272,256]{1,0:T(8,128)(2,1)S(1)}, bf16[272,256]{1,0:T(8,128)(2,1)S(1)}, u32[]{:S(2)}, u32[]{:S(2)}) collective-permute-start(bf16[272,256]{1,0:T(8,128)(2,1)S(1)} %get-tuple-element.42.after.a_ref), channel_id=1, source_target_pairs={{0,8},{4,12},{8,0},{12,4},{1,9},{5,13},{9,1},{13,5},{2,10},{6,14},... | collective-permute-start | bytes 417800 | tf_op jit(solution)/shard_map/ppermute | solution.py:32
  23.8 1.6 %collective-permute-start.7 = (bf16[128,512]{1,0:T(8,128)(2,1)S(1)}, bf16[128,512]{1,0:T(8,128)(2,1)S(1)}, u32[]{:S(2)}, u32[]{:S(2)}) collective-permute-start(bf16[128,512]{1,0:T(8,128)(2,1)S(1)} %get-tuple-element.48), channel_id=1, source_target_pairs={{0,1},{1,0},{2,3},{3,2},{4,5},{5,4},{6,7},{7,6},{8,9},{9,8},{10,11... | collective-permute-start | bytes 393224 | tf_op jit(solution)/shard_map/ppermute | solution.py:32
  23.9 12.3 %collective-permute-start.5 = (bf16[128,512]{1,0:T(8,128)(2,1)S(1)}, bf16[128,512]{1,0:T(8,128)(2,1)S(1)}, u32[]{:S(2)}, u32[]{:S(2)}) collective-permute-start(bf16[128,512]{1,0:T(8,128)(2,1)S(1)} %add_convert_fusion.1.a_ref), channel_id=1, source_target_pairs={{0,2},{1,3},{2,0},{3,1},{4,6},{5,7},{6,4},{7,5},{8,10},{9,11},{10,... | collective-permute-start | bytes 393224 | tf_op jit(solution)/shard_map/ppermute | solution.py:32
  25.5 10.8 %collective-permute-start.8 = (bf16[128,512]{1,0:T(8,128)(2,1)S(1)}, bf16[128,512]{1,0:T(8,128)(2,1)S(1)}, u32[]{:S(2)}, u32[]{:S(2)}) collective-permute-start(bf16[128,512]{1,0:T(8,128)(2,1)S(1)} %add_convert_fusion.a_ref), channel_id=1, source_target_pairs={{0,2},{1,3},{2,0},{3,1},{4,6},{5,7},{6,4},{7,5},{8,10},{9,11},{10,... | collective-permute-start | bytes 393224 | tf_op jit(solution)/shard_map/ppermute | solution.py:32
  28.6 11.3 %collective-permute-start.2 = (bf16[128,640]{1,0:T(8,128)(2,1)S(1)}, bf16[128,640]{1,0:T(8,128)(2,1)S(1)}, u32[]{:S(2)}, u32[]{:S(2)}) collective-permute-start(bf16[128,640]{1,0:T(8,128)(2,1)S(1)} %get-tuple-element.43.a_ref), channel_id=1, source_target_pairs={{0,2},{1,3},{2,0},{3,1},{4,6},{5,7},{6,4},{7,5},{8,10},{9,11},{10,... | collective-permute-start | bytes 491528 | tf_op jit(solution)/shard_map/ppermute | solution.py:32
  29.5 10.9 %collective-permute-start.15 = (bf16[128,640]{1,0:T(8,128)(2,1)S(1)}, bf16[128,640]{1,0:T(8,128)(2,1)S(1)}, u32[]{:S(2)}, u32[]{:S(2)}) collective-permute-start(bf16[128,640]{1,0:T(8,128)(2,1)S(1)} %get-tuple-element.54.a_ref), channel_id=1, source_target_pairs={{0,2},{1,3},{2,0},{3,1},{4,6},{5,7},{6,4},{7,5},{8,10},{9,11},{10,... | collective-permute-start | bytes 491528 | tf_op jit(solution)/shard_map/ppermute | solution.py:32
  34.5 5.4 %collective-permute-start.3 = (bf16[272,256]{1,0:T(8,128)(2,1)S(1)}, bf16[272,256]{1,0:T(8,128)(2,1)S(1)}, u32[]{:S(2)}, u32[]{:S(2)}) collective-permute-start(bf16[272,256]{1,0:T(8,128)(2,1)S(1)} %attention_forward.1.after.a_ref), channel_id=1, source_target_pairs={{0,4},{4,0},{8,12},{12,8},{1,5},{5,1},{9,13},{13,9},{2,6},{6,2},{1... | collective-permute-start | bytes 417800 | tf_op jit(solution)/shard_map/ppermute | solution.py:32
  36.2 1.4 %collective-permute-start.9 = (bf16[128,512]{1,0:T(8,128)(2,1)S(1)}, bf16[128,512]{1,0:T(8,128)(2,1)S(1)}, u32[]{:S(2)}, u32[]{:S(2)}) collective-permute-start(bf16[128,512]{1,0:T(8,128)(2,1)S(1)} %pair_sum.8.refs_0_), channel_id=1, source_target_pairs={{0,1},{1,0},{2,3},{3,2},{4,5},{5,4},{6,7},{7,6},{8,9},{9,8},{10,11... | collective-permute-start | bytes 393224 | tf_op jit(solution)/shard_map/ppermute | solution.py:32
  36.3 1.5 %collective-permute-start.10 = (bf16[128,512]{1,0:T(8,128)(2,1)S(1)}, bf16[128,512]{1,0:T(8,128)(2,1)S(1)}, u32[]{:S(2)}, u32[]{:S(2)}) collective-permute-start(bf16[128,512]{1,0:T(8,128)(2,1)S(1)} %pair_sum.9.refs_1_), channel_id=1, source_target_pairs={{0,1},{1,0},{2,3},{3,2},{4,5},{5,4},{6,7},{7,6},{8,9},{9,8},{10,11... | collective-permute-start | bytes 393224 | tf_op jit(solution)/shard_map/ppermute | solution.py:32
  40.0 12.6 %collective-permute-start.16 = (bf16[128,640]{1,0:T(8,128)(2,1)S(1)}, bf16[128,640]{1,0:T(8,128)(2,1)S(1)}, u32[]{:S(2)}, u32[]{:S(2)}) collective-permute-start(bf16[128,640]{1,0:T(8,128)(2,1)S(1)} %pair_sum.10.after.refs_0_), channel_id=1, source_target_pairs={{0,1},{1,0},{2,3},{3,2},{4,5},{5,4},{6,7},{7,6},{8,9},{9,8},{10,11... | collective-permute-start | bytes 491528 | tf_op jit(solution)/shard_map/ppermute | solution.py:32
  40.5 12.2 %collective-permute-start.17 = (bf16[128,640]{1,0:T(8,128)(2,1)S(1)}, bf16[128,640]{1,0:T(8,128)(2,1)S(1)}, u32[]{:S(2)}, u32[]{:S(2)}) collective-permute-start(bf16[128,640]{1,0:T(8,128)(2,1)S(1)} %pair_sum.12.refs_1_), channel_id=1, source_target_pairs={{0,1},{1,0},{2,3},{3,2},{4,5},{5,4},{6,7},{7,6},{8,9},{9,8},{10,11... | collective-permute-start | bytes 491528 | tf_op jit(solution)/shard_map/ppermute | solution.py:32
  40.7 14.3 %collective-permute-start.12 = (bf16[272,256]{1,0:T(8,128)(2,1)S(1)}, bf16[272,256]{1,0:T(8,128)(2,1)S(1)}, u32[]{:S(2)}, u32[]{:S(2)}) collective-permute-start(bf16[272,256]{1,0:T(8,128)(2,1)S(1)} %pair_sum.7.after.refs_4_.x_ref), channel_id=1, source_target_pairs={{0,4},{4,0},{8,12},{12,8},{1,5},{5,1},{9,13},{13,9},{2,6},{6,2},{1... | collective-permute-start | bytes 417800 | tf_op jit(solution)/shard_map/ppermute | solution.py:32
  42.0 13.0 %collective-permute-start.11 = (bf16[256,256]{1,0:T(8,128)(2,1)S(1)}, bf16[256,256]{1,0:T(8,128)(2,1)S(1)}, u32[]{:S(2)}, u32[]{:S(2)}) collective-permute-start(bf16[256,256]{1,0:T(8,128)(2,1)S(1)} %get-tuple-element.49.after.y_ref), channel_id=1, source_target_pairs={{0,8},{4,12},{8,0},{12,4},{1,9},{5,13},{9,1},{13,5},{2,10},{6,14},... | collective-permute-start | bytes 393224 | tf_op jit(solution)/shard_map/ppermute | solution.py:32
  42.6 10.0 %copy-start.5 = (f32[1,4096]{1,0:T(1,128)S(1)}, f32[1,4096]{1,0:T(1,128)}, u32[]{:S(2)}) copy-start(f32[1,4096]{1,0:T(1,128)} %gain_ref.1) | copy-start | bytes 49156
  42.6 8.6 %collective-permute-start.13 = (f32[8,256]{1,0:T(8,128)S(1)}, f32[8,256]{1,0:T(8,128)S(1)}, u32[]{:S(2)}, u32[]{:S(2)}) collective-permute-start(f32[8,256]{1,0:T(8,128)S(1)} %get-tuple-element.53.a_ref), channel_id=1, source_target_pairs={{0,8},{4,12},{8,0},{12,4},{1,9},{5,13},{9,1},{13,5},{2,10},{6,14},... | collective-permute-start | bytes 24584 | tf_op jit(solution)/shard_map/ppermute | solution.py:32
  51.2 3.7 %collective-permute-start.14 = (f32[8,256]{1,0:T(8,128)S(1)}, f32[8,256]{1,0:T(8,128)S(1)}, u32[]{:S(2)}, u32[]{:S(2)}) collective-permute-start(f32[8,256]{1,0:T(8,128)S(1)} %pair_sum.11.refs_4_.a_ref), channel_id=1, source_target_pairs={{0,2},{1,3},{2,0},{3,1},{4,6},{5,7},{6,4},{7,5},{8,10},{9,11},{10,... | collective-permute-start | bytes 24584 | tf_op jit(solution)/shard_map/ppermute | solution.py:32
  54.9 1.2 %collective-permute-start.18 = (f32[8,256]{1,0:T(8,128)S(1)}, f32[8,256]{1,0:T(8,128)S(1)}, u32[]{:S(2)}, u32[]{:S(2)}) collective-permute-start(f32[8,256]{1,0:T(8,128)S(1)} %pair_sum.13.gain_ref), channel_id=1, source_target_pairs={{0,1},{1,0},{2,3},{3,2},{4,5},{5,4},{6,7},{7,6},{8,9},{9,8},{10,11... | collective-permute-start | bytes 24584 | tf_op jit(solution)/shard_map/ppermute | solution.py:32
  (1 other events, 3.9 us)

commit v7 on v5

--- a/solution.py
+++ b/solution.py
@@ -384,7 +384,8 @@
     for h in range(heads.shape[1] // HD):
         at = slice(h * length, (h + 1) * length)
         heads[:, h * HD : (h + 1) * HD] = (mixed[at, :HD] / mixed[at, HD:]).astype(BF)
-    y_ref[...] = nn(heads[...], o_ref[...]).astype(BF)
+    y_ref[:length, :] = nn(heads[...], o_ref[...]).astype(BF)
+    y_ref[length:, :] = jnp.zeros_like(y_ref[length:, :])
 
 
 def forward(new, sent, turned, m2, o2, cosine, sine, after):
@@ -395,7 +396,7 @@
         forward_kernel,
         in_specs=vmem(7) + [pl.BlockSpec(memory_space=pl.ANY)],
         out_specs=pl.BlockSpec(memory_space=pltpu.VMEM),
-        out_shape=jax.ShapeDtypeStruct((length, rank), BF),
+        out_shape=jax.ShapeDtypeStruct((length + 32, rank), BF),
         scratch_shapes=[
             pltpu.VMEM((stack, HD), BF),
             pltpu.VMEM((length, HD), BF),
@@ -517,11 +518,13 @@
 
 
 def add_kernel(a_ref, b_ref, after, out_ref):
-    out_ref[...] = add_wide(a_ref[...], b_ref[...]).astype(out_ref.dtype)
-
-
-def add_after(a, b, after):
-    return small_kernel(add_kernel, "pair_sum", jax.ShapeDtypeStruct(a.shape, a.dtype), a, b, after)
+    rows = out_ref.shape[0]
+    out_ref[...] = add_wide(a_ref[:rows, :], b_ref[:rows, :]).astype(out_ref.dtype)
+
+
+def add_after(a, b, after, rows=None):
+    shape = jax.ShapeDtypeStruct((rows or a.shape[0], a.shape[1]), a.dtype)
+    return small_kernel(add_kernel, "pair_sum", shape, a, b, after)
 
 
 def gather_halves(own_refs, other_refs, whole):
@@ -678,20 +681,20 @@
     pair_got = swap(pair, "dp", 2)
     x_got = swap(x, "tensor", 2)
     y = forward(new_coeffs, arrived, turned, m2, o2, cosine, sine, pair)
-    y_got = swap(y, "tensor", 1)
-    ne = wo.shape[0]
-    out_own = own_pieces(out_pair, out_got, (ne // 2, ne - ne // 2), y)
-    x = merge(x, x_got, out_own[0])
+    y_got = swap(y, "tensor", 2)
+    out_own = add_after(out_pair, out_got, y)
+    out_other = swap(out_own, "dp", 1)
+    x = merge(x, x_got, out_own)
     x_got = swap(x, "tensor", 1)
-    out_other = [swap(piece, "dp", 1) for piece in out_own]
-    grad_o = outward_grad(basis, out_own, out_other, x)
-    y = add_after(y, y_got, *in_hbm((grad_o,)))
-    y_got = swap(y, "tensor", 2)
-    own = own_pieces(pair, pair_got, (nq // 2, nq - nq // 2, nk + nv), y)
+    grad_o = outward_grad(basis, [out_own], [out_other], x)
+    sizes = (nq // 2, nq - nq // 2, nk + nv)
+    own = own_pieces(pair, pair_got, sizes, *in_hbm((grad_o,)))
     other = [swap(piece, "dp", 1) for piece in own]
     gain = gain_total(x, x_got, own[0])
     gain_got = swap(gain, "dp", 2)
-    grad_q, grad_k, grad_v = inward_grads(basis, norm_gain, own, other, (nq, nk, nv), gain)
+    y = add_after(y, y_got, gain, rows=back.shape[0])
+    y_got = swap(y, "tensor", 1)
+    grad_q, grad_k, grad_v = inward_grads(basis, norm_gain, own, other, (nq, nk, nv), y)
     gain = add_after(gain, gain_got, *in_hbm((grad_v,)))
     gain_other = swap(gain, "dp", 1)
     forward_out, backward_out, grad_gain = results(

time: 51.8 us -> 51.9 us (level)
  the two profiles are of different devices: /device:TPU:0 before, /device:TPU:17 now
where the time goes in v7:
time: 51.9 us; the launch traced here: 51.7 us
  Pallas kernels  29 us (56%)
  starting transfers between devices  16.7 us (32%)
  waiting for transfers between devices  4.38 us (8%)
  other arithmetic  0.93 us (2%)
  between operations  0.76 us (1%)
    ppermute x15, starting transfers between devices, swap(): return lax.ppermute(x, axis, [(i, i ^ bit) for i in range(devices)])  16.7 us
    pallas_call x1, Pallas kernels, project(): pl.pallas_call(project_kernel, in_specs=[pl.BlockSpec(memory_space=pltpu....  10.9 us
    pallas_call x1, Pallas kernels, backward(): pl.pallas_call(backward_kernel, in_specs=vmem(8), out_specs=vmem(4), out_...  5.2 us
    ppermute x15, waiting for transfers between devices, swap(): return lax.ppermute(x, axis, [(i, i ^ bit) for i in range(devices)])  4.38 us
    pallas_call x1, Pallas kernels, forward(): pl.pallas_call(forward_kernel, in_specs=vmem(7) + [pl.BlockSpec(memory_sp...  3.76 us
    pallas_call x1, Pallas kernels, inward_grads(): pl.pallas_call(functools.partial(inward_kernel, len(own)), grid=(STEPS,),...  2.23 us
    pallas_call x1, Pallas kernels, outward_grad(): pl.pallas_call(functools.partial(outward_kernel, len(own)), grid=(STEPS,)...  2.01 us
    pallas_call x1, Pallas kernels, gain_part(): pl.pallas_call(gain_kernel, in_specs=vmem(6) + [pl.BlockSpec(memory_space...  1.85 us
  transfers between devices with their start and end apart: 15, of which 4 were waited for; matrix products, arithmetic and copies ran while one was open for 0% of the time, Pallas kernels for 44%

profile of v7, /device:TPU:17, one launch (start us, length us, event | category | flops | bytes accessed | tf_op | source)
XLA Modules:
  0.0 51.7 jit_solution(4470090352343204626)
XLA Ops:
  0.6 0.9 %select_bitcast_fusion = bf16[256,256]{1,0:T(8,128)(2,1)S(1)} fusion(bf16[1,256,256]{2,1,0:T(8,128)(2,1)} %param.15, bf16[1,256,256]{2,1,0:T(8,128)(2,1)} %param.16, pred[]{:T(512)S(6)} %eq.3), kind=kLoop, calls=%fused_computation | loop fusion | flops 65536 | bytes 393217 | tf_op jit(solution)/shard_map/jit(_where)/select_n | solution.py:39
  1.6 1.3 %collective-permute-start = (bf16[256,256]{1,0:T(8,128)(2,1)S(1)}, bf16[256,256]{1,0:T(8,128)(2,1)S(1)}, u32[]{:S(2)}, u32[]{:S(2)}) collective-permute-start(bf16[256,256]{1,0:T(8,128)(2,1)S(1)} %select_bitcast_fusion), channel_id=1, source_target_pairs={{0,16},{16,0},{1,17},{17,1},{2,18},{18,2},{3,19},{19,3},{4,20},{20... | collective-permute-start | bytes 393224 | tf_op jit(solution)/shard_map/ppermute | solution.py:32
  2.9 10.9 %project_weights.1 = (bf16[512,1280]{1,0:T(8,128)(2,1)S(1)}, bf16[1024,256]{1,0:T(8,128)(2,1)S(1)}, f32[256,128]{1,0:T(8,128)S(1)}, bf16[4096,256]{1,0:T(8,128)(...) custom-call(bf16[256,256]{1,0:T(8,128)(2,1)} %bitcast.13, ...), custom_call_target="tpu_custom_call" | custom-call | flops 6000000000 | bytes 20000000 | tf_op jit(solution)/shard_map/project_weights/pallas_call | solution.py:180
  13.9 5.2 %attention_backward.1 = (bf16[256,1280]{1,0:T(8,128)(2,1)S(1)}, bf16[128,1024]{1,0:T(8,128)(2,1)S(1)}, bf16[128,1024]{1,0:T(8,128)(2,1)S(1)}, bf16[256,256]{1,0:T(8,128)(2,1)S(1)}) custom-call(bf16[256,256]{1,0:T(8,128)(2,1)S(1)} %bitcast.14, bf16[256,256]{1,0:T(8,128)(2,1)S(1)} %copy-done.1, ...), custom_call_target="tpu_custom_call" | custom-call | flops 10000 | bytes 1000 | tf_op jit(solution)/shard_map/attention_backward/pallas_call | solution.py:302
  19.1 1.0 %collective-permute-start.1 = (bf16[256,1280]{1,0:T(8,128)(2,1)S(1)}, bf16[256,1280]{1,0:T(8,128)(2,1)S(1)}, u32[]{:S(2)}, u32[]{:S(2)}) collective-permute-start(bf16[256,1280]{1,0:T(8,128)(2,1)S(1)} %get-tuple-element.41.inner_ref), channel_id=1, source_target_pairs={{0,1},{1,0},{2,3},{3,2},{4,5},{5,4},{6,7},{7,6},{8,9},{9,8},{10,11... | collective-permute-start | bytes 1966088 | tf_op jit(solution)/shard_map/ppermute | solution.py:32
  20.2 1.7 %encoded_again.1 = (f32[256,256]{1,0:T(8,128)S(1)}, f32[256,256]{1,0:T(8,128)S(1)}, f32[256,256]{1,0:T(8,128)S(1)}) custom-call(bf16[256,256]{1,0:T(8,128)(2,1)S(1)} %bitcast.15, bf16[256,256]{1,0:T(8,128)(2,1)S(1)} %copy-done.1, bf16[256,256]{1,0:T(8,128)(2,1)S(1)} %collective-permute-done.sent_ref.returned_ref.arrived_ref, bf16[256,256]{1,0:T(8,128)(2,1)S(1)} %copy-done.2, ...), custom_call_target="tpu_custom_call" | custom-call | flops 10000 | bytes 1000 | tf_op jit(solution)/shard_map/encoded_again/pallas_call | solution.py:353
  21.9 0.3 collective-permute-done.2.b_ref
  22.2 1.3 %collective-permute-start.5 = (bf16[128,1024]{1,0:T(8,128)(2,1)S(1)}, bf16[128,1024]{1,0:T(8,128)(2,1)S(1)}, u32[]{:S(2)}, u32[]{:S(2)}) collective-permute-start(bf16[128,1024]{1,0:T(8,128)(2,1)S(1)} %pair_sum.4.after.a_ref), channel_id=1, source_target_pairs={{0,2},{1,3},{2,0},{3,1},{4,6},{5,7},{6,4},{7,5},{8,10},{9,11},{10,... | collective-permute-start | bytes 786440 | tf_op jit(solution)/shard_map/ppermute | solution.py:32
  23.5 1.8 %pair_sum_and_gain_gradient.1 = (bf16[128,1280]{1,0:T(8,128)(2,1)S(1)}, bf16[272,256]{1,0:T(8,128)(2,1)S(1)}) custom-call(bf16[4096,256]{1,0:T(8,128)(2,1)S(1)} %get-tuple-element.32.u_ref, bf16[4096,1024]{1,0:T(8,128)(2,1)S(1)} %get-tuple-element.39.wq_ref, bf16[4096,256]{1,0:T(8,128)(2,1)S(1)} %get-tuple-element.40.narrow_ref, ...), custom_call_target="tpu_custom_call" | custom-call | flops 10000 | bytes 1000 | tf_op jit(solution)/shard_map/pair_sum_and_gain_gradient/pallas_call | solution.py:458
  25.7 3.8 %attention_forward.1.after.a_ref = bf16[288,256]{1,0:T(8,128)(2,1)S(1)} custom-call(bf16[256,256]{1,0:T(8,128)(2,1)S(1)} %copy-done.2, bf16[256,256]{1,0:T(8,128)(2,1)S(1)} %collective-permute-done.sent_ref.returned_ref.arrived_ref, bf16[256,4096]{1,0:T(8,128)(2,1)S(1)} %get-tuple-element.33.turned_ref, bf16[512,1280]{1,0:T(8,128)(2,1)S(1)} %get-tuple-element.35.m_ref, ...), custom_call_target="tpu_custom_call" | custom-call | flops 10000 | bytes 1000 | tf_op jit(solution)/shard_map/attention_forward/pallas_call | solution.py:395
  29.5 0.3 collective-permute-done.5.b_ref
  29.9 2.1 %collective-permute-start.8 = (bf16[128,1024]{1,0:T(8,128)(2,1)S(1)}, bf16[128,1024]{1,0:T(8,128)(2,1)S(1)}, u32[]{:S(2)}, u32[]{:S(2)}) collective-permute-start(bf16[128,1024]{1,0:T(8,128)(2,1)S(1)} %pair_sum.5.after.refs_0_), channel_id=1, source_target_pairs={{0,1},{1,0},{2,3},{3,2},{4,5},{5,4},{6,7},{7,6},{8,9},{9,8},{10,11... | collective-permute-start | bytes 786440 | tf_op jit(solution)/shard_map/ppermute | solution.py:32
  32.0 1.2 %collective-permute-start.3 = (bf16[288,256]{1,0:T(8,128)(2,1)S(1)}, bf16[288,256]{1,0:T(8,128)(2,1)S(1)}, u32[]{:S(2)}, u32[]{:S(2)}) collective-permute-start(bf16[288,256]{1,0:T(8,128)(2,1)S(1)} %attention_forward.1.after.a_ref), channel_id=1, source_target_pairs={{0,8},{4,12},{8,0},{12,4},{1,9},{5,13},{9,1},{13,5},{2,10},{6,14},... | collective-permute-start | bytes 442376 | tf_op jit(solution)/shard_map/ppermute | solution.py:32
  33.2 3.2 %collective-permute-start.6 = (bf16[272,256]{1,0:T(8,128)(2,1)S(1)}, bf16[272,256]{1,0:T(8,128)(2,1)S(1)}, u32[]{:S(2)}, u32[]{:S(2)}) collective-permute-start(bf16[272,256]{1,0:T(8,128)(2,1)S(1)} %sum_with_gain.1.refs_2_.a_ref.x_ref), channel_id=1, source_target_pairs={{0,4},{4,0},{8,12},{12,8},{1,5},{5,1},{9,13},{13,9},{2,6},{6,2},{1... | collective-permute-start | bytes 417800 | tf_op jit(solution)/shard_map/ppermute | solution.py:32
  36.4 2.0 %output_weight_gradient.1.after = bf16[1024,1024]{1,0:T(8,128)(2,1)} custom-call(bf16[4096,256]{1,0:T(8,128)(2,1)S(1)} %get-tuple-element.32.u_ref, bf16[128,1024]{1,0:T(8,128)(2,1)S(1)} %pair_sum.5.after.refs_0_, bf16[128,1024]{1,0:T(8,128)(2,1)S(1)} %collective-permute-done.8.refs_1_, bf16[272,256]{1,0:T(8,128)(2,1)S(1)} %sum_with_gain.1.refs_2_.a_ref.x_ref), custom_call_target="tpu_custom_call" | custom-call | flops 10000 | bytes 1000 | tf_op jit(solution)/shard_map/output_weight_gradient/pallas_call | solution.py:598
  38.5 0.8 %collective-permute-start.11 = (bf16[128,512]{1,0:T(8,128)(2,1)S(1)}, bf16[128,512]{1,0:T(8,128)(2,1)S(1)}, u32[]{:S(2)}, u32[]{:S(2)}) collective-permute-start(bf16[128,512]{1,0:T(8,128)(2,1)S(1)} %get-tuple-element.46.after.refs_0_), channel_id=1, source_target_pairs={{0,1},{1,0},{2,3},{3,2},{4,5},{5,4},{6,7},{7,6},{8,9},{9,8},{10,11... | collective-permute-start | bytes 393224 | tf_op jit(solution)/shard_map/ppermute | solution.py:32
  39.5 2.8 %collective-permute-done.6.b_ref.xgot_ref = bf16[272,256]{1,0:T(8,128)(2,1)S(1)} collective-permute-done((bf16[272,256]{1,0:T(8,128)(2,1)S(1)}, bf16[272,256]{1,0:T(8,128)(2,1)S(1)}, u32[]{:S(2)}, u32[]{:S(2)}) %collective-permute-start.6) | collective-permute-done | bytes 139296 | tf_op jit(solution)/shard_map/ppermute | solution.py:32
  42.3 2.3 %collective-permute-start.9 = (bf16[256,256]{1,0:T(8,128)(2,1)S(1)}, bf16[256,256]{1,0:T(8,128)(2,1)S(1)}, u32[]{:S(2)}, u32[]{:S(2)}) collective-permute-start(bf16[256,256]{1,0:T(8,128)(2,1)S(1)} %pair_sum.6.refs_6_.y_ref), channel_id=1, source_target_pairs={{0,4},{4,0},{8,12},{12,8},{1,5},{5,1},{9,13},{13,9},{2,6},{6,2},{1... | collective-permute-start | bytes 393224 | tf_op jit(solution)/shard_map/ppermute | solution.py:32
  44.6 1.4 %collective-permute-start.13 = (bf16[128,256]{1,0:T(8,128)(2,1)S(1)}, bf16[128,256]{1,0:T(8,128)(2,1)S(1)}, u32[]{:S(2)}, u32[]{:S(2)}) collective-permute-start(bf16[128,256]{1,0:T(8,128)(2,1)S(1)} %get-tuple-element.50.refs_2_), channel_id=1, source_target_pairs={{0,1},{1,0},{2,3},{3,2},{4,5},{5,4},{6,7},{7,6},{8,9},{9,8},{10,11... | collective-permute-start | bytes 196616 | tf_op jit(solution)/shard_map/ppermute | solution.py:32
  46.0 1.2 %collective-permute-start.10 = (f32[8,256]{1,0:T(8,128)S(1)}, f32[8,256]{1,0:T(8,128)S(1)}, u32[]{:S(2)}, u32[]{:S(2)}) collective-permute-start(f32[8,256]{1,0:T(8,128)S(1)} %gain_total.1.after.a_ref), channel_id=1, source_target_pairs={{0,2},{1,3},{2,0},{3,1},{4,6},{5,7},{6,4},{7,5},{8,10},{9,11},{10,... | collective-permute-start | bytes 24584 | tf_op jit(solution)/shard_map/ppermute | solution.py:32
  47.3 2.2 %inward_weight_gradients.1 = (bf16[1024,1024]{1,0:T(8,128)(2,1)}, bf16[1024,128]{1,0:T(8,128)(2,1)}, bf16[1024,128]{1,0:T(8,128)(2,1)}) custom-call(bf16[4096,256]{1,0:T(8,128)(2,1)S(1)} %get-tuple-element.32.u_ref, f32[1,4096]{1,0:T(1,128)S(1)} %copy-done.5, bf16[128,512]{1,0:T(8,128)(2,1)S(1)} %get-tuple-element.46.after.refs_0_, ...), custom_call_target="tpu_custom_call" | custom-call | flops 10000 | bytes 1000 | tf_op jit(solution)/shard_map/inward_weight_gradients/pallas_call | solution.py:581
  49.5 0.3 collective-permute-start.14
  49.8 0.9 %collective-permute-done.14.gain_other_ref = f32[8,256]{1,0:T(8,128)S(1)} collective-permute-done((f32[8,256]{1,0:T(8,128)S(1)}, f32[8,256]{1,0:T(8,128)S(1)}, u32[]{:S(2)}, u32[]{:S(2)}) %collective-permute-start.14) | collective-permute-done | bytes 8224 | tf_op jit(solution)/shard_map/ppermute | solution.py:32
  50.7 1.0 %section_results.1 = (bf16[256,256]{1,0:T(8,128)(2,1)}, bf16[256,256]{1,0:T(8,128)(2,1)}, f32[1,4096]{1,0:T(1,128)}) custom-call(f32[256,256]{1,0:T(8,128)S(1)} %get-tuple-element.38.after.fbase_ref, bf16[256,256]{1,0:T(8,128)(2,1)S(1)} %pair_sum.6.refs_6_.y_ref, bf16[256,256]{1,0:T(8,128)(2,1)S(1)} %collective-permute-done.9.ygot_ref, ...), custom_call_target="tpu_custom_call" | custom-call | flops 10000 | bytes 1000 | tf_op jit(solution)/shard_map/section_results/pallas_call | solution.py:636
  (34 shorter events, 0.8 us)
Async XLA Ops:
  1.6 12.2 %collective-permute-start = (bf16[256,256]{1,0:T(8,128)(2,1)S(1)}, bf16[256,256]{1,0:T(8,128)(2,1)S(1)}, u32[]{:S(2)}, u32[]{:S(2)}) collective-permute-start(bf16[256,256]{1,0:T(8,128)(2,1)S(1)} %select_bitcast_fusion), channel_id=1, source_target_pairs={{0,16},{16,0},{1,17},{17,1},{2,18},{18,2},{3,19},{19,3},{4,20},{20... | collective-permute-start | bytes 393224 | tf_op jit(solution)/shard_map/ppermute | solution.py:32
  2.9 11.0 %copy-start = (bf16[1,256,256]{2,1,0:T(8,128)(2,1)S(1)}, bf16[1,256,256]{2,1,0:T(8,128)(2,1)}, u32[]{:S(2)}) copy-start(bf16[1,256,256]{2,1,0:T(8,128)(2,1)} %param.17) | copy-start | bytes 393220
  2.9 11.0 %copy-start.1 = (bf16[256,256]{1,0:T(8,128)(2,1)S(1)}, bf16[256,256]{1,0:T(8,128)(2,1)}, u32[]{:S(2)}) copy-start(bf16[256,256]{1,0:T(8,128)(2,1)} %loss_ref.3) | copy-start | bytes 393220
  2.9 11.0 %copy-start.3 = (f32[256,128]{1,0:T(8,128)S(1)}, f32[256,128]{1,0:T(8,128)}, u32[]{:S(2)}) copy-start(f32[256,128]{1,0:T(8,128)} %constant.12.clone.cos_ref) | copy-start | bytes 393220
  2.9 11.0 %copy-start.4 = (f32[256,128]{1,0:T(8,128)S(1)}, f32[256,128]{1,0:T(8,128)}, u32[]{:S(2)}) copy-start(f32[256,128]{1,0:T(8,128)} %constant.13.clone.sin_ref) | copy-start | bytes 393220
  13.8 6.4 %copy-start.2 = (bf16[256,256]{1,0:T(8,128)(2,1)S(1)}, bf16[256,256]{1,0:T(8,128)(2,1)}, u32[]{:S(2)}) copy-start(bf16[256,256]{1,0:T(8,128)(2,1)} %new_ref.3) | copy-start | bytes 393220
  19.1 4.5 %collective-permute-start.1 = (bf16[256,1280]{1,0:T(8,128)(2,1)S(1)}, bf16[256,1280]{1,0:T(8,128)(2,1)S(1)}, u32[]{:S(2)}, u32[]{:S(2)}) collective-permute-start(bf16[256,1280]{1,0:T(8,128)(2,1)S(1)} %get-tuple-element.41.inner_ref), channel_id=1, source_target_pairs={{0,1},{1,0},{2,3},{3,2},{4,5},{5,4},{6,7},{7,6},{8,9},{9,8},{10,11... | collective-permute-start | bytes 1966088 | tf_op jit(solution)/shard_map/ppermute | solution.py:32
  20.1 2.1 %collective-permute-start.2 = (bf16[128,1024]{1,0:T(8,128)(2,1)S(1)}, bf16[128,1024]{1,0:T(8,128)(2,1)S(1)}, u32[]{:S(2)}, u32[]{:S(2)}) collective-permute-start(bf16[128,1024]{1,0:T(8,128)(2,1)S(1)} %get-tuple-element.43), channel_id=1, source_target_pairs={{0,1},{1,0},{2,3},{3,2},{4,5},{5,4},{6,7},{7,6},{8,9},{9,8},{10,11... | collective-permute-start | bytes 786440 | tf_op jit(solution)/shard_map/ppermute | solution.py:32
  22.2 7.6 %collective-permute-start.5 = (bf16[128,1024]{1,0:T(8,128)(2,1)S(1)}, bf16[128,1024]{1,0:T(8,128)(2,1)S(1)}, u32[]{:S(2)}, u32[]{:S(2)}) collective-permute-start(bf16[128,1024]{1,0:T(8,128)(2,1)S(1)} %pair_sum.4.after.a_ref), channel_id=1, source_target_pairs={{0,2},{1,3},{2,0},{3,1},{4,6},{5,7},{6,4},{7,5},{8,10},{9,11},{10,... | collective-permute-start | bytes 786440 | tf_op jit(solution)/shard_map/ppermute | solution.py:32
  25.4 13.1 %collective-permute-start.7 = (bf16[128,1280]{1,0:T(8,128)(2,1)S(1)}, bf16[128,1280]{1,0:T(8,128)(2,1)S(1)}, u32[]{:S(2)}, u32[]{:S(2)}) collective-permute-start(bf16[128,1280]{1,0:T(8,128)(2,1)S(1)} %get-tuple-element.44.after.a_ref), channel_id=1, source_target_pairs={{0,2},{1,3},{2,0},{3,1},{4,6},{5,7},{6,4},{7,5},{8,10},{9,11},{10,... | collective-permute-start | bytes 983048 | tf_op jit(solution)/shard_map/ppermute | solution.py:32
  25.7 7.5 %collective-permute-start.4 = (bf16[272,256]{1,0:T(8,128)(2,1)S(1)}, bf16[272,256]{1,0:T(8,128)(2,1)S(1)}, u32[]{:S(2)}, u32[]{:S(2)}) collective-permute-start(bf16[272,256]{1,0:T(8,128)(2,1)S(1)} %get-tuple-element.45.a_ref), channel_id=1, source_target_pairs={{0,8},{4,12},{8,0},{12,4},{1,9},{5,13},{9,1},{13,5},{2,10},{6,14},... | collective-permute-start | bytes 417800 | tf_op jit(solution)/shard_map/ppermute | solution.py:32
  29.9 6.6 %collective-permute-start.8 = (bf16[128,1024]{1,0:T(8,128)(2,1)S(1)}, bf16[128,1024]{1,0:T(8,128)(2,1)S(1)}, u32[]{:S(2)}, u32[]{:S(2)}) collective-permute-start(bf16[128,1024]{1,0:T(8,128)(2,1)S(1)} %pair_sum.5.after.refs_0_), channel_id=1, source_target_pairs={{0,1},{1,0},{2,3},{3,2},{4,5},{5,4},{6,7},{7,6},{8,9},{9,8},{10,11... | collective-permute-start | bytes 786440 | tf_op jit(solution)/shard_map/ppermute | solution.py:32
  32.0 10.3 %collective-permute-start.3 = (bf16[288,256]{1,0:T(8,128)(2,1)S(1)}, bf16[288,256]{1,0:T(8,128)(2,1)S(1)}, u32[]{:S(2)}, u32[]{:S(2)}) collective-permute-start(bf16[288,256]{1,0:T(8,128)(2,1)S(1)} %attention_forward.1.after.a_ref), channel_id=1, source_target_pairs={{0,8},{4,12},{8,0},{12,4},{1,9},{5,13},{9,1},{13,5},{2,10},{6,14},... | collective-permute-start | bytes 442376 | tf_op jit(solution)/shard_map/ppermute | solution.py:32
  33.2 9.1 %collective-permute-start.6 = (bf16[272,256]{1,0:T(8,128)(2,1)S(1)}, bf16[272,256]{1,0:T(8,128)(2,1)S(1)}, u32[]{:S(2)}, u32[]{:S(2)}) collective-permute-start(bf16[272,256]{1,0:T(8,128)(2,1)S(1)} %sum_with_gain.1.refs_2_.a_ref.x_ref), channel_id=1, source_target_pairs={{0,4},{4,0},{8,12},{12,8},{1,5},{5,1},{9,13},{13,9},{2,6},{6,2},{1... | collective-permute-start | bytes 417800 | tf_op jit(solution)/shard_map/ppermute | solution.py:32
  38.5 8.8 %copy-start.5 = (f32[1,4096]{1,0:T(1,128)S(1)}, f32[1,4096]{1,0:T(1,128)}, u32[]{:S(2)}) copy-start(f32[1,4096]{1,0:T(1,128)} %gain_ref.1) | copy-start | bytes 49156
  38.5 8.7 %collective-permute-start.11 = (bf16[128,512]{1,0:T(8,128)(2,1)S(1)}, bf16[128,512]{1,0:T(8,128)(2,1)S(1)}, u32[]{:S(2)}, u32[]{:S(2)}) collective-permute-start(bf16[128,512]{1,0:T(8,128)(2,1)S(1)} %get-tuple-element.46.after.refs_0_), channel_id=1, source_target_pairs={{0,1},{1,0},{2,3},{3,2},{4,5},{5,4},{6,7},{7,6},{8,9},{9,8},{10,11... | collective-permute-start | bytes 393224 | tf_op jit(solution)/shard_map/ppermute | solution.py:32
  39.4 7.9 %collective-permute-start.12 = (bf16[128,512]{1,0:T(8,128)(2,1)S(1)}, bf16[128,512]{1,0:T(8,128)(2,1)S(1)}, u32[]{:S(2)}, u32[]{:S(2)}) collective-permute-start(bf16[128,512]{1,0:T(8,128)(2,1)S(1)} %get-tuple-element.49.refs_1_), channel_id=1, source_target_pairs={{0,1},{1,0},{2,3},{3,2},{4,5},{5,4},{6,7},{7,6},{8,9},{9,8},{10,11... | collective-permute-start | bytes 393224 | tf_op jit(solution)/shard_map/ppermute | solution.py:32
  42.3 7.5 %collective-permute-start.9 = (bf16[256,256]{1,0:T(8,128)(2,1)S(1)}, bf16[256,256]{1,0:T(8,128)(2,1)S(1)}, u32[]{:S(2)}, u32[]{:S(2)}) collective-permute-start(bf16[256,256]{1,0:T(8,128)(2,1)S(1)} %pair_sum.6.refs_6_.y_ref), channel_id=1, source_target_pairs={{0,4},{4,0},{8,12},{12,8},{1,5},{5,1},{9,13},{13,9},{2,6},{6,2},{1... | collective-permute-start | bytes 393224 | tf_op jit(solution)/shard_map/ppermute | solution.py:32
  44.6 2.6 %collective-permute-start.13 = (bf16[128,256]{1,0:T(8,128)(2,1)S(1)}, bf16[128,256]{1,0:T(8,128)(2,1)S(1)}, u32[]{:S(2)}, u32[]{:S(2)}) collective-permute-start(bf16[128,256]{1,0:T(8,128)(2,1)S(1)} %get-tuple-element.50.refs_2_), channel_id=1, source_target_pairs={{0,1},{1,0},{2,3},{3,2},{4,5},{5,4},{6,7},{7,6},{8,9},{9,8},{10,11... | collective-permute-start | bytes 196616 | tf_op jit(solution)/shard_map/ppermute | solution.py:32
  46.0 3.5 %collective-permute-start.10 = (f32[8,256]{1,0:T(8,128)S(1)}, f32[8,256]{1,0:T(8,128)S(1)}, u32[]{:S(2)}, u32[]{:S(2)}) collective-permute-start(f32[8,256]{1,0:T(8,128)S(1)} %gain_total.1.after.a_ref), channel_id=1, source_target_pairs={{0,2},{1,3},{2,0},{3,1},{4,6},{5,7},{6,4},{7,5},{8,10},{9,11},{10,... | collective-permute-start | bytes 24584 | tf_op jit(solution)/shard_map/ppermute | solution.py:32
  49.5 1.2 %collective-permute-start.14 = (f32[8,256]{1,0:T(8,128)S(1)}, f32[8,256]{1,0:T(8,128)S(1)}, u32[]{:S(2)}, u32[]{:S(2)}) collective-permute-start(f32[8,256]{1,0:T(8,128)S(1)} %pair_sum.7.gain_ref), channel_id=1, source_target_pairs={{0,1},{1,0},{2,3},{3,2},{4,5},{5,4},{6,7},{7,6},{8,9},{9,8},{10,11... | collective-permute-start | bytes 24584 | tf_op jit(solution)/shard_map/ppermute | solution.py:32

commit v8 on v7

--- a/solution.py
+++ b/solution.py
@@ -362,9 +362,9 @@
     )(back, loss, returned, new, arrived, basis, turned, inv, after)
 
 
-def forward_kernel(
-    new_ref, sent_ref, turned_ref, m_ref, o_ref, cos_ref, sin_ref, after,
-    y_ref, q, k, v1, scores, low, mixed, heads,
+def scores_kernel(
+    new_ref, sent_ref, turned_ref, m_ref, cos_ref, sin_ref, after,
+    low_ref, v1_ref, q, k, scores,
 ):
     length, rank = new_ref.shape
     wide = turned_ref.shape[1]
@@ -377,10 +377,36 @@
             part = decoded[:, side : side + HD]
             square = square + part * part
     inv = inverse_root(jnp.sum(square, axis=1, keepdims=True), wide)
-    project_heads(coeffs, inv, m_ref, cos_ref[...], sin_ref[...], q, k, v1)
+    project_heads(coeffs, inv, m_ref, cos_ref[...], sin_ref[...], q, k, v1_ref)
     scores[...] = nt(q[...], k[...])
-    exps_of(scores, None, low, length)
-    mixed[...] = nn(low[...], v1[...])
+    exps_of(scores, None, low_ref, length)
+
+
+def forward_scores(new, sent, turned, m2, cosine, sine, count, after):
+    length, rank = new.shape
+    stack = count * length
+    return pl.pallas_call(
+        scores_kernel,
+        in_specs=vmem(6) + [pl.BlockSpec(memory_space=pl.ANY)],
+        out_specs=vmem(2),
+        out_shape=[
+            jax.ShapeDtypeStruct((stack, length), BF),
+            jax.ShapeDtypeStruct((length, 2 * HD), BF),
+        ],
+        scratch_shapes=[
+            pltpu.VMEM((stack, HD), BF),
+            pltpu.VMEM((length, HD), BF),
+            pltpu.VMEM((stack, length), F32),
+        ],
+        compiler_params=pltpu.CompilerParams(vmem_limit_bytes=VMEM_BYTES),
+        cost_estimate=cost(10**4, 10**3),
+        name="forward_scores",
+    )(new, sent, turned, m2, cosine, sine, after)
+
+
+def output_kernel(low_ref, v1_ref, o_ref, after, y_ref, mixed, heads):
+    length = v1_ref.shape[0]
+    mixed[...] = nn(low_ref[...], v1_ref[...])
     for h in range(heads.shape[1] // HD):
         at = slice(h * length, (h + 1) * length)
         heads[:, h * HD : (h + 1) * HD] = (mixed[at, :HD] / mixed[at, HD:]).astype(BF)
@@ -388,28 +414,22 @@
     y_ref[length:, :] = jnp.zeros_like(y_ref[length:, :])
 
 
-def forward(new, sent, turned, m2, o2, cosine, sine, after):
-    length, rank = new.shape
-    ne = o2.shape[0]
-    stack = ne // HD * length
-    return pl.pallas_call(
-        forward_kernel,
-        in_specs=vmem(7) + [pl.BlockSpec(memory_space=pl.ANY)],
+def forward_output(low, v1, o2, after):
+    length = v1.shape[0]
+    ne, rank = o2.shape
+    return pl.pallas_call(
+        output_kernel,
+        in_specs=vmem(3) + [pl.BlockSpec(memory_space=pl.ANY)],
         out_specs=pl.BlockSpec(memory_space=pltpu.VMEM),
         out_shape=jax.ShapeDtypeStruct((length + 32, rank), BF),
         scratch_shapes=[
-            pltpu.VMEM((stack, HD), BF),
-            pltpu.VMEM((length, HD), BF),
-            pltpu.VMEM((length, 2 * HD), BF),
-            pltpu.VMEM((stack, length), F32),
-            pltpu.VMEM((stack, length), BF),
-            pltpu.VMEM((stack, 2 * HD), F32),
+            pltpu.VMEM((low.shape[0], 2 * HD), F32),
             pltpu.VMEM((length, ne), BF),
         ],
         compiler_params=pltpu.CompilerParams(vmem_limit_bytes=VMEM_BYTES),
         cost_estimate=cost(10**4, 10**3),
-        name="attention_forward",
-    )(new, sent, turned, m2, o2, cosine, sine, after)
+        name="forward_output",
+    )(low, v1, o2, after)
 
 
 def write_split(ref, value):
@@ -672,25 +692,28 @@
     )
     out_got = swap(out_give, "dp", 1)
     inner_got = swap(inner, "dp", 1)
-    base, unit, fbase = bases(
-        back, loss_grad, returned, new_coeffs, arrived, basis, turned, inv, out_keep
+    low, values = forward_scores(
+        new_coeffs, arrived, turned, m2, cosine, sine, wo.shape[0] // HD, out_keep
     )
-    out_pair = add_after(out_keep, out_got, fbase)
+    out_pair = add_after(out_keep, out_got, values)
     out_got = swap(out_pair, "dp", 2)
     pair, x = gain_part(basis, wq, narrow, inner, inner_got, x, out_pair)
     pair_got = swap(pair, "dp", 2)
     x_got = swap(x, "tensor", 2)
-    y = forward(new_coeffs, arrived, turned, m2, o2, cosine, sine, pair)
+    y = forward_output(low, values, o2, pair)
     y_got = swap(y, "tensor", 2)
-    out_own = add_after(out_pair, out_got, y)
-    out_other = swap(out_own, "dp", 1)
-    x = merge(x, x_got, out_own)
+    ne = wo.shape[0]
+    out_own = own_pieces(out_pair, out_got, (ne // 2, ne - ne // 2), y)
+    out_other = [swap(piece, "dp", 1) for piece in out_own]
+    grad_o = outward_grad(basis, out_own, out_other, y)
+    x = merge(x, x_got, *in_hbm((grad_o,)))
     x_got = swap(x, "tensor", 1)
-    grad_o = outward_grad(basis, [out_own], [out_other], x)
-    sizes = (nq // 2, nq - nq // 2, nk + nv)
-    own = own_pieces(pair, pair_got, sizes, *in_hbm((grad_o,)))
+    own = own_pieces(pair, pair_got, (nq // 2, nq - nq // 2, nk + nv), x)
     other = [swap(piece, "dp", 1) for piece in own]
-    gain = gain_total(x, x_got, own[0])
+    base, unit, fbase = bases(
+        back, loss_grad, returned, new_coeffs, arrived, basis, turned, inv, own[0]
+    )
+    gain = gain_total(x, x_got, base)
     gain_got = swap(gain, "dp", 2)
     y = add_after(y, y_got, gain, rows=back.shape[0])
     y_got = swap(y, "tensor", 1)

time: 51.9 us -> 52.9 us (1.019)
  the two profiles are of different devices: /device:TPU:17 before, /device:TPU:0 now
where the time goes in v8:
time: 52.9 us; the launch traced here: 52.4 us
  Pallas kernels  28.7 us (54%)
  starting transfers between devices  15.6 us (29%)
  waiting for transfers between devices  6.28 us (12%)
  other arithmetic  0.93 us (2%)
  between operations  0.83 us (2%)
    ppermute x16, starting transfers between devices, swap(): return lax.ppermute(x, axis, [(i, i ^ bit) for i in range(devices)])  15.6 us
    pallas_call x1, Pallas kernels, project(): pl.pallas_call(project_kernel, in_specs=[pl.BlockSpec(memory_space=pltpu....  10.9 us
    ppermute x16, waiting for transfers between devices, swap(): return lax.ppermute(x, axis, [(i, i ^ bit) for i in range(devices)])  6.28 us
    pallas_call x1, Pallas kernels, backward(): pl.pallas_call(backward_kernel, in_specs=vmem(8), out_specs=vmem(4), out_...  5.2 us
    pallas_call x1, Pallas kernels, forward_scores(): pl.pallas_call(scores_kernel, in_specs=vmem(6) + [pl.BlockSpec(memory_spa...  2.67 us
    pallas_call x1, Pallas kernels, inward_grads(): pl.pallas_call(functools.partial(inward_kernel, len(own)), grid=(STEPS,),...  2.21 us
    pallas_call x1, Pallas kernels, outward_grad(): pl.pallas_call(functools.partial(outward_kernel, len(own)), grid=(STEPS,)...  2.01 us
    pallas_call x1, Pallas kernels, gain_part(): pl.pallas_call(gain_kernel, in_specs=vmem(6) + [pl.BlockSpec(memory_space...  1.85 us
  transfers between devices with their start and end apart: 16, of which 4 were waited for; matrix products, arithmetic and copies ran while one was open for 0% of the time, Pallas kernels for 43%

profile of v8, /device:TPU:0, one launch (start us, length us, event | category | flops | bytes accessed | tf_op | source)
XLA Modules:
  0.0 52.4 jit_solution(18176062958097965454)
XLA Ops:
  0.6 0.9 %select_bitcast_fusion = bf16[256,256]{1,0:T(8,128)(2,1)S(1)} fusion(bf16[1,256,256]{2,1,0:T(8,128)(2,1)} %param.15, bf16[1,256,256]{2,1,0:T(8,128)(2,1)} %param.16, pred[]{:T(512)S(6)} %eq.3), kind=kLoop, calls=%fused_computation | loop fusion | flops 65536 | bytes 393217 | tf_op jit(solution)/shard_map/jit(_where)/select_n | solution.py:39
  1.6 3.0 %collective-permute-start = (bf16[256,256]{1,0:T(8,128)(2,1)S(1)}, bf16[256,256]{1,0:T(8,128)(2,1)S(1)}, u32[]{:S(2)}, u32[]{:S(2)}) collective-permute-start(bf16[256,256]{1,0:T(8,128)(2,1)S(1)} %select_bitcast_fusion), channel_id=1, source_target_pairs={{0,16},{16,0},{1,17},{17,1},{2,18},{18,2},{3,19},{19,3},{4,20},{20... | collective-permute-start | bytes 393224 | tf_op jit(solution)/shard_map/ppermute | solution.py:32
  4.6 10.9 %project_weights.1 = (bf16[512,1280]{1,0:T(8,128)(2,1)S(1)}, bf16[1024,256]{1,0:T(8,128)(2,1)S(1)}, f32[256,128]{1,0:T(8,128)S(1)}, bf16[4096,256]{1,0:T(8,128)(...) custom-call(bf16[256,256]{1,0:T(8,128)(2,1)} %bitcast.13, ...), custom_call_target="tpu_custom_call" | custom-call | flops 6000000000 | bytes 20000000 | tf_op jit(solution)/shard_map/project_weights/pallas_call | solution.py:180
  15.6 5.2 %attention_backward.1 = (bf16[256,1280]{1,0:T(8,128)(2,1)S(1)}, bf16[128,1024]{1,0:T(8,128)(2,1)S(1)}, bf16[128,1024]{1,0:T(8,128)(2,1)S(1)}, bf16[256,256]{1,0:T(8,128)(2,1)S(1)}) custom-call(bf16[256,256]{1,0:T(8,128)(2,1)S(1)} %bitcast.14, bf16[256,256]{1,0:T(8,128)(2,1)S(1)} %copy-done.1, ...), custom_call_target="tpu_custom_call" | custom-call | flops 10000 | bytes 1000 | tf_op jit(solution)/shard_map/attention_backward/pallas_call | solution.py:302
  20.9 0.5 collective-permute-start.2
  21.4 2.7 %forward_scores.1 = (bf16[2048,256]{1,0:T(8,128)(2,1)S(1)}, bf16[256,256]{1,0:T(8,128)(2,1)S(1)}) custom-call(bf16[256,256]{1,0:T(8,128)(2,1)S(1)} %copy-done.2, bf16[256,256]{1,0:T(8,128)(2,1)S(1)} %collective-permute-done.sent_ref.returned_ref.arrived_ref, bf16[256,4096]{1,0:T(8,128)(2,1)S(1)} %get-tuple-element.37.turned_ref, ...), custom_call_target="tpu_custom_call" | custom-call | flops 10000 | bytes 1000 | tf_op jit(solution)/shard_map/forward_scores/pallas_call | solution.py:388
  24.1 1.6 %collective-permute-start.5 = (bf16[128,1024]{1,0:T(8,128)(2,1)S(1)}, bf16[128,1024]{1,0:T(8,128)(2,1)S(1)}, u32[]{:S(2)}, u32[]{:S(2)}) collective-permute-start(bf16[128,1024]{1,0:T(8,128)(2,1)S(1)} %pair_sum.3.after.a_ref), channel_id=1, source_target_pairs={{0,2},{1,3},{2,0},{3,1},{4,6},{5,7},{6,4},{7,5},{8,10},{9,11},{10,... | collective-permute-start | bytes 786440 | tf_op jit(solution)/shard_map/ppermute | solution.py:32
  25.7 1.8 %pair_sum_and_gain_gradient.1 = (bf16[128,1280]{1,0:T(8,128)(2,1)S(1)}, bf16[272,256]{1,0:T(8,128)(2,1)S(1)}) custom-call(bf16[4096,256]{1,0:T(8,128)(2,1)S(1)} %get-tuple-element.36.u_ref, bf16[4096,1024]{1,0:T(8,128)(2,1)S(1)} %get-tuple-element.39.wq_ref, bf16[4096,256]{1,0:T(8,128)(2,1)S(1)} %get-tuple-element.40.narrow_ref, ...), custom_call_target="tpu_custom_call" | custom-call | flops 10000 | bytes 1000 | tf_op jit(solution)/shard_map/pair_sum_and_gain_gradient/pallas_call | solution.py:478
  27.6 0.6 %collective-permute-start.3 = (bf16[128,1280]{1,0:T(8,128)(2,1)S(1)}, bf16[128,1280]{1,0:T(8,128)(2,1)S(1)}, u32[]{:S(2)}, u32[]{:S(2)}) collective-permute-start(bf16[128,1280]{1,0:T(8,128)(2,1)S(1)} %get-tuple-element.48.after.a_ref), channel_id=1, source_target_pairs={{0,2},{1,3},{2,0},{3,1},{4,6},{5,7},{6,4},{7,5},{8,10},{9,11},{10,... | collective-permute-start | bytes 983048 | tf_op jit(solution)/shard_map/ppermute | solution.py:32
  28.1 2.6 %collective-permute-start.4 = (bf16[272,256]{1,0:T(8,128)(2,1)S(1)}, bf16[272,256]{1,0:T(8,128)(2,1)S(1)}, u32[]{:S(2)}, u32[]{:S(2)}) collective-permute-start(bf16[272,256]{1,0:T(8,128)(2,1)S(1)} %get-tuple-element.49.a_ref), channel_id=1, source_target_pairs={{0,8},{4,12},{8,0},{12,4},{1,9},{5,13},{9,1},{13,5},{2,10},{6,14},... | collective-permute-start | bytes 417800 | tf_op jit(solution)/shard_map/ppermute | solution.py:32
  30.7 0.8 %forward_output.1.after.refs_4_.a_ref = bf16[288,256]{1,0:T(8,128)(2,1)S(1)} custom-call(bf16[2048,256]{1,0:T(8,128)(2,1)S(1)} %get-tuple-element.50.low_ref, bf16[256,256]{1,0:T(8,128)(2,1)S(1)} %get-tuple-element.47.after.v1_ref, bf16[1024,256]{1,0:T(8,128)(2,1)S(1)} %get-tuple-element.42.o_ref, bf16[128,1280]{1,0:T(8,128)(2,1)S(1)} %get-tuple-element.48.after.a_ref), custom_call_target="tpu_custom_call" | custom-call | flops 10000 | bytes 1000 | tf_op jit(solution)/shard_map/forward_output/pallas_call | solution.py:420
  31.6 1.8 %collective-permute-done.5.b_ref = bf16[128,1024]{1,0:T(8,128)(2,1)S(1)} collective-permute-done((bf16[128,1024]{1,0:T(8,128)(2,1)S(1)}, bf16[128,1024]{1,0:T(8,128)(2,1)S(1)}, u32[]{:S(2)}, u32[]{:S(2)}) %collective-permute-start.5) | collective-permute-done | bytes 262176 | tf_op jit(solution)/shard_map/ppermute | solution.py:32
  33.5 0.5 collective-permute-start.7
  34.0 2.6 %collective-permute-start.8 = (bf16[288,256]{1,0:T(8,128)(2,1)S(1)}, bf16[288,256]{1,0:T(8,128)(2,1)S(1)}, u32[]{:S(2)}, u32[]{:S(2)}) collective-permute-start(bf16[288,256]{1,0:T(8,128)(2,1)S(1)} %forward_output.1.after.refs_4_.a_ref), channel_id=1, source_target_pairs={{0,8},{4,12},{8,0},{12,4},{1,9},{5,13},{9,1},{13,5},{2,10},{6,14},... | collective-permute-start | bytes 442376 | tf_op jit(solution)/shard_map/ppermute | solution.py:32
  36.6 2.0 %output_weight_gradient.1.after = bf16[1024,1024]{1,0:T(8,128)(2,1)} custom-call(bf16[4096,256]{1,0:T(8,128)(2,1)S(1)} %get-tuple-element.36.u_ref, bf16[128,512]{1,0:T(8,128)(2,1)S(1)} %get-tuple-element.51.refs_0_, bf16[128,512]{1,0:T(8,128)(2,1)S(1)} %get-tuple-element.52.refs_1_, bf16[128,512]{1,0:T(8,128)(2,1)S(1)} %collective-permute-done.6.refs_2_, ...), custom_call_target="tpu_custom_call" | custom-call | flops 10000 | bytes 1000 | tf_op jit(solution)/shard_map/output_weight_gradient/pallas_call | solution.py:618
  38.6 1.6 %collective-permute-start.9 = (bf16[272,256]{1,0:T(8,128)(2,1)S(1)}, bf16[272,256]{1,0:T(8,128)(2,1)S(1)}, u32[]{:S(2)}, u32[]{:S(2)}) collective-permute-start(bf16[272,256]{1,0:T(8,128)(2,1)S(1)} %sum_with_gain.1.after.a_ref.x_ref), channel_id=1, source_target_pairs={{0,4},{4,0},{8,12},{12,8},{1,5},{5,1},{9,13},{13,9},{2,6},{6,2},{1... | collective-permute-start | bytes 417800 | tf_op jit(solution)/shard_map/ppermute | solution.py:32
  40.5 0.5 collective-permute-start.12
  40.9 1.7 %encoded_again.1 = (f32[256,256]{1,0:T(8,128)S(1)}, f32[256,256]{1,0:T(8,128)S(1)}, f32[256,256]{1,0:T(8,128)S(1)}) custom-call(bf16[256,256]{1,0:T(8,128)(2,1)S(1)} %bitcast.15, bf16[256,256]{1,0:T(8,128)(2,1)S(1)} %copy-done.1, bf16[256,256]{1,0:T(8,128)(2,1)S(1)} %collective-permute-done.sent_ref.returned_ref.arrived_ref, bf16[256,256]{1,0:T(8,128)(2,1)S(1)} %copy-done.2, ...), custom_call_target="tpu_custom_call" | custom-call | flops 10000 | bytes 1000 | tf_op jit(solution)/shard_map/encoded_again/pallas_call | solution.py:353
  42.7 3.5 %collective-permute-done.9.b_ref.xgot_ref = bf16[272,256]{1,0:T(8,128)(2,1)S(1)} collective-permute-done((bf16[272,256]{1,0:T(8,128)(2,1)S(1)}, bf16[272,256]{1,0:T(8,128)(2,1)S(1)}, u32[]{:S(2)}, u32[]{:S(2)}) %collective-permute-start.9) | collective-permute-done | bytes 139296 | tf_op jit(solution)/shard_map/ppermute | solution.py:32
  46.3 1.6 %collective-permute-start.11 = (f32[8,256]{1,0:T(8,128)S(1)}, f32[8,256]{1,0:T(8,128)S(1)}, u32[]{:S(2)}, u32[]{:S(2)}) collective-permute-start(f32[8,256]{1,0:T(8,128)S(1)} %gain_total.1.after.a_ref), channel_id=1, source_target_pairs={{0,2},{1,3},{2,0},{3,1},{4,6},{5,7},{6,4},{7,5},{8,10},{9,11},{10,... | collective-permute-start | bytes 24584 | tf_op jit(solution)/shard_map/ppermute | solution.py:32
  47.9 2.2 %inward_weight_gradients.1 = (bf16[1024,1024]{1,0:T(8,128)(2,1)}, bf16[1024,128]{1,0:T(8,128)(2,1)}, bf16[1024,128]{1,0:T(8,128)(2,1)}) custom-call(bf16[4096,256]{1,0:T(8,128)(2,1)S(1)} %get-tuple-element.36.u_ref, f32[1,4096]{1,0:T(1,128)S(1)} %copy-done.5, bf16[128,512]{1,0:T(8,128)(2,1)S(1)} %get-tuple-element.53.after.refs_0_, ...), custom_call_target="tpu_custom_call" | custom-call | flops 10000 | bytes 1000 | tf_op jit(solution)/shard_map/inward_weight_gradients/pallas_call | solution.py:601
  50.2 0.2 collective-permute-start.15
  50.4 0.8 %collective-permute-done.10.ygot_ref = bf16[256,256]{1,0:T(8,128)(2,1)S(1)} collective-permute-done((bf16[256,256]{1,0:T(8,128)(2,1)S(1)}, bf16[256,256]{1,0:T(8,128)(2,1)S(1)}, u32[]{:S(2)}, u32[]{:S(2)}) %collective-permute-start.10) | collective-permute-done | bytes 131104 | tf_op jit(solution)/shard_map/ppermute | solution.py:32
  51.4 1.0 %section_results.1 = (bf16[256,256]{1,0:T(8,128)(2,1)}, bf16[256,256]{1,0:T(8,128)(2,1)}, f32[1,4096]{1,0:T(1,128)}) custom-call(f32[256,256]{1,0:T(8,128)S(1)} %get-tuple-element.54.fbase_ref, bf16[256,256]{1,0:T(8,128)(2,1)S(1)} %pair_sum.4.refs_6_.y_ref, bf16[256,256]{1,0:T(8,128)(2,1)S(1)} %collective-permute-done.10.ygot_ref, ...), custom_call_target="tpu_custom_call" | custom-call | flops 10000 | bytes 1000 | tf_op jit(solution)/shard_map/section_results/pallas_call | solution.py:656
  (37 shorter events, 0.9 us)
Async XLA Ops:
  1.6 14.0 %collective-permute-start = (bf16[256,256]{1,0:T(8,128)(2,1)S(1)}, bf16[256,256]{1,0:T(8,128)(2,1)S(1)}, u32[]{:S(2)}, u32[]{:S(2)}) collective-permute-start(bf16[256,256]{1,0:T(8,128)(2,1)S(1)} %select_bitcast_fusion), channel_id=1, source_target_pairs={{0,16},{16,0},{1,17},{17,1},{2,18},{18,2},{3,19},{19,3},{4,20},{20... | collective-permute-start | bytes 393224 | tf_op jit(solution)/shard_map/ppermute | solution.py:32
  4.6 11.0 %copy-start = (bf16[1,256,256]{2,1,0:T(8,128)(2,1)S(1)}, bf16[1,256,256]{2,1,0:T(8,128)(2,1)}, u32[]{:S(2)}) copy-start(bf16[1,256,256]{2,1,0:T(8,128)(2,1)} %param.17) | copy-start | bytes 393220
  4.6 11.0 %copy-start.1 = (bf16[256,256]{1,0:T(8,128)(2,1)S(1)}, bf16[256,256]{1,0:T(8,128)(2,1)}, u32[]{:S(2)}) copy-start(bf16[256,256]{1,0:T(8,128)(2,1)} %loss_ref.3) | copy-start | bytes 393220
  4.6 11.0 %copy-start.3 = (f32[256,128]{1,0:T(8,128)S(1)}, f32[256,128]{1,0:T(8,128)}, u32[]{:S(2)}) copy-start(f32[256,128]{1,0:T(8,128)} %constant.13.clone.sin_ref) | copy-start | bytes 393220
  4.6 11.0 %copy-start.4 = (f32[256,128]{1,0:T(8,128)S(1)}, f32[256,128]{1,0:T(8,128)}, u32[]{:S(2)}) copy-start(f32[256,128]{1,0:T(8,128)} %constant.12.clone.cos_ref) | copy-start | bytes 393220
  15.5 5.8 %copy-start.2 = (bf16[256,256]{1,0:T(8,128)(2,1)S(1)}, bf16[256,256]{1,0:T(8,128)(2,1)}, u32[]{:S(2)}) copy-start(bf16[256,256]{1,0:T(8,128)(2,1)} %new_ref.3) | copy-start | bytes 393220
  20.8 4.9 %collective-permute-start.1 = (bf16[256,1280]{1,0:T(8,128)(2,1)S(1)}, bf16[256,1280]{1,0:T(8,128)(2,1)S(1)}, u32[]{:S(2)}, u32[]{:S(2)}) collective-permute-start(bf16[256,1280]{1,0:T(8,128)(2,1)S(1)} %get-tuple-element.43.inner_ref), channel_id=1, source_target_pairs={{0,1},{1,0},{2,3},{3,2},{4,5},{5,4},{6,7},{7,6},{8,9},{9,8},{10,11... | collective-permute-start | bytes 1966088 | tf_op jit(solution)/shard_map/ppermute | solution.py:32
  20.9 3.2 %collective-permute-start.2 = (bf16[128,1024]{1,0:T(8,128)(2,1)S(1)}, bf16[128,1024]{1,0:T(8,128)(2,1)S(1)}, u32[]{:S(2)}, u32[]{:S(2)}) collective-permute-start(bf16[128,1024]{1,0:T(8,128)(2,1)S(1)} %get-tuple-element.46), channel_id=1, source_target_pairs={{0,1},{1,0},{2,3},{3,2},{4,5},{5,4},{6,7},{7,6},{8,9},{9,8},{10,11... | collective-permute-start | bytes 786440 | tf_op jit(solution)/shard_map/ppermute | solution.py:32
  24.1 9.2 %collective-permute-start.5 = (bf16[128,1024]{1,0:T(8,128)(2,1)S(1)}, bf16[128,1024]{1,0:T(8,128)(2,1)S(1)}, u32[]{:S(2)}, u32[]{:S(2)}) collective-permute-start(bf16[128,1024]{1,0:T(8,128)(2,1)S(1)} %pair_sum.3.after.a_ref), channel_id=1, source_target_pairs={{0,2},{1,3},{2,0},{3,1},{4,6},{5,7},{6,4},{7,5},{8,10},{9,11},{10,... | collective-permute-start | bytes 786440 | tf_op jit(solution)/shard_map/ppermute | solution.py:32
  27.6 12.7 %collective-permute-start.3 = (bf16[128,1280]{1,0:T(8,128)(2,1)S(1)}, bf16[128,1280]{1,0:T(8,128)(2,1)S(1)}, u32[]{:S(2)}, u32[]{:S(2)}) collective-permute-start(bf16[128,1280]{1,0:T(8,128)(2,1)S(1)} %get-tuple-element.48.after.a_ref), channel_id=1, source_target_pairs={{0,2},{1,3},{2,0},{3,1},{4,6},{5,7},{6,4},{7,5},{8,10},{9,11},{10,... | collective-permute-start | bytes 983048 | tf_op jit(solution)/shard_map/ppermute | solution.py:32
  28.1 10.5 %collective-permute-start.4 = (bf16[272,256]{1,0:T(8,128)(2,1)S(1)}, bf16[272,256]{1,0:T(8,128)(2,1)S(1)}, u32[]{:S(2)}, u32[]{:S(2)}) collective-permute-start(bf16[272,256]{1,0:T(8,128)(2,1)S(1)} %get-tuple-element.49.a_ref), channel_id=1, source_target_pairs={{0,8},{4,12},{8,0},{12,4},{1,9},{5,13},{9,1},{13,5},{2,10},{6,14},... | collective-permute-start | bytes 417800 | tf_op jit(solution)/shard_map/ppermute | solution.py:32
  33.4 3.2 %collective-permute-start.6 = (bf16[128,512]{1,0:T(8,128)(2,1)S(1)}, bf16[128,512]{1,0:T(8,128)(2,1)S(1)}, u32[]{:S(2)}, u32[]{:S(2)}) collective-permute-start(bf16[128,512]{1,0:T(8,128)(2,1)S(1)} %get-tuple-element.51.refs_0_), channel_id=1, source_target_pairs={{0,1},{1,0},{2,3},{3,2},{4,5},{5,4},{6,7},{7,6},{8,9},{9,8},{10,11... | collective-permute-start | bytes 393224 | tf_op jit(solution)/shard_map/ppermute | solution.py:32
  33.5 3.1 %collective-permute-start.7 = (bf16[128,512]{1,0:T(8,128)(2,1)S(1)}, bf16[128,512]{1,0:T(8,128)(2,1)S(1)}, u32[]{:S(2)}, u32[]{:S(2)}) collective-permute-start(bf16[128,512]{1,0:T(8,128)(2,1)S(1)} %get-tuple-element.52.refs_1_), channel_id=1, source_target_pairs={{0,1},{1,0},{2,3},{3,2},{4,5},{5,4},{6,7},{7,6},{8,9},{9,8},{10,11... | collective-permute-start | bytes 393224 | tf_op jit(solution)/shard_map/ppermute | solution.py:32
  34.0 12.1 %collective-permute-start.8 = (bf16[288,256]{1,0:T(8,128)(2,1)S(1)}, bf16[288,256]{1,0:T(8,128)(2,1)S(1)}, u32[]{:S(2)}, u32[]{:S(2)}) collective-permute-start(bf16[288,256]{1,0:T(8,128)(2,1)S(1)} %forward_output.1.after.refs_4_.a_ref), channel_id=1, source_target_pairs={{0,8},{4,12},{8,0},{12,4},{1,9},{5,13},{9,1},{13,5},{2,10},{6,14},... | collective-permute-start | bytes 442376 | tf_op jit(solution)/shard_map/ppermute | solution.py:32
  38.6 7.5 %collective-permute-start.9 = (bf16[272,256]{1,0:T(8,128)(2,1)S(1)}, bf16[272,256]{1,0:T(8,128)(2,1)S(1)}, u32[]{:S(2)}, u32[]{:S(2)}) collective-permute-start(bf16[272,256]{1,0:T(8,128)(2,1)S(1)} %sum_with_gain.1.after.a_ref.x_ref), channel_id=1, source_target_pairs={{0,4},{4,0},{8,12},{12,8},{1,5},{5,1},{9,13},{13,9},{2,6},{6,2},{1... | collective-permute-start | bytes 417800 | tf_op jit(solution)/shard_map/ppermute | solution.py:32
  40.4 7.6 %collective-permute-start.13 = (bf16[128,512]{1,0:T(8,128)(2,1)S(1)}, bf16[128,512]{1,0:T(8,128)(2,1)S(1)}, u32[]{:S(2)}, u32[]{:S(2)}) collective-permute-start(bf16[128,512]{1,0:T(8,128)(2,1)S(1)} %get-tuple-element.57.refs_1_), channel_id=1, source_target_pairs={{0,1},{1,0},{2,3},{3,2},{4,5},{5,4},{6,7},{7,6},{8,9},{9,8},{10,11... | collective-permute-start | bytes 393224 | tf_op jit(solution)/shard_map/ppermute | solution.py:32
  40.4 7.5 %copy-start.5 = (f32[1,4096]{1,0:T(1,128)S(1)}, f32[1,4096]{1,0:T(1,128)}, u32[]{:S(2)}) copy-start(f32[1,4096]{1,0:T(1,128)} %gain_ref.1) | copy-start | bytes 49156
  40.5 7.5 %collective-permute-start.12 = (bf16[128,512]{1,0:T(8,128)(2,1)S(1)}, bf16[128,512]{1,0:T(8,128)(2,1)S(1)}, u32[]{:S(2)}, u32[]{:S(2)}) collective-permute-start(bf16[128,512]{1,0:T(8,128)(2,1)S(1)} %get-tuple-element.53.after.refs_0_), channel_id=1, source_target_pairs={{0,1},{1,0},{2,3},{3,2},{4,5},{5,4},{6,7},{7,6},{8,9},{9,8},{10,11... | collective-permute-start | bytes 393224 | tf_op jit(solution)/shard_map/ppermute | solution.py:32
  46.2 5.0 %collective-permute-start.10 = (bf16[256,256]{1,0:T(8,128)(2,1)S(1)}, bf16[256,256]{1,0:T(8,128)(2,1)S(1)}, u32[]{:S(2)}, u32[]{:S(2)}) collective-permute-start(bf16[256,256]{1,0:T(8,128)(2,1)S(1)} %pair_sum.4.refs_6_.y_ref), channel_id=1, source_target_pairs={{0,4},{4,0},{8,12},{12,8},{1,5},{5,1},{9,13},{13,9},{2,6},{6,2},{1... | collective-permute-start | bytes 393224 | tf_op jit(solution)/shard_map/ppermute | solution.py:32
  46.3 1.7 %collective-permute-start.14 = (bf16[128,256]{1,0:T(8,128)(2,1)S(1)}, bf16[128,256]{1,0:T(8,128)(2,1)S(1)}, u32[]{:S(2)}, u32[]{:S(2)}) collective-permute-start(bf16[128,256]{1,0:T(8,128)(2,1)S(1)} %get-tuple-element.58.refs_2_), channel_id=1, source_target_pairs={{0,1},{1,0},{2,3},{3,2},{4,5},{5,4},{6,7},{7,6},{8,9},{9,8},{10,11... | collective-permute-start | bytes 196616 | tf_op jit(solution)/shard_map/ppermute | solution.py:32
  46.3 3.8 %collective-permute-start.11 = (f32[8,256]{1,0:T(8,128)S(1)}, f32[8,256]{1,0:T(8,128)S(1)}, u32[]{:S(2)}, u32[]{:S(2)}) collective-permute-start(f32[8,256]{1,0:T(8,128)S(1)} %gain_total.1.after.a_ref), channel_id=1, source_target_pairs={{0,2},{1,3},{2,0},{3,1},{4,6},{5,7},{6,4},{7,5},{8,10},{9,11},{10,... | collective-permute-start | bytes 24584 | tf_op jit(solution)/shard_map/ppermute | solution.py:32
  50.2 1.2 %collective-permute-start.15 = (f32[8,256]{1,0:T(8,128)S(1)}, f32[8,256]{1,0:T(8,128)S(1)}, u32[]{:S(2)}, u32[]{:S(2)}) collective-permute-start(f32[8,256]{1,0:T(8,128)S(1)} %pair_sum.5.gain_ref), channel_id=1, source_target_pairs={{0,1},{1,0},{2,3},{3,2},{4,5},{5,4},{6,7},{7,6},{8,9},{9,8},{10,11... | collective-permute-start | bytes 24584 | tf_op jit(solution)/shard_map/ppermute | solution.py:32

commit v9 on v7

--- a/solution.py
+++ b/solution.py
@@ -106,11 +106,11 @@
     pieces = [pl.ds(i * PIECE, PIECE) for i in range(parts)]
     pairs = [(back_hbm, back), (gain_hbm, gain)]
     pairs += [(u_hbm.at[at, :], u.at[at, :]) for at in pieces]
+    pairs += [(wo_hbm.at[:, at], wo.at[:, at]) for at in pieces]
     pairs += [(wq_hbm.at[at, :], wq.at[at, :]) for at in pieces[:2]]
     pairs += [(wk_hbm, narrow.at[:, pl.ds(0, nk)])]
     pairs += [(wv_hbm, narrow.at[:, pl.ds(nk, narrow.shape[1] - nk)])]
     pairs += [(wq_hbm.at[at, :], wq.at[at, :]) for at in pieces[2:]]
-    pairs += [(wo_hbm.at[:, at], wo.at[:, at]) for at in pieces]
     copies = [
         pltpu.make_async_copy(source, target, sems.at[n])
         for n, (source, target) in enumerate(pairs)
@@ -130,19 +130,35 @@
     start_to(2 + parts + AHEAD)
     copies[0].wait()
     copies[1].wait()
-    square = jnp.zeros((back.shape[0], HD), F32)
-    for i, at in enumerate(pieces):
+    squares = [jnp.zeros((back.shape[0], HD), F32)]
+
+    def decode(i):
+        at = pieces[i]
         copies[2 + i].wait()
         turned[:, at] = u[at, :].T
         scaled[:, at] = (turned[:, at].astype(F32) * gain[:, at]).astype(BF)
         decoded = nn(back[...], turned[:, at])
         for side in range(0, PIECE, HD):
             part = decoded[:, side : side + HD]
-            square = square + part * part
+            squares[0] = squares[0] + part * part
+
+    decode(0)
+    place = 2 + parts
+    for i, at in enumerate(pieces):
+        wait(place)
+        place += 1
+        if i + 1 < parts:
+            decode(i + 1)
+        part = nn(wo[:, at], u[at, :])
+        if i == 0:
+            o_acc[...] = part
+        elif i + 1 < parts:
+            o_acc[...] += part
+        else:
+            o_ref[...] = (o_acc[...] + part).astype(BF)
     inv_ref[...] = jnp.broadcast_to(
-        inverse_root(jnp.sum(square, axis=1, keepdims=True), wide), inv_ref.shape
+        inverse_root(jnp.sum(squares[0], axis=1, keepdims=True), wide), inv_ref.shape
     )
-    place = 2 + parts
     for i, at in enumerate(pieces):
         if i == 2:
             wait(place)
@@ -155,19 +171,11 @@
         part = nn(scaled[:, at], wq[at, :])
         if i == 0:
             m_acc[...] = part
+        elif i + 1 < parts:
+            m_acc[...] += part
         else:
-            m_acc[...] += part
-    for p, piece in enumerate(split(m_acc[...], 2)):
-        m_ref[p * rank : (p + 1) * rank, :nq] = piece
-    for i, at in enumerate(pieces):
-        wait(place)
-        place += 1
-        part = nn(wo[:, at], u[at, :])
-        if i == 0:
-            o_acc[...] = part
-        else:
-            o_acc[...] += part
-    o_ref[...] = o_acc[...].astype(BF)
+            for p, piece in enumerate(split(m_acc[...] + part, 2)):
+                m_ref[p * rank : (p + 1) * rank, :nq] = piece
 
 
 def project(back, gain, basis, wq, wk, wv, wo):
@@ -209,9 +217,10 @@
     length = coeffs.shape[0]
     heads = q.shape[0] // length
     twice = jnp.concatenate([coeffs, coeffs], axis=1)
-    for h in range(heads):
-        part = nn(twice, m_ref[:, h * HD : (h + 1) * HD]) * inv
-        q[h * length : (h + 1) * length, :] = rope(part, cosine, sine).astype(BF)
+    for h in range(0, heads, 2):
+        both = nn(twice, m_ref[:, h * HD : (h + 2) * HD]) * inv
+        for part, at in ((both[:, :HD], h * length), (both[:, HD:], (h + 1) * length)):
+            q[at : at + length, :] = rope(part, cosine, sine).astype(BF)
     part = nn(twice, m_ref[:, heads * HD :]) * inv
     k[...] = rope(part[:, :HD], cosine, sine).astype(BF)
     v1[:, :HD] = part[:, HD:].astype(BF)
@@ -253,8 +262,10 @@
     inv = inv_ref[...]
     project_heads(back, inv[:, :1], m_ref, cosine, sine, q, k, v1)
     scores[...] = nt(q[...], k[...])
-    for h in range(count):
-        gh[h * length : (h + 1) * length, :] = nt(up, o_ref[h * HD : (h + 1) * HD, :]).astype(BF)
+    for h in range(0, count, 2):
+        both = nt(up, o_ref[h * HD : (h + 2) * HD, :]).astype(BF)
+        gh[h * length : (h + 1) * length, :] = both[:, :HD]
+        gh[(h + 1) * length : (h + 2) * length, :] = both[:, HD:]
     exps_of(scores, scores, low, length)
     mixed[...] = nn(low[...], v1[...])
     gp[...] = nt(gh[...], v1[:, :HD])

time: 51.9 us -> 54.9 us (1.058)
  Pallas kernels: 29 us -> 31.7 us
    pallas_call x1, Pallas kernels: 10.9 us -> 14.3 us  [project(): pl.pallas_call(project_kernel, in_specs=[pl.BlockSpec(memory_space=pltpu....]
  transfers between devices with their start and end apart: 15 -> 15, of which waited for: 4 -> 4; matrix products, arithmetic and copies ran while one was open for 0% -> 0% of each run, Pallas kernels for 44% -> 47%
where the time goes in v9:
time: 54.9 us; the launch traced here: 54.7 us
  Pallas kernels  31.7 us (58%)
  starting transfers between devices  16.7 us (30%)
  waiting for transfers between devices  4.61 us (8%)
  other arithmetic  0.93 us (2%)
  between operations  0.76 us (1%)
    ppermute x15, starting transfers between devices, swap(): return lax.ppermute(x, axis, [(i, i ^ bit) for i in range(devices)])  16.7 us
    pallas_call x1, Pallas kernels, project(): pl.pallas_call(project_kernel, in_specs=[pl.BlockSpec(memory_space=pltpu....  14.3 us
    pallas_call x1, Pallas kernels, backward(): pl.pallas_call(backward_kernel, in_specs=vmem(8), out_specs=vmem(4), out_...  4.89 us
    ppermute x15, waiting for transfers between devices, swap(): return lax.ppermute(x, axis, [(i, i ^ bit) for i in range(devices)])  4.61 us
    pallas_call x1, Pallas kernels, forward(): pl.pallas_call(forward_kernel, in_specs=vmem(7) + [pl.BlockSpec(memory_sp...  3.51 us
    pallas_call x1, Pallas kernels, inward_grads(): pl.pallas_call(functools.partial(inward_kernel, len(own)), grid=(STEPS,),...  2.21 us
    pallas_call x1, Pallas kernels, outward_grad(): pl.pallas_call(functools.partial(outward_kernel, len(own)), grid=(STEPS,)...  2 us
    pallas_call x1, Pallas kernels, gain_part(): pl.pallas_call(gain_kernel, in_specs=vmem(6) + [pl.BlockSpec(memory_space...  1.84 us
  transfers between devices with their start and end apart: 15, of which 4 were waited for; matrix products, arithmetic and copies ran while one was open for 0% of the time, Pallas kernels for 47%

profile of v9, /device:TPU:17, one launch (start us, length us, event | category | flops | bytes accessed | tf_op | source)
XLA Modules:
  0.0 54.7 jit_solution(1944854108651179521)
XLA Ops:
  0.6 0.9 %select_bitcast_fusion = bf16[256,256]{1,0:T(8,128)(2,1)S(1)} fusion(bf16[1,256,256]{2,1,0:T(8,128)(2,1)} %param.15, bf16[1,256,256]{2,1,0:T(8,128)(2,1)} %param.16, pred[]{:T(512)S(6)} %eq.3), kind=kLoop, calls=%fused_computation | loop fusion | flops 65536 | bytes 393217 | tf_op jit(solution)/shard_map/jit(_where)/select_n | solution.py:39
  1.6 1.3 %collective-permute-start = (bf16[256,256]{1,0:T(8,128)(2,1)S(1)}, bf16[256,256]{1,0:T(8,128)(2,1)S(1)}, u32[]{:S(2)}, u32[]{:S(2)}) collective-permute-start(bf16[256,256]{1,0:T(8,128)(2,1)S(1)} %select_bitcast_fusion), channel_id=1, source_target_pairs={{0,16},{16,0},{1,17},{17,1},{2,18},{18,2},{3,19},{19,3},{4,20},{20... | collective-permute-start | bytes 393224 | tf_op jit(solution)/shard_map/ppermute | solution.py:32
  2.9 14.3 %project_weights.1 = (bf16[512,1280]{1,0:T(8,128)(2,1)S(1)}, bf16[1024,256]{1,0:T(8,128)(2,1)S(1)}, f32[256,128]{1,0:T(8,128)S(1)}, bf16[4096,256]{1,0:T(8,128)(...) custom-call(bf16[256,256]{1,0:T(8,128)(2,1)} %bitcast.13, ...), custom_call_target="tpu_custom_call" | custom-call | flops 6000000000 | bytes 20000000 | tf_op jit(solution)/shard_map/project_weights/pallas_call | solution.py:188
  17.2 4.9 %attention_backward.1 = (bf16[256,1280]{1,0:T(8,128)(2,1)S(1)}, bf16[128,1024]{1,0:T(8,128)(2,1)S(1)}, bf16[128,1024]{1,0:T(8,128)(2,1)S(1)}, bf16[256,256]{1,0:T(8,128)(2,1)S(1)}) custom-call(bf16[256,256]{1,0:T(8,128)(2,1)S(1)} %bitcast.14, bf16[256,256]{1,0:T(8,128)(2,1)S(1)} %copy-done.1, ...), custom_call_target="tpu_custom_call" | custom-call | flops 10000 | bytes 1000 | tf_op jit(solution)/shard_map/attention_backward/pallas_call | solution.py:313
  22.1 1.0 %collective-permute-start.1 = (bf16[256,1280]{1,0:T(8,128)(2,1)S(1)}, bf16[256,1280]{1,0:T(8,128)(2,1)S(1)}, u32[]{:S(2)}, u32[]{:S(2)}) collective-permute-start(bf16[256,1280]{1,0:T(8,128)(2,1)S(1)} %get-tuple-element.41.inner_ref), channel_id=1, source_target_pairs={{0,1},{1,0},{2,3},{3,2},{4,5},{5,4},{6,7},{7,6},{8,9},{9,8},{10,11... | collective-permute-start | bytes 1966088 | tf_op jit(solution)/shard_map/ppermute | solution.py:32
  23.2 1.7 %encoded_again.1 = (f32[256,256]{1,0:T(8,128)S(1)}, f32[256,256]{1,0:T(8,128)S(1)}, f32[256,256]{1,0:T(8,128)S(1)}) custom-call(bf16[256,256]{1,0:T(8,128)(2,1)S(1)} %bitcast.15, bf16[256,256]{1,0:T(8,128)(2,1)S(1)} %copy-done.1, bf16[256,256]{1,0:T(8,128)(2,1)S(1)} %collective-permute-done.sent_ref.returned_ref.arrived_ref, bf16[256,256]{1,0:T(8,128)(2,1)S(1)} %copy-done.2, ...), custom_call_target="tpu_custom_call" | custom-call | flops 10000 | bytes 1000 | tf_op jit(solution)/shard_map/encoded_again/pallas_call | solution.py:364
  24.9 0.3 collective-permute-done.2.b_ref
  25.3 1.3 %collective-permute-start.5 = (bf16[128,1024]{1,0:T(8,128)(2,1)S(1)}, bf16[128,1024]{1,0:T(8,128)(2,1)S(1)}, u32[]{:S(2)}, u32[]{:S(2)}) collective-permute-start(bf16[128,1024]{1,0:T(8,128)(2,1)S(1)} %pair_sum.4.after.a_ref), channel_id=1, source_target_pairs={{0,2},{1,3},{2,0},{3,1},{4,6},{5,7},{6,4},{7,5},{8,10},{9,11},{10,... | collective-permute-start | bytes 786440 | tf_op jit(solution)/shard_map/ppermute | solution.py:32
  26.6 1.8 %pair_sum_and_gain_gradient.1 = (bf16[128,1280]{1,0:T(8,128)(2,1)S(1)}, bf16[272,256]{1,0:T(8,128)(2,1)S(1)}) custom-call(bf16[4096,256]{1,0:T(8,128)(2,1)S(1)} %get-tuple-element.32.u_ref, bf16[4096,1024]{1,0:T(8,128)(2,1)S(1)} %get-tuple-element.39.wq_ref, bf16[4096,256]{1,0:T(8,128)(2,1)S(1)} %get-tuple-element.40.narrow_ref, ...), custom_call_target="tpu_custom_call" | custom-call | flops 10000 | bytes 1000 | tf_op jit(solution)/shard_map/pair_sum_and_gain_gradient/pallas_call | solution.py:469
  28.8 3.5 %attention_forward.1.after.a_ref = bf16[288,256]{1,0:T(8,128)(2,1)S(1)} custom-call(bf16[256,256]{1,0:T(8,128)(2,1)S(1)} %copy-done.2, bf16[256,256]{1,0:T(8,128)(2,1)S(1)} %collective-permute-done.sent_ref.returned_ref.arrived_ref, bf16[256,4096]{1,0:T(8,128)(2,1)S(1)} %get-tuple-element.33.turned_ref, bf16[512,1280]{1,0:T(8,128)(2,1)S(1)} %get-tuple-element.35.m_ref, ...), custom_call_target="tpu_custom_call" | custom-call | flops 10000 | bytes 1000 | tf_op jit(solution)/shard_map/attention_forward/pallas_call | solution.py:406
  32.3 0.6 %collective-permute-done.5.b_ref = bf16[128,1024]{1,0:T(8,128)(2,1)S(1)} collective-permute-done((bf16[128,1024]{1,0:T(8,128)(2,1)S(1)}, bf16[128,1024]{1,0:T(8,128)(2,1)S(1)}, u32[]{:S(2)}, u32[]{:S(2)}) %collective-permute-start.5) | collective-permute-done | bytes 262176 | tf_op jit(solution)/shard_map/ppermute | solution.py:32
  32.9 2.1 %collective-permute-start.8 = (bf16[128,1024]{1,0:T(8,128)(2,1)S(1)}, bf16[128,1024]{1,0:T(8,128)(2,1)S(1)}, u32[]{:S(2)}, u32[]{:S(2)}) collective-permute-start(bf16[128,1024]{1,0:T(8,128)(2,1)S(1)} %pair_sum.5.after.refs_0_), channel_id=1, source_target_pairs={{0,1},{1,0},{2,3},{3,2},{4,5},{5,4},{6,7},{7,6},{8,9},{9,8},{10,11... | collective-permute-start | bytes 786440 | tf_op jit(solution)/shard_map/ppermute | solution.py:32
  35.0 1.0 %collective-permute-start.3 = (bf16[288,256]{1,0:T(8,128)(2,1)S(1)}, bf16[288,256]{1,0:T(8,128)(2,1)S(1)}, u32[]{:S(2)}, u32[]{:S(2)}) collective-permute-start(bf16[288,256]{1,0:T(8,128)(2,1)S(1)} %attention_forward.1.after.a_ref), channel_id=1, source_target_pairs={{0,8},{4,12},{8,0},{12,4},{1,9},{5,13},{9,1},{13,5},{2,10},{6,14},... | collective-permute-start | bytes 442376 | tf_op jit(solution)/shard_map/ppermute | solution.py:32
  36.0 3.5 %collective-permute-start.6 = (bf16[272,256]{1,0:T(8,128)(2,1)S(1)}, bf16[272,256]{1,0:T(8,128)(2,1)S(1)}, u32[]{:S(2)}, u32[]{:S(2)}) collective-permute-start(bf16[272,256]{1,0:T(8,128)(2,1)S(1)} %sum_with_gain.1.refs_2_.a_ref.x_ref), channel_id=1, source_target_pairs={{0,4},{4,0},{8,12},{12,8},{1,5},{5,1},{9,13},{13,9},{2,6},{6,2},{1... | collective-permute-start | bytes 417800 | tf_op jit(solution)/shard_map/ppermute | solution.py:32
  39.5 2.0 %output_weight_gradient.1.after = bf16[1024,1024]{1,0:T(8,128)(2,1)} custom-call(bf16[4096,256]{1,0:T(8,128)(2,1)S(1)} %get-tuple-element.32.u_ref, bf16[128,1024]{1,0:T(8,128)(2,1)S(1)} %pair_sum.5.after.refs_0_, bf16[128,1024]{1,0:T(8,128)(2,1)S(1)} %collective-permute-done.8.refs_1_, bf16[272,256]{1,0:T(8,128)(2,1)S(1)} %sum_with_gain.1.refs_2_.a_ref.x_ref), custom_call_target="tpu_custom_call" | custom-call | flops 10000 | bytes 1000 | tf_op jit(solution)/shard_map/output_weight_gradient/pallas_call | solution.py:609
  41.6 0.8 %collective-permute-start.11 = (bf16[128,512]{1,0:T(8,128)(2,1)S(1)}, bf16[128,512]{1,0:T(8,128)(2,1)S(1)}, u32[]{:S(2)}, u32[]{:S(2)}) collective-permute-start(bf16[128,512]{1,0:T(8,128)(2,1)S(1)} %get-tuple-element.46.after.refs_0_), channel_id=1, source_target_pairs={{0,1},{1,0},{2,3},{3,2},{4,5},{5,4},{6,7},{7,6},{8,9},{9,8},{10,11... | collective-permute-start | bytes 393224 | tf_op jit(solution)/shard_map/ppermute | solution.py:32
  42.5 2.8 %collective-permute-done.6.b_ref.xgot_ref = bf16[272,256]{1,0:T(8,128)(2,1)S(1)} collective-permute-done((bf16[272,256]{1,0:T(8,128)(2,1)S(1)}, bf16[272,256]{1,0:T(8,128)(2,1)S(1)}, u32[]{:S(2)}, u32[]{:S(2)}) %collective-permute-start.6) | collective-permute-done | bytes 139296 | tf_op jit(solution)/shard_map/ppermute | solution.py:32
  45.4 2.3 %collective-permute-start.9 = (bf16[256,256]{1,0:T(8,128)(2,1)S(1)}, bf16[256,256]{1,0:T(8,128)(2,1)S(1)}, u32[]{:S(2)}, u32[]{:S(2)}) collective-permute-start(bf16[256,256]{1,0:T(8,128)(2,1)S(1)} %pair_sum.6.refs_6_.y_ref), channel_id=1, source_target_pairs={{0,4},{4,0},{8,12},{12,8},{1,5},{5,1},{9,13},{13,9},{2,6},{6,2},{1... | collective-permute-start | bytes 393224 | tf_op jit(solution)/shard_map/ppermute | solution.py:32
  47.6 1.4 %collective-permute-start.13 = (bf16[128,256]{1,0:T(8,128)(2,1)S(1)}, bf16[128,256]{1,0:T(8,128)(2,1)S(1)}, u32[]{:S(2)}, u32[]{:S(2)}) collective-permute-start(bf16[128,256]{1,0:T(8,128)(2,1)S(1)} %get-tuple-element.50.refs_2_), channel_id=1, source_target_pairs={{0,1},{1,0},{2,3},{3,2},{4,5},{5,4},{6,7},{7,6},{8,9},{9,8},{10,11... | collective-permute-start | bytes 196616 | tf_op jit(solution)/shard_map/ppermute | solution.py:32
  49.0 1.2 %collective-permute-start.10 = (f32[8,256]{1,0:T(8,128)S(1)}, f32[8,256]{1,0:T(8,128)S(1)}, u32[]{:S(2)}, u32[]{:S(2)}) collective-permute-start(f32[8,256]{1,0:T(8,128)S(1)} %gain_total.1.after.a_ref), channel_id=1, source_target_pairs={{0,2},{1,3},{2,0},{3,1},{4,6},{5,7},{6,4},{7,5},{8,10},{9,11},{10,... | collective-permute-start | bytes 24584 | tf_op jit(solution)/shard_map/ppermute | solution.py:32
  50.3 2.2 %inward_weight_gradients.1 = (bf16[1024,1024]{1,0:T(8,128)(2,1)}, bf16[1024,128]{1,0:T(8,128)(2,1)}, bf16[1024,128]{1,0:T(8,128)(2,1)}) custom-call(bf16[4096,256]{1,0:T(8,128)(2,1)S(1)} %get-tuple-element.32.u_ref, f32[1,4096]{1,0:T(1,128)S(1)} %copy-done.5, bf16[128,512]{1,0:T(8,128)(2,1)S(1)} %get-tuple-element.46.after.refs_0_, ...), custom_call_target="tpu_custom_call" | custom-call | flops 10000 | bytes 1000 | tf_op jit(solution)/shard_map/inward_weight_gradients/pallas_call | solution.py:592
  52.5 0.3 collective-permute-start.14
  52.8 0.9 %collective-permute-done.14.gain_other_ref = f32[8,256]{1,0:T(8,128)S(1)} collective-permute-done((f32[8,256]{1,0:T(8,128)S(1)}, f32[8,256]{1,0:T(8,128)S(1)}, u32[]{:S(2)}, u32[]{:S(2)}) %collective-permute-start.14) | collective-permute-done | bytes 8224 | tf_op jit(solution)/shard_map/ppermute | solution.py:32
  53.7 1.0 %section_results.1 = (bf16[256,256]{1,0:T(8,128)(2,1)}, bf16[256,256]{1,0:T(8,128)(2,1)}, f32[1,4096]{1,0:T(1,128)}) custom-call(f32[256,256]{1,0:T(8,128)S(1)} %get-tuple-element.38.after.fbase_ref, bf16[256,256]{1,0:T(8,128)(2,1)S(1)} %pair_sum.6.refs_6_.y_ref, bf16[256,256]{1,0:T(8,128)(2,1)S(1)} %collective-permute-done.9.ygot_ref, ...), custom_call_target="tpu_custom_call" | custom-call | flops 10000 | bytes 1000 | tf_op jit(solution)/shard_map/section_results/pallas_call | solution.py:647
  (34 shorter events, 0.8 us)
Async XLA Ops:
  1.6 15.6 %collective-permute-start = (bf16[256,256]{1,0:T(8,128)(2,1)S(1)}, bf16[256,256]{1,0:T(8,128)(2,1)S(1)}, u32[]{:S(2)}, u32[]{:S(2)}) collective-permute-start(bf16[256,256]{1,0:T(8,128)(2,1)S(1)} %select_bitcast_fusion), channel_id=1, source_target_pairs={{0,16},{16,0},{1,17},{17,1},{2,18},{18,2},{3,19},{19,3},{4,20},{20... | collective-permute-start | bytes 393224 | tf_op jit(solution)/shard_map/ppermute | solution.py:32
  2.9 14.3 %copy-start = (bf16[1,256,256]{2,1,0:T(8,128)(2,1)S(1)}, bf16[1,256,256]{2,1,0:T(8,128)(2,1)}, u32[]{:S(2)}) copy-start(bf16[1,256,256]{2,1,0:T(8,128)(2,1)} %param.17) | copy-start | bytes 393220
  2.9 14.3 %copy-start.1 = (bf16[256,256]{1,0:T(8,128)(2,1)S(1)}, bf16[256,256]{1,0:T(8,128)(2,1)}, u32[]{:S(2)}) copy-start(bf16[256,256]{1,0:T(8,128)(2,1)} %loss_ref.3) | copy-start | bytes 393220
  2.9 14.3 %copy-start.3 = (f32[256,128]{1,0:T(8,128)S(1)}, f32[256,128]{1,0:T(8,128)}, u32[]{:S(2)}) copy-start(f32[256,128]{1,0:T(8,128)} %constant.12.clone.cos_ref) | copy-start | bytes 393220
  2.9 14.3 %copy-start.4 = (f32[256,128]{1,0:T(8,128)S(1)}, f32[256,128]{1,0:T(8,128)}, u32[]{:S(2)}) copy-start(f32[256,128]{1,0:T(8,128)} %constant.13.clone.sin_ref) | copy-start | bytes 393220
  17.1 6.0 %copy-start.2 = (bf16[256,256]{1,0:T(8,128)(2,1)S(1)}, bf16[256,256]{1,0:T(8,128)(2,1)}, u32[]{:S(2)}) copy-start(bf16[256,256]{1,0:T(8,128)(2,1)} %new_ref.3) | copy-start | bytes 393220
  22.1 4.5 %collective-permute-start.1 = (bf16[256,1280]{1,0:T(8,128)(2,1)S(1)}, bf16[256,1280]{1,0:T(8,128)(2,1)S(1)}, u32[]{:S(2)}, u32[]{:S(2)}) collective-permute-start(bf16[256,1280]{1,0:T(8,128)(2,1)S(1)} %get-tuple-element.41.inner_ref), channel_id=1, source_target_pairs={{0,1},{1,0},{2,3},{3,2},{4,5},{5,4},{6,7},{7,6},{8,9},{9,8},{10,11... | collective-permute-start | bytes 1966088 | tf_op jit(solution)/shard_map/ppermute | solution.py:32
  23.1 2.1 %collective-permute-start.2 = (bf16[128,1024]{1,0:T(8,128)(2,1)S(1)}, bf16[128,1024]{1,0:T(8,128)(2,1)S(1)}, u32[]{:S(2)}, u32[]{:S(2)}) collective-permute-start(bf16[128,1024]{1,0:T(8,128)(2,1)S(1)} %get-tuple-element.43), channel_id=1, source_target_pairs={{0,1},{1,0},{2,3},{3,2},{4,5},{5,4},{6,7},{7,6},{8,9},{9,8},{10,11... | collective-permute-start | bytes 786440 | tf_op jit(solution)/shard_map/ppermute | solution.py:32
  25.3 7.6 %collective-permute-start.5 = (bf16[128,1024]{1,0:T(8,128)(2,1)S(1)}, bf16[128,1024]{1,0:T(8,128)(2,1)S(1)}, u32[]{:S(2)}, u32[]{:S(2)}) collective-permute-start(bf16[128,1024]{1,0:T(8,128)(2,1)S(1)} %pair_sum.4.after.a_ref), channel_id=1, source_target_pairs={{0,2},{1,3},{2,0},{3,1},{4,6},{5,7},{6,4},{7,5},{8,10},{9,11},{10,... | collective-permute-start | bytes 786440 | tf_op jit(solution)/shard_map/ppermute | solution.py:32
  28.4 13.1 %collective-permute-start.7 = (bf16[128,1280]{1,0:T(8,128)(2,1)S(1)}, bf16[128,1280]{1,0:T(8,128)(2,1)S(1)}, u32[]{:S(2)}, u32[]{:S(2)}) collective-permute-start(bf16[128,1280]{1,0:T(8,128)(2,1)S(1)} %get-tuple-element.44.after.a_ref), channel_id=1, source_target_pairs={{0,2},{1,3},{2,0},{3,1},{4,6},{5,7},{6,4},{7,5},{8,10},{9,11},{10,... | collective-permute-start | bytes 983048 | tf_op jit(solution)/shard_map/ppermute | solution.py:32
  28.7 7.3 %collective-permute-start.4 = (bf16[272,256]{1,0:T(8,128)(2,1)S(1)}, bf16[272,256]{1,0:T(8,128)(2,1)S(1)}, u32[]{:S(2)}, u32[]{:S(2)}) collective-permute-start(bf16[272,256]{1,0:T(8,128)(2,1)S(1)} %get-tuple-element.45.a_ref), channel_id=1, source_target_pairs={{0,8},{4,12},{8,0},{12,4},{1,9},{5,13},{9,1},{13,5},{2,10},{6,14},... | collective-permute-start | bytes 417800 | tf_op jit(solution)/shard_map/ppermute | solution.py:32
  32.9 6.6 %collective-permute-start.8 = (bf16[128,1024]{1,0:T(8,128)(2,1)S(1)}, bf16[128,1024]{1,0:T(8,128)(2,1)S(1)}, u32[]{:S(2)}, u32[]{:S(2)}) collective-permute-start(bf16[128,1024]{1,0:T(8,128)(2,1)S(1)} %pair_sum.5.after.refs_0_), channel_id=1, source_target_pairs={{0,1},{1,0},{2,3},{3,2},{4,5},{5,4},{6,7},{7,6},{8,9},{9,8},{10,11... | collective-permute-start | bytes 786440 | tf_op jit(solution)/shard_map/ppermute | solution.py:32
  35.0 10.3 %collective-permute-start.3 = (bf16[288,256]{1,0:T(8,128)(2,1)S(1)}, bf16[288,256]{1,0:T(8,128)(2,1)S(1)}, u32[]{:S(2)}, u32[]{:S(2)}) collective-permute-start(bf16[288,256]{1,0:T(8,128)(2,1)S(1)} %attention_forward.1.after.a_ref), channel_id=1, source_target_pairs={{0,8},{4,12},{8,0},{12,4},{1,9},{5,13},{9,1},{13,5},{2,10},{6,14},... | collective-permute-start | bytes 442376 | tf_op jit(solution)/shard_map/ppermute | solution.py:32
  36.0 9.3 %collective-permute-start.6 = (bf16[272,256]{1,0:T(8,128)(2,1)S(1)}, bf16[272,256]{1,0:T(8,128)(2,1)S(1)}, u32[]{:S(2)}, u32[]{:S(2)}) collective-permute-start(bf16[272,256]{1,0:T(8,128)(2,1)S(1)} %sum_with_gain.1.refs_2_.a_ref.x_ref), channel_id=1, source_target_pairs={{0,4},{4,0},{8,12},{12,8},{1,5},{5,1},{9,13},{13,9},{2,6},{6,2},{1... | collective-permute-start | bytes 417800 | tf_op jit(solution)/shard_map/ppermute | solution.py:32
  41.5 8.8 %copy-start.5 = (f32[1,4096]{1,0:T(1,128)S(1)}, f32[1,4096]{1,0:T(1,128)}, u32[]{:S(2)}) copy-start(f32[1,4096]{1,0:T(1,128)} %gain_ref.1) | copy-start | bytes 49156
  41.6 8.7 %collective-permute-start.11 = (bf16[128,512]{1,0:T(8,128)(2,1)S(1)}, bf16[128,512]{1,0:T(8,128)(2,1)S(1)}, u32[]{:S(2)}, u32[]{:S(2)}) collective-permute-start(bf16[128,512]{1,0:T(8,128)(2,1)S(1)} %get-tuple-element.46.after.refs_0_), channel_id=1, source_target_pairs={{0,1},{1,0},{2,3},{3,2},{4,5},{5,4},{6,7},{7,6},{8,9},{9,8},{10,11... | collective-permute-start | bytes 393224 | tf_op jit(solution)/shard_map/ppermute | solution.py:32
  42.4 7.9 %collective-permute-start.12 = (bf16[128,512]{1,0:T(8,128)(2,1)S(1)}, bf16[128,512]{1,0:T(8,128)(2,1)S(1)}, u32[]{:S(2)}, u32[]{:S(2)}) collective-permute-start(bf16[128,512]{1,0:T(8,128)(2,1)S(1)} %get-tuple-element.49.refs_1_), channel_id=1, source_target_pairs={{0,1},{1,0},{2,3},{3,2},{4,5},{5,4},{6,7},{7,6},{8,9},{9,8},{10,11... | collective-permute-start | bytes 393224 | tf_op jit(solution)/shard_map/ppermute | solution.py:32
  45.4 7.5 %collective-permute-start.9 = (bf16[256,256]{1,0:T(8,128)(2,1)S(1)}, bf16[256,256]{1,0:T(8,128)(2,1)S(1)}, u32[]{:S(2)}, u32[]{:S(2)}) collective-permute-start(bf16[256,256]{1,0:T(8,128)(2,1)S(1)} %pair_sum.6.refs_6_.y_ref), channel_id=1, source_target_pairs={{0,4},{4,0},{8,12},{12,8},{1,5},{5,1},{9,13},{13,9},{2,6},{6,2},{1... | collective-permute-start | bytes 393224 | tf_op jit(solution)/shard_map/ppermute | solution.py:32
  47.6 2.6 %collective-permute-start.13 = (bf16[128,256]{1,0:T(8,128)(2,1)S(1)}, bf16[128,256]{1,0:T(8,128)(2,1)S(1)}, u32[]{:S(2)}, u32[]{:S(2)}) collective-permute-start(bf16[128,256]{1,0:T(8,128)(2,1)S(1)} %get-tuple-element.50.refs_2_), channel_id=1, source_target_pairs={{0,1},{1,0},{2,3},{3,2},{4,5},{5,4},{6,7},{7,6},{8,9},{9,8},{10,11... | collective-permute-start | bytes 196616 | tf_op jit(solution)/shard_map/ppermute | solution.py:32
  49.0 3.5 %collective-permute-start.10 = (f32[8,256]{1,0:T(8,128)S(1)}, f32[8,256]{1,0:T(8,128)S(1)}, u32[]{:S(2)}, u32[]{:S(2)}) collective-permute-start(f32[8,256]{1,0:T(8,128)S(1)} %gain_total.1.after.a_ref), channel_id=1, source_target_pairs={{0,2},{1,3},{2,0},{3,1},{4,6},{5,7},{6,4},{7,5},{8,10},{9,11},{10,... | collective-permute-start | bytes 24584 | tf_op jit(solution)/shard_map/ppermute | solution.py:32
  52.5 1.2 %collective-permute-start.14 = (f32[8,256]{1,0:T(8,128)S(1)}, f32[8,256]{1,0:T(8,128)S(1)}, u32[]{:S(2)}, u32[]{:S(2)}) collective-permute-start(f32[8,256]{1,0:T(8,128)S(1)} %pair_sum.7.gain_ref), channel_id=1, source_target_pairs={{0,1},{1,0},{2,3},{3,2},{4,5},{5,4},{6,7},{7,6},{8,9},{9,8},{10,11... | collective-permute-start | bytes 24584 | tf_op jit(solution)/shard_map/ppermute | solution.py:32

commit v10 on v9

--- a/solution.py
+++ b/solution.py
@@ -17,7 +17,7 @@
 VMEM_BYTES = 24 * 1024 * 1024
 CHUNK = 512
 PIECE = 1024
-AHEAD = 3
+AHEAD = 5
 LOG2E = 1.4426950408889634
 
 
@@ -97,7 +97,7 @@
 def project_kernel(
     back_hbm, gain_hbm, u_hbm, wq_hbm, wk_hbm, wv_hbm, wo_hbm,
     m_ref, o_ref, inv_ref, u, wq, narrow, turned,
-    back, gain, wo, scaled, m_acc, o_acc, sems,
+    back, gain, wo, scaled, m_acc, sems,
 ):
     wide, rank = u.shape
     nq = wq.shape[1]
@@ -106,11 +106,12 @@
     pieces = [pl.ds(i * PIECE, PIECE) for i in range(parts)]
     pairs = [(back_hbm, back), (gain_hbm, gain)]
     pairs += [(u_hbm.at[at, :], u.at[at, :]) for at in pieces]
-    pairs += [(wo_hbm.at[:, at], wo.at[:, at]) for at in pieces]
-    pairs += [(wq_hbm.at[at, :], wq.at[at, :]) for at in pieces[:2]]
+    pairs += [(wq_hbm.at[at, :], wq.at[at, :]) for at in pieces]
     pairs += [(wk_hbm, narrow.at[:, pl.ds(0, nk)])]
     pairs += [(wv_hbm, narrow.at[:, pl.ds(nk, narrow.shape[1] - nk)])]
-    pairs += [(wq_hbm.at[at, :], wq.at[at, :]) for at in pieces[2:]]
+    block = wo.shape[0] // parts
+    blocks = [pl.ds(i * block, block) for i in range(parts)]
+    pairs += [(wo_hbm.at[at, :], wo.at[at, :]) for at in blocks]
     copies = [
         pltpu.make_async_copy(source, target, sems.at[n])
         for n, (source, target) in enumerate(pairs)
@@ -149,25 +150,6 @@
         place += 1
         if i + 1 < parts:
             decode(i + 1)
-        part = nn(wo[:, at], u[at, :])
-        if i == 0:
-            o_acc[...] = part
-        elif i + 1 < parts:
-            o_acc[...] += part
-        else:
-            o_ref[...] = (o_acc[...] + part).astype(BF)
-    inv_ref[...] = jnp.broadcast_to(
-        inverse_root(jnp.sum(squares[0], axis=1, keepdims=True), wide), inv_ref.shape
-    )
-    for i, at in enumerate(pieces):
-        if i == 2:
-            wait(place)
-            wait(place + 1)
-            place += 2
-            for p, piece in enumerate(split(nn(scaled[...], narrow[...]), 2)):
-                m_ref[p * rank : (p + 1) * rank, nq:] = piece
-        wait(place)
-        place += 1
         part = nn(scaled[:, at], wq[at, :])
         if i == 0:
             m_acc[...] = part
@@ -176,6 +158,18 @@
         else:
             for p, piece in enumerate(split(m_acc[...] + part, 2)):
                 m_ref[p * rank : (p + 1) * rank, :nq] = piece
+    inv_ref[...] = jnp.broadcast_to(
+        inverse_root(jnp.sum(squares[0], axis=1, keepdims=True), wide), inv_ref.shape
+    )
+    wait(place)
+    wait(place + 1)
+    place += 2
+    for p, piece in enumerate(split(nn(scaled[...], narrow[...]), 2)):
+        m_ref[p * rank : (p + 1) * rank, nq:] = piece
+    for at in blocks:
+        wait(place)
+        place += 1
+        o_ref[at, :] = nn(wo[at, :], u[...]).astype(BF)
 
 
 def project(back, gain, basis, wq, wk, wv, wo):
@@ -204,7 +198,6 @@
             pltpu.VMEM(wo.shape, BF),
             pltpu.VMEM((rank, wide), BF),
             pltpu.VMEM((rank, nq), F32),
-            pltpu.VMEM((ne, rank), F32),
             pltpu.SemaphoreType.DMA((4 + 3 * (wide // PIECE),)),
         ],
         compiler_params=pltpu.CompilerParams(vmem_limit_bytes=VMEM_BYTES * 3 // 2),

time: 54.9 us -> 53 us (0.965)
  Pallas kernels: 31.7 us -> 29.8 us
    pallas_call x1, Pallas kernels: 14.3 us -> 12.4 us  [project(): pl.pallas_call(project_kernel, in_specs=[pl.BlockSpec(memory_space=pltpu....]
  transfers between devices with their start and end apart: 15 -> 15, of which waited for: 4 -> 4; matrix products, arithmetic and copies ran while one was open for 0% -> 0% of each run, Pallas kernels for 47% -> 45%
where the time goes in v10:
time: 53 us; the launch traced here: 52.9 us
  Pallas kernels  29.8 us (56%)
  starting transfers between devices  16.7 us (32%)
  waiting for transfers between devices  4.6 us (9%)
  other arithmetic  0.93 us (2%)
  between operations  0.76 us (1%)
    ppermute x15, starting transfers between devices, swap(): return lax.ppermute(x, axis, [(i, i ^ bit) for i in range(devices)])  16.7 us
    pallas_call x1, Pallas kernels, project(): pl.pallas_call(project_kernel, in_specs=[pl.BlockSpec(memory_space=pltpu....  12.4 us
    pallas_call x1, Pallas kernels, backward(): pl.pallas_call(backward_kernel, in_specs=vmem(8), out_specs=vmem(4), out_...  4.89 us
    ppermute x15, waiting for transfers between devices, swap(): return lax.ppermute(x, axis, [(i, i ^ bit) for i in range(devices)])  4.6 us
    pallas_call x1, Pallas kernels, forward(): pl.pallas_call(forward_kernel, in_specs=vmem(7) + [pl.BlockSpec(memory_sp...  3.51 us
    pallas_call x1, Pallas kernels, inward_grads(): pl.pallas_call(functools.partial(inward_kernel, len(own)), grid=(STEPS,),...  2.21 us
    pallas_call x1, Pallas kernels, outward_grad(): pl.pallas_call(functools.partial(outward_kernel, len(own)), grid=(STEPS,)...  2 us
    pallas_call x1, Pallas kernels, gain_part(): pl.pallas_call(gain_kernel, in_specs=vmem(6) + [pl.BlockSpec(memory_space...  1.84 us
  transfers between devices with their start and end apart: 15, of which 4 were waited for; matrix products, arithmetic and copies ran while one was open for 0% of the time, Pallas kernels for 45%

profile of v10, /device:TPU:17, one launch (start us, length us, event | category | flops | bytes accessed | tf_op | source)
XLA Modules:
  0.0 52.9 jit_solution(15767610884240736100)
XLA Ops:
  0.6 0.9 %select_bitcast_fusion = bf16[256,256]{1,0:T(8,128)(2,1)S(1)} fusion(bf16[1,256,256]{2,1,0:T(8,128)(2,1)} %param.15, bf16[1,256,256]{2,1,0:T(8,128)(2,1)} %param.16, pred[]{:T(512)S(6)} %eq.3), kind=kLoop, calls=%fused_computation | loop fusion | flops 65536 | bytes 393217 | tf_op jit(solution)/shard_map/jit(_where)/select_n | solution.py:39
  1.6 1.3 %collective-permute-start = (bf16[256,256]{1,0:T(8,128)(2,1)S(1)}, bf16[256,256]{1,0:T(8,128)(2,1)S(1)}, u32[]{:S(2)}, u32[]{:S(2)}) collective-permute-start(bf16[256,256]{1,0:T(8,128)(2,1)S(1)} %select_bitcast_fusion), channel_id=1, source_target_pairs={{0,16},{16,0},{1,17},{17,1},{2,18},{18,2},{3,19},{19,3},{4,20},{20... | collective-permute-start | bytes 393224 | tf_op jit(solution)/shard_map/ppermute | solution.py:32
  2.9 12.4 %project_weights.1 = (bf16[512,1280]{1,0:T(8,128)(2,1)S(1)}, bf16[1024,256]{1,0:T(8,128)(2,1)S(1)}, f32[256,128]{1,0:T(8,128)S(1)}, bf16[4096,256]{1,0:T(8,128)(...) custom-call(bf16[256,256]{1,0:T(8,128)(2,1)} %bitcast.13, ...), custom_call_target="tpu_custom_call" | custom-call | flops 6000000000 | bytes 20000000 | tf_op jit(solution)/shard_map/project_weights/pallas_call | solution.py:182
  15.3 4.9 %attention_backward.1 = (bf16[256,1280]{1,0:T(8,128)(2,1)S(1)}, bf16[128,1024]{1,0:T(8,128)(2,1)S(1)}, bf16[128,1024]{1,0:T(8,128)(2,1)S(1)}, bf16[256,256]{1,0:T(8,128)(2,1)S(1)}) custom-call(bf16[256,256]{1,0:T(8,128)(2,1)S(1)} %bitcast.14, bf16[256,256]{1,0:T(8,128)(2,1)S(1)} %copy-done.1, ...), custom_call_target="tpu_custom_call" | custom-call | flops 10000 | bytes 1000 | tf_op jit(solution)/shard_map/attention_backward/pallas_call | solution.py:306
  20.2 1.0 %collective-permute-start.1 = (bf16[256,1280]{1,0:T(8,128)(2,1)S(1)}, bf16[256,1280]{1,0:T(8,128)(2,1)S(1)}, u32[]{:S(2)}, u32[]{:S(2)}) collective-permute-start(bf16[256,1280]{1,0:T(8,128)(2,1)S(1)} %get-tuple-element.41.inner_ref), channel_id=1, source_target_pairs={{0,1},{1,0},{2,3},{3,2},{4,5},{5,4},{6,7},{7,6},{8,9},{9,8},{10,11... | collective-permute-start | bytes 1966088 | tf_op jit(solution)/shard_map/ppermute | solution.py:32
  21.3 1.7 %encoded_again.1 = (f32[256,256]{1,0:T(8,128)S(1)}, f32[256,256]{1,0:T(8,128)S(1)}, f32[256,256]{1,0:T(8,128)S(1)}) custom-call(bf16[256,256]{1,0:T(8,128)(2,1)S(1)} %bitcast.15, bf16[256,256]{1,0:T(8,128)(2,1)S(1)} %copy-done.1, bf16[256,256]{1,0:T(8,128)(2,1)S(1)} %collective-permute-done.sent_ref.returned_ref.arrived_ref, bf16[256,256]{1,0:T(8,128)(2,1)S(1)} %copy-done.2, ...), custom_call_target="tpu_custom_call" | custom-call | flops 10000 | bytes 1000 | tf_op jit(solution)/shard_map/encoded_again/pallas_call | solution.py:357
  23.0 0.3 collective-permute-done.2.b_ref
  23.4 1.3 %collective-permute-start.5 = (bf16[128,1024]{1,0:T(8,128)(2,1)S(1)}, bf16[128,1024]{1,0:T(8,128)(2,1)S(1)}, u32[]{:S(2)}, u32[]{:S(2)}) collective-permute-start(bf16[128,1024]{1,0:T(8,128)(2,1)S(1)} %pair_sum.4.after.a_ref), channel_id=1, source_target_pairs={{0,2},{1,3},{2,0},{3,1},{4,6},{5,7},{6,4},{7,5},{8,10},{9,11},{10,... | collective-permute-start | bytes 786440 | tf_op jit(solution)/shard_map/ppermute | solution.py:32
  24.7 1.8 %pair_sum_and_gain_gradient.1 = (bf16[128,1280]{1,0:T(8,128)(2,1)S(1)}, bf16[272,256]{1,0:T(8,128)(2,1)S(1)}) custom-call(bf16[4096,256]{1,0:T(8,128)(2,1)S(1)} %get-tuple-element.32.u_ref, bf16[4096,1024]{1,0:T(8,128)(2,1)S(1)} %get-tuple-element.39.wq_ref, bf16[4096,256]{1,0:T(8,128)(2,1)S(1)} %get-tuple-element.40.narrow_ref, ...), custom_call_target="tpu_custom_call" | custom-call | flops 10000 | bytes 1000 | tf_op jit(solution)/shard_map/pair_sum_and_gain_gradient/pallas_call | solution.py:462
  26.9 3.5 %attention_forward.1.after.a_ref = bf16[288,256]{1,0:T(8,128)(2,1)S(1)} custom-call(bf16[256,256]{1,0:T(8,128)(2,1)S(1)} %copy-done.2, bf16[256,256]{1,0:T(8,128)(2,1)S(1)} %collective-permute-done.sent_ref.returned_ref.arrived_ref, bf16[256,4096]{1,0:T(8,128)(2,1)S(1)} %get-tuple-element.33.turned_ref, bf16[512,1280]{1,0:T(8,128)(2,1)S(1)} %get-tuple-element.35.m_ref, ...), custom_call_target="tpu_custom_call" | custom-call | flops 10000 | bytes 1000 | tf_op jit(solution)/shard_map/attention_forward/pallas_call | solution.py:399
  30.4 0.6 %collective-permute-done.5.b_ref = bf16[128,1024]{1,0:T(8,128)(2,1)S(1)} collective-permute-done((bf16[128,1024]{1,0:T(8,128)(2,1)S(1)}, bf16[128,1024]{1,0:T(8,128)(2,1)S(1)}, u32[]{:S(2)}, u32[]{:S(2)}) %collective-permute-start.5) | collective-permute-done | bytes 262176 | tf_op jit(solution)/shard_map/ppermute | solution.py:32
  31.0 2.1 %collective-permute-start.8 = (bf16[128,1024]{1,0:T(8,128)(2,1)S(1)}, bf16[128,1024]{1,0:T(8,128)(2,1)S(1)}, u32[]{:S(2)}, u32[]{:S(2)}) collective-permute-start(bf16[128,1024]{1,0:T(8,128)(2,1)S(1)} %pair_sum.5.after.refs_0_), channel_id=1, source_target_pairs={{0,1},{1,0},{2,3},{3,2},{4,5},{5,4},{6,7},{7,6},{8,9},{9,8},{10,11... | collective-permute-start | bytes 786440 | tf_op jit(solution)/shard_map/ppermute | solution.py:32
  33.1 1.0 %collective-permute-start.3 = (bf16[288,256]{1,0:T(8,128)(2,1)S(1)}, bf16[288,256]{1,0:T(8,128)(2,1)S(1)}, u32[]{:S(2)}, u32[]{:S(2)}) collective-permute-start(bf16[288,256]{1,0:T(8,128)(2,1)S(1)} %attention_forward.1.after.a_ref), channel_id=1, source_target_pairs={{0,8},{4,12},{8,0},{12,4},{1,9},{5,13},{9,1},{13,5},{2,10},{6,14},... | collective-permute-start | bytes 442376 | tf_op jit(solution)/shard_map/ppermute | solution.py:32
  34.1 3.5 %collective-permute-start.6 = (bf16[272,256]{1,0:T(8,128)(2,1)S(1)}, bf16[272,256]{1,0:T(8,128)(2,1)S(1)}, u32[]{:S(2)}, u32[]{:S(2)}) collective-permute-start(bf16[272,256]{1,0:T(8,128)(2,1)S(1)} %sum_with_gain.1.refs_2_.a_ref.x_ref), channel_id=1, source_target_pairs={{0,4},{4,0},{8,12},{12,8},{1,5},{5,1},{9,13},{13,9},{2,6},{6,2},{1... | collective-permute-start | bytes 417800 | tf_op jit(solution)/shard_map/ppermute | solution.py:32
  37.6 2.0 %output_weight_gradient.1.after = bf16[1024,1024]{1,0:T(8,128)(2,1)} custom-call(bf16[4096,256]{1,0:T(8,128)(2,1)S(1)} %get-tuple-element.32.u_ref, bf16[128,1024]{1,0:T(8,128)(2,1)S(1)} %pair_sum.5.after.refs_0_, bf16[128,1024]{1,0:T(8,128)(2,1)S(1)} %collective-permute-done.8.refs_1_, bf16[272,256]{1,0:T(8,128)(2,1)S(1)} %sum_with_gain.1.refs_2_.a_ref.x_ref), custom_call_target="tpu_custom_call" | custom-call | flops 10000 | bytes 1000 | tf_op jit(solution)/shard_map/output_weight_gradient/pallas_call | solution.py:602
  39.7 0.8 %collective-permute-start.11 = (bf16[128,512]{1,0:T(8,128)(2,1)S(1)}, bf16[128,512]{1,0:T(8,128)(2,1)S(1)}, u32[]{:S(2)}, u32[]{:S(2)}) collective-permute-start(bf16[128,512]{1,0:T(8,128)(2,1)S(1)} %get-tuple-element.46.after.refs_0_), channel_id=1, source_target_pairs={{0,1},{1,0},{2,3},{3,2},{4,5},{5,4},{6,7},{7,6},{8,9},{9,8},{10,11... | collective-permute-start | bytes 393224 | tf_op jit(solution)/shard_map/ppermute | solution.py:32
  40.6 2.8 %collective-permute-done.6.b_ref.xgot_ref = bf16[272,256]{1,0:T(8,128)(2,1)S(1)} collective-permute-done((bf16[272,256]{1,0:T(8,128)(2,1)S(1)}, bf16[272,256]{1,0:T(8,128)(2,1)S(1)}, u32[]{:S(2)}, u32[]{:S(2)}) %collective-permute-start.6) | collective-permute-done | bytes 139296 | tf_op jit(solution)/shard_map/ppermute | solution.py:32
  43.5 2.3 %collective-permute-start.9 = (bf16[256,256]{1,0:T(8,128)(2,1)S(1)}, bf16[256,256]{1,0:T(8,128)(2,1)S(1)}, u32[]{:S(2)}, u32[]{:S(2)}) collective-permute-start(bf16[256,256]{1,0:T(8,128)(2,1)S(1)} %pair_sum.6.refs_6_.y_ref), channel_id=1, source_target_pairs={{0,4},{4,0},{8,12},{12,8},{1,5},{5,1},{9,13},{13,9},{2,6},{6,2},{1... | collective-permute-start | bytes 393224 | tf_op jit(solution)/shard_map/ppermute | solution.py:32
  45.8 1.4 %collective-permute-start.13 = (bf16[128,256]{1,0:T(8,128)(2,1)S(1)}, bf16[128,256]{1,0:T(8,128)(2,1)S(1)}, u32[]{:S(2)}, u32[]{:S(2)}) collective-permute-start(bf16[128,256]{1,0:T(8,128)(2,1)S(1)} %get-tuple-element.50.refs_2_), channel_id=1, source_target_pairs={{0,1},{1,0},{2,3},{3,2},{4,5},{5,4},{6,7},{7,6},{8,9},{9,8},{10,11... | collective-permute-start | bytes 196616 | tf_op jit(solution)/shard_map/ppermute | solution.py:32
  47.1 1.2 %collective-permute-start.10 = (f32[8,256]{1,0:T(8,128)S(1)}, f32[8,256]{1,0:T(8,128)S(1)}, u32[]{:S(2)}, u32[]{:S(2)}) collective-permute-start(f32[8,256]{1,0:T(8,128)S(1)} %gain_total.1.after.a_ref), channel_id=1, source_target_pairs={{0,2},{1,3},{2,0},{3,1},{4,6},{5,7},{6,4},{7,5},{8,10},{9,11},{10,... | collective-permute-start | bytes 24584 | tf_op jit(solution)/shard_map/ppermute | solution.py:32
  48.4 2.2 %inward_weight_gradients.1 = (bf16[1024,1024]{1,0:T(8,128)(2,1)}, bf16[1024,128]{1,0:T(8,128)(2,1)}, bf16[1024,128]{1,0:T(8,128)(2,1)}) custom-call(bf16[4096,256]{1,0:T(8,128)(2,1)S(1)} %get-tuple-element.32.u_ref, f32[1,4096]{1,0:T(1,128)S(1)} %copy-done.5, bf16[128,512]{1,0:T(8,128)(2,1)S(1)} %get-tuple-element.46.after.refs_0_, ...), custom_call_target="tpu_custom_call" | custom-call | flops 10000 | bytes 1000 | tf_op jit(solution)/shard_map/inward_weight_gradients/pallas_call | solution.py:585
  50.6 0.4 collective-permute-start.14
  51.0 0.9 %collective-permute-done.14.gain_other_ref = f32[8,256]{1,0:T(8,128)S(1)} collective-permute-done((f32[8,256]{1,0:T(8,128)S(1)}, f32[8,256]{1,0:T(8,128)S(1)}, u32[]{:S(2)}, u32[]{:S(2)}) %collective-permute-start.14) | collective-permute-done | bytes 8224 | tf_op jit(solution)/shard_map/ppermute | solution.py:32
  51.8 1.0 %section_results.1 = (bf16[256,256]{1,0:T(8,128)(2,1)}, bf16[256,256]{1,0:T(8,128)(2,1)}, f32[1,4096]{1,0:T(1,128)}) custom-call(f32[256,256]{1,0:T(8,128)S(1)} %get-tuple-element.38.after.fbase_ref, bf16[256,256]{1,0:T(8,128)(2,1)S(1)} %pair_sum.6.refs_6_.y_ref, bf16[256,256]{1,0:T(8,128)(2,1)S(1)} %collective-permute-done.9.ygot_ref, ...), custom_call_target="tpu_custom_call" | custom-call | flops 10000 | bytes 1000 | tf_op jit(solution)/shard_map/section_results/pallas_call | solution.py:640
  (34 shorter events, 0.8 us)
Async XLA Ops:
  1.6 13.7 %collective-permute-start = (bf16[256,256]{1,0:T(8,128)(2,1)S(1)}, bf16[256,256]{1,0:T(8,128)(2,1)S(1)}, u32[]{:S(2)}, u32[]{:S(2)}) collective-permute-start(bf16[256,256]{1,0:T(8,128)(2,1)S(1)} %select_bitcast_fusion), channel_id=1, source_target_pairs={{0,16},{16,0},{1,17},{17,1},{2,18},{18,2},{3,19},{19,3},{4,20},{20... | collective-permute-start | bytes 393224 | tf_op jit(solution)/shard_map/ppermute | solution.py:32
  2.9 12.4 %copy-start = (bf16[1,256,256]{2,1,0:T(8,128)(2,1)S(1)}, bf16[1,256,256]{2,1,0:T(8,128)(2,1)}, u32[]{:S(2)}) copy-start(bf16[1,256,256]{2,1,0:T(8,128)(2,1)} %param.17) | copy-start | bytes 393220
  2.9 12.4 %copy-start.1 = (bf16[256,256]{1,0:T(8,128)(2,1)S(1)}, bf16[256,256]{1,0:T(8,128)(2,1)}, u32[]{:S(2)}) copy-start(bf16[256,256]{1,0:T(8,128)(2,1)} %loss_ref.3) | copy-start | bytes 393220
  2.9 12.4 %copy-start.3 = (f32[256,128]{1,0:T(8,128)S(1)}, f32[256,128]{1,0:T(8,128)}, u32[]{:S(2)}) copy-start(f32[256,128]{1,0:T(8,128)} %constant.12.clone.cos_ref) | copy-start | bytes 393220
  2.9 12.5 %copy-start.4 = (f32[256,128]{1,0:T(8,128)S(1)}, f32[256,128]{1,0:T(8,128)}, u32[]{:S(2)}) copy-start(f32[256,128]{1,0:T(8,128)} %constant.13.clone.sin_ref) | copy-start | bytes 393220
  15.3 6.0 %copy-start.2 = (bf16[256,256]{1,0:T(8,128)(2,1)S(1)}, bf16[256,256]{1,0:T(8,128)(2,1)}, u32[]{:S(2)}) copy-start(bf16[256,256]{1,0:T(8,128)(2,1)} %new_ref.3) | copy-start | bytes 393220
  20.2 4.5 %collective-permute-start.1 = (bf16[256,1280]{1,0:T(8,128)(2,1)S(1)}, bf16[256,1280]{1,0:T(8,128)(2,1)S(1)}, u32[]{:S(2)}, u32[]{:S(2)}) collective-permute-start(bf16[256,1280]{1,0:T(8,128)(2,1)S(1)} %get-tuple-element.41.inner_ref), channel_id=1, source_target_pairs={{0,1},{1,0},{2,3},{3,2},{4,5},{5,4},{6,7},{7,6},{8,9},{9,8},{10,11... | collective-permute-start | bytes 1966088 | tf_op jit(solution)/shard_map/ppermute | solution.py:32
  21.2 2.1 %collective-permute-start.2 = (bf16[128,1024]{1,0:T(8,128)(2,1)S(1)}, bf16[128,1024]{1,0:T(8,128)(2,1)S(1)}, u32[]{:S(2)}, u32[]{:S(2)}) collective-permute-start(bf16[128,1024]{1,0:T(8,128)(2,1)S(1)} %get-tuple-element.43), channel_id=1, source_target_pairs={{0,1},{1,0},{2,3},{3,2},{4,5},{5,4},{6,7},{7,6},{8,9},{9,8},{10,11... | collective-permute-start | bytes 786440 | tf_op jit(solution)/shard_map/ppermute | solution.py:32
  23.4 7.6 %collective-permute-start.5 = (bf16[128,1024]{1,0:T(8,128)(2,1)S(1)}, bf16[128,1024]{1,0:T(8,128)(2,1)S(1)}, u32[]{:S(2)}, u32[]{:S(2)}) collective-permute-start(bf16[128,1024]{1,0:T(8,128)(2,1)S(1)} %pair_sum.4.after.a_ref), channel_id=1, source_target_pairs={{0,2},{1,3},{2,0},{3,1},{4,6},{5,7},{6,4},{7,5},{8,10},{9,11},{10,... | collective-permute-start | bytes 786440 | tf_op jit(solution)/shard_map/ppermute | solution.py:32
  26.5 13.1 %collective-permute-start.7 = (bf16[128,1280]{1,0:T(8,128)(2,1)S(1)}, bf16[128,1280]{1,0:T(8,128)(2,1)S(1)}, u32[]{:S(2)}, u32[]{:S(2)}) collective-permute-start(bf16[128,1280]{1,0:T(8,128)(2,1)S(1)} %get-tuple-element.44.after.a_ref), channel_id=1, source_target_pairs={{0,2},{1,3},{2,0},{3,1},{4,6},{5,7},{6,4},{7,5},{8,10},{9,11},{10,... | collective-permute-start | bytes 983048 | tf_op jit(solution)/shard_map/ppermute | solution.py:32
  26.8 7.3 %collective-permute-start.4 = (bf16[272,256]{1,0:T(8,128)(2,1)S(1)}, bf16[272,256]{1,0:T(8,128)(2,1)S(1)}, u32[]{:S(2)}, u32[]{:S(2)}) collective-permute-start(bf16[272,256]{1,0:T(8,128)(2,1)S(1)} %get-tuple-element.45.a_ref), channel_id=1, source_target_pairs={{0,8},{4,12},{8,0},{12,4},{1,9},{5,13},{9,1},{13,5},{2,10},{6,14},... | collective-permute-start | bytes 417800 | tf_op jit(solution)/shard_map/ppermute | solution.py:32
  31.0 6.6 %collective-permute-start.8 = (bf16[128,1024]{1,0:T(8,128)(2,1)S(1)}, bf16[128,1024]{1,0:T(8,128)(2,1)S(1)}, u32[]{:S(2)}, u32[]{:S(2)}) collective-permute-start(bf16[128,1024]{1,0:T(8,128)(2,1)S(1)} %pair_sum.5.after.refs_0_), channel_id=1, source_target_pairs={{0,1},{1,0},{2,3},{3,2},{4,5},{5,4},{6,7},{7,6},{8,9},{9,8},{10,11... | collective-permute-start | bytes 786440 | tf_op jit(solution)/shard_map/ppermute | solution.py:32
  33.1 10.3 %collective-permute-start.3 = (bf16[288,256]{1,0:T(8,128)(2,1)S(1)}, bf16[288,256]{1,0:T(8,128)(2,1)S(1)}, u32[]{:S(2)}, u32[]{:S(2)}) collective-permute-start(bf16[288,256]{1,0:T(8,128)(2,1)S(1)} %attention_forward.1.after.a_ref), channel_id=1, source_target_pairs={{0,8},{4,12},{8,0},{12,4},{1,9},{5,13},{9,1},{13,5},{2,10},{6,14},... | collective-permute-start | bytes 442376 | tf_op jit(solution)/shard_map/ppermute | solution.py:32
  34.1 9.3 %collective-permute-start.6 = (bf16[272,256]{1,0:T(8,128)(2,1)S(1)}, bf16[272,256]{1,0:T(8,128)(2,1)S(1)}, u32[]{:S(2)}, u32[]{:S(2)}) collective-permute-start(bf16[272,256]{1,0:T(8,128)(2,1)S(1)} %sum_with_gain.1.refs_2_.a_ref.x_ref), channel_id=1, source_target_pairs={{0,4},{4,0},{8,12},{12,8},{1,5},{5,1},{9,13},{13,9},{2,6},{6,2},{1... | collective-permute-start | bytes 417800 | tf_op jit(solution)/shard_map/ppermute | solution.py:32
  39.6 8.8 %copy-start.5 = (f32[1,4096]{1,0:T(1,128)S(1)}, f32[1,4096]{1,0:T(1,128)}, u32[]{:S(2)}) copy-start(f32[1,4096]{1,0:T(1,128)} %gain_ref.1) | copy-start | bytes 49156
  39.7 8.7 %collective-permute-start.11 = (bf16[128,512]{1,0:T(8,128)(2,1)S(1)}, bf16[128,512]{1,0:T(8,128)(2,1)S(1)}, u32[]{:S(2)}, u32[]{:S(2)}) collective-permute-start(bf16[128,512]{1,0:T(8,128)(2,1)S(1)} %get-tuple-element.46.after.refs_0_), channel_id=1, source_target_pairs={{0,1},{1,0},{2,3},{3,2},{4,5},{5,4},{6,7},{7,6},{8,9},{9,8},{10,11... | collective-permute-start | bytes 393224 | tf_op jit(solution)/shard_map/ppermute | solution.py:32
  40.5 7.9 %collective-permute-start.12 = (bf16[128,512]{1,0:T(8,128)(2,1)S(1)}, bf16[128,512]{1,0:T(8,128)(2,1)S(1)}, u32[]{:S(2)}, u32[]{:S(2)}) collective-permute-start(bf16[128,512]{1,0:T(8,128)(2,1)S(1)} %get-tuple-element.49.refs_1_), channel_id=1, source_target_pairs={{0,1},{1,0},{2,3},{3,2},{4,5},{5,4},{6,7},{7,6},{8,9},{9,8},{10,11... | collective-permute-start | bytes 393224 | tf_op jit(solution)/shard_map/ppermute | solution.py:32
  43.5 7.5 %collective-permute-start.9 = (bf16[256,256]{1,0:T(8,128)(2,1)S(1)}, bf16[256,256]{1,0:T(8,128)(2,1)S(1)}, u32[]{:S(2)}, u32[]{:S(2)}) collective-permute-start(bf16[256,256]{1,0:T(8,128)(2,1)S(1)} %pair_sum.6.refs_6_.y_ref), channel_id=1, source_target_pairs={{0,4},{4,0},{8,12},{12,8},{1,5},{5,1},{9,13},{13,9},{2,6},{6,2},{1... | collective-permute-start | bytes 393224 | tf_op jit(solution)/shard_map/ppermute | solution.py:32
  45.8 2.6 %collective-permute-start.13 = (bf16[128,256]{1,0:T(8,128)(2,1)S(1)}, bf16[128,256]{1,0:T(8,128)(2,1)S(1)}, u32[]{:S(2)}, u32[]{:S(2)}) collective-permute-start(bf16[128,256]{1,0:T(8,128)(2,1)S(1)} %get-tuple-element.50.refs_2_), channel_id=1, source_target_pairs={{0,1},{1,0},{2,3},{3,2},{4,5},{5,4},{6,7},{7,6},{8,9},{9,8},{10,11... | collective-permute-start | bytes 196616 | tf_op jit(solution)/shard_map/ppermute | solution.py:32
  47.1 3.5 %collective-permute-start.10 = (f32[8,256]{1,0:T(8,128)S(1)}, f32[8,256]{1,0:T(8,128)S(1)}, u32[]{:S(2)}, u32[]{:S(2)}) collective-permute-start(f32[8,256]{1,0:T(8,128)S(1)} %gain_total.1.after.a_ref), channel_id=1, source_target_pairs={{0,2},{1,3},{2,0},{3,1},{4,6},{5,7},{6,4},{7,5},{8,10},{9,11},{10,... | collective-permute-start | bytes 24584 | tf_op jit(solution)/shard_map/ppermute | solution.py:32
  50.6 1.2 %collective-permute-start.14 = (f32[8,256]{1,0:T(8,128)S(1)}, f32[8,256]{1,0:T(8,128)S(1)}, u32[]{:S(2)}, u32[]{:S(2)}) collective-permute-start(f32[8,256]{1,0:T(8,128)S(1)} %pair_sum.7.gain_ref), channel_id=1, source_target_pairs={{0,1},{1,0},{2,3},{3,2},{4,5},{5,4},{6,7},{7,6},{8,9},{9,8},{10,11... | collective-permute-start | bytes 24584 | tf_op jit(solution)/shard_map/ppermute | solution.py:32

commit v11 on v7

--- a/solution.py
+++ b/solution.py
@@ -17,7 +17,7 @@
 VMEM_BYTES = 24 * 1024 * 1024
 CHUNK = 512
 PIECE = 1024
-AHEAD = 3
+AHEAD = 4
 LOG2E = 1.4426950408889634
 
 
@@ -97,7 +97,7 @@
 def project_kernel(
     back_hbm, gain_hbm, u_hbm, wq_hbm, wk_hbm, wv_hbm, wo_hbm,
     m_ref, o_ref, inv_ref, u, wq, narrow, turned,
-    back, gain, wo, scaled, m_acc, o_acc, sems,
+    back, gain, wo, scaled, m_acc, sems,
 ):
     wide, rank = u.shape
     nq = wq.shape[1]
@@ -110,7 +110,9 @@
     pairs += [(wk_hbm, narrow.at[:, pl.ds(0, nk)])]
     pairs += [(wv_hbm, narrow.at[:, pl.ds(nk, narrow.shape[1] - nk)])]
     pairs += [(wq_hbm.at[at, :], wq.at[at, :]) for at in pieces[2:]]
-    pairs += [(wo_hbm.at[:, at], wo.at[:, at]) for at in pieces]
+    block = wo.shape[0] // parts
+    blocks = [pl.ds(i * block, block) for i in range(parts)]
+    pairs += [(wo_hbm.at[at, :], wo.at[at, :]) for at in blocks]
     copies = [
         pltpu.make_async_copy(source, target, sems.at[n])
         for n, (source, target) in enumerate(pairs)
@@ -159,15 +161,10 @@
             m_acc[...] += part
     for p, piece in enumerate(split(m_acc[...], 2)):
         m_ref[p * rank : (p + 1) * rank, :nq] = piece
-    for i, at in enumerate(pieces):
+    for _ in blocks:
         wait(place)
         place += 1
-        part = nn(wo[:, at], u[at, :])
-        if i == 0:
-            o_acc[...] = part
-        else:
-            o_acc[...] += part
-    o_ref[...] = o_acc[...].astype(BF)
+    o_ref[...] = nn(wo[...], u[...]).astype(BF)
 
 
 def project(back, gain, basis, wq, wk, wv, wo):
@@ -196,7 +193,6 @@
             pltpu.VMEM(wo.shape, BF),
             pltpu.VMEM((rank, wide), BF),
             pltpu.VMEM((rank, nq), F32),
-            pltpu.VMEM((ne, rank), F32),
             pltpu.SemaphoreType.DMA((4 + 3 * (wide // PIECE),)),
         ],
         compiler_params=pltpu.CompilerParams(vmem_limit_bytes=VMEM_BYTES * 3 // 2),
@@ -209,9 +205,10 @@
     length = coeffs.shape[0]
     heads = q.shape[0] // length
     twice = jnp.concatenate([coeffs, coeffs], axis=1)
-    for h in range(heads):
-        part = nn(twice, m_ref[:, h * HD : (h + 1) * HD]) * inv
-        q[h * length : (h + 1) * length, :] = rope(part, cosine, sine).astype(BF)
+    for h in range(0, heads, 2):
+        both = nn(twice, m_ref[:, h * HD : (h + 2) * HD]) * inv
+        for part, at in ((both[:, :HD], h * length), (both[:, HD:], (h + 1) * length)):
+            q[at : at + length, :] = rope(part, cosine, sine).astype(BF)
     part = nn(twice, m_ref[:, heads * HD :]) * inv
     k[...] = rope(part[:, :HD], cosine, sine).astype(BF)
     v1[:, :HD] = part[:, HD:].astype(BF)
@@ -253,8 +250,10 @@
     inv = inv_ref[...]
     project_heads(back, inv[:, :1], m_ref, cosine, sine, q, k, v1)
     scores[...] = nt(q[...], k[...])
-    for h in range(count):
-        gh[h * length : (h + 1) * length, :] = nt(up, o_ref[h * HD : (h + 1) * HD, :]).astype(BF)
+    for h in range(0, count, 2):
+        both = nt(up, o_ref[h * HD : (h + 2) * HD, :]).astype(BF)
+        gh[h * length : (h + 1) * length, :] = both[:, :HD]
+        gh[(h + 1) * length : (h + 2) * length, :] = both[:, HD:]
     exps_of(scores, scores, low, length)
     mixed[...] = nn(low[...], v1[...])
     gp[...] = nt(gh[...], v1[:, :HD])

time: 51.9 us -> 51.2 us (0.987)
  Pallas kernels: 29 us -> 28.1 us
  transfers between devices with their start and end apart: 15 -> 15, of which waited for: 4 -> 4; matrix products, arithmetic and copies ran while one was open for 0% -> 0% of each run, Pallas kernels for 44% -> 43%
where the time goes in v11:
time: 51.2 us; the launch traced here: 51.1 us
  Pallas kernels  28.1 us (55%)
  starting transfers between devices  16.7 us (33%)
  waiting for transfers between devices  4.61 us (9%)
  other arithmetic  0.93 us (2%)
  between operations  0.76 us (1%)
    ppermute x15, starting transfers between devices, swap(): return lax.ppermute(x, axis, [(i, i ^ bit) for i in range(devices)])  16.7 us
    pallas_call x1, Pallas kernels, project(): pl.pallas_call(project_kernel, in_specs=[pl.BlockSpec(memory_space=pltpu....  10.6 us
    pallas_call x1, Pallas kernels, backward(): pl.pallas_call(backward_kernel, in_specs=vmem(8), out_specs=vmem(4), out_...  4.89 us
    ppermute x15, waiting for transfers between devices, swap(): return lax.ppermute(x, axis, [(i, i ^ bit) for i in range(devices)])  4.61 us
    pallas_call x1, Pallas kernels, forward(): pl.pallas_call(forward_kernel, in_specs=vmem(7) + [pl.BlockSpec(memory_sp...  3.51 us
    pallas_call x1, Pallas kernels, inward_grads(): pl.pallas_call(functools.partial(inward_kernel, len(own)), grid=(STEPS,),...  2.21 us
    pallas_call x1, Pallas kernels, outward_grad(): pl.pallas_call(functools.partial(outward_kernel, len(own)), grid=(STEPS,)...  2 us
    pallas_call x1, Pallas kernels, gain_part(): pl.pallas_call(gain_kernel, in_specs=vmem(6) + [pl.BlockSpec(memory_space...  1.84 us
  transfers between devices with their start and end apart: 15, of which 4 were waited for; matrix products, arithmetic and copies ran while one was open for 0% of the time, Pallas kernels for 43%

profile of v11, /device:TPU:17, one launch (start us, length us, event | category | flops | bytes accessed | tf_op | source)
XLA Modules:
  0.0 51.1 jit_solution(3878086019804696190)
XLA Ops:
  0.6 0.9 %select_bitcast_fusion = bf16[256,256]{1,0:T(8,128)(2,1)S(1)} fusion(bf16[1,256,256]{2,1,0:T(8,128)(2,1)} %param.15, bf16[1,256,256]{2,1,0:T(8,128)(2,1)} %param.16, pred[]{:T(512)S(6)} %eq.3), kind=kLoop, calls=%fused_computation | loop fusion | flops 65536 | bytes 393217 | tf_op jit(solution)/shard_map/jit(_where)/select_n | solution.py:39
  1.6 1.3 %collective-permute-start = (bf16[256,256]{1,0:T(8,128)(2,1)S(1)}, bf16[256,256]{1,0:T(8,128)(2,1)S(1)}, u32[]{:S(2)}, u32[]{:S(2)}) collective-permute-start(bf16[256,256]{1,0:T(8,128)(2,1)S(1)} %select_bitcast_fusion), channel_id=1, source_target_pairs={{0,16},{16,0},{1,17},{17,1},{2,18},{18,2},{3,19},{19,3},{4,20},{20... | collective-permute-start | bytes 393224 | tf_op jit(solution)/shard_map/ppermute | solution.py:32
  2.9 10.6 %project_weights.1 = (bf16[512,1280]{1,0:T(8,128)(2,1)S(1)}, bf16[1024,256]{1,0:T(8,128)(2,1)S(1)}, f32[256,128]{1,0:T(8,128)S(1)}, bf16[4096,256]{1,0:T(8,128)(...) custom-call(bf16[256,256]{1,0:T(8,128)(2,1)} %bitcast.13, ...), custom_call_target="tpu_custom_call" | custom-call | flops 6000000000 | bytes 20000000 | tf_op jit(solution)/shard_map/project_weights/pallas_call | solution.py:177
  13.5 4.9 %attention_backward.1 = (bf16[256,1280]{1,0:T(8,128)(2,1)S(1)}, bf16[128,1024]{1,0:T(8,128)(2,1)S(1)}, bf16[128,1024]{1,0:T(8,128)(2,1)S(1)}, bf16[256,256]{1,0:T(8,128)(2,1)S(1)}) custom-call(bf16[256,256]{1,0:T(8,128)(2,1)S(1)} %bitcast.14, bf16[256,256]{1,0:T(8,128)(2,1)S(1)} %copy-done.1, ...), custom_call_target="tpu_custom_call" | custom-call | flops 10000 | bytes 1000 | tf_op jit(solution)/shard_map/attention_backward/pallas_call | solution.py:301
  18.4 1.0 %collective-permute-start.1 = (bf16[256,1280]{1,0:T(8,128)(2,1)S(1)}, bf16[256,1280]{1,0:T(8,128)(2,1)S(1)}, u32[]{:S(2)}, u32[]{:S(2)}) collective-permute-start(bf16[256,1280]{1,0:T(8,128)(2,1)S(1)} %get-tuple-element.41.inner_ref), channel_id=1, source_target_pairs={{0,1},{1,0},{2,3},{3,2},{4,5},{5,4},{6,7},{7,6},{8,9},{9,8},{10,11... | collective-permute-start | bytes 1966088 | tf_op jit(solution)/shard_map/ppermute | solution.py:32
  19.5 1.7 %encoded_again.1 = (f32[256,256]{1,0:T(8,128)S(1)}, f32[256,256]{1,0:T(8,128)S(1)}, f32[256,256]{1,0:T(8,128)S(1)}) custom-call(bf16[256,256]{1,0:T(8,128)(2,1)S(1)} %bitcast.15, bf16[256,256]{1,0:T(8,128)(2,1)S(1)} %copy-done.1, bf16[256,256]{1,0:T(8,128)(2,1)S(1)} %collective-permute-done.sent_ref.returned_ref.arrived_ref, bf16[256,256]{1,0:T(8,128)(2,1)S(1)} %copy-done.2, ...), custom_call_target="tpu_custom_call" | custom-call | flops 10000 | bytes 1000 | tf_op jit(solution)/shard_map/encoded_again/pallas_call | solution.py:352
  21.2 0.3 collective-permute-done.2.b_ref
  21.6 1.3 %collective-permute-start.5 = (bf16[128,1024]{1,0:T(8,128)(2,1)S(1)}, bf16[128,1024]{1,0:T(8,128)(2,1)S(1)}, u32[]{:S(2)}, u32[]{:S(2)}) collective-permute-start(bf16[128,1024]{1,0:T(8,128)(2,1)S(1)} %pair_sum.4.after.a_ref), channel_id=1, source_target_pairs={{0,2},{1,3},{2,0},{3,1},{4,6},{5,7},{6,4},{7,5},{8,10},{9,11},{10,... | collective-permute-start | bytes 786440 | tf_op jit(solution)/shard_map/ppermute | solution.py:32
  22.9 1.8 %pair_sum_and_gain_gradient.1 = (bf16[128,1280]{1,0:T(8,128)(2,1)S(1)}, bf16[272,256]{1,0:T(8,128)(2,1)S(1)}) custom-call(bf16[4096,256]{1,0:T(8,128)(2,1)S(1)} %get-tuple-element.32.u_ref, bf16[4096,1024]{1,0:T(8,128)(2,1)S(1)} %get-tuple-element.39.wq_ref, bf16[4096,256]{1,0:T(8,128)(2,1)S(1)} %get-tuple-element.40.narrow_ref, ...), custom_call_target="tpu_custom_call" | custom-call | flops 10000 | bytes 1000 | tf_op jit(solution)/shard_map/pair_sum_and_gain_gradient/pallas_call | solution.py:457
  25.1 3.5 %attention_forward.1.after.a_ref = bf16[288,256]{1,0:T(8,128)(2,1)S(1)} custom-call(bf16[256,256]{1,0:T(8,128)(2,1)S(1)} %copy-done.2, bf16[256,256]{1,0:T(8,128)(2,1)S(1)} %collective-permute-done.sent_ref.returned_ref.arrived_ref, bf16[256,4096]{1,0:T(8,128)(2,1)S(1)} %get-tuple-element.33.turned_ref, bf16[512,1280]{1,0:T(8,128)(2,1)S(1)} %get-tuple-element.35.m_ref, ...), custom_call_target="tpu_custom_call" | custom-call | flops 10000 | bytes 1000 | tf_op jit(solution)/shard_map/attention_forward/pallas_call | solution.py:394
  28.6 0.6 %collective-permute-done.5.b_ref = bf16[128,1024]{1,0:T(8,128)(2,1)S(1)} collective-permute-done((bf16[128,1024]{1,0:T(8,128)(2,1)S(1)}, bf16[128,1024]{1,0:T(8,128)(2,1)S(1)}, u32[]{:S(2)}, u32[]{:S(2)}) %collective-permute-start.5) | collective-permute-done | bytes 262176 | tf_op jit(solution)/shard_map/ppermute | solution.py:32
  29.2 2.1 %collective-permute-start.8 = (bf16[128,1024]{1,0:T(8,128)(2,1)S(1)}, bf16[128,1024]{1,0:T(8,128)(2,1)S(1)}, u32[]{:S(2)}, u32[]{:S(2)}) collective-permute-start(bf16[128,1024]{1,0:T(8,128)(2,1)S(1)} %pair_sum.5.after.refs_0_), channel_id=1, source_target_pairs={{0,1},{1,0},{2,3},{3,2},{4,5},{5,4},{6,7},{7,6},{8,9},{9,8},{10,11... | collective-permute-start | bytes 786440 | tf_op jit(solution)/shard_map/ppermute | solution.py:32
  31.3 1.0 %collective-permute-start.3 = (bf16[288,256]{1,0:T(8,128)(2,1)S(1)}, bf16[288,256]{1,0:T(8,128)(2,1)S(1)}, u32[]{:S(2)}, u32[]{:S(2)}) collective-permute-start(bf16[288,256]{1,0:T(8,128)(2,1)S(1)} %attention_forward.1.after.a_ref), channel_id=1, source_target_pairs={{0,8},{4,12},{8,0},{12,4},{1,9},{5,13},{9,1},{13,5},{2,10},{6,14},... | collective-permute-start | bytes 442376 | tf_op jit(solution)/shard_map/ppermute | solution.py:32
  32.3 3.5 %collective-permute-start.6 = (bf16[272,256]{1,0:T(8,128)(2,1)S(1)}, bf16[272,256]{1,0:T(8,128)(2,1)S(1)}, u32[]{:S(2)}, u32[]{:S(2)}) collective-permute-start(bf16[272,256]{1,0:T(8,128)(2,1)S(1)} %sum_with_gain.1.refs_2_.a_ref.x_ref), channel_id=1, source_target_pairs={{0,4},{4,0},{8,12},{12,8},{1,5},{5,1},{9,13},{13,9},{2,6},{6,2},{1... | collective-permute-start | bytes 417800 | tf_op jit(solution)/shard_map/ppermute | solution.py:32
  35.8 2.0 %output_weight_gradient.1.after = bf16[1024,1024]{1,0:T(8,128)(2,1)} custom-call(bf16[4096,256]{1,0:T(8,128)(2,1)S(1)} %get-tuple-element.32.u_ref, bf16[128,1024]{1,0:T(8,128)(2,1)S(1)} %pair_sum.5.after.refs_0_, bf16[128,1024]{1,0:T(8,128)(2,1)S(1)} %collective-permute-done.8.refs_1_, bf16[272,256]{1,0:T(8,128)(2,1)S(1)} %sum_with_gain.1.refs_2_.a_ref.x_ref), custom_call_target="tpu_custom_call" | custom-call | flops 10000 | bytes 1000 | tf_op jit(solution)/shard_map/output_weight_gradient/pallas_call | solution.py:597
  37.9 0.8 %collective-permute-start.11 = (bf16[128,512]{1,0:T(8,128)(2,1)S(1)}, bf16[128,512]{1,0:T(8,128)(2,1)S(1)}, u32[]{:S(2)}, u32[]{:S(2)}) collective-permute-start(bf16[128,512]{1,0:T(8,128)(2,1)S(1)} %get-tuple-element.46.after.refs_0_), channel_id=1, source_target_pairs={{0,1},{1,0},{2,3},{3,2},{4,5},{5,4},{6,7},{7,6},{8,9},{9,8},{10,11... | collective-permute-start | bytes 393224 | tf_op jit(solution)/shard_map/ppermute | solution.py:32
  38.8 2.8 %collective-permute-done.6.b_ref.xgot_ref = bf16[272,256]{1,0:T(8,128)(2,1)S(1)} collective-permute-done((bf16[272,256]{1,0:T(8,128)(2,1)S(1)}, bf16[272,256]{1,0:T(8,128)(2,1)S(1)}, u32[]{:S(2)}, u32[]{:S(2)}) %collective-permute-start.6) | collective-permute-done | bytes 139296 | tf_op jit(solution)/shard_map/ppermute | solution.py:32
  41.7 2.3 %collective-permute-start.9 = (bf16[256,256]{1,0:T(8,128)(2,1)S(1)}, bf16[256,256]{1,0:T(8,128)(2,1)S(1)}, u32[]{:S(2)}, u32[]{:S(2)}) collective-permute-start(bf16[256,256]{1,0:T(8,128)(2,1)S(1)} %pair_sum.6.refs_6_.y_ref), channel_id=1, source_target_pairs={{0,4},{4,0},{8,12},{12,8},{1,5},{5,1},{9,13},{13,9},{2,6},{6,2},{1... | collective-permute-start | bytes 393224 | tf_op jit(solution)/shard_map/ppermute | solution.py:32
  44.0 1.4 %collective-permute-start.13 = (bf16[128,256]{1,0:T(8,128)(2,1)S(1)}, bf16[128,256]{1,0:T(8,128)(2,1)S(1)}, u32[]{:S(2)}, u32[]{:S(2)}) collective-permute-start(bf16[128,256]{1,0:T(8,128)(2,1)S(1)} %get-tuple-element.50.refs_2_), channel_id=1, source_target_pairs={{0,1},{1,0},{2,3},{3,2},{4,5},{5,4},{6,7},{7,6},{8,9},{9,8},{10,11... | collective-permute-start | bytes 196616 | tf_op jit(solution)/shard_map/ppermute | solution.py:32
  45.4 1.2 %collective-permute-start.10 = (f32[8,256]{1,0:T(8,128)S(1)}, f32[8,256]{1,0:T(8,128)S(1)}, u32[]{:S(2)}, u32[]{:S(2)}) collective-permute-start(f32[8,256]{1,0:T(8,128)S(1)} %gain_total.1.after.a_ref), channel_id=1, source_target_pairs={{0,2},{1,3},{2,0},{3,1},{4,6},{5,7},{6,4},{7,5},{8,10},{9,11},{10,... | collective-permute-start | bytes 24584 | tf_op jit(solution)/shard_map/ppermute | solution.py:32
  46.6 2.2 %inward_weight_gradients.1 = (bf16[1024,1024]{1,0:T(8,128)(2,1)}, bf16[1024,128]{1,0:T(8,128)(2,1)}, bf16[1024,128]{1,0:T(8,128)(2,1)}) custom-call(bf16[4096,256]{1,0:T(8,128)(2,1)S(1)} %get-tuple-element.32.u_ref, f32[1,4096]{1,0:T(1,128)S(1)} %copy-done.5, bf16[128,512]{1,0:T(8,128)(2,1)S(1)} %get-tuple-element.46.after.refs_0_, ...), custom_call_target="tpu_custom_call" | custom-call | flops 10000 | bytes 1000 | tf_op jit(solution)/shard_map/inward_weight_gradients/pallas_call | solution.py:580
  48.8 0.3 collective-permute-start.14
  49.2 0.9 %collective-permute-done.14.gain_other_ref = f32[8,256]{1,0:T(8,128)S(1)} collective-permute-done((f32[8,256]{1,0:T(8,128)S(1)}, f32[8,256]{1,0:T(8,128)S(1)}, u32[]{:S(2)}, u32[]{:S(2)}) %collective-permute-start.14) | collective-permute-done | bytes 8224 | tf_op jit(solution)/shard_map/ppermute | solution.py:32
  50.1 1.0 %section_results.1 = (bf16[256,256]{1,0:T(8,128)(2,1)}, bf16[256,256]{1,0:T(8,128)(2,1)}, f32[1,4096]{1,0:T(1,128)}) custom-call(f32[256,256]{1,0:T(8,128)S(1)} %get-tuple-element.38.after.fbase_ref, bf16[256,256]{1,0:T(8,128)(2,1)S(1)} %pair_sum.6.refs_6_.y_ref, bf16[256,256]{1,0:T(8,128)(2,1)S(1)} %collective-permute-done.9.ygot_ref, ...), custom_call_target="tpu_custom_call" | custom-call | flops 10000 | bytes 1000 | tf_op jit(solution)/shard_map/section_results/pallas_call | solution.py:635
  (34 shorter events, 0.8 us)
Async XLA Ops:
  1.6 11.9 %collective-permute-start = (bf16[256,256]{1,0:T(8,128)(2,1)S(1)}, bf16[256,256]{1,0:T(8,128)(2,1)S(1)}, u32[]{:S(2)}, u32[]{:S(2)}) collective-permute-start(bf16[256,256]{1,0:T(8,128)(2,1)S(1)} %select_bitcast_fusion), channel_id=1, source_target_pairs={{0,16},{16,0},{1,17},{17,1},{2,18},{18,2},{3,19},{19,3},{4,20},{20... | collective-permute-start | bytes 393224 | tf_op jit(solution)/shard_map/ppermute | solution.py:32
  2.9 10.6 %copy-start = (bf16[1,256,256]{2,1,0:T(8,128)(2,1)S(1)}, bf16[1,256,256]{2,1,0:T(8,128)(2,1)}, u32[]{:S(2)}) copy-start(bf16[1,256,256]{2,1,0:T(8,128)(2,1)} %param.17) | copy-start | bytes 393220
  2.9 10.6 %copy-start.1 = (bf16[256,256]{1,0:T(8,128)(2,1)S(1)}, bf16[256,256]{1,0:T(8,128)(2,1)}, u32[]{:S(2)}) copy-start(bf16[256,256]{1,0:T(8,128)(2,1)} %loss_ref.3) | copy-start | bytes 393220
  2.9 10.7 %copy-start.3 = (f32[256,128]{1,0:T(8,128)S(1)}, f32[256,128]{1,0:T(8,128)}, u32[]{:S(2)}) copy-start(f32[256,128]{1,0:T(8,128)} %constant.12.clone.cos_ref) | copy-start | bytes 393220
  2.9 10.7 %copy-start.4 = (f32[256,128]{1,0:T(8,128)S(1)}, f32[256,128]{1,0:T(8,128)}, u32[]{:S(2)}) copy-start(f32[256,128]{1,0:T(8,128)} %constant.13.clone.sin_ref) | copy-start | bytes 393220
  13.5 6.1 %copy-start.2 = (bf16[256,256]{1,0:T(8,128)(2,1)S(1)}, bf16[256,256]{1,0:T(8,128)(2,1)}, u32[]{:S(2)}) copy-start(bf16[256,256]{1,0:T(8,128)(2,1)} %new_ref.3) | copy-start | bytes 393220
  18.4 4.5 %collective-permute-start.1 = (bf16[256,1280]{1,0:T(8,128)(2,1)S(1)}, bf16[256,1280]{1,0:T(8,128)(2,1)S(1)}, u32[]{:S(2)}, u32[]{:S(2)}) collective-permute-start(bf16[256,1280]{1,0:T(8,128)(2,1)S(1)} %get-tuple-element.41.inner_ref), channel_id=1, source_target_pairs={{0,1},{1,0},{2,3},{3,2},{4,5},{5,4},{6,7},{7,6},{8,9},{9,8},{10,11... | collective-permute-start | bytes 1966088 | tf_op jit(solution)/shard_map/ppermute | solution.py:32
  19.4 2.1 %collective-permute-start.2 = (bf16[128,1024]{1,0:T(8,128)(2,1)S(1)}, bf16[128,1024]{1,0:T(8,128)(2,1)S(1)}, u32[]{:S(2)}, u32[]{:S(2)}) collective-permute-start(bf16[128,1024]{1,0:T(8,128)(2,1)S(1)} %get-tuple-element.43), channel_id=1, source_target_pairs={{0,1},{1,0},{2,3},{3,2},{4,5},{5,4},{6,7},{7,6},{8,9},{9,8},{10,11... | collective-permute-start | bytes 786440 | tf_op jit(solution)/shard_map/ppermute | solution.py:32
  21.6 7.6 %collective-permute-start.5 = (bf16[128,1024]{1,0:T(8,128)(2,1)S(1)}, bf16[128,1024]{1,0:T(8,128)(2,1)S(1)}, u32[]{:S(2)}, u32[]{:S(2)}) collective-permute-start(bf16[128,1024]{1,0:T(8,128)(2,1)S(1)} %pair_sum.4.after.a_ref), channel_id=1, source_target_pairs={{0,2},{1,3},{2,0},{3,1},{4,6},{5,7},{6,4},{7,5},{8,10},{9,11},{10,... | collective-permute-start | bytes 786440 | tf_op jit(solution)/shard_map/ppermute | solution.py:32
  24.7 13.1 %collective-permute-start.7 = (bf16[128,1280]{1,0:T(8,128)(2,1)S(1)}, bf16[128,1280]{1,0:T(8,128)(2,1)S(1)}, u32[]{:S(2)}, u32[]{:S(2)}) collective-permute-start(bf16[128,1280]{1,0:T(8,128)(2,1)S(1)} %get-tuple-element.44.after.a_ref), channel_id=1, source_target_pairs={{0,2},{1,3},{2,0},{3,1},{4,6},{5,7},{6,4},{7,5},{8,10},{9,11},{10,... | collective-permute-start | bytes 983048 | tf_op jit(solution)/shard_map/ppermute | solution.py:32
  25.0 7.3 %collective-permute-start.4 = (bf16[272,256]{1,0:T(8,128)(2,1)S(1)}, bf16[272,256]{1,0:T(8,128)(2,1)S(1)}, u32[]{:S(2)}, u32[]{:S(2)}) collective-permute-start(bf16[272,256]{1,0:T(8,128)(2,1)S(1)} %get-tuple-element.45.a_ref), channel_id=1, source_target_pairs={{0,8},{4,12},{8,0},{12,4},{1,9},{5,13},{9,1},{13,5},{2,10},{6,14},... | collective-permute-start | bytes 417800 | tf_op jit(solution)/shard_map/ppermute | solution.py:32
  29.2 6.6 %collective-permute-start.8 = (bf16[128,1024]{1,0:T(8,128)(2,1)S(1)}, bf16[128,1024]{1,0:T(8,128)(2,1)S(1)}, u32[]{:S(2)}, u32[]{:S(2)}) collective-permute-start(bf16[128,1024]{1,0:T(8,128)(2,1)S(1)} %pair_sum.5.after.refs_0_), channel_id=1, source_target_pairs={{0,1},{1,0},{2,3},{3,2},{4,5},{5,4},{6,7},{7,6},{8,9},{9,8},{10,11... | collective-permute-start | bytes 786440 | tf_op jit(solution)/shard_map/ppermute | solution.py:32
  31.3 10.3 %collective-permute-start.3 = (bf16[288,256]{1,0:T(8,128)(2,1)S(1)}, bf16[288,256]{1,0:T(8,128)(2,1)S(1)}, u32[]{:S(2)}, u32[]{:S(2)}) collective-permute-start(bf16[288,256]{1,0:T(8,128)(2,1)S(1)} %attention_forward.1.after.a_ref), channel_id=1, source_target_pairs={{0,8},{4,12},{8,0},{12,4},{1,9},{5,13},{9,1},{13,5},{2,10},{6,14},... | collective-permute-start | bytes 442376 | tf_op jit(solution)/shard_map/ppermute | solution.py:32
  32.3 9.3 %collective-permute-start.6 = (bf16[272,256]{1,0:T(8,128)(2,1)S(1)}, bf16[272,256]{1,0:T(8,128)(2,1)S(1)}, u32[]{:S(2)}, u32[]{:S(2)}) collective-permute-start(bf16[272,256]{1,0:T(8,128)(2,1)S(1)} %sum_with_gain.1.refs_2_.a_ref.x_ref), channel_id=1, source_target_pairs={{0,4},{4,0},{8,12},{12,8},{1,5},{5,1},{9,13},{13,9},{2,6},{6,2},{1... | collective-permute-start | bytes 417800 | tf_op jit(solution)/shard_map/ppermute | solution.py:32
  37.8 8.8 %copy-start.5 = (f32[1,4096]{1,0:T(1,128)S(1)}, f32[1,4096]{1,0:T(1,128)}, u32[]{:S(2)}) copy-start(f32[1,4096]{1,0:T(1,128)} %gain_ref.1) | copy-start | bytes 49156
  37.9 8.7 %collective-permute-start.11 = (bf16[128,512]{1,0:T(8,128)(2,1)S(1)}, bf16[128,512]{1,0:T(8,128)(2,1)S(1)}, u32[]{:S(2)}, u32[]{:S(2)}) collective-permute-start(bf16[128,512]{1,0:T(8,128)(2,1)S(1)} %get-tuple-element.46.after.refs_0_), channel_id=1, source_target_pairs={{0,1},{1,0},{2,3},{3,2},{4,5},{5,4},{6,7},{7,6},{8,9},{9,8},{10,11... | collective-permute-start | bytes 393224 | tf_op jit(solution)/shard_map/ppermute | solution.py:32
  38.7 7.9 %collective-permute-start.12 = (bf16[128,512]{1,0:T(8,128)(2,1)S(1)}, bf16[128,512]{1,0:T(8,128)(2,1)S(1)}, u32[]{:S(2)}, u32[]{:S(2)}) collective-permute-start(bf16[128,512]{1,0:T(8,128)(2,1)S(1)} %get-tuple-element.49.refs_1_), channel_id=1, source_target_pairs={{0,1},{1,0},{2,3},{3,2},{4,5},{5,4},{6,7},{7,6},{8,9},{9,8},{10,11... | collective-permute-start | bytes 393224 | tf_op jit(solution)/shard_map/ppermute | solution.py:32
  41.7 7.5 %collective-permute-start.9 = (bf16[256,256]{1,0:T(8,128)(2,1)S(1)}, bf16[256,256]{1,0:T(8,128)(2,1)S(1)}, u32[]{:S(2)}, u32[]{:S(2)}) collective-permute-start(bf16[256,256]{1,0:T(8,128)(2,1)S(1)} %pair_sum.6.refs_6_.y_ref), channel_id=1, source_target_pairs={{0,4},{4,0},{8,12},{12,8},{1,5},{5,1},{9,13},{13,9},{2,6},{6,2},{1... | collective-permute-start | bytes 393224 | tf_op jit(solution)/shard_map/ppermute | solution.py:32
  44.0 2.6 %collective-permute-start.13 = (bf16[128,256]{1,0:T(8,128)(2,1)S(1)}, bf16[128,256]{1,0:T(8,128)(2,1)S(1)}, u32[]{:S(2)}, u32[]{:S(2)}) collective-permute-start(bf16[128,256]{1,0:T(8,128)(2,1)S(1)} %get-tuple-element.50.refs_2_), channel_id=1, source_target_pairs={{0,1},{1,0},{2,3},{3,2},{4,5},{5,4},{6,7},{7,6},{8,9},{9,8},{10,11... | collective-permute-start | bytes 196616 | tf_op jit(solution)/shard_map/ppermute | solution.py:32
  45.4 3.5 %collective-permute-start.10 = (f32[8,256]{1,0:T(8,128)S(1)}, f32[8,256]{1,0:T(8,128)S(1)}, u32[]{:S(2)}, u32[]{:S(2)}) collective-permute-start(f32[8,256]{1,0:T(8,128)S(1)} %gain_total.1.after.a_ref), channel_id=1, source_target_pairs={{0,2},{1,3},{2,0},{3,1},{4,6},{5,7},{6,4},{7,5},{8,10},{9,11},{10,... | collective-permute-start | bytes 24584 | tf_op jit(solution)/shard_map/ppermute | solution.py:32
  48.8 1.2 %collective-permute-start.14 = (f32[8,256]{1,0:T(8,128)S(1)}, f32[8,256]{1,0:T(8,128)S(1)}, u32[]{:S(2)}, u32[]{:S(2)}) collective-permute-start(f32[8,256]{1,0:T(8,128)S(1)} %pair_sum.7.gain_ref), channel_id=1, source_target_pairs={{0,1},{1,0},{2,3},{3,2},{4,5},{5,4},{6,7},{7,6},{8,9},{9,8},{10,11... | collective-permute-start | bytes 24584 | tf_op jit(solution)/shard_map/ppermute | solution.py:32

commit v12 on v11

--- a/solution.py
+++ b/solution.py
@@ -383,8 +383,7 @@
     for h in range(heads.shape[1] // HD):
         at = slice(h * length, (h + 1) * length)
         heads[:, h * HD : (h + 1) * HD] = (mixed[at, :HD] / mixed[at, HD:]).astype(BF)
-    y_ref[:length, :] = nn(heads[...], o_ref[...]).astype(BF)
-    y_ref[length:, :] = jnp.zeros_like(y_ref[length:, :])
+    y_ref[...] = nn(heads[...], o_ref[...]).astype(BF)
 
 
 def forward(new, sent, turned, m2, o2, cosine, sine, after):
@@ -395,7 +394,7 @@
         forward_kernel,
         in_specs=vmem(7) + [pl.BlockSpec(memory_space=pl.ANY)],
         out_specs=pl.BlockSpec(memory_space=pltpu.VMEM),
-        out_shape=jax.ShapeDtypeStruct((length + 32, rank), BF),
+        out_shape=jax.ShapeDtypeStruct((length, rank), BF),
         scratch_shapes=[
             pltpu.VMEM((stack, HD), BF),
             pltpu.VMEM((length, HD), BF),
@@ -681,19 +680,20 @@
     x_got = swap(x, "tensor", 2)
     y = forward(new_coeffs, arrived, turned, m2, o2, cosine, sine, pair)
     y_got = swap(y, "tensor", 2)
-    out_own = add_after(out_pair, out_got, y)
-    out_other = swap(out_own, "dp", 1)
-    x = merge(x, x_got, out_own)
+    ne = wo.shape[0]
+    out_own = own_pieces(out_pair, out_got, (ne // 2, ne - ne // 2), y)
+    out_other = [swap(piece, "dp", 1) for piece in out_own]
+    x = merge(x, x_got, out_own[0])
     x_got = swap(x, "tensor", 1)
-    grad_o = outward_grad(basis, [out_own], [out_other], x)
+    grad_o = outward_grad(basis, out_own, out_other, x)
     sizes = (nq // 2, nq - nq // 2, nk + nv)
     own = own_pieces(pair, pair_got, sizes, *in_hbm((grad_o,)))
     other = [swap(piece, "dp", 1) for piece in own]
-    gain = gain_total(x, x_got, own[0])
+    y = add_after(y, y_got, own[0])
+    y_got = swap(y, "tensor", 1)
+    gain = gain_total(x, x_got, y)
     gain_got = swap(gain, "dp", 2)
-    y = add_after(y, y_got, gain, rows=back.shape[0])
-    y_got = swap(y, "tensor", 1)
-    grad_q, grad_k, grad_v = inward_grads(basis, norm_gain, own, other, (nq, nk, nv), y)
+    grad_q, grad_k, grad_v = inward_grads(basis, norm_gain, own, other, (nq, nk, nv), gain)
     gain = add_after(gain, gain_got, *in_hbm((grad_v,)))
     gain_other = swap(gain, "dp", 1)
     forward_out, backward_out, grad_gain = results(

time: 51.2 us -> 49.2 us (0.961)
  the two profiles are of different devices: /device:TPU:17 before, /device:TPU:0 now
where the time goes in v12:
time: 49.2 us; the launch traced here: 49.1 us
  Pallas kernels  28.1 us (57%)
  starting transfers between devices  14.2 us (29%)
  waiting for transfers between devices  5.08 us (10%)
  other arithmetic  0.93 us (2%)
  between operations  0.83 us (2%)
    ppermute x16, starting transfers between devices, swap(): return lax.ppermute(x, axis, [(i, i ^ bit) for i in range(devices)])  14.2 us
    pallas_call x1, Pallas kernels, project(): pl.pallas_call(project_kernel, in_specs=[pl.BlockSpec(memory_space=pltpu....  10.6 us
    ppermute x16, waiting for transfers between devices, swap(): return lax.ppermute(x, axis, [(i, i ^ bit) for i in range(devices)])  5.08 us
    pallas_call x1, Pallas kernels, backward(): pl.pallas_call(backward_kernel, in_specs=vmem(8), out_specs=vmem(4), out_...  4.88 us
    pallas_call x1, Pallas kernels, forward(): pl.pallas_call(forward_kernel, in_specs=vmem(7) + [pl.BlockSpec(memory_sp...  3.51 us
    pallas_call x1, Pallas kernels, inward_grads(): pl.pallas_call(functools.partial(inward_kernel, len(own)), grid=(STEPS,),...  2.22 us
    pallas_call x1, Pallas kernels, outward_grad(): pl.pallas_call(functools.partial(outward_kernel, len(own)), grid=(STEPS,)...  2.02 us
    pallas_call x1, Pallas kernels, gain_part(): pl.pallas_call(gain_kernel, in_specs=vmem(6) + [pl.BlockSpec(memory_space...  1.85 us
  transfers between devices with their start and end apart: 16, of which 5 were waited for; matrix products, arithmetic and copies ran while one was open for 0% of the time, Pallas kernels for 45%

profile of v12, /device:TPU:0, one launch (start us, length us, event | category | flops | bytes accessed | tf_op | source)
XLA Modules:
  0.0 49.1 jit_solution(740177832043457566)
XLA Ops:
  0.6 0.9 %select_bitcast_fusion = bf16[256,256]{1,0:T(8,128)(2,1)S(1)} fusion(bf16[1,256,256]{2,1,0:T(8,128)(2,1)} %param.15, bf16[1,256,256]{2,1,0:T(8,128)(2,1)} %param.16, pred[]{:T(512)S(6)} %eq.3), kind=kLoop, calls=%fused_computation | loop fusion | flops 65536 | bytes 393217 | tf_op jit(solution)/shard_map/jit(_where)/select_n | solution.py:39
  1.6 3.0 %collective-permute-start = (bf16[256,256]{1,0:T(8,128)(2,1)S(1)}, bf16[256,256]{1,0:T(8,128)(2,1)S(1)}, u32[]{:S(2)}, u32[]{:S(2)}) collective-permute-start(bf16[256,256]{1,0:T(8,128)(2,1)S(1)} %select_bitcast_fusion), channel_id=1, source_target_pairs={{0,16},{16,0},{1,17},{17,1},{2,18},{18,2},{3,19},{19,3},{4,20},{20... | collective-permute-start | bytes 393224 | tf_op jit(solution)/shard_map/ppermute | solution.py:32
  4.6 10.6 %project_weights.1 = (bf16[512,1280]{1,0:T(8,128)(2,1)S(1)}, bf16[1024,256]{1,0:T(8,128)(2,1)S(1)}, f32[256,128]{1,0:T(8,128)S(1)}, bf16[4096,256]{1,0:T(8,128)(...) custom-call(bf16[256,256]{1,0:T(8,128)(2,1)} %bitcast.13, ...), custom_call_target="tpu_custom_call" | custom-call | flops 6000000000 | bytes 20000000 | tf_op jit(solution)/shard_map/project_weights/pallas_call | solution.py:177
  15.2 4.9 %attention_backward.1 = (bf16[256,1280]{1,0:T(8,128)(2,1)S(1)}, bf16[128,1024]{1,0:T(8,128)(2,1)S(1)}, bf16[128,1024]{1,0:T(8,128)(2,1)S(1)}, bf16[256,256]{1,0:T(8,128)(2,1)S(1)}) custom-call(bf16[256,256]{1,0:T(8,128)(2,1)S(1)} %bitcast.14, bf16[256,256]{1,0:T(8,128)(2,1)S(1)} %copy-done.1, ...), custom_call_target="tpu_custom_call" | custom-call | flops 10000 | bytes 1000 | tf_op jit(solution)/shard_map/attention_backward/pallas_call | solution.py:301
  20.2 0.5 %collective-permute-start.2 = (bf16[128,1024]{1,0:T(8,128)(2,1)S(1)}, bf16[128,1024]{1,0:T(8,128)(2,1)S(1)}, u32[]{:S(2)}, u32[]{:S(2)}) collective-permute-start(bf16[128,1024]{1,0:T(8,128)(2,1)S(1)} %get-tuple-element.45), channel_id=1, source_target_pairs={{0,1},{1,0},{2,3},{3,2},{4,5},{5,4},{6,7},{7,6},{8,9},{9,8},{10,11... | collective-permute-start | bytes 786440 | tf_op jit(solution)/shard_map/ppermute | solution.py:32
  20.7 1.7 %encoded_again.1 = (f32[256,256]{1,0:T(8,128)S(1)}, f32[256,256]{1,0:T(8,128)S(1)}, f32[256,256]{1,0:T(8,128)S(1)}) custom-call(bf16[256,256]{1,0:T(8,128)(2,1)S(1)} %bitcast.15, bf16[256,256]{1,0:T(8,128)(2,1)S(1)} %copy-done.1, bf16[256,256]{1,0:T(8,128)(2,1)S(1)} %collective-permute-done.sent_ref.returned_ref.arrived_ref, bf16[256,256]{1,0:T(8,128)(2,1)S(1)} %copy-done.2, ...), custom_call_target="tpu_custom_call" | custom-call | flops 10000 | bytes 1000 | tf_op jit(solution)/shard_map/encoded_again/pallas_call | solution.py:352
  22.4 0.2 collective-permute-done.2.b_ref
  22.7 1.6 %collective-permute-start.5 = (bf16[128,1024]{1,0:T(8,128)(2,1)S(1)}, bf16[128,1024]{1,0:T(8,128)(2,1)S(1)}, u32[]{:S(2)}, u32[]{:S(2)}) collective-permute-start(bf16[128,1024]{1,0:T(8,128)(2,1)S(1)} %pair_sum.3.after.a_ref), channel_id=1, source_target_pairs={{0,2},{1,3},{2,0},{3,1},{4,6},{5,7},{6,4},{7,5},{8,10},{9,11},{10,... | collective-permute-start | bytes 786440 | tf_op jit(solution)/shard_map/ppermute | solution.py:32
  24.3 1.8 %pair_sum_and_gain_gradient.1 = (bf16[128,1280]{1,0:T(8,128)(2,1)S(1)}, bf16[272,256]{1,0:T(8,128)(2,1)S(1)}) custom-call(bf16[4096,256]{1,0:T(8,128)(2,1)S(1)} %get-tuple-element.34.u_ref, bf16[4096,1024]{1,0:T(8,128)(2,1)S(1)} %get-tuple-element.41.wq_ref, bf16[4096,256]{1,0:T(8,128)(2,1)S(1)} %get-tuple-element.42.narrow_ref, ...), custom_call_target="tpu_custom_call" | custom-call | flops 10000 | bytes 1000 | tf_op jit(solution)/shard_map/pair_sum_and_gain_gradient/pallas_call | solution.py:456
  26.2 0.6 %collective-permute-start.4 = (bf16[128,1280]{1,0:T(8,128)(2,1)S(1)}, bf16[128,1280]{1,0:T(8,128)(2,1)S(1)}, u32[]{:S(2)}, u32[]{:S(2)}) collective-permute-start(bf16[128,1280]{1,0:T(8,128)(2,1)S(1)} %get-tuple-element.46.after.a_ref), channel_id=1, source_target_pairs={{0,2},{1,3},{2,0},{3,1},{4,6},{5,7},{6,4},{7,5},{8,10},{9,11},{10,... | collective-permute-start | bytes 983048 | tf_op jit(solution)/shard_map/ppermute | solution.py:32
  26.7 2.6 %collective-permute-start.8 = (bf16[272,256]{1,0:T(8,128)(2,1)S(1)}, bf16[272,256]{1,0:T(8,128)(2,1)S(1)}, u32[]{:S(2)}, u32[]{:S(2)}) collective-permute-start(bf16[272,256]{1,0:T(8,128)(2,1)S(1)} %get-tuple-element.49.a_ref), channel_id=1, source_target_pairs={{0,8},{4,12},{8,0},{12,4},{1,9},{5,13},{9,1},{13,5},{2,10},{6,14},... | collective-permute-start | bytes 417800 | tf_op jit(solution)/shard_map/ppermute | solution.py:32
  29.3 3.5 %attention_forward.1.after.a_ref = bf16[256,256]{1,0:T(8,128)(2,1)S(1)} custom-call(bf16[256,256]{1,0:T(8,128)(2,1)S(1)} %copy-done.2, bf16[256,256]{1,0:T(8,128)(2,1)S(1)} %collective-permute-done.sent_ref.returned_ref.arrived_ref, bf16[256,4096]{1,0:T(8,128)(2,1)S(1)} %get-tuple-element.35.turned_ref, bf16[512,1280]{1,0:T(8,128)(2,1)S(1)} %get-tuple-element.37.m_ref, ...), custom_call_target="tpu_custom_call" | custom-call | flops 10000 | bytes 1000 | tf_op jit(solution)/shard_map/attention_forward/pallas_call | solution.py:393
  33.0 0.5 %collective-permute-start.7 = (bf16[128,512]{1,0:T(8,128)(2,1)S(1)}, bf16[128,512]{1,0:T(8,128)(2,1)S(1)}, u32[]{:S(2)}, u32[]{:S(2)}) collective-permute-start(bf16[128,512]{1,0:T(8,128)(2,1)S(1)} %get-tuple-element.48.refs_1_), channel_id=1, source_target_pairs={{0,1},{1,0},{2,3},{3,2},{4,5},{5,4},{6,7},{7,6},{8,9},{9,8},{10,11... | collective-permute-start | bytes 393224 | tf_op jit(solution)/shard_map/ppermute | solution.py:32
  33.5 1.7 %collective-permute-start.3 = (bf16[256,256]{1,0:T(8,128)(2,1)S(1)}, bf16[256,256]{1,0:T(8,128)(2,1)S(1)}, u32[]{:S(2)}, u32[]{:S(2)}) collective-permute-start(bf16[256,256]{1,0:T(8,128)(2,1)S(1)} %attention_forward.1.after.a_ref), channel_id=1, source_target_pairs={{0,8},{4,12},{8,0},{12,4},{1,9},{5,13},{9,1},{13,5},{2,10},{6,14},... | collective-permute-start | bytes 393224 | tf_op jit(solution)/shard_map/ppermute | solution.py:32
  35.2 0.6 %collective-permute-done.8.b_ref = bf16[272,256]{1,0:T(8,128)(2,1)S(1)} collective-permute-done((bf16[272,256]{1,0:T(8,128)(2,1)S(1)}, bf16[272,256]{1,0:T(8,128)(2,1)S(1)}, u32[]{:S(2)}, u32[]{:S(2)}) %collective-permute-start.8) | collective-permute-done | bytes 139296 | tf_op jit(solution)/shard_map/ppermute | solution.py:32
  35.8 1.1 %collective-permute-start.10 = (bf16[272,256]{1,0:T(8,128)(2,1)S(1)}, bf16[272,256]{1,0:T(8,128)(2,1)S(1)}, u32[]{:S(2)}, u32[]{:S(2)}) collective-permute-start(bf16[272,256]{1,0:T(8,128)(2,1)S(1)} %sum_with_gain.1.refs_4_.a_ref.x_ref), channel_id=1, source_target_pairs={{0,4},{4,0},{8,12},{12,8},{1,5},{5,1},{9,13},{13,9},{2,6},{6,2},{1... | collective-permute-start | bytes 417800 | tf_op jit(solution)/shard_map/ppermute | solution.py:32
  36.9 2.0 %output_weight_gradient.1.after = bf16[1024,1024]{1,0:T(8,128)(2,1)} custom-call(bf16[4096,256]{1,0:T(8,128)(2,1)S(1)} %get-tuple-element.34.u_ref, bf16[128,512]{1,0:T(8,128)(2,1)S(1)} %get-tuple-element.47.after.refs_0_, bf16[128,512]{1,0:T(8,128)(2,1)S(1)} %get-tuple-element.48.refs_1_, bf16[128,512]{1,0:T(8,128)(2,1)S(1)} %collective-permute-done.6.refs_2_, ...), custom_call_target="tpu_custom_call" | custom-call | flops 10000 | bytes 1000 | tf_op jit(solution)/shard_map/output_weight_gradient/pallas_call | solution.py:596
  39.1 0.5 %collective-permute-start.13 = (bf16[128,512]{1,0:T(8,128)(2,1)S(1)}, bf16[128,512]{1,0:T(8,128)(2,1)S(1)}, u32[]{:S(2)}, u32[]{:S(2)}) collective-permute-start(bf16[128,512]{1,0:T(8,128)(2,1)S(1)} %get-tuple-element.53.refs_1_), channel_id=1, source_target_pairs={{0,1},{1,0},{2,3},{3,2},{4,5},{5,4},{6,7},{7,6},{8,9},{9,8},{10,11... | collective-permute-start | bytes 393224 | tf_op jit(solution)/shard_map/ppermute | solution.py:32
  39.6 3.2 %collective-permute-done.3.b_ref = bf16[256,256]{1,0:T(8,128)(2,1)S(1)} collective-permute-done((bf16[256,256]{1,0:T(8,128)(2,1)S(1)}, bf16[256,256]{1,0:T(8,128)(2,1)S(1)}, u32[]{:S(2)}, u32[]{:S(2)}) %collective-permute-start.3) | collective-permute-done | bytes 131104 | tf_op jit(solution)/shard_map/ppermute | solution.py:32
  43.0 1.6 %collective-permute-start.11 = (f32[8,256]{1,0:T(8,128)S(1)}, f32[8,256]{1,0:T(8,128)S(1)}, u32[]{:S(2)}, u32[]{:S(2)}) collective-permute-start(f32[8,256]{1,0:T(8,128)S(1)} %gain_total.1.refs_6_.a_ref), channel_id=1, source_target_pairs={{0,2},{1,3},{2,0},{3,1},{4,6},{5,7},{6,4},{7,5},{8,10},{9,11},{10,... | collective-permute-start | bytes 24584 | tf_op jit(solution)/shard_map/ppermute | solution.py:32
  44.6 2.2 %inward_weight_gradients.1 = (bf16[1024,1024]{1,0:T(8,128)(2,1)}, bf16[1024,128]{1,0:T(8,128)(2,1)}, bf16[1024,128]{1,0:T(8,128)(2,1)}) custom-call(bf16[4096,256]{1,0:T(8,128)(2,1)S(1)} %get-tuple-element.34.u_ref, f32[1,4096]{1,0:T(1,128)S(1)} %copy-done.5, bf16[128,512]{1,0:T(8,128)(2,1)S(1)} %get-tuple-element.50.after.refs_0_, ...), custom_call_target="tpu_custom_call" | custom-call | flops 10000 | bytes 1000 | tf_op jit(solution)/shard_map/inward_weight_gradients/pallas_call | solution.py:579
  46.9 0.2 collective-permute-start.15
  47.1 0.8 %collective-permute-done.9.ygot_ref = bf16[256,256]{1,0:T(8,128)(2,1)S(1)} collective-permute-done((bf16[256,256]{1,0:T(8,128)(2,1)S(1)}, bf16[256,256]{1,0:T(8,128)(2,1)S(1)}, u32[]{:S(2)}, u32[]{:S(2)}) %collective-permute-start.9) | collective-permute-done | bytes 131104 | tf_op jit(solution)/shard_map/ppermute | solution.py:32
  48.1 1.0 %section_results.1 = (bf16[256,256]{1,0:T(8,128)(2,1)}, bf16[256,256]{1,0:T(8,128)(2,1)}, f32[1,4096]{1,0:T(1,128)}) custom-call(f32[256,256]{1,0:T(8,128)S(1)} %get-tuple-element.40.after.fbase_ref, bf16[256,256]{1,0:T(8,128)(2,1)S(1)} %pair_sum.4.after.y_ref, bf16[256,256]{1,0:T(8,128)(2,1)S(1)} %collective-permute-done.9.ygot_ref, ...), custom_call_target="tpu_custom_call" | custom-call | flops 10000 | bytes 1000 | tf_op jit(solution)/shard_map/section_results/pallas_call | solution.py:634
  (36 shorter events, 0.9 us)
Async XLA Ops:
  1.6 13.6 %collective-permute-start = (bf16[256,256]{1,0:T(8,128)(2,1)S(1)}, bf16[256,256]{1,0:T(8,128)(2,1)S(1)}, u32[]{:S(2)}, u32[]{:S(2)}) collective-permute-start(bf16[256,256]{1,0:T(8,128)(2,1)S(1)} %select_bitcast_fusion), channel_id=1, source_target_pairs={{0,16},{16,0},{1,17},{17,1},{2,18},{18,2},{3,19},{19,3},{4,20},{20... | collective-permute-start | bytes 393224 | tf_op jit(solution)/shard_map/ppermute | solution.py:32
  4.6 10.6 %copy-start = (bf16[1,256,256]{2,1,0:T(8,128)(2,1)S(1)}, bf16[1,256,256]{2,1,0:T(8,128)(2,1)}, u32[]{:S(2)}) copy-start(bf16[1,256,256]{2,1,0:T(8,128)(2,1)} %param.17) | copy-start | bytes 393220
  4.6 10.6 %copy-start.1 = (bf16[256,256]{1,0:T(8,128)(2,1)S(1)}, bf16[256,256]{1,0:T(8,128)(2,1)}, u32[]{:S(2)}) copy-start(bf16[256,256]{1,0:T(8,128)(2,1)} %loss_ref.3) | copy-start | bytes 393220
  4.6 10.7 %copy-start.3 = (f32[256,128]{1,0:T(8,128)S(1)}, f32[256,128]{1,0:T(8,128)}, u32[]{:S(2)}) copy-start(f32[256,128]{1,0:T(8,128)} %constant.12.clone.cos_ref) | copy-start | bytes 393220
  4.6 10.7 %copy-start.4 = (f32[256,128]{1,0:T(8,128)S(1)}, f32[256,128]{1,0:T(8,128)}, u32[]{:S(2)}) copy-start(f32[256,128]{1,0:T(8,128)} %constant.13.clone.sin_ref) | copy-start | bytes 393220
  15.2 5.5 %copy-start.2 = (bf16[256,256]{1,0:T(8,128)(2,1)S(1)}, bf16[256,256]{1,0:T(8,128)(2,1)}, u32[]{:S(2)}) copy-start(bf16[256,256]{1,0:T(8,128)(2,1)} %new_ref.3) | copy-start | bytes 393220
  20.1 4.2 %collective-permute-start.1 = (bf16[256,1280]{1,0:T(8,128)(2,1)S(1)}, bf16[256,1280]{1,0:T(8,128)(2,1)S(1)}, u32[]{:S(2)}, u32[]{:S(2)}) collective-permute-start(bf16[256,1280]{1,0:T(8,128)(2,1)S(1)} %get-tuple-element.43.inner_ref), channel_id=1, source_target_pairs={{0,1},{1,0},{2,3},{3,2},{4,5},{5,4},{6,7},{7,6},{8,9},{9,8},{10,11... | collective-permute-start | bytes 1966088 | tf_op jit(solution)/shard_map/ppermute | solution.py:32
  20.2 2.5 %collective-permute-start.2 = (bf16[128,1024]{1,0:T(8,128)(2,1)S(1)}, bf16[128,1024]{1,0:T(8,128)(2,1)S(1)}, u32[]{:S(2)}, u32[]{:S(2)}) collective-permute-start(bf16[128,1024]{1,0:T(8,128)(2,1)S(1)} %get-tuple-element.45), channel_id=1, source_target_pairs={{0,1},{1,0},{2,3},{3,2},{4,5},{5,4},{6,7},{7,6},{8,9},{9,8},{10,11... | collective-permute-start | bytes 786440 | tf_op jit(solution)/shard_map/ppermute | solution.py:32
  22.7 10.1 %collective-permute-start.5 = (bf16[128,1024]{1,0:T(8,128)(2,1)S(1)}, bf16[128,1024]{1,0:T(8,128)(2,1)S(1)}, u32[]{:S(2)}, u32[]{:S(2)}) collective-permute-start(bf16[128,1024]{1,0:T(8,128)(2,1)S(1)} %pair_sum.3.after.a_ref), channel_id=1, source_target_pairs={{0,2},{1,3},{2,0},{3,1},{4,6},{5,7},{6,4},{7,5},{8,10},{9,11},{10,... | collective-permute-start | bytes 786440 | tf_op jit(solution)/shard_map/ppermute | solution.py:32
  26.2 12.7 %collective-permute-start.4 = (bf16[128,1280]{1,0:T(8,128)(2,1)S(1)}, bf16[128,1280]{1,0:T(8,128)(2,1)S(1)}, u32[]{:S(2)}, u32[]{:S(2)}) collective-permute-start(bf16[128,1280]{1,0:T(8,128)(2,1)S(1)} %get-tuple-element.46.after.a_ref), channel_id=1, source_target_pairs={{0,2},{1,3},{2,0},{3,1},{4,6},{5,7},{6,4},{7,5},{8,10},{9,11},{10,... | collective-permute-start | bytes 983048 | tf_op jit(solution)/shard_map/ppermute | solution.py:32
  26.7 9.0 %collective-permute-start.8 = (bf16[272,256]{1,0:T(8,128)(2,1)S(1)}, bf16[272,256]{1,0:T(8,128)(2,1)S(1)}, u32[]{:S(2)}, u32[]{:S(2)}) collective-permute-start(bf16[272,256]{1,0:T(8,128)(2,1)S(1)} %get-tuple-element.49.a_ref), channel_id=1, source_target_pairs={{0,8},{4,12},{8,0},{12,4},{1,9},{5,13},{9,1},{13,5},{2,10},{6,14},... | collective-permute-start | bytes 417800 | tf_op jit(solution)/shard_map/ppermute | solution.py:32
  32.9 3.9 %collective-permute-start.6 = (bf16[128,512]{1,0:T(8,128)(2,1)S(1)}, bf16[128,512]{1,0:T(8,128)(2,1)S(1)}, u32[]{:S(2)}, u32[]{:S(2)}) collective-permute-start(bf16[128,512]{1,0:T(8,128)(2,1)S(1)} %get-tuple-element.47.after.refs_0_), channel_id=1, source_target_pairs={{0,1},{1,0},{2,3},{3,2},{4,5},{5,4},{6,7},{7,6},{8,9},{9,8},{10,11... | collective-permute-start | bytes 393224 | tf_op jit(solution)/shard_map/ppermute | solution.py:32
  33.0 3.9 %collective-permute-start.7 = (bf16[128,512]{1,0:T(8,128)(2,1)S(1)}, bf16[128,512]{1,0:T(8,128)(2,1)S(1)}, u32[]{:S(2)}, u32[]{:S(2)}) collective-permute-start(bf16[128,512]{1,0:T(8,128)(2,1)S(1)} %get-tuple-element.48.refs_1_), channel_id=1, source_target_pairs={{0,1},{1,0},{2,3},{3,2},{4,5},{5,4},{6,7},{7,6},{8,9},{9,8},{10,11... | collective-permute-start | bytes 393224 | tf_op jit(solution)/shard_map/ppermute | solution.py:32
  33.5 9.3 %collective-permute-start.3 = (bf16[256,256]{1,0:T(8,128)(2,1)S(1)}, bf16[256,256]{1,0:T(8,128)(2,1)S(1)}, u32[]{:S(2)}, u32[]{:S(2)}) collective-permute-start(bf16[256,256]{1,0:T(8,128)(2,1)S(1)} %attention_forward.1.after.a_ref), channel_id=1, source_target_pairs={{0,8},{4,12},{8,0},{12,4},{1,9},{5,13},{9,1},{13,5},{2,10},{6,14},... | collective-permute-start | bytes 393224 | tf_op jit(solution)/shard_map/ppermute | solution.py:32
  35.8 7.2 %collective-permute-start.10 = (bf16[272,256]{1,0:T(8,128)(2,1)S(1)}, bf16[272,256]{1,0:T(8,128)(2,1)S(1)}, u32[]{:S(2)}, u32[]{:S(2)}) collective-permute-start(bf16[272,256]{1,0:T(8,128)(2,1)S(1)} %sum_with_gain.1.refs_4_.a_ref.x_ref), channel_id=1, source_target_pairs={{0,4},{4,0},{8,12},{12,8},{1,5},{5,1},{9,13},{13,9},{2,6},{6,2},{1... | collective-permute-start | bytes 417800 | tf_op jit(solution)/shard_map/ppermute | solution.py:32
  38.9 5.7 %copy-start.5 = (f32[1,4096]{1,0:T(1,128)S(1)}, f32[1,4096]{1,0:T(1,128)}, u32[]{:S(2)}) copy-start(f32[1,4096]{1,0:T(1,128)} %gain_ref.1) | copy-start | bytes 49156
  39.0 5.6 %collective-permute-start.12 = (bf16[128,512]{1,0:T(8,128)(2,1)S(1)}, bf16[128,512]{1,0:T(8,128)(2,1)S(1)}, u32[]{:S(2)}, u32[]{:S(2)}) collective-permute-start(bf16[128,512]{1,0:T(8,128)(2,1)S(1)} %get-tuple-element.50.after.refs_0_), channel_id=1, source_target_pairs={{0,1},{1,0},{2,3},{3,2},{4,5},{5,4},{6,7},{7,6},{8,9},{9,8},{10,11... | collective-permute-start | bytes 393224 | tf_op jit(solution)/shard_map/ppermute | solution.py:32
  39.1 5.6 %collective-permute-start.13 = (bf16[128,512]{1,0:T(8,128)(2,1)S(1)}, bf16[128,512]{1,0:T(8,128)(2,1)S(1)}, u32[]{:S(2)}, u32[]{:S(2)}) collective-permute-start(bf16[128,512]{1,0:T(8,128)(2,1)S(1)} %get-tuple-element.53.refs_1_), channel_id=1, source_target_pairs={{0,1},{1,0},{2,3},{3,2},{4,5},{5,4},{6,7},{7,6},{8,9},{9,8},{10,11... | collective-permute-start | bytes 393224 | tf_op jit(solution)/shard_map/ppermute | solution.py:32
  42.8 5.0 %collective-permute-start.9 = (bf16[256,256]{1,0:T(8,128)(2,1)S(1)}, bf16[256,256]{1,0:T(8,128)(2,1)S(1)}, u32[]{:S(2)}, u32[]{:S(2)}) collective-permute-start(bf16[256,256]{1,0:T(8,128)(2,1)S(1)} %pair_sum.4.after.y_ref), channel_id=1, source_target_pairs={{0,4},{4,0},{8,12},{12,8},{1,5},{5,1},{9,13},{13,9},{2,6},{6,2},{1... | collective-permute-start | bytes 393224 | tf_op jit(solution)/shard_map/ppermute | solution.py:32
  42.9 1.7 %collective-permute-start.14 = (bf16[128,256]{1,0:T(8,128)(2,1)S(1)}, bf16[128,256]{1,0:T(8,128)(2,1)S(1)}, u32[]{:S(2)}, u32[]{:S(2)}) collective-permute-start(bf16[128,256]{1,0:T(8,128)(2,1)S(1)} %get-tuple-element.54.refs_2_), channel_id=1, source_target_pairs={{0,1},{1,0},{2,3},{3,2},{4,5},{5,4},{6,7},{7,6},{8,9},{9,8},{10,11... | collective-permute-start | bytes 196616 | tf_op jit(solution)/shard_map/ppermute | solution.py:32
  43.0 3.8 %collective-permute-start.11 = (f32[8,256]{1,0:T(8,128)S(1)}, f32[8,256]{1,0:T(8,128)S(1)}, u32[]{:S(2)}, u32[]{:S(2)}) collective-permute-start(f32[8,256]{1,0:T(8,128)S(1)} %gain_total.1.refs_6_.a_ref), channel_id=1, source_target_pairs={{0,2},{1,3},{2,0},{3,1},{4,6},{5,7},{6,4},{7,5},{8,10},{9,11},{10,... | collective-permute-start | bytes 24584 | tf_op jit(solution)/shard_map/ppermute | solution.py:32
  46.9 1.2 %collective-permute-start.15 = (f32[8,256]{1,0:T(8,128)S(1)}, f32[8,256]{1,0:T(8,128)S(1)}, u32[]{:S(2)}, u32[]{:S(2)}) collective-permute-start(f32[8,256]{1,0:T(8,128)S(1)} %pair_sum.5.gain_ref), channel_id=1, source_target_pairs={{0,1},{1,0},{2,3},{3,2},{4,5},{5,4},{6,7},{7,6},{8,9},{9,8},{10,11... | collective-permute-start | bytes 24584 | tf_op jit(solution)/shard_map/ppermute | solution.py:32

commit v13 on v12

--- a/solution.py
+++ b/solution.py
@@ -681,7 +681,7 @@
     y = forward(new_coeffs, arrived, turned, m2, o2, cosine, sine, pair)
     y_got = swap(y, "tensor", 2)
     ne = wo.shape[0]
-    out_own = own_pieces(out_pair, out_got, (ne // 2, ne - ne // 2), y)
+    out_own = own_pieces(out_pair, out_got, (ne // 4,) * 4, y)
     out_other = [swap(piece, "dp", 1) for piece in out_own]
     x = merge(x, x_got, out_own[0])
     x_got = swap(x, "tensor", 1)

time: 49.2 us -> 49.8 us (1.012)
    ppermute x16 -> x18, starting transfers between devices: 14.2 us -> 14.5 us  [swap(): return lax.ppermute(x, axis, [(i, i ^ bit) for i in range(devices)])]
    ppermute x16 -> x18, waiting for transfers between devices: 5.08 us -> 5.31 us  [swap(): return lax.ppermute(x, axis, [(i, i ^ bit) for i in range(devices)])]
  transfers between devices with their start and end apart: 16 -> 18, of which waited for: 5 -> 7; matrix products, arithmetic and copies ran while one was open for 0% -> 0% of each run, Pallas kernels for 45% -> 45%
where the time goes in v13:
time: 49.8 us; the launch traced here: 49.7 us
  Pallas kernels  28.1 us (56%)
  starting transfers between devices  14.5 us (29%)
  waiting for transfers between devices  5.31 us (11%)
  other arithmetic  0.93 us (2%)
  between operations  0.83 us (2%)
    ppermute x18, starting transfers between devices, swap(): return lax.ppermute(x, axis, [(i, i ^ bit) for i in range(devices)])  14.5 us
    pallas_call x1, Pallas kernels, project(): pl.pallas_call(project_kernel, in_specs=[pl.BlockSpec(memory_space=pltpu....  10.6 us
    ppermute x18, waiting for transfers between devices, swap(): return lax.ppermute(x, axis, [(i, i ^ bit) for i in range(devices)])  5.31 us
    pallas_call x1, Pallas kernels, backward(): pl.pallas_call(backward_kernel, in_specs=vmem(8), out_specs=vmem(4), out_...  4.88 us
    pallas_call x1, Pallas kernels, forward(): pl.pallas_call(forward_kernel, in_specs=vmem(7) + [pl.BlockSpec(memory_sp...  3.51 us
    pallas_call x1, Pallas kernels, inward_grads(): pl.pallas_call(functools.partial(inward_kernel, len(own)), grid=(STEPS,),...  2.21 us
    pallas_call x1, Pallas kernels, outward_grad(): pl.pallas_call(functools.partial(outward_kernel, len(own)), grid=(STEPS,)...  2.03 us
    pallas_call x1, Pallas kernels, gain_part(): pl.pallas_call(gain_kernel, in_specs=vmem(6) + [pl.BlockSpec(memory_space...  1.85 us
  transfers between devices with their start and end apart: 18, of which 7 were waited for; matrix products, arithmetic and copies ran while one was open for 0% of the time, Pallas kernels for 45%

profile of v13, /device:TPU:0, one launch (start us, length us, event | category | flops | bytes accessed | tf_op | source)
XLA Modules:
  0.0 49.7 jit_solution(301534854593393631)
XLA Ops:
  0.6 0.9 %select_bitcast_fusion = bf16[256,256]{1,0:T(8,128)(2,1)S(1)} fusion(bf16[1,256,256]{2,1,0:T(8,128)(2,1)} %param.15, bf16[1,256,256]{2,1,0:T(8,128)(2,1)} %param.16, pred[]{:T(512)S(6)} %eq.3), kind=kLoop, calls=%fused_computation | loop fusion | flops 65536 | bytes 393217 | tf_op jit(solution)/shard_map/jit(_where)/select_n | solution.py:39
  1.6 3.0 %collective-permute-start = (bf16[256,256]{1,0:T(8,128)(2,1)S(1)}, bf16[256,256]{1,0:T(8,128)(2,1)S(1)}, u32[]{:S(2)}, u32[]{:S(2)}) collective-permute-start(bf16[256,256]{1,0:T(8,128)(2,1)S(1)} %select_bitcast_fusion), channel_id=1, source_target_pairs={{0,16},{16,0},{1,17},{17,1},{2,18},{18,2},{3,19},{19,3},{4,20},{20... | collective-permute-start | bytes 393224 | tf_op jit(solution)/shard_map/ppermute | solution.py:32
  4.6 10.6 %project_weights.1 = (bf16[512,1280]{1,0:T(8,128)(2,1)S(1)}, bf16[1024,256]{1,0:T(8,128)(2,1)S(1)}, f32[256,128]{1,0:T(8,128)S(1)}, bf16[4096,256]{1,0:T(8,128)(...) custom-call(bf16[256,256]{1,0:T(8,128)(2,1)} %bitcast.13, ...), custom_call_target="tpu_custom_call" | custom-call | flops 6000000000 | bytes 20000000 | tf_op jit(solution)/shard_map/project_weights/pallas_call | solution.py:177
  15.2 4.9 %attention_backward.1 = (bf16[256,1280]{1,0:T(8,128)(2,1)S(1)}, bf16[128,1024]{1,0:T(8,128)(2,1)S(1)}, bf16[128,1024]{1,0:T(8,128)(2,1)S(1)}, bf16[256,256]{1,0:T(8,128)(2,1)S(1)}) custom-call(bf16[256,256]{1,0:T(8,128)(2,1)S(1)} %bitcast.14, bf16[256,256]{1,0:T(8,128)(2,1)S(1)} %copy-done.1, ...), custom_call_target="tpu_custom_call" | custom-call | flops 10000 | bytes 1000 | tf_op jit(solution)/shard_map/attention_backward/pallas_call | solution.py:301
  20.2 0.5 collective-permute-start.2
  20.7 1.7 %encoded_again.1 = (f32[256,256]{1,0:T(8,128)S(1)}, f32[256,256]{1,0:T(8,128)S(1)}, f32[256,256]{1,0:T(8,128)S(1)}) custom-call(bf16[256,256]{1,0:T(8,128)(2,1)S(1)} %bitcast.15, bf16[256,256]{1,0:T(8,128)(2,1)S(1)} %copy-done.1, bf16[256,256]{1,0:T(8,128)(2,1)S(1)} %collective-permute-done.sent_ref.returned_ref.arrived_ref, bf16[256,256]{1,0:T(8,128)(2,1)S(1)} %copy-done.2, ...), custom_call_target="tpu_custom_call" | custom-call | flops 10000 | bytes 1000 | tf_op jit(solution)/shard_map/encoded_again/pallas_call | solution.py:352
  22.7 1.6 %collective-permute-start.5 = (bf16[128,1024]{1,0:T(8,128)(2,1)S(1)}, bf16[128,1024]{1,0:T(8,128)(2,1)S(1)}, u32[]{:S(2)}, u32[]{:S(2)}) collective-permute-start(bf16[128,1024]{1,0:T(8,128)(2,1)S(1)} %pair_sum.3.after.a_ref), channel_id=1, source_target_pairs={{0,2},{1,3},{2,0},{3,1},{4,6},{5,7},{6,4},{7,5},{8,10},{9,11},{10,... | collective-permute-start | bytes 786440 | tf_op jit(solution)/shard_map/ppermute | solution.py:32
  24.3 1.8 %pair_sum_and_gain_gradient.1 = (bf16[128,1280]{1,0:T(8,128)(2,1)S(1)}, bf16[272,256]{1,0:T(8,128)(2,1)S(1)}) custom-call(bf16[4096,256]{1,0:T(8,128)(2,1)S(1)} %get-tuple-element.36.u_ref, bf16[4096,1024]{1,0:T(8,128)(2,1)S(1)} %get-tuple-element.43.wq_ref, bf16[4096,256]{1,0:T(8,128)(2,1)S(1)} %get-tuple-element.44.narrow_ref, ...), custom_call_target="tpu_custom_call" | custom-call | flops 10000 | bytes 1000 | tf_op jit(solution)/shard_map/pair_sum_and_gain_gradient/pallas_call | solution.py:456
  26.2 0.6 %collective-permute-start.4 = (bf16[128,1280]{1,0:T(8,128)(2,1)S(1)}, bf16[128,1280]{1,0:T(8,128)(2,1)S(1)}, u32[]{:S(2)}, u32[]{:S(2)}) collective-permute-start(bf16[128,1280]{1,0:T(8,128)(2,1)S(1)} %get-tuple-element.48.after.a_ref), channel_id=1, source_target_pairs={{0,2},{1,3},{2,0},{3,1},{4,6},{5,7},{6,4},{7,5},{8,10},{9,11},{10,... | collective-permute-start | bytes 983048 | tf_op jit(solution)/shard_map/ppermute | solution.py:32
  26.7 2.6 %collective-permute-start.10 = (bf16[272,256]{1,0:T(8,128)(2,1)S(1)}, bf16[272,256]{1,0:T(8,128)(2,1)S(1)}, u32[]{:S(2)}, u32[]{:S(2)}) collective-permute-start(bf16[272,256]{1,0:T(8,128)(2,1)S(1)} %get-tuple-element.53.a_ref), channel_id=1, source_target_pairs={{0,8},{4,12},{8,0},{12,4},{1,9},{5,13},{9,1},{13,5},{2,10},{6,14},... | collective-permute-start | bytes 417800 | tf_op jit(solution)/shard_map/ppermute | solution.py:32
  29.3 3.5 %attention_forward.1.after.a_ref = bf16[256,256]{1,0:T(8,128)(2,1)S(1)} custom-call(bf16[256,256]{1,0:T(8,128)(2,1)S(1)} %copy-done.2, bf16[256,256]{1,0:T(8,128)(2,1)S(1)} %collective-permute-done.sent_ref.returned_ref.arrived_ref, bf16[256,4096]{1,0:T(8,128)(2,1)S(1)} %get-tuple-element.37.turned_ref, bf16[512,1280]{1,0:T(8,128)(2,1)S(1)} %get-tuple-element.39.m_ref, ...), custom_call_target="tpu_custom_call" | custom-call | flops 10000 | bytes 1000 | tf_op jit(solution)/shard_map/attention_forward/pallas_call | solution.py:393
  33.0 1.7 %collective-permute-start.3 = (bf16[256,256]{1,0:T(8,128)(2,1)S(1)}, bf16[256,256]{1,0:T(8,128)(2,1)S(1)}, u32[]{:S(2)}, u32[]{:S(2)}) collective-permute-start(bf16[256,256]{1,0:T(8,128)(2,1)S(1)} %attention_forward.1.after.a_ref), channel_id=1, source_target_pairs={{0,8},{4,12},{8,0},{12,4},{1,9},{5,13},{9,1},{13,5},{2,10},{6,14},... | collective-permute-start | bytes 393224 | tf_op jit(solution)/shard_map/ppermute | solution.py:32
  34.9 0.3 collective-permute-start.8
  35.3 0.5 %collective-permute-done.10.b_ref = bf16[272,256]{1,0:T(8,128)(2,1)S(1)} collective-permute-done((bf16[272,256]{1,0:T(8,128)(2,1)S(1)}, bf16[272,256]{1,0:T(8,128)(2,1)S(1)}, u32[]{:S(2)}, u32[]{:S(2)}) %collective-permute-start.10) | collective-permute-done | bytes 139296 | tf_op jit(solution)/shard_map/ppermute | solution.py:32
  36.0 1.6 %collective-permute-start.12 = (bf16[272,256]{1,0:T(8,128)(2,1)S(1)}, bf16[272,256]{1,0:T(8,128)(2,1)S(1)}, u32[]{:S(2)}, u32[]{:S(2)}) collective-permute-start(bf16[272,256]{1,0:T(8,128)(2,1)S(1)} %sum_with_gain.1.refs_8_.a_ref.x_ref), channel_id=1, source_target_pairs={{0,4},{4,0},{8,12},{12,8},{1,5},{5,1},{9,13},{13,9},{2,6},{6,2},{1... | collective-permute-start | bytes 417800 | tf_op jit(solution)/shard_map/ppermute | solution.py:32
  37.6 2.0 %output_weight_gradient.1.after = bf16[1024,1024]{1,0:T(8,128)(2,1)} custom-call(bf16[4096,256]{1,0:T(8,128)(2,1)S(1)} %get-tuple-element.36.u_ref, bf16[128,256]{1,0:T(8,128)(2,1)S(1)} %get-tuple-element.49.after.refs_0_, bf16[128,256]{1,0:T(8,128)(2,1)S(1)} %get-tuple-element.50.refs_1_, bf16[128,256]{1,0:T(8,128)(2,1)S(1)} %get-tuple-element.51.refs_2_, ...), custom_call_target="tpu_custom_call" | custom-call | flops 10000 | bytes 1000 | tf_op jit(solution)/shard_map/output_weight_gradient/pallas_call | solution.py:596
  39.8 0.5 collective-permute-start.15
  40.3 2.4 %collective-permute-done.3.b_ref = bf16[256,256]{1,0:T(8,128)(2,1)S(1)} collective-permute-done((bf16[256,256]{1,0:T(8,128)(2,1)S(1)}, bf16[256,256]{1,0:T(8,128)(2,1)S(1)}, u32[]{:S(2)}, u32[]{:S(2)}) %collective-permute-start.3) | collective-permute-done | bytes 131104 | tf_op jit(solution)/shard_map/ppermute | solution.py:32
  42.9 0.7 %collective-permute-done.12.b_ref.xgot_ref = bf16[272,256]{1,0:T(8,128)(2,1)S(1)} collective-permute-done((bf16[272,256]{1,0:T(8,128)(2,1)S(1)}, bf16[272,256]{1,0:T(8,128)(2,1)S(1)}, u32[]{:S(2)}, u32[]{:S(2)}) %collective-permute-start.12) | collective-permute-done | bytes 139296 | tf_op jit(solution)/shard_map/ppermute | solution.py:32
  43.7 1.5 %collective-permute-start.13 = (f32[8,256]{1,0:T(8,128)S(1)}, f32[8,256]{1,0:T(8,128)S(1)}, u32[]{:S(2)}, u32[]{:S(2)}) collective-permute-start(f32[8,256]{1,0:T(8,128)S(1)} %gain_total.1.refs_6_.a_ref), channel_id=1, source_target_pairs={{0,2},{1,3},{2,0},{3,1},{4,6},{5,7},{6,4},{7,5},{8,10},{9,11},{10,... | collective-permute-start | bytes 24584 | tf_op jit(solution)/shard_map/ppermute | solution.py:32
  45.2 2.2 %inward_weight_gradients.1 = (bf16[1024,1024]{1,0:T(8,128)(2,1)}, bf16[1024,128]{1,0:T(8,128)(2,1)}, bf16[1024,128]{1,0:T(8,128)(2,1)}) custom-call(bf16[4096,256]{1,0:T(8,128)(2,1)S(1)} %get-tuple-element.36.u_ref, f32[1,4096]{1,0:T(1,128)S(1)} %copy-done.5, bf16[128,512]{1,0:T(8,128)(2,1)S(1)} %get-tuple-element.54.after.refs_0_, ...), custom_call_target="tpu_custom_call" | custom-call | flops 10000 | bytes 1000 | tf_op jit(solution)/shard_map/inward_weight_gradients/pallas_call | solution.py:579
  47.5 0.3 collective-permute-done.11.ygot_ref
  47.8 0.8 %collective-permute-done.17.gain_other_ref = f32[8,256]{1,0:T(8,128)S(1)} collective-permute-done((f32[8,256]{1,0:T(8,128)S(1)}, f32[8,256]{1,0:T(8,128)S(1)}, u32[]{:S(2)}, u32[]{:S(2)}) %collective-permute-start.17) | collective-permute-done | bytes 8224 | tf_op jit(solution)/shard_map/ppermute | solution.py:32
  48.7 1.0 %section_results.1 = (bf16[256,256]{1,0:T(8,128)(2,1)}, bf16[256,256]{1,0:T(8,128)(2,1)}, f32[1,4096]{1,0:T(1,128)}) custom-call(f32[256,256]{1,0:T(8,128)S(1)} %get-tuple-element.42.after.fbase_ref, bf16[256,256]{1,0:T(8,128)(2,1)S(1)} %pair_sum.4.after.y_ref, bf16[256,256]{1,0:T(8,128)(2,1)S(1)} %collective-permute-done.11.ygot_ref, ...), custom_call_target="tpu_custom_call" | custom-call | flops 10000 | bytes 1000 | tf_op jit(solution)/shard_map/section_results/pallas_call | solution.py:634
  (40 shorter events, 1.4 us)
Async XLA Ops:
  1.6 13.6 %collective-permute-start = (bf16[256,256]{1,0:T(8,128)(2,1)S(1)}, bf16[256,256]{1,0:T(8,128)(2,1)S(1)}, u32[]{:S(2)}, u32[]{:S(2)}) collective-permute-start(bf16[256,256]{1,0:T(8,128)(2,1)S(1)} %select_bitcast_fusion), channel_id=1, source_target_pairs={{0,16},{16,0},{1,17},{17,1},{2,18},{18,2},{3,19},{19,3},{4,20},{20... | collective-permute-start | bytes 393224 | tf_op jit(solution)/shard_map/ppermute | solution.py:32
  4.6 10.6 %copy-start = (bf16[1,256,256]{2,1,0:T(8,128)(2,1)S(1)}, bf16[1,256,256]{2,1,0:T(8,128)(2,1)}, u32[]{:S(2)}) copy-start(bf16[1,256,256]{2,1,0:T(8,128)(2,1)} %param.17) | copy-start | bytes 393220
  4.6 10.6 %copy-start.1 = (bf16[256,256]{1,0:T(8,128)(2,1)S(1)}, bf16[256,256]{1,0:T(8,128)(2,1)}, u32[]{:S(2)}) copy-start(bf16[256,256]{1,0:T(8,128)(2,1)} %loss_ref.3) | copy-start | bytes 393220
  4.6 10.7 %copy-start.3 = (f32[256,128]{1,0:T(8,128)S(1)}, f32[256,128]{1,0:T(8,128)}, u32[]{:S(2)}) copy-start(f32[256,128]{1,0:T(8,128)} %constant.12.clone.cos_ref) | copy-start | bytes 393220
  4.6 10.7 %copy-start.4 = (f32[256,128]{1,0:T(8,128)S(1)}, f32[256,128]{1,0:T(8,128)}, u32[]{:S(2)}) copy-start(f32[256,128]{1,0:T(8,128)} %constant.13.clone.sin_ref) | copy-start | bytes 393220
  15.2 5.5 %copy-start.2 = (bf16[256,256]{1,0:T(8,128)(2,1)S(1)}, bf16[256,256]{1,0:T(8,128)(2,1)}, u32[]{:S(2)}) copy-start(bf16[256,256]{1,0:T(8,128)(2,1)} %new_ref.3) | copy-start | bytes 393220
  20.1 4.2 %collective-permute-start.1 = (bf16[256,1280]{1,0:T(8,128)(2,1)S(1)}, bf16[256,1280]{1,0:T(8,128)(2,1)S(1)}, u32[]{:S(2)}, u32[]{:S(2)}) collective-permute-start(bf16[256,1280]{1,0:T(8,128)(2,1)S(1)} %get-tuple-element.45.inner_ref), channel_id=1, source_target_pairs={{0,1},{1,0},{2,3},{3,2},{4,5},{5,4},{6,7},{7,6},{8,9},{9,8},{10,11... | collective-permute-start | bytes 1966088 | tf_op jit(solution)/shard_map/ppermute | solution.py:32
  20.2 2.5 %collective-permute-start.2 = (bf16[128,1024]{1,0:T(8,128)(2,1)S(1)}, bf16[128,1024]{1,0:T(8,128)(2,1)S(1)}, u32[]{:S(2)}, u32[]{:S(2)}) collective-permute-start(bf16[128,1024]{1,0:T(8,128)(2,1)S(1)} %get-tuple-element.47), channel_id=1, source_target_pairs={{0,1},{1,0},{2,3},{3,2},{4,5},{5,4},{6,7},{7,6},{8,9},{9,8},{10,11... | collective-permute-start | bytes 786440 | tf_op jit(solution)/shard_map/ppermute | solution.py:32
  22.7 10.1 %collective-permute-start.5 = (bf16[128,1024]{1,0:T(8,128)(2,1)S(1)}, bf16[128,1024]{1,0:T(8,128)(2,1)S(1)}, u32[]{:S(2)}, u32[]{:S(2)}) collective-permute-start(bf16[128,1024]{1,0:T(8,128)(2,1)S(1)} %pair_sum.3.after.a_ref), channel_id=1, source_target_pairs={{0,2},{1,3},{2,0},{3,1},{4,6},{5,7},{6,4},{7,5},{8,10},{9,11},{10,... | collective-permute-start | bytes 786440 | tf_op jit(solution)/shard_map/ppermute | solution.py:32
  26.2 13.5 %collective-permute-start.4 = (bf16[128,1280]{1,0:T(8,128)(2,1)S(1)}, bf16[128,1280]{1,0:T(8,128)(2,1)S(1)}, u32[]{:S(2)}, u32[]{:S(2)}) collective-permute-start(bf16[128,1280]{1,0:T(8,128)(2,1)S(1)} %get-tuple-element.48.after.a_ref), channel_id=1, source_target_pairs={{0,2},{1,3},{2,0},{3,1},{4,6},{5,7},{6,4},{7,5},{8,10},{9,11},{10,... | collective-permute-start | bytes 983048 | tf_op jit(solution)/shard_map/ppermute | solution.py:32
  26.7 9.0 %collective-permute-start.10 = (bf16[272,256]{1,0:T(8,128)(2,1)S(1)}, bf16[272,256]{1,0:T(8,128)(2,1)S(1)}, u32[]{:S(2)}, u32[]{:S(2)}) collective-permute-start(bf16[272,256]{1,0:T(8,128)(2,1)S(1)} %get-tuple-element.53.a_ref), channel_id=1, source_target_pairs={{0,8},{4,12},{8,0},{12,4},{1,9},{5,13},{9,1},{13,5},{2,10},{6,14},... | collective-permute-start | bytes 417800 | tf_op jit(solution)/shard_map/ppermute | solution.py:32
  32.9 2.0 %collective-permute-start.6 = (bf16[128,256]{1,0:T(8,128)(2,1)S(1)}, bf16[128,256]{1,0:T(8,128)(2,1)S(1)}, u32[]{:S(2)}, u32[]{:S(2)}) collective-permute-start(bf16[128,256]{1,0:T(8,128)(2,1)S(1)} %get-tuple-element.49.after.refs_0_), channel_id=1, source_target_pairs={{0,1},{1,0},{2,3},{3,2},{4,5},{5,4},{6,7},{7,6},{8,9},{9,8},{10,11... | collective-permute-start | bytes 196616 | tf_op jit(solution)/shard_map/ppermute | solution.py:32
  33.0 9.7 %collective-permute-start.3 = (bf16[256,256]{1,0:T(8,128)(2,1)S(1)}, bf16[256,256]{1,0:T(8,128)(2,1)S(1)}, u32[]{:S(2)}, u32[]{:S(2)}) collective-permute-start(bf16[256,256]{1,0:T(8,128)(2,1)S(1)} %attention_forward.1.after.a_ref), channel_id=1, source_target_pairs={{0,8},{4,12},{8,0},{12,4},{1,9},{5,13},{9,1},{13,5},{2,10},{6,14},... | collective-permute-start | bytes 393224 | tf_op jit(solution)/shard_map/ppermute | solution.py:32
  34.8 1.3 %collective-permute-start.7 = (bf16[128,256]{1,0:T(8,128)(2,1)S(1)}, bf16[128,256]{1,0:T(8,128)(2,1)S(1)}, u32[]{:S(2)}, u32[]{:S(2)}) collective-permute-start(bf16[128,256]{1,0:T(8,128)(2,1)S(1)} %get-tuple-element.50.refs_1_), channel_id=1, source_target_pairs={{0,1},{1,0},{2,3},{3,2},{4,5},{5,4},{6,7},{7,6},{8,9},{9,8},{10,11... | collective-permute-start | bytes 196616 | tf_op jit(solution)/shard_map/ppermute | solution.py:32
  34.9 2.7 %collective-permute-start.8 = (bf16[128,256]{1,0:T(8,128)(2,1)S(1)}, bf16[128,256]{1,0:T(8,128)(2,1)S(1)}, u32[]{:S(2)}, u32[]{:S(2)}) collective-permute-start(bf16[128,256]{1,0:T(8,128)(2,1)S(1)} %get-tuple-element.51.refs_2_), channel_id=1, source_target_pairs={{0,1},{1,0},{2,3},{3,2},{4,5},{5,4},{6,7},{7,6},{8,9},{9,8},{10,11... | collective-permute-start | bytes 196616 | tf_op jit(solution)/shard_map/ppermute | solution.py:32
  35.8 1.8 %collective-permute-start.9 = (bf16[128,256]{1,0:T(8,128)(2,1)S(1)}, bf16[128,256]{1,0:T(8,128)(2,1)S(1)}, u32[]{:S(2)}, u32[]{:S(2)}) collective-permute-start(bf16[128,256]{1,0:T(8,128)(2,1)S(1)} %get-tuple-element.52.refs_3_), channel_id=1, source_target_pairs={{0,1},{1,0},{2,3},{3,2},{4,5},{5,4},{6,7},{7,6},{8,9},{9,8},{10,11... | collective-permute-start | bytes 196616 | tf_op jit(solution)/shard_map/ppermute | solution.py:32
  36.0 7.7 %collective-permute-start.12 = (bf16[272,256]{1,0:T(8,128)(2,1)S(1)}, bf16[272,256]{1,0:T(8,128)(2,1)S(1)}, u32[]{:S(2)}, u32[]{:S(2)}) collective-permute-start(bf16[272,256]{1,0:T(8,128)(2,1)S(1)} %sum_with_gain.1.refs_8_.a_ref.x_ref), channel_id=1, source_target_pairs={{0,4},{4,0},{8,12},{12,8},{1,5},{5,1},{9,13},{13,9},{2,6},{6,2},{1... | collective-permute-start | bytes 417800 | tf_op jit(solution)/shard_map/ppermute | solution.py:32
  39.6 5.6 %copy-start.5 = (f32[1,4096]{1,0:T(1,128)S(1)}, f32[1,4096]{1,0:T(1,128)}, u32[]{:S(2)}) copy-start(f32[1,4096]{1,0:T(1,128)} %gain_ref.1) | copy-start | bytes 49156
  39.7 5.5 %collective-permute-start.14 = (bf16[128,512]{1,0:T(8,128)(2,1)S(1)}, bf16[128,512]{1,0:T(8,128)(2,1)S(1)}, u32[]{:S(2)}, u32[]{:S(2)}) collective-permute-start(bf16[128,512]{1,0:T(8,128)(2,1)S(1)} %get-tuple-element.54.after.refs_0_), channel_id=1, source_target_pairs={{0,1},{1,0},{2,3},{3,2},{4,5},{5,4},{6,7},{7,6},{8,9},{9,8},{10,11... | collective-permute-start | bytes 393224 | tf_op jit(solution)/shard_map/ppermute | solution.py:32
  39.8 5.4 %collective-permute-start.15 = (bf16[128,512]{1,0:T(8,128)(2,1)S(1)}, bf16[128,512]{1,0:T(8,128)(2,1)S(1)}, u32[]{:S(2)}, u32[]{:S(2)}) collective-permute-start(bf16[128,512]{1,0:T(8,128)(2,1)S(1)} %get-tuple-element.57.refs_1_), channel_id=1, source_target_pairs={{0,1},{1,0},{2,3},{3,2},{4,5},{5,4},{6,7},{7,6},{8,9},{9,8},{10,11... | collective-permute-start | bytes 393224 | tf_op jit(solution)/shard_map/ppermute | solution.py:32
  42.8 5.1 %collective-permute-start.11 = (bf16[256,256]{1,0:T(8,128)(2,1)S(1)}, bf16[256,256]{1,0:T(8,128)(2,1)S(1)}, u32[]{:S(2)}, u32[]{:S(2)}) collective-permute-start(bf16[256,256]{1,0:T(8,128)(2,1)S(1)} %pair_sum.4.after.y_ref), channel_id=1, source_target_pairs={{0,4},{4,0},{8,12},{12,8},{1,5},{5,1},{9,13},{13,9},{2,6},{6,2},{1... | collective-permute-start | bytes 393224 | tf_op jit(solution)/shard_map/ppermute | solution.py:32
  42.9 2.3 %collective-permute-start.16 = (bf16[128,256]{1,0:T(8,128)(2,1)S(1)}, bf16[128,256]{1,0:T(8,128)(2,1)S(1)}, u32[]{:S(2)}, u32[]{:S(2)}) collective-permute-start(bf16[128,256]{1,0:T(8,128)(2,1)S(1)} %get-tuple-element.58.refs_2_), channel_id=1, source_target_pairs={{0,1},{1,0},{2,3},{3,2},{4,5},{5,4},{6,7},{7,6},{8,9},{9,8},{10,11... | collective-permute-start | bytes 196616 | tf_op jit(solution)/shard_map/ppermute | solution.py:32
  43.7 3.8 %collective-permute-start.13 = (f32[8,256]{1,0:T(8,128)S(1)}, f32[8,256]{1,0:T(8,128)S(1)}, u32[]{:S(2)}, u32[]{:S(2)}) collective-permute-start(f32[8,256]{1,0:T(8,128)S(1)} %gain_total.1.refs_6_.a_ref), channel_id=1, source_target_pairs={{0,2},{1,3},{2,0},{3,1},{4,6},{5,7},{6,4},{7,5},{8,10},{9,11},{10,... | collective-permute-start | bytes 24584 | tf_op jit(solution)/shard_map/ppermute | solution.py:32
  47.4 1.2 %collective-permute-start.17 = (f32[8,256]{1,0:T(8,128)S(1)}, f32[8,256]{1,0:T(8,128)S(1)}, u32[]{:S(2)}, u32[]{:S(2)}) collective-permute-start(f32[8,256]{1,0:T(8,128)S(1)} %pair_sum.5.gain_ref), channel_id=1, source_target_pairs={{0,1},{1,0},{2,3},{3,2},{4,5},{5,4},{6,7},{7,6},{8,9},{9,8},{10,11... | collective-permute-start | bytes 24584 | tf_op jit(solution)/shard_map/ppermute | solution.py:32

commit v14 on v12

--- a/solution.py
+++ b/solution.py
@@ -129,12 +129,13 @@
         start_to(n + 1 + AHEAD)
         copies[n].wait()
 
-    start_to(2 + parts + AHEAD)
+    start_to(2 + parts + 1)
     copies[0].wait()
     copies[1].wait()
     square = jnp.zeros((back.shape[0], HD), F32)
     for i, at in enumerate(pieces):
         copies[2 + i].wait()
+        start_to(2 + parts + 2 + i)
         turned[:, at] = u[at, :].T
         scaled[:, at] = (turned[:, at].astype(F32) * gain[:, at]).astype(BF)
         decoded = nn(back[...], turned[:, at])

time: 49.2 us -> 49.3 us (level)
  no operation moved by 1% of the time
where the time goes in v14:
time: 49.3 us; the launch traced here: 49.1 us
  Pallas kernels  28.1 us (57%)
  starting transfers between devices  14.2 us (29%)
  waiting for transfers between devices  5.09 us (10%)
  other arithmetic  0.93 us (2%)
  between operations  0.83 us (2%)
    ppermute x16, starting transfers between devices, swap(): return lax.ppermute(x, axis, [(i, i ^ bit) for i in range(devices)])  14.2 us
    pallas_call x1, Pallas kernels, project(): pl.pallas_call(project_kernel, in_specs=[pl.BlockSpec(memory_space=pltpu....  10.6 us
    ppermute x16, waiting for transfers between devices, swap(): return lax.ppermute(x, axis, [(i, i ^ bit) for i in range(devices)])  5.09 us
    pallas_call x1, Pallas kernels, backward(): pl.pallas_call(backward_kernel, in_specs=vmem(8), out_specs=vmem(4), out_...  4.88 us
    pallas_call x1, Pallas kernels, forward(): pl.pallas_call(forward_kernel, in_specs=vmem(7) + [pl.BlockSpec(memory_sp...  3.51 us
    pallas_call x1, Pallas kernels, inward_grads(): pl.pallas_call(functools.partial(inward_kernel, len(own)), grid=(STEPS,),...  2.22 us
    pallas_call x1, Pallas kernels, outward_grad(): pl.pallas_call(functools.partial(outward_kernel, len(own)), grid=(STEPS,)...  2.01 us
    pallas_call x1, Pallas kernels, gain_part(): pl.pallas_call(gain_kernel, in_specs=vmem(6) + [pl.BlockSpec(memory_space...  1.85 us
  transfers between devices with their start and end apart: 16, of which 5 were waited for; matrix products, arithmetic and copies ran while one was open for 0% of the time, Pallas kernels for 45%

profile of v14, /device:TPU:0, one launch (start us, length us, event | category | flops | bytes accessed | tf_op | source)
XLA Modules:
  0.0 49.1 jit_solution(12395685319495430053)
XLA Ops:
  0.6 0.9 %select_bitcast_fusion = bf16[256,256]{1,0:T(8,128)(2,1)S(1)} fusion(bf16[1,256,256]{2,1,0:T(8,128)(2,1)} %param.15, bf16[1,256,256]{2,1,0:T(8,128)(2,1)} %param.16, pred[]{:T(512)S(6)} %eq.3), kind=kLoop, calls=%fused_computation | loop fusion | flops 65536 | bytes 393217 | tf_op jit(solution)/shard_map/jit(_where)/select_n | solution.py:39
  1.6 3.0 %collective-permute-start = (bf16[256,256]{1,0:T(8,128)(2,1)S(1)}, bf16[256,256]{1,0:T(8,128)(2,1)S(1)}, u32[]{:S(2)}, u32[]{:S(2)}) collective-permute-start(bf16[256,256]{1,0:T(8,128)(2,1)S(1)} %select_bitcast_fusion), channel_id=1, source_target_pairs={{0,16},{16,0},{1,17},{17,1},{2,18},{18,2},{3,19},{19,3},{4,20},{20... | collective-permute-start | bytes 393224 | tf_op jit(solution)/shard_map/ppermute | solution.py:32
  4.6 10.6 %project_weights.1 = (bf16[512,1280]{1,0:T(8,128)(2,1)S(1)}, bf16[1024,256]{1,0:T(8,128)(2,1)S(1)}, f32[256,128]{1,0:T(8,128)S(1)}, bf16[4096,256]{1,0:T(8,128)(...) custom-call(bf16[256,256]{1,0:T(8,128)(2,1)} %bitcast.13, ...), custom_call_target="tpu_custom_call" | custom-call | flops 6000000000 | bytes 20000000 | tf_op jit(solution)/shard_map/project_weights/pallas_call | solution.py:178
  15.3 4.9 %attention_backward.1 = (bf16[256,1280]{1,0:T(8,128)(2,1)S(1)}, bf16[128,1024]{1,0:T(8,128)(2,1)S(1)}, bf16[128,1024]{1,0:T(8,128)(2,1)S(1)}, bf16[256,256]{1,0:T(8,128)(2,1)S(1)}) custom-call(bf16[256,256]{1,0:T(8,128)(2,1)S(1)} %bitcast.14, bf16[256,256]{1,0:T(8,128)(2,1)S(1)} %copy-done.1, ...), custom_call_target="tpu_custom_call" | custom-call | flops 10000 | bytes 1000 | tf_op jit(solution)/shard_map/attention_backward/pallas_call | solution.py:302
  20.3 0.5 %collective-permute-start.2 = (bf16[128,1024]{1,0:T(8,128)(2,1)S(1)}, bf16[128,1024]{1,0:T(8,128)(2,1)S(1)}, u32[]{:S(2)}, u32[]{:S(2)}) collective-permute-start(bf16[128,1024]{1,0:T(8,128)(2,1)S(1)} %get-tuple-element.45), channel_id=1, source_target_pairs={{0,1},{1,0},{2,3},{3,2},{4,5},{5,4},{6,7},{7,6},{8,9},{9,8},{10,11... | collective-permute-start | bytes 786440 | tf_op jit(solution)/shard_map/ppermute | solution.py:32
  20.8 1.7 %encoded_again.1 = (f32[256,256]{1,0:T(8,128)S(1)}, f32[256,256]{1,0:T(8,128)S(1)}, f32[256,256]{1,0:T(8,128)S(1)}) custom-call(bf16[256,256]{1,0:T(8,128)(2,1)S(1)} %bitcast.15, bf16[256,256]{1,0:T(8,128)(2,1)S(1)} %copy-done.1, bf16[256,256]{1,0:T(8,128)(2,1)S(1)} %collective-permute-done.sent_ref.returned_ref.arrived_ref, bf16[256,256]{1,0:T(8,128)(2,1)S(1)} %copy-done.2, ...), custom_call_target="tpu_custom_call" | custom-call | flops 10000 | bytes 1000 | tf_op jit(solution)/shard_map/encoded_again/pallas_call | solution.py:353
  22.5 0.2 collective-permute-done.2.b_ref
  22.8 1.6 %collective-permute-start.5 = (bf16[128,1024]{1,0:T(8,128)(2,1)S(1)}, bf16[128,1024]{1,0:T(8,128)(2,1)S(1)}, u32[]{:S(2)}, u32[]{:S(2)}) collective-permute-start(bf16[128,1024]{1,0:T(8,128)(2,1)S(1)} %pair_sum.3.after.a_ref), channel_id=1, source_target_pairs={{0,2},{1,3},{2,0},{3,1},{4,6},{5,7},{6,4},{7,5},{8,10},{9,11},{10,... | collective-permute-start | bytes 786440 | tf_op jit(solution)/shard_map/ppermute | solution.py:32
  24.4 1.8 %pair_sum_and_gain_gradient.1 = (bf16[128,1280]{1,0:T(8,128)(2,1)S(1)}, bf16[272,256]{1,0:T(8,128)(2,1)S(1)}) custom-call(bf16[4096,256]{1,0:T(8,128)(2,1)S(1)} %get-tuple-element.34.u_ref, bf16[4096,1024]{1,0:T(8,128)(2,1)S(1)} %get-tuple-element.41.wq_ref, bf16[4096,256]{1,0:T(8,128)(2,1)S(1)} %get-tuple-element.42.narrow_ref, ...), custom_call_target="tpu_custom_call" | custom-call | flops 10000 | bytes 1000 | tf_op jit(solution)/shard_map/pair_sum_and_gain_gradient/pallas_call | solution.py:457
  26.2 0.6 %collective-permute-start.4 = (bf16[128,1280]{1,0:T(8,128)(2,1)S(1)}, bf16[128,1280]{1,0:T(8,128)(2,1)S(1)}, u32[]{:S(2)}, u32[]{:S(2)}) collective-permute-start(bf16[128,1280]{1,0:T(8,128)(2,1)S(1)} %get-tuple-element.46.after.a_ref), channel_id=1, source_target_pairs={{0,2},{1,3},{2,0},{3,1},{4,6},{5,7},{6,4},{7,5},{8,10},{9,11},{10,... | collective-permute-start | bytes 983048 | tf_op jit(solution)/shard_map/ppermute | solution.py:32
  26.8 2.6 %collective-permute-start.8 = (bf16[272,256]{1,0:T(8,128)(2,1)S(1)}, bf16[272,256]{1,0:T(8,128)(2,1)S(1)}, u32[]{:S(2)}, u32[]{:S(2)}) collective-permute-start(bf16[272,256]{1,0:T(8,128)(2,1)S(1)} %get-tuple-element.49.a_ref), channel_id=1, source_target_pairs={{0,8},{4,12},{8,0},{12,4},{1,9},{5,13},{9,1},{13,5},{2,10},{6,14},... | collective-permute-start | bytes 417800 | tf_op jit(solution)/shard_map/ppermute | solution.py:32
  29.4 3.5 %attention_forward.1.after.a_ref = bf16[256,256]{1,0:T(8,128)(2,1)S(1)} custom-call(bf16[256,256]{1,0:T(8,128)(2,1)S(1)} %copy-done.2, bf16[256,256]{1,0:T(8,128)(2,1)S(1)} %collective-permute-done.sent_ref.returned_ref.arrived_ref, bf16[256,4096]{1,0:T(8,128)(2,1)S(1)} %get-tuple-element.35.turned_ref, bf16[512,1280]{1,0:T(8,128)(2,1)S(1)} %get-tuple-element.37.m_ref, ...), custom_call_target="tpu_custom_call" | custom-call | flops 10000 | bytes 1000 | tf_op jit(solution)/shard_map/attention_forward/pallas_call | solution.py:394
  33.1 0.5 %collective-permute-start.7 = (bf16[128,512]{1,0:T(8,128)(2,1)S(1)}, bf16[128,512]{1,0:T(8,128)(2,1)S(1)}, u32[]{:S(2)}, u32[]{:S(2)}) collective-permute-start(bf16[128,512]{1,0:T(8,128)(2,1)S(1)} %get-tuple-element.48.refs_1_), channel_id=1, source_target_pairs={{0,1},{1,0},{2,3},{3,2},{4,5},{5,4},{6,7},{7,6},{8,9},{9,8},{10,11... | collective-permute-start | bytes 393224 | tf_op jit(solution)/shard_map/ppermute | solution.py:32
  33.6 1.7 %collective-permute-start.3 = (bf16[256,256]{1,0:T(8,128)(2,1)S(1)}, bf16[256,256]{1,0:T(8,128)(2,1)S(1)}, u32[]{:S(2)}, u32[]{:S(2)}) collective-permute-start(bf16[256,256]{1,0:T(8,128)(2,1)S(1)} %attention_forward.1.after.a_ref), channel_id=1, source_target_pairs={{0,8},{4,12},{8,0},{12,4},{1,9},{5,13},{9,1},{13,5},{2,10},{6,14},... | collective-permute-start | bytes 393224 | tf_op jit(solution)/shard_map/ppermute | solution.py:32
  35.2 0.6 %collective-permute-done.8.b_ref = bf16[272,256]{1,0:T(8,128)(2,1)S(1)} collective-permute-done((bf16[272,256]{1,0:T(8,128)(2,1)S(1)}, bf16[272,256]{1,0:T(8,128)(2,1)S(1)}, u32[]{:S(2)}, u32[]{:S(2)}) %collective-permute-start.8) | collective-permute-done | bytes 139296 | tf_op jit(solution)/shard_map/ppermute | solution.py:32
  35.9 1.1 %collective-permute-start.10 = (bf16[272,256]{1,0:T(8,128)(2,1)S(1)}, bf16[272,256]{1,0:T(8,128)(2,1)S(1)}, u32[]{:S(2)}, u32[]{:S(2)}) collective-permute-start(bf16[272,256]{1,0:T(8,128)(2,1)S(1)} %sum_with_gain.1.refs_4_.a_ref.x_ref), channel_id=1, source_target_pairs={{0,4},{4,0},{8,12},{12,8},{1,5},{5,1},{9,13},{13,9},{2,6},{6,2},{1... | collective-permute-start | bytes 417800 | tf_op jit(solution)/shard_map/ppermute | solution.py:32
  36.9 2.0 %output_weight_gradient.1.after = bf16[1024,1024]{1,0:T(8,128)(2,1)} custom-call(bf16[4096,256]{1,0:T(8,128)(2,1)S(1)} %get-tuple-element.34.u_ref, bf16[128,512]{1,0:T(8,128)(2,1)S(1)} %get-tuple-element.47.after.refs_0_, bf16[128,512]{1,0:T(8,128)(2,1)S(1)} %get-tuple-element.48.refs_1_, bf16[128,512]{1,0:T(8,128)(2,1)S(1)} %collective-permute-done.6.refs_2_, ...), custom_call_target="tpu_custom_call" | custom-call | flops 10000 | bytes 1000 | tf_op jit(solution)/shard_map/output_weight_gradient/pallas_call | solution.py:597
  39.1 0.5 %collective-permute-start.13 = (bf16[128,512]{1,0:T(8,128)(2,1)S(1)}, bf16[128,512]{1,0:T(8,128)(2,1)S(1)}, u32[]{:S(2)}, u32[]{:S(2)}) collective-permute-start(bf16[128,512]{1,0:T(8,128)(2,1)S(1)} %get-tuple-element.53.refs_1_), channel_id=1, source_target_pairs={{0,1},{1,0},{2,3},{3,2},{4,5},{5,4},{6,7},{7,6},{8,9},{9,8},{10,11... | collective-permute-start | bytes 393224 | tf_op jit(solution)/shard_map/ppermute | solution.py:32
  39.6 3.3 %collective-permute-done.3.b_ref = bf16[256,256]{1,0:T(8,128)(2,1)S(1)} collective-permute-done((bf16[256,256]{1,0:T(8,128)(2,1)S(1)}, bf16[256,256]{1,0:T(8,128)(2,1)S(1)}, u32[]{:S(2)}, u32[]{:S(2)}) %collective-permute-start.3) | collective-permute-done | bytes 131104 | tf_op jit(solution)/shard_map/ppermute | solution.py:32
  43.1 1.6 %collective-permute-start.11 = (f32[8,256]{1,0:T(8,128)S(1)}, f32[8,256]{1,0:T(8,128)S(1)}, u32[]{:S(2)}, u32[]{:S(2)}) collective-permute-start(f32[8,256]{1,0:T(8,128)S(1)} %gain_total.1.refs_6_.a_ref), channel_id=1, source_target_pairs={{0,2},{1,3},{2,0},{3,1},{4,6},{5,7},{6,4},{7,5},{8,10},{9,11},{10,... | collective-permute-start | bytes 24584 | tf_op jit(solution)/shard_map/ppermute | solution.py:32
  44.7 2.2 %inward_weight_gradients.1 = (bf16[1024,1024]{1,0:T(8,128)(2,1)}, bf16[1024,128]{1,0:T(8,128)(2,1)}, bf16[1024,128]{1,0:T(8,128)(2,1)}) custom-call(bf16[4096,256]{1,0:T(8,128)(2,1)S(1)} %get-tuple-element.34.u_ref, f32[1,4096]{1,0:T(1,128)S(1)} %copy-done.5, bf16[128,512]{1,0:T(8,128)(2,1)S(1)} %get-tuple-element.50.after.refs_0_, ...), custom_call_target="tpu_custom_call" | custom-call | flops 10000 | bytes 1000 | tf_op jit(solution)/shard_map/inward_weight_gradients/pallas_call | solution.py:580
  46.9 0.2 collective-permute-start.15
  47.1 0.8 %collective-permute-done.9.ygot_ref = bf16[256,256]{1,0:T(8,128)(2,1)S(1)} collective-permute-done((bf16[256,256]{1,0:T(8,128)(2,1)S(1)}, bf16[256,256]{1,0:T(8,128)(2,1)S(1)}, u32[]{:S(2)}, u32[]{:S(2)}) %collective-permute-start.9) | collective-permute-done | bytes 131104 | tf_op jit(solution)/shard_map/ppermute | solution.py:32
  48.1 1.0 %section_results.1 = (bf16[256,256]{1,0:T(8,128)(2,1)}, bf16[256,256]{1,0:T(8,128)(2,1)}, f32[1,4096]{1,0:T(1,128)}) custom-call(f32[256,256]{1,0:T(8,128)S(1)} %get-tuple-element.40.after.fbase_ref, bf16[256,256]{1,0:T(8,128)(2,1)S(1)} %pair_sum.4.after.y_ref, bf16[256,256]{1,0:T(8,128)(2,1)S(1)} %collective-permute-done.9.ygot_ref, ...), custom_call_target="tpu_custom_call" | custom-call | flops 10000 | bytes 1000 | tf_op jit(solution)/shard_map/section_results/pallas_call | solution.py:635
  (36 shorter events, 0.9 us)
Async XLA Ops:
  1.6 13.7 %collective-permute-start = (bf16[256,256]{1,0:T(8,128)(2,1)S(1)}, bf16[256,256]{1,0:T(8,128)(2,1)S(1)}, u32[]{:S(2)}, u32[]{:S(2)}) collective-permute-start(bf16[256,256]{1,0:T(8,128)(2,1)S(1)} %select_bitcast_fusion), channel_id=1, source_target_pairs={{0,16},{16,0},{1,17},{17,1},{2,18},{18,2},{3,19},{19,3},{4,20},{20... | collective-permute-start | bytes 393224 | tf_op jit(solution)/shard_map/ppermute | solution.py:32
  4.6 10.7 %copy-start = (bf16[1,256,256]{2,1,0:T(8,128)(2,1)S(1)}, bf16[1,256,256]{2,1,0:T(8,128)(2,1)}, u32[]{:S(2)}) copy-start(bf16[1,256,256]{2,1,0:T(8,128)(2,1)} %param.17) | copy-start | bytes 393220
  4.6 10.7 %copy-start.1 = (bf16[256,256]{1,0:T(8,128)(2,1)S(1)}, bf16[256,256]{1,0:T(8,128)(2,1)}, u32[]{:S(2)}) copy-start(bf16[256,256]{1,0:T(8,128)(2,1)} %loss_ref.3) | copy-start | bytes 393220
  4.6 10.7 %copy-start.3 = (f32[256,128]{1,0:T(8,128)S(1)}, f32[256,128]{1,0:T(8,128)}, u32[]{:S(2)}) copy-start(f32[256,128]{1,0:T(8,128)} %constant.12.clone.cos_ref) | copy-start | bytes 393220
  4.6 10.7 %copy-start.4 = (f32[256,128]{1,0:T(8,128)S(1)}, f32[256,128]{1,0:T(8,128)}, u32[]{:S(2)}) copy-start(f32[256,128]{1,0:T(8,128)} %constant.13.clone.sin_ref) | copy-start | bytes 393220
  15.2 5.5 %copy-start.2 = (bf16[256,256]{1,0:T(8,128)(2,1)S(1)}, bf16[256,256]{1,0:T(8,128)(2,1)}, u32[]{:S(2)}) copy-start(bf16[256,256]{1,0:T(8,128)(2,1)} %new_ref.3) | copy-start | bytes 393220
  20.2 4.2 %collective-permute-start.1 = (bf16[256,1280]{1,0:T(8,128)(2,1)S(1)}, bf16[256,1280]{1,0:T(8,128)(2,1)S(1)}, u32[]{:S(2)}, u32[]{:S(2)}) collective-permute-start(bf16[256,1280]{1,0:T(8,128)(2,1)S(1)} %get-tuple-element.43.inner_ref), channel_id=1, source_target_pairs={{0,1},{1,0},{2,3},{3,2},{4,5},{5,4},{6,7},{7,6},{8,9},{9,8},{10,11... | collective-permute-start | bytes 1966088 | tf_op jit(solution)/shard_map/ppermute | solution.py:32
  20.3 2.5 %collective-permute-start.2 = (bf16[128,1024]{1,0:T(8,128)(2,1)S(1)}, bf16[128,1024]{1,0:T(8,128)(2,1)S(1)}, u32[]{:S(2)}, u32[]{:S(2)}) collective-permute-start(bf16[128,1024]{1,0:T(8,128)(2,1)S(1)} %get-tuple-element.45), channel_id=1, source_target_pairs={{0,1},{1,0},{2,3},{3,2},{4,5},{5,4},{6,7},{7,6},{8,9},{9,8},{10,11... | collective-permute-start | bytes 786440 | tf_op jit(solution)/shard_map/ppermute | solution.py:32
  22.8 10.1 %collective-permute-start.5 = (bf16[128,1024]{1,0:T(8,128)(2,1)S(1)}, bf16[128,1024]{1,0:T(8,128)(2,1)S(1)}, u32[]{:S(2)}, u32[]{:S(2)}) collective-permute-start(bf16[128,1024]{1,0:T(8,128)(2,1)S(1)} %pair_sum.3.after.a_ref), channel_id=1, source_target_pairs={{0,2},{1,3},{2,0},{3,1},{4,6},{5,7},{6,4},{7,5},{8,10},{9,11},{10,... | collective-permute-start | bytes 786440 | tf_op jit(solution)/shard_map/ppermute | solution.py:32
  26.2 12.7 %collective-permute-start.4 = (bf16[128,1280]{1,0:T(8,128)(2,1)S(1)}, bf16[128,1280]{1,0:T(8,128)(2,1)S(1)}, u32[]{:S(2)}, u32[]{:S(2)}) collective-permute-start(bf16[128,1280]{1,0:T(8,128)(2,1)S(1)} %get-tuple-element.46.after.a_ref), channel_id=1, source_target_pairs={{0,2},{1,3},{2,0},{3,1},{4,6},{5,7},{6,4},{7,5},{8,10},{9,11},{10,... | collective-permute-start | bytes 983048 | tf_op jit(solution)/shard_map/ppermute | solution.py:32
  26.8 9.0 %collective-permute-start.8 = (bf16[272,256]{1,0:T(8,128)(2,1)S(1)}, bf16[272,256]{1,0:T(8,128)(2,1)S(1)}, u32[]{:S(2)}, u32[]{:S(2)}) collective-permute-start(bf16[272,256]{1,0:T(8,128)(2,1)S(1)} %get-tuple-element.49.a_ref), channel_id=1, source_target_pairs={{0,8},{4,12},{8,0},{12,4},{1,9},{5,13},{9,1},{13,5},{2,10},{6,14},... | collective-permute-start | bytes 417800 | tf_op jit(solution)/shard_map/ppermute | solution.py:32
  33.0 3.9 %collective-permute-start.6 = (bf16[128,512]{1,0:T(8,128)(2,1)S(1)}, bf16[128,512]{1,0:T(8,128)(2,1)S(1)}, u32[]{:S(2)}, u32[]{:S(2)}) collective-permute-start(bf16[128,512]{1,0:T(8,128)(2,1)S(1)} %get-tuple-element.47.after.refs_0_), channel_id=1, source_target_pairs={{0,1},{1,0},{2,3},{3,2},{4,5},{5,4},{6,7},{7,6},{8,9},{9,8},{10,11... | collective-permute-start | bytes 393224 | tf_op jit(solution)/shard_map/ppermute | solution.py:32
  33.1 3.9 %collective-permute-start.7 = (bf16[128,512]{1,0:T(8,128)(2,1)S(1)}, bf16[128,512]{1,0:T(8,128)(2,1)S(1)}, u32[]{:S(2)}, u32[]{:S(2)}) collective-permute-start(bf16[128,512]{1,0:T(8,128)(2,1)S(1)} %get-tuple-element.48.refs_1_), channel_id=1, source_target_pairs={{0,1},{1,0},{2,3},{3,2},{4,5},{5,4},{6,7},{7,6},{8,9},{9,8},{10,11... | collective-permute-start | bytes 393224 | tf_op jit(solution)/shard_map/ppermute | solution.py:32
  33.6 9.3 %collective-permute-start.3 = (bf16[256,256]{1,0:T(8,128)(2,1)S(1)}, bf16[256,256]{1,0:T(8,128)(2,1)S(1)}, u32[]{:S(2)}, u32[]{:S(2)}) collective-permute-start(bf16[256,256]{1,0:T(8,128)(2,1)S(1)} %attention_forward.1.after.a_ref), channel_id=1, source_target_pairs={{0,8},{4,12},{8,0},{12,4},{1,9},{5,13},{9,1},{13,5},{2,10},{6,14},... | collective-permute-start | bytes 393224 | tf_op jit(solution)/shard_map/ppermute | solution.py:32
  35.9 7.2 %collective-permute-start.10 = (bf16[272,256]{1,0:T(8,128)(2,1)S(1)}, bf16[272,256]{1,0:T(8,128)(2,1)S(1)}, u32[]{:S(2)}, u32[]{:S(2)}) collective-permute-start(bf16[272,256]{1,0:T(8,128)(2,1)S(1)} %sum_with_gain.1.refs_4_.a_ref.x_ref), channel_id=1, source_target_pairs={{0,4},{4,0},{8,12},{12,8},{1,5},{5,1},{9,13},{13,9},{2,6},{6,2},{1... | collective-permute-start | bytes 417800 | tf_op jit(solution)/shard_map/ppermute | solution.py:32
  38.9 5.7 %copy-start.5 = (f32[1,4096]{1,0:T(1,128)S(1)}, f32[1,4096]{1,0:T(1,128)}, u32[]{:S(2)}) copy-start(f32[1,4096]{1,0:T(1,128)} %gain_ref.1) | copy-start | bytes 49156
  39.0 5.6 %collective-permute-start.12 = (bf16[128,512]{1,0:T(8,128)(2,1)S(1)}, bf16[128,512]{1,0:T(8,128)(2,1)S(1)}, u32[]{:S(2)}, u32[]{:S(2)}) collective-permute-start(bf16[128,512]{1,0:T(8,128)(2,1)S(1)} %get-tuple-element.50.after.refs_0_), channel_id=1, source_target_pairs={{0,1},{1,0},{2,3},{3,2},{4,5},{5,4},{6,7},{7,6},{8,9},{9,8},{10,11... | collective-permute-start | bytes 393224 | tf_op jit(solution)/shard_map/ppermute | solution.py:32
  39.1 5.6 %collective-permute-start.13 = (bf16[128,512]{1,0:T(8,128)(2,1)S(1)}, bf16[128,512]{1,0:T(8,128)(2,1)S(1)}, u32[]{:S(2)}, u32[]{:S(2)}) collective-permute-start(bf16[128,512]{1,0:T(8,128)(2,1)S(1)} %get-tuple-element.53.refs_1_), channel_id=1, source_target_pairs={{0,1},{1,0},{2,3},{3,2},{4,5},{5,4},{6,7},{7,6},{8,9},{9,8},{10,11... | collective-permute-start | bytes 393224 | tf_op jit(solution)/shard_map/ppermute | solution.py:32
  42.9 5.0 %collective-permute-start.9 = (bf16[256,256]{1,0:T(8,128)(2,1)S(1)}, bf16[256,256]{1,0:T(8,128)(2,1)S(1)}, u32[]{:S(2)}, u32[]{:S(2)}) collective-permute-start(bf16[256,256]{1,0:T(8,128)(2,1)S(1)} %pair_sum.4.after.y_ref), channel_id=1, source_target_pairs={{0,4},{4,0},{8,12},{12,8},{1,5},{5,1},{9,13},{13,9},{2,6},{6,2},{1... | collective-permute-start | bytes 393224 | tf_op jit(solution)/shard_map/ppermute | solution.py:32
  43.0 1.7 %collective-permute-start.14 = (bf16[128,256]{1,0:T(8,128)(2,1)S(1)}, bf16[128,256]{1,0:T(8,128)(2,1)S(1)}, u32[]{:S(2)}, u32[]{:S(2)}) collective-permute-start(bf16[128,256]{1,0:T(8,128)(2,1)S(1)} %get-tuple-element.54.refs_2_), channel_id=1, source_target_pairs={{0,1},{1,0},{2,3},{3,2},{4,5},{5,4},{6,7},{7,6},{8,9},{9,8},{10,11... | collective-permute-start | bytes 196616 | tf_op jit(solution)/shard_map/ppermute | solution.py:32
  43.1 3.8 %collective-permute-start.11 = (f32[8,256]{1,0:T(8,128)S(1)}, f32[8,256]{1,0:T(8,128)S(1)}, u32[]{:S(2)}, u32[]{:S(2)}) collective-permute-start(f32[8,256]{1,0:T(8,128)S(1)} %gain_total.1.refs_6_.a_ref), channel_id=1, source_target_pairs={{0,2},{1,3},{2,0},{3,1},{4,6},{5,7},{6,4},{7,5},{8,10},{9,11},{10,... | collective-permute-start | bytes 24584 | tf_op jit(solution)/shard_map/ppermute | solution.py:32
  46.9 1.2 %collective-permute-start.15 = (f32[8,256]{1,0:T(8,128)S(1)}, f32[8,256]{1,0:T(8,128)S(1)}, u32[]{:S(2)}, u32[]{:S(2)}) collective-permute-start(f32[8,256]{1,0:T(8,128)S(1)} %pair_sum.5.gain_ref), channel_id=1, source_target_pairs={{0,1},{1,0},{2,3},{3,2},{4,5},{5,4},{6,7},{7,6},{8,9},{9,8},{10,11... | collective-permute-start | bytes 24584 | tf_op jit(solution)/shard_map/ppermute | solution.py:32
